TPU v7x, 32 devices: a whole 2x2x4 slice. The times are simulated.
32 devices in a mesh: space: 8 (over z, x), modes: 4 (over y, core).
Axes of the slice: x: 2, y: 2, z: 4, core: 2. Of those that a mesh axis runs over, the one named last changes fastest.
Arguments:
- mode_field: bfloat16 [16, 128, 256, 256], P('space', 'modes'), may hold values from -8 to 8
- diffusion: float32 [16, 256, 256], P('space'), may hold values from 0.1 to 0.16
- joule_load: float32 [16, 256, 256], P('space'), may hold values from 0.5 to 1.5
- chaos_basis: bfloat16 [343, 128], replicated, may hold values from -0.5 to 0.5
- quad_weight: float32 [343], replicated, may hold values from 0.25 to 1
- base_conductivity: float32 [343], replicated, may hold values from 0.5 to 2
- thermal_slope: float32 [343], replicated, may hold values from 0.2 to 0.8
Outputs:
- advanced: bfloat16 [16, 128, 256, 256], P('space', 'modes')
All inputs are finite; a program needn't handle non-finite values.
Results may differ from a plain program's by a relative error of at most 0.0054.
Values may be sent and summed in bfloat16 or wider, within the bound.
No kernel may reach another device: no remote copies, remote signals or barrier semaphores. Data moves between devices by JAX's collectives and lax.ppermute only.
A program may use at most 128 MiB of HBM per device.

v0:
```python
import jax
import jax.numpy as jnp
from jax import lax
from jax.sharding import PartitionSpec as P


def with_halo(x, sides, width):
    for axis, dim in sides:
        size, length = (lax.axis_size(axis), x.shape[dim])
        up = [(i, (i + 1) % size) for i in range(size - 1)]
        down = [(j, i) for i, j in up]
        last = lax.slice_in_dim(x, length - width, length, axis=dim)
        initial = lax.slice_in_dim(x, 0, width, axis=dim)
        before = lax.ppermute(last, axis, up)
        after = lax.ppermute(initial, axis, down)
        x = jnp.concatenate([before, x, after], axis=dim)
    return x


def advance(extended, rate_mid):
    middle = extended[1:-1]
    padded_xy = jnp.pad(middle, ((0, 0), (0, 0), (1, 1), (1, 1)))
    beside = extended[2:] + extended[:-2]
    beside = beside + padded_xy[:, :, 2:, 1:-1] + padded_xy[:, :, :-2, 1:-1]
    beside = beside + padded_xy[:, :, 1:-1, 2:] + padded_xy[:, :, 1:-1, :-2]
    return middle + rate_mid[:, None] * (beside - 6.0 * middle)


def on_device(
    mode_field, diffusion, joule_load, chaos_basis, quad_weight, base_conductivity, thermal_slope
):
    extended = with_halo(mode_field, (("space", 0),), 1).astype(jnp.float32)
    first = advance(extended, diffusion)
    second_ext = with_halo(first, (("space", 0),), 1)
    values = advance(second_ext, diffusion)
    settled = values.astype(jnp.bfloat16)
    point_temp = jnp.einsum(
        "qm,zmxy->zqxy",
        chaos_basis,
        lax.all_to_all(settled, "modes", split_axis=2, concat_axis=1, tiled=True),
        preferred_element_type=jnp.float32,
    )
    conductivity = base_conductivity[:, None, None] * (
        1.0 + thermal_slope[:, None, None] * jnp.tanh(point_temp)
    )
    weighted = (quad_weight[:, None, None] * conductivity).astype(jnp.bfloat16)
    summed = jnp.einsum("qm,zqxy->zmxy", chaos_basis, weighted, preferred_element_type=jnp.float32)
    cell_source = summed.astype(jnp.bfloat16)
    projected = lax.all_to_all(cell_source, "modes", split_axis=1, concat_axis=2, tiled=True)
    kept_modes = lax.optimization_barrier(settled).astype(jnp.float32)
    return (kept_modes + joule_load[:, None] * projected.astype(jnp.float32)).astype(jnp.bfloat16)


def solution(mesh):
    return jax.shard_map(
        on_device,
        mesh=mesh,
        in_specs=(
            P("space", "modes", None, None),
            P("space", None, None),
            P("space", None, None),
            P(),
            P(),
            P(),
            P(),
        ),
        out_specs=P("space", "modes", None, None),
        check_vma=False,
    )
```

profile of v0, /device:TPU:0, one launch (start us, length us, event | category | flops | bytes accessed | tf_op | source)
XLA Modules:
  0.0 961.0 jit_solution(12614685564426955366)
XLA Ops:
  0.0 0.0 copy-start
  0.0 3.9 fusion.33
  3.9 5.1 collective-permute-start
  9.1 1.3 collective-permute-start.1
  10.4 178.1 %collective-permute-done = bf16[1,32,256,256]{3,2,1,0:T(8,128)(2,1)S(1)} collective-permute-done((bf16[1,32,256,256]{3,2,1,0:T(8,128)(2,1)S(1)}, bf16[1,32,256,256]{3,2,1,0:T(8,128)(2,1)S(1)}, u32[]{:S(2)}, u32[]{:S(2)}) %collective-permute-start) | collective-permute-done | bytes 4194336 | tf_op jit(solution)/shard_map/ppermute | solution.py:14
  188.5 0.0 collective-permute-done.1
  188.5 7.7 maximum_convert_fusion
  196.2 0.0 copy-start.2
  196.2 11.1 %copy-done.2 = f32[4,32,256,256]{3,2,1,0:T(8,128)} copy-done((f32[4,32,256,256]{3,2,1,0:T(8,128)}, f32[4,32,256,256]{3,2,1,0:T(8,128)S(1)}, u32[]{:S(2)}) %copy-start.2) | copy-done | bytes 33554456
  207.3 0.0 copy-start.3
  207.3 6.4 slice.70
  213.6 0.0 copy-done.3
  213.6 44.9 %fusion.11 = f32[2,32,256,256]{3,2,1,0:T(8,128)} fusion(f32[2,32,256,256]{3,2,1,0:T(8,128)} %slice.70, f32[4,32,256,256]{3,2,1,0:T(8,128)} %copy-done.2, f32[2,256,256]{2,1,0:T(8,128)S(1)} %copy-done.3), kind=kLoop, calls=%fused_computation.18 | loop fusion | flops 37748736 | bytes 67633152 | tf_op jit(solution)/shard_map/add | solution.py:26
  258.5 10.0 %fusion.32 = (f32[1,32,256,256]{3,2,1,0:T(8,128)}, f32[1,32,256,256]{3,2,1,0:T(8,128)S(1)}) fusion(f32[2,32,256,256]{3,2,1,0:T(8,128)} %fusion.11), kind=kLoop, calls=%fused_computation.40 | loop fusion | bytes 33554432 | tf_op jit(solution)/shard_map/slice | solution.py:13
  268.6 1.3 collective-permute-start.2
  269.9 8.3 collective-permute-start.3
  278.1 174.6 %collective-permute-done.2 = f32[1,32,256,256]{3,2,1,0:T(8,128)S(1)} collective-permute-done((f32[1,32,256,256]{3,2,1,0:T(8,128)}, f32[1,32,256,256]{3,2,1,0:T(8,128)S(1)}, u32[]{:S(2)}, u32[]{:S(2)}) %collective-permute-start.2) | collective-permute-done | bytes 8388640 | tf_op jit(solution)/shard_map/ppermute | solution.py:15
  452.7 180.7 %collective-permute-done.3 = f32[1,32,256,256]{3,2,1,0:T(8,128)} collective-permute-done((f32[1,32,256,256]{3,2,1,0:T(8,128)S(1)}, f32[1,32,256,256]{3,2,1,0:T(8,128)}, u32[]{:S(2)}, u32[]{:S(2)}) %collective-permute-start.3) | collective-permute-done | bytes 8388640 | tf_op jit(solution)/shard_map/ppermute | solution.py:14
  633.5 37.6 %fusion.19 = bf16[2,32,256,256]{3,2,1,0:T(8,128)(2,1)} fusion(f32[2,32,256,256]{3,2,1,0:T(8,128)} %fusion.11, f32[1,32,256,256]{3,2,1,0:T(8,128)} %collective-permute-done.3, f32[1,32,256,256]{3,2,1,0:T(8,128)S(1)} %collective-permute-done.2, f32[2,256,256]{2,1,0:T(8,128)S(1)} %copy-done.3), kind=kLoop, calls=%fused_computation.26 | loop fusion | flops 50331648 | bytes 42467328 | tf_op jit(solution)/shard_map/convert_element_type | solution.py:36
  671.1 11.4 %copy.14 = bf16[2,32,256,256]{3,1,0,2:T(8,128)(2,1)} copy(bf16[2,32,256,256]{3,2,1,0:T(8,128)(2,1)} %fusion.19) | data formatting | bytes 16777216 | tf_op jit(solution)/shard_map/convert_element_type | solution.py:36
  682.5 0.0 copy-start.5
  682.5 0.0 copy-start.6
  682.5 0.0 copy-start.7
  682.5 100.7 %all_to_all.27 = bf16[2,32,256,256]{3,1,0,2:T(8,128)(2,1)} all-to-all(bf16[2,32,256,256]{3,1,0,2:T(8,128)(2,1)} %copy.14), channel_id=1, replica_groups=mesh['space'=8,'modes'=4] {'modes'}, dimensions={2} | all-to-all | bytes 16777216 | tf_op jit(solution)/shard_map/all_to_all | solution.py:40
  783.2 11.8 %copy.16 = bf16[2,4,32,64,256]{4,3,2,1,0:T(8,128)(2,1)} copy(bf16[2,4,32,64,256]{4,2,0,3,1:T(8,128)(2,1)} %bitcast.30) | data formatting | bytes 16777216 | tf_op jit(solution)/shard_map/all_to_all | solution.py:40
  795.0 0.0 copy-done
  795.0 0.0 copy-done.5
  795.0 0.0 copy-done.6
  795.0 0.0 copy-done.7
  795.0 22.2 %convert_bitcast_fusion.1 = bf16[2,128,64,256]{1,3,2,0:T(8,128)(2,1)} fusion(f32[343]{0:T(512)S(1)} %copy-done.5, f32[343]{0:T(512)S(1)} %copy-done.6, f32[343]{0:T(512)S(1)} %copy-done.7, bf16[2,128,64,256]{3,2,1,0:T(8,128)(2,1)} %bitcast.31, bf16[343,128]{1,0:T(8,128)(2,1)S(1)} %copy-done), kind=kOutput, calls=%fused_computation.37 | convolution fusion | flops 5814976512 | bytes 16869140 | tf_op jit(solution)/shard_map/qm,zqxy->zmxy/dot_general | solution.py:47
  817.2 12.2 %copy.18 = bf16[2,128,64,256]{3,2,0,1:T(8,128)(2,1)} copy(bf16[2,128,64,256]{1,3,2,0:T(8,128)(2,1)} %convert_bitcast_fusion.1) | data formatting | bytes 16777216 | tf_op jit(solution)/shard_map/convert_element_type | solution.py:48
  829.4 5.9 all-to-all-start.1
  835.2 93.0 %all-to-all-done.1 = bf16[2,128,64,256]{3,2,0,1:T(8,128)(2,1)} async-done(((bf16[2,128,64,256]{3,2,0,1:T(8,128)(2,1)}), bf16[2,128,64,256]{3,2,0,1:T(8,128)(2,1)}, u32[]{:S(2)}, u32[]{:S(2)}) %all-to-all-start.1) | async-done | bytes 8388640 | tf_op jit(solution)/shard_map/all_to_all | solution.py:49
  928.2 8.3 copy.19
  936.5 0.0 slice-start
  936.5 11.5 %convert_bitcast_fusion = f32[2,32,4,64,256]{4,3,1,2,0:T(8,128)} fusion(bf16[2,4,32,64,256]{4,3,2,1,0:T(8,128)(2,1)} %bitcast.29), kind=kLoop, calls=%fused_computation.32 | loop fusion | flops 4194304 | bytes 25165824 | tf_op jit(solution)/shard_map/convert_element_type | solution.py:51
  947.9 0.0 slice-start.1
  947.9 0.0 copy-start.4
  947.9 0.0 copy-start.1
  947.9 7.3 copy.20
  955.3 0.0 slice-done
  955.3 0.0 slice-done.1
  955.3 0.0 copy-done.4
  955.3 5.6 fusion.22
  961.0 0.0 copy-done.1
  (1 shorter events, 0.0 us)
Async XLA Ops:
  0.0 795.0 %copy-start = (bf16[343,128]{1,0:T(8,128)(2,1)S(1)}, bf16[343,128]{1,0:T(8,128)(2,1)}, u32[]{:S(2)}) copy-start(bf16[343,128]{1,0:T(8,128)(2,1)} %param.10) | copy-start | bytes 263428
  3.9 184.5 %collective-permute-start = (bf16[1,32,256,256]{3,2,1,0:T(8,128)(2,1)S(1)}, bf16[1,32,256,256]{3,2,1,0:T(8,128)(2,1)S(1)}, u32[]{:S(2)}, u32[]{:S(2)}) collective-permute-start(bf16[1,32,256,256]{3,2,1,0:T(8,128)(2,1)S(1)} %get-tuple-element.7), channel_id=1, source_target_pairs={{0,4},{4,8},{8,12},{12,16},{16,20},{20,24},{24,28},{1,5},{5,9},{9,... | collective-permute-start | bytes 12582920 | tf_op jit(solution)/shard_map/ppermute | solution.py:14
  9.1 179.4 %collective-permute-start.1 = (bf16[1,32,256,256]{3,2,1,0:T(8,128)(2,1)S(1)}, bf16[1,32,256,256]{3,2,1,0:T(8,128)(2,1)}, u32[]{:S(2)}, u32[]{:S(2)}) collective-permute-start(bf16[1,32,256,256]{3,2,1,0:T(8,128)(2,1)S(1)} %get-tuple-element.8), channel_id=1, source_target_pairs={{4,0},{8,4},{12,8},{16,12},{20,16},{24,20},{28,24},{5,1},{9,5},{13... | collective-permute-start | bytes 12582920 | tf_op jit(solution)/shard_map/ppermute | solution.py:15
  196.2 11.1 %copy-start.2 = (f32[4,32,256,256]{3,2,1,0:T(8,128)}, f32[4,32,256,256]{3,2,1,0:T(8,128)S(1)}, u32[]{:S(2)}) copy-start(f32[4,32,256,256]{3,2,1,0:T(8,128)S(1)} %maximum_convert_fusion) | copy-start | bytes 100663296
  207.3 6.4 copy-start.3
  268.6 184.2 %collective-permute-start.2 = (f32[1,32,256,256]{3,2,1,0:T(8,128)}, f32[1,32,256,256]{3,2,1,0:T(8,128)S(1)}, u32[]{:S(2)}, u32[]{:S(2)}) collective-permute-start(f32[1,32,256,256]{3,2,1,0:T(8,128)} %get-tuple-element.5), channel_id=1, source_target_pairs={{4,0},{8,4},{12,8},{16,12},{20,16},{24,20},{28,24},{5,1},{9,5},{13... | collective-permute-start | bytes 25165832 | tf_op jit(solution)/shard_map/ppermute | solution.py:15
  269.9 363.6 %collective-permute-start.3 = (f32[1,32,256,256]{3,2,1,0:T(8,128)S(1)}, f32[1,32,256,256]{3,2,1,0:T(8,128)}, u32[]{:S(2)}, u32[]{:S(2)}) collective-permute-start(f32[1,32,256,256]{3,2,1,0:T(8,128)S(1)} %get-tuple-element.6), channel_id=1, source_target_pairs={{0,4},{4,8},{8,12},{12,16},{16,20},{20,24},{24,28},{1,5},{5,9},{9,... | collective-permute-start | bytes 25165832 | tf_op jit(solution)/shard_map/ppermute | solution.py:14
  682.5 112.5 %copy-start.5 = (f32[343]{0:T(512)S(1)}, f32[343]{0:T(512)}, u32[]{:S(2)}) copy-start(f32[343]{0:T(512)} %param.11) | copy-start | bytes 4120
  682.5 112.5 %copy-start.6 = (f32[343]{0:T(512)S(1)}, f32[343]{0:T(512)}, u32[]{:S(2)}) copy-start(f32[343]{0:T(512)} %param.13) | copy-start | bytes 4120
  682.5 112.5 %copy-start.7 = (f32[343]{0:T(512)S(1)}, f32[343]{0:T(512)}, u32[]{:S(2)}) copy-start(f32[343]{0:T(512)} %param.12) | copy-start | bytes 4120
  829.4 98.8 %all-to-all-start.1 = ((bf16[2,128,64,256]{3,2,0,1:T(8,128)(2,1)}), bf16[2,128,64,256]{3,2,0,1:T(8,128)(2,1)}, u32[]{:S(2)}, u32[]{:S(2)}) async-start(bf16[2,128,64,256]{3,2,0,1:T(8,128)(2,1)} %copy.18), calls=%async_computation.1 | async-start | bytes 16777216 | tf_op jit(solution)/shard_map/all_to_all | solution.py:49
  936.5 18.8 %slice-start = ((s8[8388608]{0:T(1024)(128)(4,1)}), s8[4194304]{0:T(1024)(128)(4,1)S(1)}, s32[]{:S(2)}) async-start(s8[8388608]{0:T(1024)(128)(4,1)} %bitcast.27), calls=%async_computation.2 | async-start | bytes 8388608
  947.9 7.3 slice-start.1
  947.9 7.3 copy-start.4
  947.9 13.0 %copy-start.1 = (bf16[343,128]{1,0:T(8,128)(2,1)S(1)}, bf16[343,128]{1,0:T(8,128)(2,1)}, u32[]{:S(2)}) copy-start(bf16[343,128]{1,0:T(8,128)(2,1)} %param.10) | copy-start | bytes 263428
where the time goes:
time: 962 us; the launch traced here: 961 us
  waiting for transfers between devices  626 us (65%)
  other arithmetic  107 us (11%)
  blocking collectives  101 us (10%)
  local copies, waits for them, and re-layouts  82.4 us (9%)
  matrix products  22.2 us (2%)
  starting transfers between devices  21.8 us (2%)
    ppermute x2, waiting for transfers between devices, with_halo(): before = lax.ppermute(last, axis, up)  359 us
    ppermute x2, waiting for transfers between devices, with_halo(): after = lax.ppermute(initial, axis, down)  175 us
    all_to_all x1, blocking collectives, on_device(): lax.all_to_all(settled, 'modes', split_axis=2, concat_axis=1, tiled=True)  101 us
    all_to_all x1, waiting for transfers between devices, on_device(): lax.all_to_all(cell_source, 'modes', split_axis=1, concat_axis=2, tiled=T...  93 us
    add x1, other arithmetic, advance(): return middle + rate_mid[:, None] * (beside - 6.0 * middle)  44.9 us
    convert_element_type x1, other arithmetic, on_device(): settled = values.astype(jnp.bfloat16)  37.6 us
    dot_general x1, matrix products, on_device(): jnp.einsum('qm,zqxy->zmxy', chaos_basis, weighted, preferred_element_type...  22.2 us
  transfers between devices with their start and end apart: 5, of which 4 were waited for; matrix products, arithmetic and copies ran while one was open for 0% of the time, Pallas kernels for 0%

commit v1 on v0

v1 whole, which is shorter than its diff:
```python
import functools

import jax
import jax.numpy as jnp
from jax import lax
from jax.experimental import pallas as pl
from jax.experimental.pallas import tpu as pltpu
from jax.sharding import PartitionSpec as P

F32, BF16 = jnp.float32, jnp.bfloat16
ANY = pl.BlockSpec(memory_space=pl.ANY)
VMEM = pl.BlockSpec(memory_space=pltpu.VMEM)
SMEM = pl.BlockSpec(memory_space=pltpu.SMEM)
VMEM_LIMIT = 44 * 1024 * 1024
EDGE = 2
LANES = 128


def lanes(h):
    return pl.ds(h * LANES, LANES)


def params():
    return pltpu.CompilerParams(vmem_limit_bytes=VMEM_LIMIT)


def cost(flops, bytes_accessed):
    return pl.CostEstimate(flops=int(flops), bytes_accessed=int(bytes_accessed), transcendentals=0)


def to_bf16_rows(x):
    a, m, y = x.shape
    if m % 16 == 0:
        return x.astype(BF16).reshape(a * m, y)
    return x.astype(F32).reshape(a * m, y).astype(BF16)


def spread_kernel(pos, field, own, send, window, wide, sems, *, begin, skip):
    side = pos[0]
    _, planes, modes, depth, _ = window.shape
    size = field.shape[2]
    rows = own.shape[0]
    parts = wide.shape[2]
    copies = []
    for a in range(2):
        far = side if a == 0 else 1 - side
        start = jnp.where(far == 1, size - depth - begin, begin)
        start = pl.multiple_of(start, 16)
        copy = pltpu.make_async_copy(
            field.at[:, :, pl.ds(start, depth), :], window.at[a], sems.at[a]
        )
        copy.start()
        copies.append(copy)
    for a, out in ((1, send), (0, own)):
        far = side if a == 0 else 1 - side
        copies[a].wait()
        for z in range(planes):
            for h in range(parts):
                wide[a, z, h] = window[a, z, :, :, lanes(h)].astype(F32).reshape(modes * depth, LANES)

        def row(i, _):
            w = jnp.where(far == 1, depth - 1 - skip - i, skip + i)
            for z in range(planes):
                to = jnp.where(far == 1, z, planes - 1 - z)
                for h in range(parts):
                    out[i, to, :, lanes(h)] = wide[a, z, h, pl.ds(w, modes, stride=depth), :].astype(BF16)
            return 0

        lax.fori_loop(0, rows, row, 0)


def spread(pos, field, begin, skip, rows, depth):
    planes, modes, _, cols = field.shape
    piece = jax.ShapeDtypeStruct((rows, planes, modes, cols), BF16)
    return pl.pallas_call(
        functools.partial(spread_kernel, begin=begin, skip=skip),
        out_shape=(piece, piece),
        in_specs=[SMEM, ANY],
        out_specs=(VMEM, VMEM),
        scratch_shapes=[
            pltpu.VMEM((2, planes, modes, depth, cols), BF16),
            pltpu.VMEM((2, planes, cols // LANES, modes * depth, LANES), F32),
            pltpu.SemaphoreType.DMA((2,)),
        ],
        compiler_params=params(),
        cost_estimate=cost(3e9, 4 * rows * planes * modes * cols * 2),
        name="spread",
    )(pos, field)


def sweep_kernel(pos, rate, shift, *refs, begin, count, heads):
    group = 4
    blocks, refs = refs[:group], refs[group:]
    tails, refs = refs[:heads], refs[heads:]
    outs, (field, first, sems) = refs[:count], refs[count:]
    _, stack, modes, cols = field.shape
    planes = stack // group
    mine = stack - 2 * planes
    rows = first.shape[0] - 2
    lead = 2 * EDGE if heads else EDGE
    copies = []
    for g in range(group):
        to = pl.ds(g * planes, planes)
        copies.append(
            pltpu.make_async_copy(blocks[g], field.at[pl.ds(lead, rows + 2 * EDGE - lead), to], sems.at[g])
        )
        if heads:
            length = tails[g].shape[0]
            copies.append(
                pltpu.make_async_copy(
                    tails[g].at[pl.ds(length - lead, lead)], field.at[pl.ds(0, lead), to], sems.at[group + g]
                )
            )
    for copy in copies:
        copy.start()
    if not heads:
        field[pl.ds(0, lead)] = jnp.zeros((lead, stack, modes, cols), BF16)
    for copy in copies:
        copy.wait()
    low = planes - 1
    wide = mine + 2

    def pair(j, _):
        i = 2 * j
        middle = field[pl.ds(i + 1, 2), pl.ds(low, wide)]
        beside = jnp.dot(
            to_bf16_rows(middle.reshape(2 * wide, modes, cols)), shift[...], preferred_element_type=F32
        ).reshape(2, wide, modes, cols)
        for a in range(2):
            line = [field[i + 1 + a, low - 1 + p].astype(F32) for p in range(wide + 2)]
            for p in range(wide):
                centre = line[p + 1]
                around = beside[a, p] + (line[p] + line[p + 2])
                around = around + (field[i + a, low + p].astype(F32) + field[i + 2 + a, low + p].astype(F32))
                speed = rate[p, pl.ds(begin + i + a, 1), :]
                first[i + a, p] = centre + speed * (around - 6.0 * centre)
        return 0

    lax.fori_loop(0, (rows + 2) // 2, pair, 0)
    part = rows // count
    for k in range(count):
        base = jnp.bitwise_xor(pos[1], k) * part

        def row(i, _):
            g = base + i
            line = [first[g + 1, p] for p in range(wide)]
            beside = jnp.dot(
                to_bf16_rows(first[g + 1, pl.ds(1, mine)]), shift[...], preferred_element_type=F32
            ).reshape(mine, modes, cols)
            for p in range(mine):
                centre = line[p + 1]
                around = beside[p] + (line[p] + line[p + 2])
                around = around + (first[g, p + 1] + first[g + 2, p + 1])
                speed = rate[p + 1, pl.ds(begin + g + 1, 1), :]
                outs[k][i, p] = (centre + speed * (around - 6.0 * centre)).astype(BF16)
            return 0

        lax.fori_loop(0, part, row, 0)


def sweep(pos, rate, shift, blocks, tails, begin, rows, count):
    _, planes, modes, cols = blocks[0].shape
    mine = 2 * planes
    piece = jax.ShapeDtypeStruct((rows // count, mine, modes, cols), BF16)
    return pl.pallas_call(
        functools.partial(sweep_kernel, begin=begin, count=count, heads=len(tails)),
        out_shape=(piece,) * count,
        in_specs=[SMEM, VMEM, VMEM] + [ANY] * (4 + len(tails)),
        out_specs=(VMEM,) * count,
        scratch_shapes=[
            pltpu.VMEM((rows + 2 * EDGE, 4 * planes, modes, cols), BF16),
            pltpu.VMEM((rows + 2, mine + 2, modes, cols), F32),
            pltpu.SemaphoreType.DMA((8,)),
        ],
        compiler_params=params(),
        cost_estimate=cost(8e9, 3 * rows * mine * modes * cols * 2),
        name="sweep",
    )(pos, rate, shift, *blocks, *tails)


def points_kernel(pos, basis, basis_t, flat, swing, load, *refs, begin):
    count = len(refs) // 2
    blocks, outs = refs[:count], refs[count:]
    part, planes, modes, cols = blocks[0].shape
    copies = cols // flat.shape[1]

    def row(i, _):
        place = begin + pos[1] * part + i
        for p in range(planes):
            if modes % 16 == 0:
                cells = jnp.concatenate([block[i, p] for block in blocks], axis=0)
            else:
                cells = jnp.concatenate([block[i, p].astype(F32) for block in blocks], axis=0).astype(BF16)
            heat = jnp.tanh(jnp.dot(basis[...], cells, preferred_element_type=F32))
            offset = jnp.concatenate([flat[...]] * copies, axis=1)
            slope = jnp.concatenate([swing[...]] * copies, axis=1)
            weighted = (offset + slope * heat).astype(BF16)
            source = jnp.dot(basis_t[...], weighted, preferred_element_type=F32).astype(BF16).astype(F32)
            done = cells.astype(F32) + load[p, pl.ds(place, 1), :] * source
            for k in range(count):
                outs[k][i, p] = done[k * modes : (k + 1) * modes].astype(BF16)
        return 0

    lax.fori_loop(0, part, row, 0)


def points(pos, basis, basis_t, flat, swing, load, blocks, begin):
    count = len(blocks)
    size = sum(block.size for block in blocks)
    return pl.pallas_call(
        functools.partial(points_kernel, begin=begin),
        out_shape=tuple(jax.ShapeDtypeStruct(block.shape, BF16) for block in blocks),
        in_specs=[SMEM] + [VMEM] * (5 + count),
        out_specs=(VMEM,) * count,
        compiler_params=params(),
        cost_estimate=cost(8e9, 4 * size),
        name="points",
    )(pos, basis, basis_t, flat, swing, load, *blocks)


def collect_kernel(pos, *refs):
    *blocks, out, sems = refs
    part, planes = blocks[0].shape[0], out.shape[1]
    copies = []
    for k, block in enumerate(blocks):
        base = jnp.bitwise_xor(pos[1], k) * part
        copies.append(
            pltpu.make_async_copy(block.at[:, pl.ds(0, planes)], out.at[pl.ds(base, part)], sems.at[k])
        )
    for copy in copies:
        copy.start()
    for copy in copies:
        copy.wait()


def collect(pos, blocks):
    part, planes, modes, cols = blocks[0].shape
    count = len(blocks)
    shape = (part * count, planes // 2, modes, cols)
    return pl.pallas_call(
        collect_kernel,
        out_shape=jax.ShapeDtypeStruct(shape, BF16),
        in_specs=[SMEM] + [ANY] * count,
        out_specs=ANY,
        scratch_shapes=[pltpu.SemaphoreType.DMA((count,))],
        compiler_params=params(),
        cost_estimate=cost(1e9, 2 * blocks[0].size * count),
        name="collect",
    )(pos, *blocks)


def settle_kernel(pos, *refs, begin, count, chained):
    if chained:
        refs = refs[1:]
    blocks, other = refs[:count], refs[count]
    out, wide, final, sems = refs[count + 1 :]
    side = pos[0]
    part = blocks[0].shape[0]
    rows, planes, modes, cols = other.shape
    size = out.shape[2]
    parts = wide.shape[2]

    for k in range(count):
        base = jnp.bitwise_xor(pos[1], k) * part

        def own_row(i, _):
            r = base + i
            to = jnp.where(side == 1, rows - 1 - r, r)
            for z in range(planes):
                place = jnp.where(side == 1, z, planes - 1 - z)
                for h in range(parts):
                    wide[0, place, h, pl.ds(pl.multiple_of(to * modes, modes), modes), :] = blocks[k][
                        i, planes + z, :, lanes(h)
                    ].astype(F32)
            return 0

        lax.fori_loop(0, part, own_row, 0)

    def other_row(r, _):
        to = jnp.where(side == 0, rows - 1 - r, r)
        for z in range(planes):
            place = jnp.where(side == 0, z, planes - 1 - z)
            for h in range(parts):
                wide[1, place, h, pl.ds(pl.multiple_of(to * modes, modes), modes), :] = other[
                    r, z, :, lanes(h)
                ].astype(F32)
        return 0

    lax.fori_loop(0, rows, other_row, 0)

    def mode(m, _):
        for a in range(2):
            for z in range(planes):
                for h in range(parts):
                    final[a, z, m, :, lanes(h)] = wide[a, z, h, pl.ds(m, rows, stride=modes), :].astype(BF16)
        return 0

    lax.fori_loop(0, modes, mode, 0)
    copies = []
    for a in range(2):
        far = side if a == 0 else 1 - side
        start = pl.multiple_of(jnp.where(far == 1, size - rows - begin, begin), 16)
        copies.append(pltpu.make_async_copy(final.at[a], out.at[:, :, pl.ds(start, rows), :], sems.at[a]))
    for copy in copies:
        copy.start()
    for copy in copies:
        copy.wait()


def settle(pos, result, blocks, other, begin, shape):
    count = len(blocks)
    rows, planes, modes, cols = other.shape
    chained = result is not None
    return pl.pallas_call(
        functools.partial(settle_kernel, begin=begin, count=count, chained=chained),
        out_shape=jax.ShapeDtypeStruct(shape, BF16),
        in_specs=[SMEM] + ([ANY] if chained else []) + [VMEM] * (count + 1),
        out_specs=ANY,
        scratch_shapes=[
            pltpu.VMEM((2, planes, cols // LANES, rows * modes, LANES), F32),
            pltpu.VMEM((2, planes, modes, rows, cols), BF16),
            pltpu.SemaphoreType.DMA((2,)),
        ],
        input_output_aliases={1: 0} if chained else {},
        compiler_params=params(),
        cost_estimate=cost(3e9, 4 * rows * planes * modes * cols * 2),
        name="settle",
    )(pos, *([result] if chained else []), *blocks, other)


def chunk_rows(half):
    return [half // 4] * 4


def on_device(field, diffusion, joule, basis, quad_weight, base_conductivity, thermal_slope):
    planes, modes, size, cols = field.shape
    half = size // 2
    spaces, count = lax.axis_size("space"), lax.axis_size("modes")
    side = lax.axis_index("space") % 2
    me = lax.axis_index("modes")
    pos = jnp.stack([side, me]).astype(jnp.int32)

    swap = [(i, i ^ 1) for i in range(spaces)]
    ahead = [(i, i + 4 * (i % 2) - 2) for i in range(spaces)]
    ahead = [(i, j) for i, j in ahead if 0 <= j < spaces]
    back = [(j, i) for i, j in ahead]

    def across(x):
        return lax.ppermute(x, "space", swap)

    def halo(own, other):
        return lax.ppermute(own, "space", ahead), lax.ppermute(other, "space", back)

    def exchange(pieces):
        moved = [pieces[0]]
        for k in range(1, count):
            moved.append(lax.ppermute(pieces[k], "modes", [(j, j ^ k) for j in range(count)]))
        return moved

    def logical(x, length):
        rows_back, planes_back = jnp.flip(x, 1)[:, :length], jnp.flip(x, 0)[:, :length]
        own = jnp.where(side == 1, rows_back, planes_back)
        return own, across(jnp.where(side == 1, planes_back, rows_back))

    own_rate, other_rate = logical(diffusion, half + EDGE)
    before, after = halo(own_rate[-1:], other_rate[:1])
    rate = jnp.concatenate([before, other_rate, own_rate, after], axis=0)
    rate = jnp.pad(rate, ((0, 0), (1, -(half + EDGE + 1) % 8), (0, 0)))
    own_load, other_load = logical(joule, half)
    load = jnp.concatenate([other_load, own_load], axis=0)

    lane = jnp.arange(cols)
    shift = (jnp.abs(lane[:, None] - lane[None, :]) == 1).astype(BF16)

    points_count = basis.shape[0]
    extra = -points_count % 32
    turned = jnp.concatenate(
        [lax.dynamic_slice_in_dim(basis, (me ^ k) * modes, modes, axis=1) for k in range(count)], axis=1
    )
    turned = jnp.pad(turned, ((0, extra), (0, 0)))
    turned_t = turned.T
    level = quad_weight * base_conductivity
    spread_out = lambda v: jnp.broadcast_to(jnp.pad(v, (0, extra))[:, None], (points_count + extra, 128))
    flat, swing = spread_out(level), spread_out(level * thermal_slope)

    rows_of = chunk_rows(half)
    begins = [sum(rows_of[:c]) for c in range(len(rows_of))]
    result = None
    tails = ()
    for begin, rows in zip(begins, rows_of):
        skip = EDGE if begin else 0
        own, send = spread(pos, field, begin, skip, rows + EDGE - skip, rows + 16)
        other = across(send)
        before, after = halo(own, other)
        blocks = (before, other, own, after)
        pieces = sweep(pos, rate, shift, blocks, tails, begin, rows, count)
        tails = blocks
        cells = exchange(pieces)
        stepped = points(pos, turned, turned_t, flat, swing, load, cells, begin)
        home = exchange(stepped)
        theirs = across(collect(pos, home))
        result = settle(pos, result, home, theirs, begin, field.shape)
    return result


def solution(mesh):
    return jax.shard_map(
        on_device,
        mesh=mesh,
        in_specs=(
            P("space", "modes", None, None),
            P("space", None, None),
            P("space", None, None),
            P(),
            P(),
            P(),
            P(),
        ),
        out_specs=P("space", "modes", None, None),
        check_vma=False,
    )
```

time: 962 us -> 419 us (0.44)
  waiting for transfers between devices: 626 us -> 186 us
  Pallas kernels: 0 us -> 147 us
  other arithmetic: 107 us -> 4.03 us
  blocking collectives: 101 us -> 0 us
  local copies, waits for them, and re-layouts: 82.4 us -> 9.03 us
  starting transfers between devices: 21.8 us -> 72 us
  matrix products: 22.2 us -> 0 us
    ppermute x4 -> x44, waiting for transfers between devices: 533 us -> 186 us  [the longest x24 88.9 us: exchange(): lax.ppermute(pieces[k], 'modes', [(j, j ^ k) for j in range(count)])]
    pallas_call x0 -> x20, Pallas kernels: none -> 147 us  [the longest x4 50.3 us: sweep(): pl.pallas_call(functools.partial(sweep_kernel, begin=begin, count=count,...]
    all_to_all x1 -> x0, blocking collectives: 101 us -> none  [on_device(): lax.all_to_all(settled, 'modes', split_axis=2, concat_axis=1, tiled=True)]
    all_to_all x1 -> x0, waiting for transfers between devices: 93 us -> none  [on_device(): lax.all_to_all(cell_source, 'modes', split_axis=1, concat_axis=2, tiled=T...]
    convert_element_type x4 -> x1, other arithmetic: 62.4 us -> 0.04 us  [on_device(): shift = (jnp.abs(lane[:, None] - lane[None, :]) == 1).astype(BF16)]
    ppermute x4 -> x44, starting transfers between devices: 15.9 us -> 72 us  [the longest x10 28.8 us: across(): return lax.ppermute(x, 'space', swap)]
    add x1 -> x0, other arithmetic: 44.9 us -> none  [advance(): return middle + rate_mid[:, None] * (beside - 6.0 * middle)]
    convert_element_type x3 -> x0, local copies, waits for them, and re-layouts: 30.9 us -> none  [the longest x1 12.2 us: on_device(): cell_source = summed.astype(jnp.bfloat16)]
  transfers between devices with their start and end apart: 5 -> 44, of which waited for: 4 -> 19; matrix products, arithmetic and copies ran while one was open for 0% -> 1% of each run, Pallas kernels for 0% -> 33%
where the time goes in v1:
time: 419 us
  waiting for transfers between devices  186 us (44%)
  Pallas kernels  147 us (35%)
  starting transfers between devices  72 us (17%)
  local copies, waits for them, and re-layouts  9.03 us (2%)
    ppermute x24, waiting for transfers between devices, exchange(): lax.ppermute(pieces[k], 'modes', [(j, j ^ k) for j in range(count)])  88.9 us
    ppermute x10, waiting for transfers between devices, across(): return lax.ppermute(x, 'space', swap)  76 us
    pallas_call x4, Pallas kernels, sweep(): pl.pallas_call(functools.partial(sweep_kernel, begin=begin, count=count,...  50.3 us
    pallas_call x4, Pallas kernels, points(): pl.pallas_call(functools.partial(points_kernel, begin=begin), out_shape=t...  40 us
    ppermute x10, starting transfers between devices, across(): return lax.ppermute(x, 'space', swap)  28.8 us
    pallas_call x4, Pallas kernels, settle(): pl.pallas_call(functools.partial(settle_kernel, begin=begin, count=count,...  27.9 us
    pallas_call x4, Pallas kernels, spread(): pl.pallas_call(functools.partial(spread_kernel, begin=begin, skip=skip),...  26.3 us
    ppermute x24, starting transfers between devices, exchange(): lax.ppermute(pieces[k], 'modes', [(j, j ^ k) for j in range(count)])  19.8 us
  transfers between devices with their start and end apart: 44, of which 19 were waited for; matrix products, arithmetic and copies ran while one was open for 1% of the time, Pallas kernels for 33%

profile of v1, /device:TPU:0, one launch (start us, length us, event | category | flops | bytes accessed | tf_op | source)
XLA Modules:
  0.0 418.8 jit_solution(7022688585717884327)
XLA Ops:
  2.4 2.9 collective-permute-start.2
  7.4 6.4 %spread.5 = (bf16[32,2,32,256]{3,2,1,0:T(8,128)(2,1)S(1)}, bf16[32,2,32,256]{3,2,1,0:T(8,128)(2,1)}) custom-call(s32[2]{0:T(128)S(1)} %pad_add_fusion.pos, bf16[2,32,256,256]{3,2,1,0:T(8,128)(2,1)} %field.7), custom_call_target="tpu_custom_call" | custom-call | flops 3000000000 | bytes 4194304 | tf_op jit(solution)/shard_map/spread/pallas_call | solution.py:75
  15.1 5.2 %collective-permute-start.15 = (bf16[32,2,32,256]{3,2,1,0:T(8,128)(2,1)}, bf16[32,2,32,256]{3,2,1,0:T(8,128)(2,1)}, u32[]{:S(2)}, u32[]{:S(2)}) collective-permute-start(bf16[32,2,32,256]{3,2,1,0:T(8,128)(2,1)} %get-tuple-element.56), channel_id=1, source_target_pairs={{0,4},{4,0},{8,12},{12,8},{16,20},{20,16},{24,28},{28,24},{1,5},{5... | collective-permute-start | bytes 3145736 | tf_op jit(solution)/shard_map/ppermute | solution.py:349
  20.3 6.8 %spread.6 = (bf16[32,2,32,256]{3,2,1,0:T(8,128)(2,1)}, bf16[32,2,32,256]{3,2,1,0:T(8,128)(2,1)}) custom-call(s32[2]{0:T(128)S(1)} %pad_add_fusion.pos, bf16[2,32,256,256]{3,2,1,0:T(8,128)(2,1)} %field.7), custom_call_target="tpu_custom_call" | custom-call | flops 3000000000 | bytes 4194304 | tf_op jit(solution)/shard_map/spread/pallas_call | solution.py:75
  28.2 2.0 collective-permute-start
  30.2 3.4 collective-permute-start.3
  33.6 6.4 %spread.7 = (bf16[32,2,32,256]{3,2,1,0:T(8,128)(2,1)S(1)}, bf16[32,2,32,256]{3,2,1,0:T(8,128)(2,1)}) custom-call(s32[2]{0:T(128)S(1)} %pad_add_fusion.pos, bf16[2,32,256,256]{3,2,1,0:T(8,128)(2,1)} %field.7), custom_call_target="tpu_custom_call" | custom-call | flops 3000000000 | bytes 4194304 | tf_op jit(solution)/shard_map/spread/pallas_call | solution.py:75
  41.1 30.1 %collective-permute-done = f32[2,128,256]{2,1,0:T(8,128)S(1)} collective-permute-done((f32[2,128,256]{2,1,0:T(8,128)S(1)}, f32[2,128,256]{2,1,0:T(8,128)S(1)}, u32[]{:S(2)}, u32[]{:S(2)}) %collective-permute-start) | collective-permute-done | bytes 262176 | tf_op jit(solution)/shard_map/ppermute | solution.py:349
  72.6 5.0 %collective-permute-start.35 = (bf16[32,2,32,256]{3,2,1,0:T(8,128)(2,1)}, bf16[32,2,32,256]{3,2,1,0:T(8,128)(2,1)}, u32[]{:S(2)}, u32[]{:S(2)}) collective-permute-start(bf16[32,2,32,256]{3,2,1,0:T(8,128)(2,1)} %get-tuple-element.76), channel_id=1, source_target_pairs={{0,4},{4,0},{8,12},{12,8},{16,20},{20,16},{24,28},{28,24},{1,5},{5... | collective-permute-start | bytes 3145736 | tf_op jit(solution)/shard_map/ppermute | solution.py:349
  77.6 6.6 %spread.4 = (bf16[34,2,32,256]{3,2,1,0:T(8,128)(2,1)S(1)}, bf16[34,2,32,256]{3,2,1,0:T(8,128)(2,1)}) custom-call(s32[2]{0:T(128)S(1)} %pad_add_fusion.pos, bf16[2,32,256,256]{3,2,1,0:T(8,128)(2,1)} %field.7), custom_call_target="tpu_custom_call" | custom-call | flops 3000000000 | bytes 4456448 | tf_op jit(solution)/shard_map/spread/pallas_call | solution.py:75
  85.3 2.6 collective-permute-start.16
  88.0 3.5 collective-permute-start.26
  93.2 4.0 collective-permute-done.24.refs_0_.refs_4_
  98.4 3.5 collective-permute-done.35.refs_1_
  101.9 2.6 collective-permute-start.36
  107.2 15.9 %collective-permute-done.5.refs_1_.refs_5_ = bf16[34,2,32,256]{3,2,1,0:T(8,128)(2,1)S(1)} collective-permute-done((bf16[34,2,32,256]{3,2,1,0:T(8,128)(2,1)}, bf16[34,2,32,256]{3,2,1,0:T(8,128)(2,1)S(1)}, u32[]{:S(2)}, u32[]{:S(2)}) %collective-permute-start.5) | collective-permute-done | bytes 1114144 | tf_op jit(solution)/shard_map/ppermute | solution.py:349
  124.3 4.8 %collective-permute-start.6 = (bf16[34,2,32,256]{3,2,1,0:T(8,128)(2,1)S(1)}, bf16[34,2,32,256]{3,2,1,0:T(8,128)(2,1)S(1)}, u32[]{:S(2)}, u32[]{:S(2)}) collective-permute-start(bf16[34,2,32,256]{3,2,1,0:T(8,128)(2,1)S(1)} %collective-permute-done.5.refs_1_.refs_5_), channel_id=1, source_target_pairs={{12,4},{0,8},{20,12},{8,16},{28,20},{16,24},{13,5},{1,9},{21,13},{... | collective-permute-start | bytes 3342344 | tf_op jit(solution)/shard_map/ppermute | solution.py:352
  129.1 4.2 %collective-permute-done.26.refs_3_.refs_7_ = bf16[32,2,32,256]{3,2,1,0:T(8,128)(2,1)} collective-permute-done((bf16[32,2,32,256]{3,2,1,0:T(8,128)(2,1)}, bf16[32,2,32,256]{3,2,1,0:T(8,128)(2,1)}, u32[]{:S(2)}, u32[]{:S(2)}) %collective-permute-start.26) | collective-permute-done | bytes 1048608 | tf_op jit(solution)/shard_map/ppermute | solution.py:352
  135.8 13.2 %sweep.6 = (bf16[8,4,32,256]{3,2,1,0:T(8,128)(2,1)S(1)}, bf16[8,4,32,256]{3,2,1,0:T(8,128)(2,1)S(1)}, bf16[8,4,32,256]{3,2,1,0:T(8,128)(2,1)S(1)}, bf16[8,4,32,256]{3,2,1,0:T(8,128)(2,1)S(1)}) custom-call(s32[2]{0:T(128)S(1)} %pad_add_fusion.pos, f32[6,136,256]{2,1,0:T(8,128)S(1)} %select_maximum_fusion.rate, bf16[256,256]{1,0:T(8,128)(2,1)S(1)} %fusion.1.shift, ...), custom_call_target="tpu_custom_call" | custom-call | flops 8000000000 | bytes 6291456 | tf_op jit(solution)/shard_map/sweep/pallas_call | solution.py:165
  150.7 5.1 %collective-permute-done.36.refs_3_ = bf16[32,2,32,256]{3,2,1,0:T(8,128)(2,1)} collective-permute-done((bf16[32,2,32,256]{3,2,1,0:T(8,128)(2,1)}, bf16[32,2,32,256]{3,2,1,0:T(8,128)(2,1)}, u32[]{:S(2)}, u32[]{:S(2)}) %collective-permute-start.36) | collective-permute-done | bytes 1048608 | tf_op jit(solution)/shard_map/ppermute | solution.py:352
  155.8 13.0 %sweep.7 = (bf16[8,4,32,256]{3,2,1,0:T(8,128)(2,1)S(1)}, bf16[8,4,32,256]{3,2,1,0:T(8,128)(2,1)S(1)}, bf16[8,4,32,256]{3,2,1,0:T(8,128)(2,1)S(1)}, bf16[8,4,32,256]{3,2,1,0:T(8,128)(2,1)S(1)}) custom-call(s32[2]{0:T(128)S(1)} %pad_add_fusion.pos, f32[6,136,256]{2,1,0:T(8,128)S(1)} %select_maximum_fusion.rate, bf16[256,256]{1,0:T(8,128)(2,1)S(1)} %fusion.1.shift, ...), custom_call_target="tpu_custom_call" | custom-call | flops 8000000000 | bytes 6291456 | tf_op jit(solution)/shard_map/sweep/pallas_call | solution.py:165
  168.8 7.5 %collective-permute-done.6.refs_3_.refs_7_ = bf16[34,2,32,256]{3,2,1,0:T(8,128)(2,1)S(1)} collective-permute-done((bf16[34,2,32,256]{3,2,1,0:T(8,128)(2,1)S(1)}, bf16[34,2,32,256]{3,2,1,0:T(8,128)(2,1)S(1)}, u32[]{:S(2)}, u32[]{:S(2)}) %collective-permute-start.6) | collective-permute-done | bytes 1114144 | tf_op jit(solution)/shard_map/ppermute | solution.py:352
  176.4 11.4 %sweep.4 = (bf16[8,4,32,256]{3,2,1,0:T(8,128)(2,1)S(1)}, bf16[8,4,32,256]{3,2,1,0:T(8,128)(2,1)S(1)}, bf16[8,4,32,256]{3,2,1,0:T(8,128)(2,1)S(1)}, bf16[8,4,32,256]{3,2,1,0:T(8,128)(2,1)S(1)}) custom-call(s32[2]{0:T(128)S(1)} %pad_add_fusion.pos, f32[6,136,256]{2,1,0:T(8,128)S(1)} %select_maximum_fusion.rate, bf16[256,256]{1,0:T(8,128)(2,1)S(1)} %fusion.1.shift, ...), custom_call_target="tpu_custom_call" | custom-call | flops 8000000000 | bytes 6291456 | tf_op jit(solution)/shard_map/sweep/pallas_call | solution.py:165
  189.7 12.7 %sweep.5 = (bf16[8,4,32,256]{3,2,1,0:T(8,128)(2,1)S(1)}, bf16[8,4,32,256]{3,2,1,0:T(8,128)(2,1)S(1)}, bf16[8,4,32,256]{3,2,1,0:T(8,128)(2,1)S(1)}, bf16[8,4,32,256]{3,2,1,0:T(8,128)(2,1)S(1)}) custom-call(s32[2]{0:T(128)S(1)} %pad_add_fusion.pos, f32[6,136,256]{2,1,0:T(8,128)S(1)} %select_maximum_fusion.rate, bf16[256,256]{1,0:T(8,128)(2,1)S(1)} %fusion.1.shift, ...), custom_call_target="tpu_custom_call" | custom-call | flops 8000000000 | bytes 6291456 | tf_op jit(solution)/shard_map/sweep/pallas_call | solution.py:165
  204.2 8.8 %collective-permute-done.9.refs_3_ = bf16[8,4,32,256]{3,2,1,0:T(8,128)(2,1)S(1)} collective-permute-done((bf16[8,4,32,256]{3,2,1,0:T(8,128)(2,1)S(1)}, bf16[8,4,32,256]{3,2,1,0:T(8,128)(2,1)S(1)}, u32[]{:S(2)}, u32[]{:S(2)}) %collective-permute-start.9) | collective-permute-done | bytes 524320 | tf_op jit(solution)/shard_map/ppermute | solution.py:357
  214.7 10.0 %points.4 = (bf16[8,4,32,256]{3,2,1,0:T(8,128)(2,1)S(1)}, bf16[8,4,32,256]{3,2,1,0:T(8,128)(2,1)S(1)}, bf16[8,4,32,256]{3,2,1,0:T(8,128)(2,1)S(1)}, bf16[8,4,32,256]{3,2,1,0:T(8,128)(2,1)S(1)}) custom-call(s32[2]{0:T(128)S(1)} %pad_add_fusion.pos, bf16[352,128]{1,0:T(8,128)(2,1)S(1)} %copy.15.basis, bf16[128,352]{1,0:T(8,128)(2,1)S(1)} %bitcast.3, ...), custom_call_target="tpu_custom_call" | custom-call | flops 8000000000 | bytes 4194304 | tf_op jit(solution)/shard_map/points/pallas_call | solution.py:210
  227.6 10.0 %points.6 = (bf16[8,4,32,256]{3,2,1,0:T(8,128)(2,1)S(1)}, bf16[8,4,32,256]{3,2,1,0:T(8,128)(2,1)S(1)}, bf16[8,4,32,256]{3,2,1,0:T(8,128)(2,1)S(1)}, bf16[8,4,32,256]{3,2,1,0:T(8,128)(2,1)S(1)}) custom-call(s32[2]{0:T(128)S(1)} %pad_add_fusion.pos, bf16[352,128]{1,0:T(8,128)(2,1)S(1)} %copy.15.basis, bf16[128,352]{1,0:T(8,128)(2,1)S(1)} %bitcast.4, ...), custom_call_target="tpu_custom_call" | custom-call | flops 8000000000 | bytes 4194304 | tf_op jit(solution)/shard_map/points/pallas_call | solution.py:210
  238.0 8.7 %collective-permute-done.19.refs_3_ = bf16[8,4,32,256]{3,2,1,0:T(8,128)(2,1)S(1)} collective-permute-done((bf16[8,4,32,256]{3,2,1,0:T(8,128)(2,1)S(1)}, bf16[8,4,32,256]{3,2,1,0:T(8,128)(2,1)S(1)}, u32[]{:S(2)}, u32[]{:S(2)}) %collective-permute-start.19) | collective-permute-done | bytes 524320 | tf_op jit(solution)/shard_map/ppermute | solution.py:357
  248.8 10.1 %collective-permute-done.11.refs_2_ = bf16[8,4,32,256]{3,2,1,0:T(8,128)(2,1)S(1)} collective-permute-done((bf16[8,4,32,256]{3,2,1,0:T(8,128)(2,1)S(1)}, bf16[8,4,32,256]{3,2,1,0:T(8,128)(2,1)S(1)}, u32[]{:S(2)}, u32[]{:S(2)}) %collective-permute-start.11) | collective-permute-done | bytes 524320 | tf_op jit(solution)/shard_map/ppermute | solution.py:357
  258.8 10.3 %collective-permute-done.12.refs_3_ = bf16[8,4,32,256]{3,2,1,0:T(8,128)(2,1)S(1)} collective-permute-done((bf16[8,4,32,256]{3,2,1,0:T(8,128)(2,1)S(1)}, bf16[8,4,32,256]{3,2,1,0:T(8,128)(2,1)S(1)}, u32[]{:S(2)}, u32[]{:S(2)}) %collective-permute-start.12) | collective-permute-done | bytes 524320 | tf_op jit(solution)/shard_map/ppermute | solution.py:357
  270.7 10.0 %points.5 = (bf16[8,4,32,256]{3,2,1,0:T(8,128)(2,1)S(1)}, bf16[8,4,32,256]{3,2,1,0:T(8,128)(2,1)S(1)}, bf16[8,4,32,256]{3,2,1,0:T(8,128)(2,1)S(1)}, bf16[8,4,32,256]{3,2,1,0:T(8,128)(2,1)S(1)}) custom-call(s32[2]{0:T(128)S(1)} %pad_add_fusion.pos, bf16[352,128]{1,0:T(8,128)(2,1)S(1)} %copy.15.basis, bf16[128,352]{1,0:T(8,128)(2,1)S(1)} %bitcast.5, ...), custom_call_target="tpu_custom_call" | custom-call | flops 8000000000 | bytes 4194304 | tf_op jit(solution)/shard_map/points/pallas_call | solution.py:210
  282.0 9.6 %collective-permute-done.39.refs_3_ = bf16[8,4,32,256]{3,2,1,0:T(8,128)(2,1)S(1)} collective-permute-done((bf16[8,4,32,256]{3,2,1,0:T(8,128)(2,1)S(1)}, bf16[8,4,32,256]{3,2,1,0:T(8,128)(2,1)S(1)}, u32[]{:S(2)}, u32[]{:S(2)}) %collective-permute-start.39) | collective-permute-done | bytes 524320 | tf_op jit(solution)/shard_map/ppermute | solution.py:357
  293.7 10.1 %collective-permute-done.31.refs_2_.refs_3_ = bf16[8,4,32,256]{3,2,1,0:T(8,128)(2,1)S(1)} collective-permute-done((bf16[8,4,32,256]{3,2,1,0:T(8,128)(2,1)S(1)}, bf16[8,4,32,256]{3,2,1,0:T(8,128)(2,1)S(1)}, u32[]{:S(2)}, u32[]{:S(2)}) %collective-permute-start.31) | collective-permute-done | bytes 524320 | tf_op jit(solution)/shard_map/ppermute | solution.py:357
  303.8 4.4 %collective-permute-start.13 = (bf16[32,2,32,256]{3,2,1,0:T(8,128)(2,1)S(1)}, bf16[32,2,32,256]{3,2,1,0:T(8,128)(2,1)S(1)}, u32[]{:S(2)}, u32[]{:S(2)}) collective-permute-start(bf16[32,2,32,256]{3,2,1,0:T(8,128)(2,1)S(1)} %collect.4), channel_id=1, source_target_pairs={{0,4},{4,0},{8,12},{12,8},{16,20},{20,16},{24,28},{28,24},{1,5},{5... | collective-permute-start | bytes 3145736 | tf_op jit(solution)/shard_map/ppermute | solution.py:349
  308.2 10.0 %points.7 = (bf16[8,4,32,256]{3,2,1,0:T(8,128)(2,1)S(1)}, bf16[8,4,32,256]{3,2,1,0:T(8,128)(2,1)S(1)}, bf16[8,4,32,256]{3,2,1,0:T(8,128)(2,1)S(1)}, bf16[8,4,32,256]{3,2,1,0:T(8,128)(2,1)S(1)}) custom-call(s32[2]{0:T(128)S(1)} %pad_add_fusion.pos, bf16[352,128]{1,0:T(8,128)(2,1)S(1)} %copy.15.basis, bf16[128,352]{1,0:T(8,128)(2,1)S(1)} %bitcast.6, ...), custom_call_target="tpu_custom_call" | custom-call | flops 8000000000 | bytes 4194304 | tf_op jit(solution)/shard_map/points/pallas_call | solution.py:210
  318.3 7.9 %collective-permute-done.21.refs_2_.refs_3_ = bf16[8,4,32,256]{3,2,1,0:T(8,128)(2,1)S(1)} collective-permute-done((bf16[8,4,32,256]{3,2,1,0:T(8,128)(2,1)S(1)}, bf16[8,4,32,256]{3,2,1,0:T(8,128)(2,1)S(1)}, u32[]{:S(2)}, u32[]{:S(2)}) %collective-permute-start.21) | collective-permute-done | bytes 524320 | tf_op jit(solution)/shard_map/ppermute | solution.py:357
  327.8 8.8 %collective-permute-done.22.refs_3_.refs_4_ = bf16[8,4,32,256]{3,2,1,0:T(8,128)(2,1)S(1)} collective-permute-done((bf16[8,4,32,256]{3,2,1,0:T(8,128)(2,1)S(1)}, bf16[8,4,32,256]{3,2,1,0:T(8,128)(2,1)S(1)}, u32[]{:S(2)}, u32[]{:S(2)}) %collective-permute-start.22) | collective-permute-done | bytes 524320 | tf_op jit(solution)/shard_map/ppermute | solution.py:357
  336.6 1.8 collective-permute-start.42
  339.1 4.5 %collective-permute-start.23 = (bf16[32,2,32,256]{3,2,1,0:T(8,128)(2,1)S(1)}, bf16[32,2,32,256]{3,2,1,0:T(8,128)(2,1)S(1)}, u32[]{:S(2)}, u32[]{:S(2)}) collective-permute-start(bf16[32,2,32,256]{3,2,1,0:T(8,128)(2,1)S(1)} %collect.5), channel_id=1, source_target_pairs={{0,4},{4,0},{8,12},{12,8},{16,20},{20,16},{24,28},{28,24},{1,5},{5... | collective-permute-start | bytes 3145736 | tf_op jit(solution)/shard_map/ppermute | solution.py:349
  344.4 4.3 %collective-permute-done.41.refs_2_.refs_3_ = bf16[8,4,32,256]{3,2,1,0:T(8,128)(2,1)S(1)} collective-permute-done((bf16[8,4,32,256]{3,2,1,0:T(8,128)(2,1)S(1)}, bf16[8,4,32,256]{3,2,1,0:T(8,128)(2,1)S(1)}, u32[]{:S(2)}, u32[]{:S(2)}) %collective-permute-start.41) | collective-permute-done | bytes 524320 | tf_op jit(solution)/shard_map/ppermute | solution.py:357
  348.7 10.3 %collective-permute-done.42.refs_3_.refs_4_ = bf16[8,4,32,256]{3,2,1,0:T(8,128)(2,1)S(1)} collective-permute-done((bf16[8,4,32,256]{3,2,1,0:T(8,128)(2,1)S(1)}, bf16[8,4,32,256]{3,2,1,0:T(8,128)(2,1)S(1)}, u32[]{:S(2)}, u32[]{:S(2)}) %collective-permute-start.42) | collective-permute-done | bytes 524320 | tf_op jit(solution)/shard_map/ppermute | solution.py:357
  359.7 4.5 %collective-permute-start.43 = (bf16[32,2,32,256]{3,2,1,0:T(8,128)(2,1)S(1)}, bf16[32,2,32,256]{3,2,1,0:T(8,128)(2,1)S(1)}, u32[]{:S(2)}, u32[]{:S(2)}) collective-permute-start(bf16[32,2,32,256]{3,2,1,0:T(8,128)(2,1)S(1)} %collect.7), channel_id=1, source_target_pairs={{0,4},{4,0},{8,12},{12,8},{16,20},{20,16},{24,28},{28,24},{1,5},{5... | collective-permute-start | bytes 3145736 | tf_op jit(solution)/shard_map/ppermute | solution.py:349
  364.2 7.0 %settle.4.refs_0_ = bf16[2,32,256,256]{3,2,1,0:T(8,128)(2,1)} custom-call(s32[2]{0:T(128)S(1)} %pad_add_fusion.pos, bf16[8,4,32,256]{3,2,1,0:T(8,128)(2,1)S(1)} %get-tuple-element.51.refs_0_, bf16[8,4,32,256]{3,2,1,0:T(8,128)(2,1)S(1)} %collective-permute-done.10.refs_1_, bf16[8,4,32,256]{3,2,1,0:T(8,128)(2,1)S(1)} %collective-permute-done.11.refs_2_, ...), custom_call_target="tpu_custom_call" | custom-call | flops 3000000000 | bytes 4194304 | tf_op jit(solution)/shard_map/settle/pallas_call | solution.py:314
  371.2 7.0 %settle.5.refs_0_ = bf16[2,32,256,256]{3,2,1,0:T(8,128)(2,1)} custom-call(s32[2]{0:T(128)S(1)} %pad_add_fusion.pos, bf16[2,32,256,256]{3,2,1,0:T(8,128)(2,1)} %settle.4.refs_0_, bf16[8,4,32,256]{3,2,1,0:T(8,128)(2,1)S(1)} %get-tuple-element.61.refs_0_.refs_1_, ...), custom_call_target="tpu_custom_call", output_to_operand_aliasing={{}: (1, {})} | custom-call | flops 3000000000 | bytes 4194304 | tf_op jit(solution)/shard_map/settle/pallas_call | solution.py:314
  378.2 11.9 %collective-permute-done.33.refs_5_ = bf16[32,2,32,256]{3,2,1,0:T(8,128)(2,1)S(1)} collective-permute-done((bf16[32,2,32,256]{3,2,1,0:T(8,128)(2,1)S(1)}, bf16[32,2,32,256]{3,2,1,0:T(8,128)(2,1)S(1)}, u32[]{:S(2)}, u32[]{:S(2)}) %collective-permute-start.33) | collective-permute-done | bytes 1048608 | tf_op jit(solution)/shard_map/ppermute | solution.py:349
  390.1 7.0 %settle.6.refs_0_ = bf16[2,32,256,256]{3,2,1,0:T(8,128)(2,1)} custom-call(s32[2]{0:T(128)S(1)} %pad_add_fusion.pos, bf16[2,32,256,256]{3,2,1,0:T(8,128)(2,1)} %settle.5.refs_0_, bf16[8,4,32,256]{3,2,1,0:T(8,128)(2,1)S(1)} %get-tuple-element.71.refs_0_.refs_1_, ...), custom_call_target="tpu_custom_call", output_to_operand_aliasing={{}: (1, {})} | custom-call | flops 3000000000 | bytes 4194304 | tf_op jit(solution)/shard_map/settle/pallas_call | solution.py:314
  397.1 14.6 %collective-permute-done.43.refs_5_ = bf16[32,2,32,256]{3,2,1,0:T(8,128)(2,1)S(1)} collective-permute-done((bf16[32,2,32,256]{3,2,1,0:T(8,128)(2,1)S(1)}, bf16[32,2,32,256]{3,2,1,0:T(8,128)(2,1)S(1)}, u32[]{:S(2)}, u32[]{:S(2)}) %collective-permute-start.43) | collective-permute-done | bytes 1048608 | tf_op jit(solution)/shard_map/ppermute | solution.py:349
  411.7 7.0 %settle.7 = bf16[2,32,256,256]{3,2,1,0:T(8,128)(2,1)} custom-call(s32[2]{0:T(128)S(1)} %pad_add_fusion.pos, bf16[2,32,256,256]{3,2,1,0:T(8,128)(2,1)} %settle.6.refs_0_, bf16[8,4,32,256]{3,2,1,0:T(8,128)(2,1)S(1)} %get-tuple-element.81.refs_0_.refs_1_, ...), custom_call_target="tpu_custom_call", output_to_operand_aliasing={{}: (1, {})} | custom-call | flops 3000000000 | bytes 4194304 | tf_op jit(solution)/shard_map/settle/pallas_call | solution.py:314
  (124 shorter events, 40.3 us)
Async XLA Ops:
  2.4 25.8 %collective-permute-start.2 = (f32[2,130,256]{2,1,0:T(8,128)}, f32[2,130,256]{2,1,0:T(8,128)S(1)}, u32[]{:S(2)}, u32[]{:S(2)}) collective-permute-start(f32[2,130,256]{2,1,0:T(8,128)} %get-tuple-element.88), channel_id=1, source_target_pairs={{0,4},{4,0},{8,12},{12,8},{16,20},{20,16},{24,28},{28,24},{1,5},{5... | collective-permute-start | bytes 798728 | tf_op jit(solution)/shard_map/ppermute | solution.py:349
  6.0 24.2 %collective-permute-start.1 = (f32[1,130,256]{2,1,0:T(8,128)}, f32[1,130,256]{2,1,0:T(8,128)}, u32[]{:S(2)}, u32[]{:S(2)}) collective-permute-start(f32[1,130,256]{2,1,0:T(8,128)} %slice.40), channel_id=1, source_target_pairs={{4,12},{8,0},{12,20},{16,8},{20,28},{24,16},{5,13},{9,1},{13,21},{... | collective-permute-start | bytes 399368 | tf_op jit(solution)/shard_map/ppermute | solution.py:352
  13.8 70.3 %collective-permute-start.14 = (bf16[32,2,32,256]{3,2,1,0:T(8,128)(2,1)S(1)}, bf16[32,2,32,256]{3,2,1,0:T(8,128)(2,1)S(1)}, u32[]{:S(2)}, u32[]{:S(2)}) collective-permute-start(bf16[32,2,32,256]{3,2,1,0:T(8,128)(2,1)S(1)} %get-tuple-element.55.refs_2_.refs_6_), channel_id=1, source_target_pairs={{4,12},{8,0},{12,20},{16,8},{20,28},{24,16},{5,13},{9,1},{13,21},{... | collective-permute-start | bytes 3145736 | tf_op jit(solution)/shard_map/ppermute | solution.py:352
  15.1 70.2 %collective-permute-start.15 = (bf16[32,2,32,256]{3,2,1,0:T(8,128)(2,1)}, bf16[32,2,32,256]{3,2,1,0:T(8,128)(2,1)}, u32[]{:S(2)}, u32[]{:S(2)}) collective-permute-start(bf16[32,2,32,256]{3,2,1,0:T(8,128)(2,1)} %get-tuple-element.56), channel_id=1, source_target_pairs={{0,4},{4,0},{8,12},{12,8},{16,20},{20,16},{24,28},{28,24},{1,5},{5... | collective-permute-start | bytes 3145736 | tf_op jit(solution)/shard_map/ppermute | solution.py:349
  27.1 60.8 %collective-permute-start.25 = (bf16[32,2,32,256]{3,2,1,0:T(8,128)(2,1)}, bf16[32,2,32,256]{3,2,1,0:T(8,128)(2,1)}, u32[]{:S(2)}, u32[]{:S(2)}) collective-permute-start(bf16[32,2,32,256]{3,2,1,0:T(8,128)(2,1)} %get-tuple-element.66), channel_id=1, source_target_pairs={{0,4},{4,0},{8,12},{12,8},{16,20},{20,16},{24,28},{28,24},{1,5},{5... | collective-permute-start | bytes 3145736 | tf_op jit(solution)/shard_map/ppermute | solution.py:349
  28.2 43.1 %collective-permute-start = (f32[2,128,256]{2,1,0:T(8,128)S(1)}, f32[2,128,256]{2,1,0:T(8,128)S(1)}, u32[]{:S(2)}, u32[]{:S(2)}) collective-permute-start(f32[2,128,256]{2,1,0:T(8,128)S(1)} %get-tuple-element.91), channel_id=1, source_target_pairs={{0,4},{4,0},{8,12},{12,8},{16,20},{20,16},{24,28},{28,24},{1,5},{5... | collective-permute-start | bytes 786440 | tf_op jit(solution)/shard_map/ppermute | solution.py:349
  30.2 42.3 %collective-permute-start.3 = (f32[1,130,256]{2,1,0:T(8,128)S(1)}, f32[1,130,256]{2,1,0:T(8,128)S(1)}, u32[]{:S(2)}, u32[]{:S(2)}) collective-permute-start(f32[1,130,256]{2,1,0:T(8,128)S(1)} %slice.41), channel_id=1, source_target_pairs={{12,4},{0,8},{20,12},{8,16},{28,20},{16,24},{13,5},{1,9},{21,13},{... | collective-permute-start | bytes 399368 | tf_op jit(solution)/shard_map/ppermute | solution.py:352
  41.1 52.0 %copy-start.17 = (f32[343]{0:T(512)S(1)}, f32[343]{0:T(512)}, u32[]{:S(2)}) copy-start(f32[343]{0:T(512)} %param.13) | copy-start | bytes 4120
  41.1 52.0 %copy-start.18 = (f32[343]{0:T(512)S(1)}, f32[343]{0:T(512)}, u32[]{:S(2)}) copy-start(f32[343]{0:T(512)} %param.11) | copy-start | bytes 4120
  41.1 52.0 %copy-start.19 = (f32[343]{0:T(512)S(1)}, f32[343]{0:T(512)}, u32[]{:S(2)}) copy-start(f32[343]{0:T(512)} %param.12) | copy-start | bytes 4120
  71.2 25.9 %collective-permute-start.24 = (bf16[32,2,32,256]{3,2,1,0:T(8,128)(2,1)}, bf16[32,2,32,256]{3,2,1,0:T(8,128)(2,1)}, u32[]{:S(2)}, u32[]{:S(2)}) collective-permute-start(bf16[32,2,32,256]{3,2,1,0:T(8,128)(2,1)} %get-tuple-element.65.refs_2_.refs_6_), channel_id=1, source_target_pairs={{4,12},{8,0},{12,20},{16,8},{20,28},{24,16},{5,13},{9,1},{13,21},{... | collective-permute-start | bytes 3145736 | tf_op jit(solution)/shard_map/ppermute | solution.py:352
  72.6 29.4 %collective-permute-start.35 = (bf16[32,2,32,256]{3,2,1,0:T(8,128)(2,1)}, bf16[32,2,32,256]{3,2,1,0:T(8,128)(2,1)}, u32[]{:S(2)}, u32[]{:S(2)}) collective-permute-start(bf16[32,2,32,256]{3,2,1,0:T(8,128)(2,1)} %get-tuple-element.76), channel_id=1, source_target_pairs={{0,4},{4,0},{8,12},{12,8},{16,20},{20,16},{24,28},{28,24},{1,5},{5... | collective-permute-start | bytes 3145736 | tf_op jit(solution)/shard_map/ppermute | solution.py:349
  84.2 92.2 %copy-start = (bf16[34,2,32,256]{3,2,1,0:T(8,128)(2,1)}, bf16[34,2,32,256]{3,2,1,0:T(8,128)(2,1)S(1)}, u32[]{:S(2)}) copy-start(bf16[34,2,32,256]{3,2,1,0:T(8,128)(2,1)S(1)} %get-tuple-element.45.refs_2_.refs_6_) | copy-start | bytes 3342340
  85.3 37.7 %collective-permute-start.5 = (bf16[34,2,32,256]{3,2,1,0:T(8,128)(2,1)}, bf16[34,2,32,256]{3,2,1,0:T(8,128)(2,1)S(1)}, u32[]{:S(2)}, u32[]{:S(2)}) collective-permute-start(bf16[34,2,32,256]{3,2,1,0:T(8,128)(2,1)} %get-tuple-element.46), channel_id=1, source_target_pairs={{0,4},{4,0},{8,12},{12,8},{16,20},{20,16},{24,28},{28,24},{1,5},{5... | collective-permute-start | bytes 3342344 | tf_op jit(solution)/shard_map/ppermute | solution.py:349
  85.3 39.0 %collective-permute-start.16 = (bf16[32,2,32,256]{3,2,1,0:T(8,128)(2,1)}, bf16[32,2,32,256]{3,2,1,0:T(8,128)(2,1)}, u32[]{:S(2)}, u32[]{:S(2)}) collective-permute-start(bf16[32,2,32,256]{3,2,1,0:T(8,128)(2,1)} %collective-permute-done.15.refs_1_.refs_5_), channel_id=1, source_target_pairs={{12,4},{0,8},{20,12},{8,16},{28,20},{16,24},{13,5},{1,9},{21,13},{... | collective-permute-start | bytes 3145736 | tf_op jit(solution)/shard_map/ppermute | solution.py:352
  88.0 45.4 %collective-permute-start.26 = (bf16[32,2,32,256]{3,2,1,0:T(8,128)(2,1)}, bf16[32,2,32,256]{3,2,1,0:T(8,128)(2,1)}, u32[]{:S(2)}, u32[]{:S(2)}) collective-permute-start(bf16[32,2,32,256]{3,2,1,0:T(8,128)(2,1)} %collective-permute-done.25.refs_1_.refs_5_), channel_id=1, source_target_pairs={{12,4},{0,8},{20,12},{8,16},{28,20},{16,24},{13,5},{1,9},{21,13},{... | collective-permute-start | bytes 3145736 | tf_op jit(solution)/shard_map/ppermute | solution.py:352
  97.2 52.0 %collective-permute-start.34 = (bf16[32,2,32,256]{3,2,1,0:T(8,128)(2,1)}, bf16[32,2,32,256]{3,2,1,0:T(8,128)(2,1)}, u32[]{:S(2)}, u32[]{:S(2)}) collective-permute-start(bf16[32,2,32,256]{3,2,1,0:T(8,128)(2,1)} %copy-done.8), channel_id=1, source_target_pairs={{4,12},{8,0},{12,20},{16,8},{20,28},{24,16},{5,13},{9,1},{13,21},{... | collective-permute-start | bytes 3145736 | tf_op jit(solution)/shard_map/ppermute | solution.py:352
  101.9 53.9 %collective-permute-start.36 = (bf16[32,2,32,256]{3,2,1,0:T(8,128)(2,1)}, bf16[32,2,32,256]{3,2,1,0:T(8,128)(2,1)}, u32[]{:S(2)}, u32[]{:S(2)}) collective-permute-start(bf16[32,2,32,256]{3,2,1,0:T(8,128)(2,1)} %collective-permute-done.35.refs_1_), channel_id=1, source_target_pairs={{12,4},{0,8},{20,12},{8,16},{28,20},{16,24},{13,5},{1,9},{21,13},{... | collective-permute-start | bytes 3145736 | tf_op jit(solution)/shard_map/ppermute | solution.py:352
  123.0 45.8 %collective-permute-start.4 = (bf16[34,2,32,256]{3,2,1,0:T(8,128)(2,1)S(1)}, bf16[34,2,32,256]{3,2,1,0:T(8,128)(2,1)S(1)}, u32[]{:S(2)}, u32[]{:S(2)}) collective-permute-start(bf16[34,2,32,256]{3,2,1,0:T(8,128)(2,1)S(1)} %get-tuple-element.45.refs_2_.refs_6_), channel_id=1, source_target_pairs={{4,12},{8,0},{12,20},{16,8},{20,28},{24,16},{5,13},{9,1},{13,21},{... | collective-permute-start | bytes 3342344 | tf_op jit(solution)/shard_map/ppermute | solution.py:352
  124.3 52.0 %collective-permute-start.6 = (bf16[34,2,32,256]{3,2,1,0:T(8,128)(2,1)S(1)}, bf16[34,2,32,256]{3,2,1,0:T(8,128)(2,1)S(1)}, u32[]{:S(2)}, u32[]{:S(2)}) collective-permute-start(bf16[34,2,32,256]{3,2,1,0:T(8,128)(2,1)S(1)} %collective-permute-done.5.refs_1_.refs_5_), channel_id=1, source_target_pairs={{12,4},{0,8},{20,12},{8,16},{28,20},{16,24},{13,5},{1,9},{21,13},{... | collective-permute-start | bytes 3342344 | tf_op jit(solution)/shard_map/ppermute | solution.py:352
  149.0 75.7 %collective-permute-start.27 = (bf16[8,4,32,256]{3,2,1,0:T(8,128)(2,1)S(1)}, bf16[8,4,32,256]{3,2,1,0:T(8,128)(2,1)S(1)}, u32[]{:S(2)}, u32[]{:S(2)}) collective-permute-start(bf16[8,4,32,256]{3,2,1,0:T(8,128)(2,1)S(1)} %get-tuple-element.68), channel_id=1, source_target_pairs={{0,1},{1,0},{2,3},{3,2},{4,5},{5,4},{6,7},{7,6},{8,9},{9,8},{10,11... | collective-permute-start | bytes 1572872 | tf_op jit(solution)/shard_map/ppermute | solution.py:357
  149.1 76.6 %collective-permute-start.28 = (bf16[8,4,32,256]{3,2,1,0:T(8,128)(2,1)S(1)}, bf16[8,4,32,256]{3,2,1,0:T(8,128)(2,1)S(1)}, u32[]{:S(2)}, u32[]{:S(2)}) collective-permute-start(bf16[8,4,32,256]{3,2,1,0:T(8,128)(2,1)S(1)} %get-tuple-element.69), channel_id=1, source_target_pairs={{0,2},{1,3},{2,0},{3,1},{4,6},{5,7},{6,4},{7,5},{8,10},{9,11},{10,... | collective-permute-start | bytes 1572872 | tf_op jit(solution)/shard_map/ppermute | solution.py:357
  187.8 14.7 %collective-permute-start.7 = (bf16[8,4,32,256]{3,2,1,0:T(8,128)(2,1)S(1)}, bf16[8,4,32,256]{3,2,1,0:T(8,128)(2,1)S(1)}, u32[]{:S(2)}, u32[]{:S(2)}) collective-permute-start(bf16[8,4,32,256]{3,2,1,0:T(8,128)(2,1)S(1)} %get-tuple-element.48), channel_id=1, source_target_pairs={{0,1},{1,0},{2,3},{3,2},{4,5},{5,4},{6,7},{7,6},{8,9},{9,8},{10,11... | collective-permute-start | bytes 1572872 | tf_op jit(solution)/shard_map/ppermute | solution.py:357
  187.9 16.2 %collective-permute-start.8 = (bf16[8,4,32,256]{3,2,1,0:T(8,128)(2,1)S(1)}, bf16[8,4,32,256]{3,2,1,0:T(8,128)(2,1)S(1)}, u32[]{:S(2)}, u32[]{:S(2)}) collective-permute-start(bf16[8,4,32,256]{3,2,1,0:T(8,128)(2,1)S(1)} %get-tuple-element.49), channel_id=1, source_target_pairs={{0,2},{1,3},{2,0},{3,1},{4,6},{5,7},{6,4},{7,5},{8,10},{9,11},{10,... | collective-permute-start | bytes 1572872 | tf_op jit(solution)/shard_map/ppermute | solution.py:357
  189.4 23.5 %collective-permute-start.9 = (bf16[8,4,32,256]{3,2,1,0:T(8,128)(2,1)S(1)}, bf16[8,4,32,256]{3,2,1,0:T(8,128)(2,1)S(1)}, u32[]{:S(2)}, u32[]{:S(2)}) collective-permute-start(bf16[8,4,32,256]{3,2,1,0:T(8,128)(2,1)S(1)} %get-tuple-element.50), channel_id=1, source_target_pairs={{0,3},{1,2},{2,1},{3,0},{4,7},{5,6},{6,5},{7,4},{8,11},{9,10},{10,... | collective-permute-start | bytes 1572872 | tf_op jit(solution)/shard_map/ppermute | solution.py:357
  202.5 23.2 %collective-permute-start.29 = (bf16[8,4,32,256]{3,2,1,0:T(8,128)(2,1)S(1)}, bf16[8,4,32,256]{3,2,1,0:T(8,128)(2,1)S(1)}, u32[]{:S(2)}, u32[]{:S(2)}) collective-permute-start(bf16[8,4,32,256]{3,2,1,0:T(8,128)(2,1)S(1)} %get-tuple-element.70), channel_id=1, source_target_pairs={{0,3},{1,2},{2,1},{3,0},{4,7},{5,6},{6,5},{7,4},{8,11},{9,10},{10,... | collective-permute-start | bytes 1572872 | tf_op jit(solution)/shard_map/ppermute | solution.py:357
  204.0 23.3 %collective-permute-start.17 = (bf16[8,4,32,256]{3,2,1,0:T(8,128)(2,1)S(1)}, bf16[8,4,32,256]{3,2,1,0:T(8,128)(2,1)S(1)}, u32[]{:S(2)}, u32[]{:S(2)}) collective-permute-start(bf16[8,4,32,256]{3,2,1,0:T(8,128)(2,1)S(1)} %get-tuple-element.58), channel_id=1, source_target_pairs={{0,1},{1,0},{2,3},{3,2},{4,5},{5,4},{6,7},{7,6},{8,9},{9,8},{10,11... | collective-permute-start | bytes 1572872 | tf_op jit(solution)/shard_map/ppermute | solution.py:357
  213.0 24.6 %collective-permute-start.18 = (bf16[8,4,32,256]{3,2,1,0:T(8,128)(2,1)S(1)}, bf16[8,4,32,256]{3,2,1,0:T(8,128)(2,1)S(1)}, u32[]{:S(2)}, u32[]{:S(2)}) collective-permute-start(bf16[8,4,32,256]{3,2,1,0:T(8,128)(2,1)S(1)} %get-tuple-element.59), channel_id=1, source_target_pairs={{0,2},{1,3},{2,0},{3,1},{4,6},{5,7},{6,4},{7,5},{8,10},{9,11},{10,... | collective-permute-start | bytes 1572872 | tf_op jit(solution)/shard_map/ppermute | solution.py:357
  224.8 21.9 %collective-permute-start.19 = (bf16[8,4,32,256]{3,2,1,0:T(8,128)(2,1)S(1)}, bf16[8,4,32,256]{3,2,1,0:T(8,128)(2,1)S(1)}, u32[]{:S(2)}, u32[]{:S(2)}) collective-permute-start(bf16[8,4,32,256]{3,2,1,0:T(8,128)(2,1)S(1)} %get-tuple-element.60), channel_id=1, source_target_pairs={{0,3},{1,2},{2,1},{3,0},{4,7},{5,6},{6,5},{7,4},{8,11},{9,10},{10,... | collective-permute-start | bytes 1572872 | tf_op jit(solution)/shard_map/ppermute | solution.py:357
  225.7 22.5 %collective-permute-start.10 = (bf16[8,4,32,256]{3,2,1,0:T(8,128)(2,1)S(1)}, bf16[8,4,32,256]{3,2,1,0:T(8,128)(2,1)S(1)}, u32[]{:S(2)}, u32[]{:S(2)}) collective-permute-start(bf16[8,4,32,256]{3,2,1,0:T(8,128)(2,1)S(1)} %get-tuple-element.52), channel_id=1, source_target_pairs={{0,1},{1,0},{2,3},{3,2},{4,5},{5,4},{6,7},{7,6},{8,9},{9,8},{10,11... | collective-permute-start | bytes 1572872 | tf_op jit(solution)/shard_map/ppermute | solution.py:357
  225.7 33.1 %collective-permute-start.11 = (bf16[8,4,32,256]{3,2,1,0:T(8,128)(2,1)S(1)}, bf16[8,4,32,256]{3,2,1,0:T(8,128)(2,1)S(1)}, u32[]{:S(2)}, u32[]{:S(2)}) collective-permute-start(bf16[8,4,32,256]{3,2,1,0:T(8,128)(2,1)S(1)} %get-tuple-element.53), channel_id=1, source_target_pairs={{0,2},{1,3},{2,0},{3,1},{4,6},{5,7},{6,4},{7,5},{8,10},{9,11},{10,... | collective-permute-start | bytes 1572872 | tf_op jit(solution)/shard_map/ppermute | solution.py:357
  227.3 41.9 %collective-permute-start.12 = (bf16[8,4,32,256]{3,2,1,0:T(8,128)(2,1)S(1)}, bf16[8,4,32,256]{3,2,1,0:T(8,128)(2,1)S(1)}, u32[]{:S(2)}, u32[]{:S(2)}) collective-permute-start(bf16[8,4,32,256]{3,2,1,0:T(8,128)(2,1)S(1)} %get-tuple-element.54), channel_id=1, source_target_pairs={{0,3},{1,2},{2,1},{3,0},{4,7},{5,6},{6,5},{7,4},{8,11},{9,10},{10,... | collective-permute-start | bytes 1572872 | tf_op jit(solution)/shard_map/ppermute | solution.py:357
  237.6 43.7 %collective-permute-start.37 = (bf16[8,4,32,256]{3,2,1,0:T(8,128)(2,1)S(1)}, bf16[8,4,32,256]{3,2,1,0:T(8,128)(2,1)S(1)}, u32[]{:S(2)}, u32[]{:S(2)}) collective-permute-start(bf16[8,4,32,256]{3,2,1,0:T(8,128)(2,1)S(1)} %get-tuple-element.78), channel_id=1, source_target_pairs={{0,1},{1,0},{2,3},{3,2},{4,5},{5,4},{6,7},{7,6},{8,9},{9,8},{10,11... | collective-permute-start | bytes 1572872 | tf_op jit(solution)/shard_map/ppermute | solution.py:357
  246.7 35.3 %collective-permute-start.38 = (bf16[8,4,32,256]{3,2,1,0:T(8,128)(2,1)S(1)}, bf16[8,4,32,256]{3,2,1,0:T(8,128)(2,1)S(1)}, u32[]{:S(2)}, u32[]{:S(2)}) collective-permute-start(bf16[8,4,32,256]{3,2,1,0:T(8,128)(2,1)S(1)} %get-tuple-element.79), channel_id=1, source_target_pairs={{0,2},{1,3},{2,0},{3,1},{4,6},{5,7},{6,4},{7,5},{8,10},{9,11},{10,... | collective-permute-start | bytes 1572872 | tf_op jit(solution)/shard_map/ppermute | solution.py:357
  248.2 43.4 %collective-permute-start.39 = (bf16[8,4,32,256]{3,2,1,0:T(8,128)(2,1)S(1)}, bf16[8,4,32,256]{3,2,1,0:T(8,128)(2,1)S(1)}, u32[]{:S(2)}, u32[]{:S(2)}) collective-permute-start(bf16[8,4,32,256]{3,2,1,0:T(8,128)(2,1)S(1)} %get-tuple-element.80), channel_id=1, source_target_pairs={{0,3},{1,2},{2,1},{3,0},{4,7},{5,6},{6,5},{7,4},{8,11},{9,10},{10,... | collective-permute-start | bytes 1572872 | tf_op jit(solution)/shard_map/ppermute | solution.py:357
  258.8 34.3 %collective-permute-start.30 = (bf16[8,4,32,256]{3,2,1,0:T(8,128)(2,1)S(1)}, bf16[8,4,32,256]{3,2,1,0:T(8,128)(2,1)S(1)}, u32[]{:S(2)}, u32[]{:S(2)}) collective-permute-start(bf16[8,4,32,256]{3,2,1,0:T(8,128)(2,1)S(1)} %get-tuple-element.72), channel_id=1, source_target_pairs={{0,1},{1,0},{2,3},{3,2},{4,5},{5,4},{6,7},{7,6},{8,9},{9,8},{10,11... | collective-permute-start | bytes 1572872 | tf_op jit(solution)/shard_map/ppermute | solution.py:357
  269.2 34.6 %collective-permute-start.31 = (bf16[8,4,32,256]{3,2,1,0:T(8,128)(2,1)S(1)}, bf16[8,4,32,256]{3,2,1,0:T(8,128)(2,1)S(1)}, u32[]{:S(2)}, u32[]{:S(2)}) collective-permute-start(bf16[8,4,32,256]{3,2,1,0:T(8,128)(2,1)S(1)} %get-tuple-element.73), channel_id=1, source_target_pairs={{0,2},{1,3},{2,0},{3,1},{4,6},{5,7},{6,4},{7,5},{8,10},{9,11},{10,... | collective-permute-start | bytes 1572872 | tf_op jit(solution)/shard_map/ppermute | solution.py:357
  281.4 57.7 %collective-permute-start.32 = (bf16[8,4,32,256]{3,2,1,0:T(8,128)(2,1)S(1)}, bf16[8,4,32,256]{3,2,1,0:T(8,128)(2,1)S(1)}, u32[]{:S(2)}, u32[]{:S(2)}) collective-permute-start(bf16[8,4,32,256]{3,2,1,0:T(8,128)(2,1)S(1)} %get-tuple-element.74), channel_id=1, source_target_pairs={{0,3},{1,2},{2,1},{3,0},{4,7},{5,6},{6,5},{7,4},{8,11},{9,10},{10,... | collective-permute-start | bytes 1572872 | tf_op jit(solution)/shard_map/ppermute | solution.py:357
  282.0 36.2 %collective-permute-start.20 = (bf16[8,4,32,256]{3,2,1,0:T(8,128)(2,1)S(1)}, bf16[8,4,32,256]{3,2,1,0:T(8,128)(2,1)S(1)}, u32[]{:S(2)}, u32[]{:S(2)}) collective-permute-start(bf16[8,4,32,256]{3,2,1,0:T(8,128)(2,1)S(1)} %get-tuple-element.62), channel_id=1, source_target_pairs={{0,1},{1,0},{2,3},{3,2},{4,5},{5,4},{6,7},{7,6},{8,9},{9,8},{10,11... | collective-permute-start | bytes 1572872 | tf_op jit(solution)/shard_map/ppermute | solution.py:357
  291.6 34.6 %collective-permute-start.21 = (bf16[8,4,32,256]{3,2,1,0:T(8,128)(2,1)S(1)}, bf16[8,4,32,256]{3,2,1,0:T(8,128)(2,1)S(1)}, u32[]{:S(2)}, u32[]{:S(2)}) collective-permute-start(bf16[8,4,32,256]{3,2,1,0:T(8,128)(2,1)S(1)} %get-tuple-element.63), channel_id=1, source_target_pairs={{0,2},{1,3},{2,0},{3,1},{4,6},{5,7},{6,4},{7,5},{8,10},{9,11},{10,... | collective-permute-start | bytes 1572872 | tf_op jit(solution)/shard_map/ppermute | solution.py:357
  293.2 43.4 %collective-permute-start.22 = (bf16[8,4,32,256]{3,2,1,0:T(8,128)(2,1)S(1)}, bf16[8,4,32,256]{3,2,1,0:T(8,128)(2,1)S(1)}, u32[]{:S(2)}, u32[]{:S(2)}) collective-permute-start(bf16[8,4,32,256]{3,2,1,0:T(8,128)(2,1)S(1)} %get-tuple-element.64), channel_id=1, source_target_pairs={{0,3},{1,2},{2,1},{3,0},{4,7},{5,6},{6,5},{7,4},{8,11},{9,10},{10,... | collective-permute-start | bytes 1572872 | tf_op jit(solution)/shard_map/ppermute | solution.py:357
  303.8 60.5 %collective-permute-start.13 = (bf16[32,2,32,256]{3,2,1,0:T(8,128)(2,1)S(1)}, bf16[32,2,32,256]{3,2,1,0:T(8,128)(2,1)S(1)}, u32[]{:S(2)}, u32[]{:S(2)}) collective-permute-start(bf16[32,2,32,256]{3,2,1,0:T(8,128)(2,1)S(1)} %collect.4), channel_id=1, source_target_pairs={{0,4},{4,0},{8,12},{12,8},{16,20},{20,16},{24,28},{28,24},{1,5},{5... | collective-permute-start | bytes 3145736 | tf_op jit(solution)/shard_map/ppermute | solution.py:349
  318.2 26.1 %collective-permute-start.40 = (bf16[8,4,32,256]{3,2,1,0:T(8,128)(2,1)S(1)}, bf16[8,4,32,256]{3,2,1,0:T(8,128)(2,1)S(1)}, u32[]{:S(2)}, u32[]{:S(2)}) collective-permute-start(bf16[8,4,32,256]{3,2,1,0:T(8,128)(2,1)S(1)} %get-tuple-element.82), channel_id=1, source_target_pairs={{0,1},{1,0},{2,3},{3,2},{4,5},{5,4},{6,7},{7,6},{8,9},{9,8},{10,11... | collective-permute-start | bytes 1572872 | tf_op jit(solution)/shard_map/ppermute | solution.py:357
  326.2 22.5 %collective-permute-start.41 = (bf16[8,4,32,256]{3,2,1,0:T(8,128)(2,1)S(1)}, bf16[8,4,32,256]{3,2,1,0:T(8,128)(2,1)S(1)}, u32[]{:S(2)}, u32[]{:S(2)}) collective-permute-start(bf16[8,4,32,256]{3,2,1,0:T(8,128)(2,1)S(1)} %get-tuple-element.83), channel_id=1, source_target_pairs={{0,2},{1,3},{2,0},{3,1},{4,6},{5,7},{6,4},{7,5},{8,10},{9,11},{10,... | collective-permute-start | bytes 1572872 | tf_op jit(solution)/shard_map/ppermute | solution.py:357
  336.6 22.5 %collective-permute-start.42 = (bf16[8,4,32,256]{3,2,1,0:T(8,128)(2,1)S(1)}, bf16[8,4,32,256]{3,2,1,0:T(8,128)(2,1)S(1)}, u32[]{:S(2)}, u32[]{:S(2)}) collective-permute-start(bf16[8,4,32,256]{3,2,1,0:T(8,128)(2,1)S(1)} %get-tuple-element.84), channel_id=1, source_target_pairs={{0,3},{1,2},{2,1},{3,0},{4,7},{5,6},{6,5},{7,4},{8,11},{9,10},{10,... | collective-permute-start | bytes 1572872 | tf_op jit(solution)/shard_map/ppermute | solution.py:357
  339.1 32.1 %collective-permute-start.23 = (bf16[32,2,32,256]{3,2,1,0:T(8,128)(2,1)S(1)}, bf16[32,2,32,256]{3,2,1,0:T(8,128)(2,1)S(1)}, u32[]{:S(2)}, u32[]{:S(2)}) collective-permute-start(bf16[32,2,32,256]{3,2,1,0:T(8,128)(2,1)S(1)} %collect.5), channel_id=1, source_target_pairs={{0,4},{4,0},{8,12},{12,8},{16,20},{20,16},{24,28},{28,24},{1,5},{5... | collective-permute-start | bytes 3145736 | tf_op jit(solution)/shard_map/ppermute | solution.py:349
  344.3 45.8 %collective-permute-start.33 = (bf16[32,2,32,256]{3,2,1,0:T(8,128)(2,1)S(1)}, bf16[32,2,32,256]{3,2,1,0:T(8,128)(2,1)S(1)}, u32[]{:S(2)}, u32[]{:S(2)}) collective-permute-start(bf16[32,2,32,256]{3,2,1,0:T(8,128)(2,1)S(1)} %collect.6), channel_id=1, source_target_pairs={{0,4},{4,0},{8,12},{12,8},{16,20},{20,16},{24,28},{28,24},{1,5},{5... | collective-permute-start | bytes 3145736 | tf_op jit(solution)/shard_map/ppermute | solution.py:349
  359.7 51.9 %collective-permute-start.43 = (bf16[32,2,32,256]{3,2,1,0:T(8,128)(2,1)S(1)}, bf16[32,2,32,256]{3,2,1,0:T(8,128)(2,1)S(1)}, u32[]{:S(2)}, u32[]{:S(2)}) collective-permute-start(bf16[32,2,32,256]{3,2,1,0:T(8,128)(2,1)S(1)} %collect.7), channel_id=1, source_target_pairs={{0,4},{4,0},{8,12},{12,8},{16,20},{20,16},{24,28},{28,24},{1,5},{5... | collective-permute-start | bytes 3145736 | tf_op jit(solution)/shard_map/ppermute | solution.py:349
  (16 other events, 246.8 us)

commit v2 on v1

v2 whole, which is shorter than its diff:
```python
import functools

import jax
import jax.numpy as jnp
from jax import lax
from jax.experimental import pallas as pl
from jax.experimental.pallas import tpu as pltpu
from jax.sharding import PartitionSpec as P

F32, BF16 = jnp.float32, jnp.bfloat16
ANY = pl.BlockSpec(memory_space=pl.ANY)
VMEM = pl.BlockSpec(memory_space=pltpu.VMEM)
SMEM = pl.BlockSpec(memory_space=pltpu.SMEM)
VMEM_LIMIT = 58 * 1024 * 1024
TOKEN = jax.ShapeDtypeStruct((2,), jnp.int32)
COST = pl.CostEstimate(flops=1, bytes_accessed=1, transcendentals=0)
EDGE = 2
TILE = 16


def params():
    return pltpu.CompilerParams(vmem_limit_bytes=VMEM_LIMIT)


def from_rows(y, group):
    if group % 16 == 0:
        return y.astype(BF16).reshape(-1, group, y.shape[1])
    return y.reshape(-1, group, y.shape[1]).astype(BF16)


def to_bf16_rows(x):
    a, m, y = x.shape
    if m % 16 == 0:
        return x.astype(BF16).reshape(a * m, y)
    return x.astype(F32).reshape(a * m, y).astype(BF16)


def spread_kernel(pos, field, turn, *refs, begin, skip):
    own, send, token, window, sems = refs[-5:]
    side = pos[0]
    token[0], token[1] = pos[0], pos[1]
    _, planes, modes, depth, cols = window.shape
    size = field.shape[2]
    rows = own.shape[0]
    group = turn.shape[1] // TILE
    copies = []
    for a in range(2):
        far = 1 - side if a == 0 else side
        start = jnp.where(far == 1, size - depth - begin, begin)
        start = pl.multiple_of(start, TILE)
        copy = pltpu.make_async_copy(
            field.at[:, :, pl.ds(start, depth), :], window.at[a], sems.at[a]
        )
        copy.start()
        copies.append(copy)
    for a, out in ((0, send), (1, own)):
        far = 1 - side if a == 0 else side
        copies[a].wait()
        for z in range(planes):
            to = jnp.where(far == 1, z, planes - 1 - z)
            for g in range(depth // TILE):
                block = jnp.where(far == 1, depth // TILE - 1 - g, g)
                low, high = max(0, skip - g * TILE), min(TILE, rows + skip - g * TILE)
                if high <= low:
                    continue
                for h in range(modes // group):
                    there = pl.ds(h * group, group)
                    x = window[a, z, there, pl.ds(pl.multiple_of(block * TILE, TILE), TILE), :]
                    y = jnp.dot(turn[far], x.reshape(group * TILE, cols), preferred_element_type=F32)
                    y = from_rows(y, group)
                    out[pl.ds(g * TILE + low - skip, high - low), to, there, :] = y[low:high]


def spread(pos, field, turn, after, begin, skip, rows, depth):
    planes, modes, _, cols = field.shape
    piece = jax.ShapeDtypeStruct((rows, planes, modes, cols), BF16)
    return pl.pallas_call(
        functools.partial(spread_kernel, begin=begin, skip=skip),
        out_shape=(piece, piece, TOKEN),
        in_specs=[SMEM, ANY, VMEM] + [ANY] * len(after),
        out_specs=(VMEM, VMEM, SMEM),
        scratch_shapes=[
            pltpu.VMEM((2, planes, modes, depth, cols), BF16),
            pltpu.SemaphoreType.DMA((2,)),
        ],
        compiler_params=params(),
        cost_estimate=COST,
        name="spread",
    )(pos, field, turn, *after)


def sweep_kernel(pos, rate, shift, *refs, begin, count, heads):
    group = 4
    blocks, refs = refs[:group], refs[group:]
    tails, refs = refs[:heads], refs[heads:]
    outs, (token, field, first, aside, final, sems) = refs[:count], refs[count:]
    token[0], token[1] = pos[0], pos[1]
    _, stack, modes, cols = field.shape
    planes = stack // group
    mine = stack - 2 * planes
    rows = final.shape[0]
    lead = 2 * EDGE if heads else EDGE
    copies = []
    for g in range(group):
        to = pl.ds(g * planes, planes)
        copies.append(
            pltpu.make_async_copy(blocks[g], field.at[pl.ds(lead, rows + 2 * EDGE - lead), to], sems.at[g])
        )
        if heads:
            length = tails[g].shape[0]
            copies.append(
                pltpu.make_async_copy(
                    tails[g].at[pl.ds(length - lead, lead)], field.at[pl.ds(0, lead), to], sems.at[group + g]
                )
            )
    for copy in copies:
        copy.start()
    if not heads:
        field[pl.ds(0, lead)] = jnp.zeros((lead, stack, modes, cols), BF16)
    for copy in copies:
        copy.wait()
    low = planes - 1
    wide = mine + 2
    piece = min(modes, 16)

    def beside(x):
        return jnp.dot(
            to_bf16_rows(x.reshape(-1, modes, cols)), shift[...], preferred_element_type=F32
        ).reshape(x.shape[:2] + (modes, cols))

    def look(j, slot):
        aside[slot] = beside(field[pl.ds(2 * j + 1, 2), pl.ds(low, wide)])

    look(0, 0)

    def pair(j, _):
        slot = j % 2
        i = 2 * j

        look(jnp.minimum(j + 1, (rows + 2) // 2 - 1), 1 - slot)
        for a in range(2):
            speeds = [rate[p, pl.ds(begin + i + a, 1), :] for p in range(wide)]
            for h in range(modes // piece):
                some = pl.ds(h * piece, piece)
                line = [field[i + 1 + a, low - 1 + p, some].astype(F32) for p in range(wide + 2)]
                for p in range(wide):
                    centre = line[p + 1]
                    around = aside[slot, a, p, some] + (line[p] + line[p + 2])
                    around = around + (
                        field[i + a, low + p, some].astype(F32) + field[i + 2 + a, low + p, some].astype(F32)
                    )
                    first[i + a, p, some] = centre + speeds[p] * (around - 6.0 * centre)
        return 0

    lax.fori_loop(0, (rows + 2) // 2, pair, 0)

    def look_again(j, slot):
        aside[slot, :, pl.ds(0, mine)] = beside(first[pl.ds(2 * j + 1, 2), pl.ds(1, mine)])

    look_again(0, 0)

    def pair_again(j, _):
        slot = j % 2
        i = 2 * j

        look_again(jnp.minimum(j + 1, rows // 2 - 1), 1 - slot)
        for a in range(2):
            speeds = [rate[p + 1, pl.ds(begin + i + a + 1, 1), :] for p in range(mine)]
            for h in range(modes // piece):
                some = pl.ds(h * piece, piece)
                line = [first[i + 1 + a, p, some] for p in range(wide)]
                for p in range(mine):
                    centre = line[p + 1]
                    around = aside[slot, a, p, some] + (line[p] + line[p + 2])
                    around = around + (first[i + a, p + 1, some] + first[i + 2 + a, p + 1, some])
                    final[i + a, p, some] = (centre + speeds[p] * (around - 6.0 * centre)).astype(BF16)
        return 0

    lax.fori_loop(0, rows // 2, pair_again, 0)
    part = rows // count
    copies = []
    for k in range(count):
        base = jnp.bitwise_xor(pos[1], k) * part
        copies.append(pltpu.make_async_copy(final.at[pl.ds(base, part)], outs[k], sems.at[2 * group + k]))
    for copy in copies:
        copy.start()
    for copy in copies:
        copy.wait()


def sweep(pos, rate, shift, blocks, tails, begin, rows, count):
    _, planes, modes, cols = blocks[0].shape
    mine = 2 * planes
    piece = jax.ShapeDtypeStruct((rows // count, mine, modes, cols), BF16)
    return pl.pallas_call(
        functools.partial(sweep_kernel, begin=begin, count=count, heads=len(tails)),
        out_shape=(piece,) * count + (TOKEN,),
        in_specs=[SMEM, VMEM, VMEM] + [ANY] * (4 + len(tails)),
        out_specs=(ANY,) * count + (SMEM,),
        scratch_shapes=[
            pltpu.VMEM((rows + 2 * EDGE, 4 * planes, modes, cols), BF16),
            pltpu.VMEM((rows + 2, mine + 2, modes, cols), F32),
            pltpu.VMEM((2, 2, mine + 2, modes, cols), F32),
            pltpu.VMEM((rows, mine, modes, cols), BF16),
            pltpu.SemaphoreType.DMA((8 + count,)),
        ],
        compiler_params=params(),
        cost_estimate=COST,
        name="sweep",
    )(pos, rate, shift, *blocks, *tails)


def points_kernel(pos, basis, basis_t, flat, swing, load, *refs, begin):
    *refs, token = refs
    token[0], token[1] = pos[0], pos[1]
    count = len(refs) // 2
    blocks, outs = refs[:count], refs[count:]
    part, planes, modes, cols = blocks[0].shape
    copies = cols // flat.shape[1]

    def row(i, _):
        place = begin + pos[1] * part + i
        for p in range(planes):
            if modes % 16 == 0:
                cells = jnp.concatenate([block[i, p] for block in blocks], axis=0)
            else:
                cells = jnp.concatenate([block[i, p].astype(F32) for block in blocks], axis=0).astype(BF16)
            heat = jnp.tanh(jnp.dot(basis[...], cells, preferred_element_type=F32))
            offset = jnp.concatenate([flat[...]] * copies, axis=1)
            slope = jnp.concatenate([swing[...]] * copies, axis=1)
            weighted = (offset + slope * heat).astype(BF16)
            source = jnp.dot(basis_t[...], weighted, preferred_element_type=F32).astype(BF16).astype(F32)
            done = cells.astype(F32) + load[p, pl.ds(place, 1), :] * source
            for k in range(count):
                outs[k][i, p] = done[k * modes : (k + 1) * modes].astype(BF16)
        return 0

    lax.fori_loop(0, part, row, 0)


def points(pos, basis, basis_t, flat, swing, load, blocks, begin):
    count = len(blocks)
    return pl.pallas_call(
        functools.partial(points_kernel, begin=begin),
        out_shape=tuple(jax.ShapeDtypeStruct(block.shape, BF16) for block in blocks) + (TOKEN,),
        in_specs=[SMEM] + [VMEM] * (5 + count),
        out_specs=(VMEM,) * count + (SMEM,),
        compiler_params=params(),
        cost_estimate=COST,
        name="points",
    )(pos, basis, basis_t, flat, swing, load, *blocks)


def collect_kernel(pos, *refs):
    *blocks, out, token, sems = refs
    token[0], token[1] = pos[0], pos[1]
    part, planes = blocks[0].shape[0], out.shape[1]
    copies = []
    for k, block in enumerate(blocks):
        base = jnp.bitwise_xor(pos[1], k) * part
        copies.append(
            pltpu.make_async_copy(block.at[:, pl.ds(0, planes)], out.at[pl.ds(base, part)], sems.at[k])
        )
    for copy in copies:
        copy.start()
    for copy in copies:
        copy.wait()


def collect(pos, blocks):
    part, planes, modes, cols = blocks[0].shape
    count = len(blocks)
    shape = (part * count, planes // 2, modes, cols)
    return pl.pallas_call(
        collect_kernel,
        out_shape=(jax.ShapeDtypeStruct(shape, BF16), TOKEN),
        in_specs=[SMEM] + [ANY] * count,
        out_specs=(ANY, SMEM),
        scratch_shapes=[pltpu.SemaphoreType.DMA((count,))],
        compiler_params=params(),
        cost_estimate=COST,
        name="collect",
    )(pos, *blocks)


def settle_kernel(pos, turn, *refs, begin, count, chained):
    if chained:
        refs = refs[1:]
    blocks, other = refs[:count], refs[count]
    out, token, both, final, sems = refs[count + 1 :]
    token[0], token[1] = pos[0], pos[1]
    side = pos[0]
    part = blocks[0].shape[0]
    _, rows, planes, modes, cols = both.shape
    size = out.shape[2]
    group = turn.shape[1] // TILE
    incoming = [pltpu.make_async_copy(other, both.at[1], sems.at[count])]
    for k in range(count):
        base = jnp.bitwise_xor(pos[1], k) * part
        incoming.append(
            pltpu.make_async_copy(blocks[k].at[:, pl.ds(planes, planes)], both.at[0, pl.ds(base, part)], sems.at[k])
        )
    for copy in incoming:
        copy.start()
    outgoing = []
    for a in (1, 0):
        for copy in incoming[:1] if a else incoming[1:]:
            copy.wait()
        far = side if a == 0 else 1 - side
        for z in range(planes):
            to = jnp.where(far == 1, z, planes - 1 - z)
            for g in range(rows // TILE):
                block = jnp.where(far == 1, rows // TILE - 1 - g, g)
                for h in range(modes // group):
                    there = pl.ds(h * group, group)
                    x = both[a, pl.ds(g * TILE, TILE), z, there, :]
                    y = jnp.dot(turn[far], to_bf16_rows(x), preferred_element_type=F32).astype(BF16)
                    final[a, to, there, pl.ds(pl.multiple_of(block * TILE, TILE), TILE), :] = y.reshape(
                        group, TILE, cols
                    )
        start = pl.multiple_of(jnp.where(far == 1, size - rows - begin, begin), TILE)
        copy = pltpu.make_async_copy(final.at[a], out.at[:, :, pl.ds(start, rows), :], sems.at[count + 1 + a])
        copy.start()
        outgoing.append(copy)
    for copy in outgoing:
        copy.wait()


def settle(pos, turn, result, blocks, other, begin, shape):
    count = len(blocks)
    rows, planes, modes, cols = other.shape
    chained = result is not None
    return pl.pallas_call(
        functools.partial(settle_kernel, begin=begin, count=count, chained=chained),
        out_shape=(jax.ShapeDtypeStruct(shape, BF16), TOKEN),
        in_specs=[SMEM, VMEM] + [ANY] * (count + 1 + chained),
        out_specs=(ANY, SMEM),
        scratch_shapes=[
            pltpu.VMEM((2, rows, planes, modes, cols), BF16),
            pltpu.VMEM((2, planes, modes, rows, cols), BF16),
            pltpu.SemaphoreType.DMA((count + 3,)),
        ],
        input_output_aliases={2: 0} if chained else {},
        compiler_params=params(),
        cost_estimate=COST,
        name="settle",
    )(pos, turn, *([result] if chained else []), *blocks, other)


def chunk_rows(half):
    unit = half // 8
    return [unit, 2 * unit, 2 * unit, 2 * unit, unit]


ORDER = "T0 T1 T2 S0 T3 T4 P0 S1 C0 S2 P1 F0 S3 P2 S4 C1 P3 F1 C2 P4 F2 C3 F3 C4 F4".split()


def on_device(field, diffusion, joule, basis, quad_weight, base_conductivity, thermal_slope):
    planes, modes, size, cols = field.shape
    half = size // 2
    spaces, count = lax.axis_size("space"), lax.axis_size("modes")
    side = lax.axis_index("space") % 2
    me = lax.axis_index("modes")
    pos = jnp.stack([side, me]).astype(jnp.int32)

    swap = [(i, i ^ 1) for i in range(spaces)]
    ahead = [(i, i + 4 * (i % 2) - 2) for i in range(spaces)]
    ahead = [(i, j) for i, j in ahead if 0 <= j < spaces]
    back = [(j, i) for i, j in ahead]

    def across(x):
        return lax.ppermute(x, "space", swap)

    def halo(own, other):
        return lax.ppermute(own, "space", ahead), lax.ppermute(other, "space", back)

    def exchange(pieces):
        moved = [pieces[0]]
        for k in range(1, count):
            moved.append(lax.ppermute(pieces[k], "modes", [(j, j ^ k) for j in range(count)]))
        return moved

    def logical(x, length, side, sent):
        rows_back, planes_back = jnp.flip(x, 1)[:, :length], jnp.flip(x, 0)[:, :length]
        own = jnp.where(side == 1, rows_back, planes_back)
        send = jnp.where(side == 1, planes_back, rows_back).astype(sent)
        return own, send

    own_rate, send_rate = logical(diffusion, half + EDGE, side, F32)
    other_rate = across(send_rate)
    before, after = halo(own_rate[-1:], other_rate[:1])
    rate = jnp.concatenate([before, other_rate, own_rate, after], axis=0)
    rate = jnp.pad(rate, ((0, 0), (1, -(half + EDGE + 1) % 8), (0, 0)))

    lane = jnp.arange(cols)
    shift = (jnp.abs(lane[:, None] - lane[None, :]) == 1).astype(BF16)

    group = min(modes, TILE)
    at = jnp.arange(group * TILE)
    row_first = (at // group, at % group)
    mode_first = (at % TILE, at // TILE)
    same = row_first[1][:, None] == mode_first[1][None, :]
    straight = row_first[0][:, None] == mode_first[0][None, :]
    reverse = row_first[0][:, None] == TILE - 1 - mode_first[0][None, :]
    to_rows = jnp.stack([same & straight, same & reverse]).astype(BF16)
    to_modes = jnp.stack([(same & straight).T, (same & reverse).T]).astype(BF16)

    points_count = basis.shape[0]
    extra = -points_count % 32
    turned = jnp.concatenate(
        [lax.dynamic_slice_in_dim(basis, (me ^ k) * modes, modes, axis=1) for k in range(count)], axis=1
    )
    turned = jnp.pad(turned, ((0, extra), (0, 0)))
    turned_t = turned.T
    level = quad_weight * base_conductivity
    spread_out = lambda v: jnp.broadcast_to(jnp.pad(v, (0, extra))[:, None], (points_count + extra, 128))
    flat, swing = spread_out(level), spread_out(level * thermal_slope)

    rows_of = chunk_rows(half)
    begins = [sum(rows_of[:c]) for c in range(len(rows_of))]
    own, other, blocks, cells, home, theirs = {}, {}, {}, {}, {}, {}
    result = None
    for step in ORDER:
        kind, c = step[0], int(step[1:])
        begin, rows = begins[c], rows_of[c]
        if kind == "T":
            skip = EDGE if c else 0
            after = () if c else (send_rate,)
            own[c], send, pos = spread(pos, field, to_rows, after, begin, skip, rows + EDGE - skip, rows + TILE)
            other[c] = across(send)
            before, after = halo(own[c], other[c])
            blocks[c] = (before, other[c], own[c], after)
            if c == 0:
                own_load, send_load = logical(joule, half, pos[0], BF16)
                load = jnp.concatenate([across(send_load).astype(F32), own_load], axis=0)
        elif kind == "S":
            *pieces, pos = sweep(pos, rate, shift, blocks[c], blocks.get(c - 1, ()), begin, rows, count)
            cells[c] = exchange(pieces)
        elif kind == "P":
            *stepped, pos = points(pos, turned, turned_t, flat, swing, load, cells[c], begin)
            home[c] = exchange(stepped)
        elif kind == "C":
            out, pos = collect(pos, home[c])
            theirs[c] = across(out)
        else:
            result, pos = settle(pos, to_modes, result, home[c], theirs[c], begin, field.shape)
    return result


def solution(mesh):
    return jax.shard_map(
        on_device,
        mesh=mesh,
        in_specs=(
            P("space", "modes", None, None),
            P("space", None, None),
            P("space", None, None),
            P(),
            P(),
            P(),
            P(),
        ),
        out_specs=P("space", "modes", None, None),
        check_vma=False,
    )
```

time: 419 us -> 522 us (1.25)
  Pallas kernels: 147 us -> 298 us
  waiting for transfers between devices: 186 us -> 120 us
  local copies, waits for them, and re-layouts: 9.03 us -> 20.6 us
    pallas_call x4 -> x5, Pallas kernels: 2.65 us -> 139 us  [collect(): pl.pallas_call(collect_kernel, out_shape=(jax.ShapeDtypeStruct(shape, BF1...]
    ppermute x10 -> x12, waiting for transfers between devices: 76 us -> 44.7 us  [across(): return lax.ppermute(x, 'space', swap)]
    ppermute x24 -> x30, waiting for transfers between devices: 88.9 us -> 69.1 us  [exchange(): lax.ppermute(pieces[k], 'modes', [(j, j ^ k) for j in range(count)])]
    pallas_call x4 -> x5, Pallas kernels: 40 us -> 52.9 us  [points(): pl.pallas_call(functools.partial(points_kernel, begin=begin), out_shape=t...]
    pallas_call x4 -> x5, Pallas kernels: 50.3 us -> 63 us  [sweep(): pl.pallas_call(functools.partial(sweep_kernel, begin=begin, count=count,...]
    ppermute x5 -> x6, waiting for transfers between devices: 16.9 us -> 6.15 us  [halo(): lax.ppermute(other, 'space', back)]
    ppermute x5 -> x6, starting transfers between devices: 16.9 us -> 24.5 us  [halo(): lax.ppermute(other, 'space', back)]
    ppermute x10 -> x12, starting transfers between devices: 28.8 us -> 21.4 us  [across(): return lax.ppermute(x, 'space', swap)]
  transfers between devices with their start and end apart: 44 -> 54, of which waited for: 19 -> 12; matrix products, arithmetic and copies ran while one was open for 1% -> 2% of each run, Pallas kernels for 33% -> 33%
where the time goes in v2:
time: 522 us; the launch traced here: 520 us
  Pallas kernels  298 us (57%)
  waiting for transfers between devices  120 us (23%)
  starting transfers between devices  72.5 us (14%)
  local copies, waits for them, and re-layouts  20.6 us (4%)
  other arithmetic  8.35 us (2%)
    pallas_call x5, Pallas kernels, collect(): pl.pallas_call(collect_kernel, out_shape=(jax.ShapeDtypeStruct(shape, BF1...  139 us
    ppermute x30, waiting for transfers between devices, exchange(): lax.ppermute(pieces[k], 'modes', [(j, j ^ k) for j in range(count)])  69.1 us
    pallas_call x5, Pallas kernels, sweep(): pl.pallas_call(functools.partial(sweep_kernel, begin=begin, count=count,...  63 us
    pallas_call x5, Pallas kernels, points(): pl.pallas_call(functools.partial(points_kernel, begin=begin), out_shape=t...  52.9 us
    ppermute x12, waiting for transfers between devices, across(): return lax.ppermute(x, 'space', swap)  44.7 us
    ppermute x6, starting transfers between devices, halo(): lax.ppermute(other, 'space', back)  24.5 us
    pallas_call x5, Pallas kernels, settle(): pl.pallas_call(functools.partial(settle_kernel, begin=begin, count=count,...  21.8 us
    ppermute x12, starting transfers between devices, across(): return lax.ppermute(x, 'space', swap)  21.4 us
  transfers between devices with their start and end apart: 54, of which 12 were waited for; matrix products, arithmetic and copies ran while one was open for 2% of the time, Pallas kernels for 33%

profile of v2, /device:TPU:0, one launch (start us, length us, event | category | flops | bytes accessed | tf_op | source)
XLA Modules:
  0.0 520.3 jit_solution(5063703788493831767)
XLA Ops:
  4.7 3.9 spread.5
  8.6 3.0 collective-permute-start.4
  11.7 4.6 spread.6
  18.3 4.5 spread.7
  25.0 7.0 %collective-permute-done.1 = f32[2,130,256]{2,1,0:T(8,128)S(1)} collective-permute-done((f32[2,130,256]{2,1,0:T(8,128)S(1)}, f32[2,130,256]{2,1,0:T(8,128)S(1)}, u32[]{:S(2)}, u32[]{:S(2)}) %collective-permute-start.1) | collective-permute-done | bytes 266272 | tf_op jit(solution)/shard_map/ppermute | solution.py:372
  33.3 5.5 %collective-permute-start.5 = (bf16[18,2,32,256]{3,2,1,0:T(8,128)(2,1)}, bf16[18,2,32,256]{3,2,1,0:T(8,128)(2,1)}, u32[]{:S(2)}, u32[]{:S(2)}) collective-permute-start(bf16[18,2,32,256]{3,2,1,0:T(8,128)(2,1)} %collective-permute-done.4.refs_1_.refs_5_), channel_id=1, source_target_pairs={{12,4},{0,8},{20,12},{8,16},{28,20},{16,24},{13,5},{1,9},{21,13},{... | collective-permute-start | bytes 1769480 | tf_op jit(solution)/shard_map/ppermute | solution.py:375
  42.4 3.4 collective-permute-start.2
  45.8 6.1 %collective-permute-done.2 = f32[1,130,256]{2,1,0:T(8,128)S(1)} collective-permute-done((f32[1,130,256]{2,1,0:T(8,128)S(1)}, f32[1,130,256]{2,1,0:T(8,128)S(1)}, u32[]{:S(2)}, u32[]{:S(2)}) %collective-permute-start.2) | collective-permute-done | bytes 133152 | tf_op jit(solution)/shard_map/ppermute | solution.py:375
  56.1 7.9 %collective-permute-start.6 = (bf16[2,128,256]{2,1,0:T(8,128)(2,1)S(1)}, bf16[2,128,256]{2,1,0:T(8,128)(2,1)}, u32[]{:S(2)}, u32[]{:S(2)}) collective-permute-start(bf16[2,128,256]{2,1,0:T(8,128)(2,1)S(1)} %select_convert_fusion), channel_id=1, source_target_pairs={{0,4},{4,0},{8,12},{12,8},{16,20},{20,16},{24,28},{28,24},{1,5},{5... | collective-permute-start | bytes 393224 | tf_op jit(solution)/shard_map/ppermute | solution.py:372
  64.0 2.0 select_maximum_fusion.rate
  66.0 9.4 %sweep.5 = (bf16[4,4,32,256]{3,2,1,0:T(8,128)(2,1)}, bf16[4,4,32,256]{3,2,1,0:T(8,128)(2,1)}, bf16[4,4,32,256]{3,2,1,0:T(8,128)(2,1)}, bf16[4,4,32,256]{3,2,1,0:T(8,128)(2,1)}, s32[2]{0:T(128)}) custom-call(s32[2]{0:T(128)} %get-tuple-element.91.pos, f32[6,136,256]{2,1,0:T(8,128)} %select_maximum_fusion.rate, bf16[256,256]{1,0:T(8,128)(2,1)} %fusion.1.shift, ...), custom_call_target="tpu_custom_call" | custom-call | flops 1 | bytes 1 | tf_op jit(solution)/shard_map/sweep/pallas_call | solution.py:195
  75.4 3.6 collective-permute-done.6
  82.5 4.7 collective-permute-start.12
  87.2 4.5 spread.8
  91.7 2.7 collective-permute-start.18
  97.5 3.8 spread.9
  102.9 7.3 %points.5 = (bf16[4,4,32,256]{3,2,1,0:T(8,128)(2,1)}, bf16[4,4,32,256]{3,2,1,0:T(8,128)(2,1)}, bf16[4,4,32,256]{3,2,1,0:T(8,128)(2,1)}, bf16[4,4,32,256]{3,2,1,0:T(8,128)(2,1)}, s32[2]{0:T(128)}) custom-call(s32[2]{0:T(128)} %get-tuple-element.96.pos, bf16[352,128]{1,0:T(8,128)(2,1)} %copy.16.basis, bf16[128,352]{1,0:T(8,128)(2,1)} %bitcast.5, ...), custom_call_target="tpu_custom_call" | custom-call | flops 1 | bytes 1 | tf_op jit(solution)/shard_map/points/pallas_call | solution.py:243
  113.3 5.9 %collective-permute-done.14.refs_2_ = bf16[4,4,32,256]{3,2,1,0:T(8,128)(2,1)S(1)} collective-permute-done((bf16[4,4,32,256]{3,2,1,0:T(8,128)(2,1)}, bf16[4,4,32,256]{3,2,1,0:T(8,128)(2,1)S(1)}, u32[]{:S(2)}, u32[]{:S(2)}) %collective-permute-start.14) | collective-permute-done | bytes 262176 | tf_op jit(solution)/shard_map/ppermute | solution.py:380
  120.6 14.7 %sweep.6 = (bf16[8,4,32,256]{3,2,1,0:T(8,128)(2,1)}, bf16[8,4,32,256]{3,2,1,0:T(8,128)(2,1)}, bf16[8,4,32,256]{3,2,1,0:T(8,128)(2,1)}, bf16[8,4,32,256]{3,2,1,0:T(8,128)(2,1)}, s32[2]{0:T(128)}) custom-call(s32[2]{0:T(128)} %get-tuple-element.101.pos, f32[6,136,256]{2,1,0:T(8,128)} %select_maximum_fusion.rate, bf16[256,256]{1,0:T(8,128)(2,1)} %fusion.1.shift, ...), custom_call_target="tpu_custom_call" | custom-call | flops 1 | bytes 1 | tf_op jit(solution)/shard_map/sweep/pallas_call | solution.py:195
  138.1 3.7 collective-permute-start.25
  141.8 18.2 %collect.5 = (bf16[16,2,32,256]{3,2,1,0:T(8,128)(2,1)}, s32[2]{0:T(128)}) custom-call(s32[2]{0:T(128)} %get-tuple-element.104.pos, bf16[4,4,32,256]{3,2,1,0:T(8,128)(2,1)} %get-tuple-element.105.refs_0_, bf16[4,4,32,256]{3,2,1,0:T(8,128)(2,1)} %copy-done.28, bf16[4,4,32,256]{3,2,1,0:T(8,128)(2,1)} %copy-done.29, bf16[4,4,32,256]{3,2,1,0:T(8,128)(2,1)} %copy-done.30), custom_call_target="tpu_custom_call" | custom-call | flops 1 | bytes 1 | tf_op jit(solution)/shard_map/collect/pallas_call | solution.py:274
  160.0 14.7 %sweep.7 = (bf16[8,4,32,256]{3,2,1,0:T(8,128)(2,1)}, bf16[8,4,32,256]{3,2,1,0:T(8,128)(2,1)}, bf16[8,4,32,256]{3,2,1,0:T(8,128)(2,1)}, bf16[8,4,32,256]{3,2,1,0:T(8,128)(2,1)}, s32[2]{0:T(128)}) custom-call(s32[2]{0:T(128)} %get-tuple-element.109.pos, f32[6,136,256]{2,1,0:T(8,128)} %select_maximum_fusion.rate, bf16[256,256]{1,0:T(8,128)(2,1)} %fusion.1.shift, ...), custom_call_target="tpu_custom_call" | custom-call | flops 1 | bytes 1 | tf_op jit(solution)/shard_map/sweep/pallas_call | solution.py:195
  176.8 12.7 %points.6 = (bf16[8,4,32,256]{3,2,1,0:T(8,128)(2,1)}, bf16[8,4,32,256]{3,2,1,0:T(8,128)(2,1)}, bf16[8,4,32,256]{3,2,1,0:T(8,128)(2,1)}, bf16[8,4,32,256]{3,2,1,0:T(8,128)(2,1)}, s32[2]{0:T(128)}) custom-call(s32[2]{0:T(128)} %get-tuple-element.112.pos, bf16[352,128]{1,0:T(8,128)(2,1)} %copy.16.basis, bf16[128,352]{1,0:T(8,128)(2,1)} %bitcast.6, ...), custom_call_target="tpu_custom_call" | custom-call | flops 1 | bytes 1 | tf_op jit(solution)/shard_map/points/pallas_call | solution.py:243
  190.9 4.6 collective-permute-start.31
  195.7 4.1 collective-permute-done.28.refs_3_
  203.7 4.0 settle.5
  207.7 14.7 %sweep.8 = (bf16[8,4,32,256]{3,2,1,0:T(8,128)(2,1)}, bf16[8,4,32,256]{3,2,1,0:T(8,128)(2,1)}, bf16[8,4,32,256]{3,2,1,0:T(8,128)(2,1)}, bf16[8,4,32,256]{3,2,1,0:T(8,128)(2,1)}, s32[2]{0:T(128)}) custom-call(s32[2]{0:T(128)} %get-tuple-element.119.pos, f32[6,136,256]{2,1,0:T(8,128)} %select_maximum_fusion.rate, bf16[256,256]{1,0:T(8,128)(2,1)} %fusion.1.shift, ...), custom_call_target="tpu_custom_call" | custom-call | flops 1 | bytes 1 | tf_op jit(solution)/shard_map/sweep/pallas_call | solution.py:195
  222.4 12.8 %points.7 = (bf16[8,4,32,256]{3,2,1,0:T(8,128)(2,1)}, bf16[8,4,32,256]{3,2,1,0:T(8,128)(2,1)}, bf16[8,4,32,256]{3,2,1,0:T(8,128)(2,1)}, bf16[8,4,32,256]{3,2,1,0:T(8,128)(2,1)}, s32[2]{0:T(128)}) custom-call(s32[2]{0:T(128)} %get-tuple-element.122.pos, bf16[352,128]{1,0:T(8,128)(2,1)} %copy.16.basis, bf16[128,352]{1,0:T(8,128)(2,1)} %bitcast.7, ...), custom_call_target="tpu_custom_call" | custom-call | flops 1 | bytes 1 | tf_op jit(solution)/shard_map/points/pallas_call | solution.py:243
  236.2 9.4 %sweep.9 = (bf16[4,4,32,256]{3,2,1,0:T(8,128)(2,1)}, bf16[4,4,32,256]{3,2,1,0:T(8,128)(2,1)}, bf16[4,4,32,256]{3,2,1,0:T(8,128)(2,1)}, bf16[4,4,32,256]{3,2,1,0:T(8,128)(2,1)}, s32[2]{0:T(128)}) custom-call(s32[2]{0:T(128)} %get-tuple-element.127.pos, f32[6,136,256]{2,1,0:T(8,128)} %select_maximum_fusion.rate, bf16[256,256]{1,0:T(8,128)(2,1)} %fusion.1.shift, ...), custom_call_target="tpu_custom_call" | custom-call | flops 1 | bytes 1 | tf_op jit(solution)/shard_map/sweep/pallas_call | solution.py:195
  246.9 34.1 %collect.6 = (bf16[32,2,32,256]{3,2,1,0:T(8,128)(2,1)}, s32[2]{0:T(128)}) custom-call(s32[2]{0:T(128)} %get-tuple-element.130.pos, bf16[8,4,32,256]{3,2,1,0:T(8,128)(2,1)} %get-tuple-element.131.refs_0_.refs_1_, bf16[8,4,32,256]{3,2,1,0:T(8,128)(2,1)} %copy-done.11, bf16[8,4,32,256]{3,2,1,0:T(8,128)(2,1)} %copy-done.12, bf16[8,4,32,256]{3,2,1,0:T(8,128)(2,1)} %copy-done.13), custom_call_target="tpu_custom_call" | custom-call | flops 1 | bytes 1 | tf_op jit(solution)/shard_map/collect/pallas_call | solution.py:274
  280.9 2.0 collective-permute-start.38
  285.8 11.9 %collective-permute-done.36.refs_2_ = bf16[8,4,32,256]{3,2,1,0:T(8,128)(2,1)S(1)} collective-permute-done((bf16[8,4,32,256]{3,2,1,0:T(8,128)(2,1)S(1)}, bf16[8,4,32,256]{3,2,1,0:T(8,128)(2,1)S(1)}, u32[]{:S(2)}, u32[]{:S(2)}) %collective-permute-start.36) | collective-permute-done | bytes 524320 | tf_op jit(solution)/shard_map/ppermute | solution.py:380
  297.7 10.5 %collective-permute-done.37.refs_3_ = bf16[8,4,32,256]{3,2,1,0:T(8,128)(2,1)S(1)} collective-permute-done((bf16[8,4,32,256]{3,2,1,0:T(8,128)(2,1)}, bf16[8,4,32,256]{3,2,1,0:T(8,128)(2,1)S(1)}, u32[]{:S(2)}, u32[]{:S(2)}) %collective-permute-start.37) | collective-permute-done | bytes 524320 | tf_op jit(solution)/shard_map/ppermute | solution.py:380
  308.9 12.7 %points.8 = (bf16[8,4,32,256]{3,2,1,0:T(8,128)(2,1)}, bf16[8,4,32,256]{3,2,1,0:T(8,128)(2,1)}, bf16[8,4,32,256]{3,2,1,0:T(8,128)(2,1)}, bf16[8,4,32,256]{3,2,1,0:T(8,128)(2,1)}, s32[2]{0:T(128)}) custom-call(s32[2]{0:T(128)} %get-tuple-element.135.pos, bf16[352,128]{1,0:T(8,128)(2,1)} %copy.16.basis, bf16[128,352]{1,0:T(8,128)(2,1)} %bitcast.8, ...), custom_call_target="tpu_custom_call" | custom-call | flops 1 | bytes 1 | tf_op jit(solution)/shard_map/points/pallas_call | solution.py:243
  322.7 4.6 settle.6
  327.4 3.2 collective-permute-done.41.refs_3_.refs_4_
  331.4 34.1 %collect.7 = (bf16[32,2,32,256]{3,2,1,0:T(8,128)(2,1)}, s32[2]{0:T(128)}) custom-call(s32[2]{0:T(128)} %get-tuple-element.143.pos, bf16[8,4,32,256]{3,2,1,0:T(8,128)(2,1)} %get-tuple-element.144.refs_0_.refs_1_, bf16[8,4,32,256]{3,2,1,0:T(8,128)(2,1)} %copy-done.14, bf16[8,4,32,256]{3,2,1,0:T(8,128)(2,1)} %copy-done.15, bf16[8,4,32,256]{3,2,1,0:T(8,128)(2,1)} %copy-done.16), custom_call_target="tpu_custom_call" | custom-call | flops 1 | bytes 1 | tf_op jit(solution)/shard_map/collect/pallas_call | solution.py:274
  368.4 6.6 %collective-permute-done.43.refs_2_ = bf16[4,4,32,256]{3,2,1,0:T(8,128)(2,1)S(1)} collective-permute-done((bf16[4,4,32,256]{3,2,1,0:T(8,128)(2,1)S(1)}, bf16[4,4,32,256]{3,2,1,0:T(8,128)(2,1)S(1)}, u32[]{:S(2)}, u32[]{:S(2)}) %collective-permute-start.43) | collective-permute-done | bytes 262176 | tf_op jit(solution)/shard_map/ppermute | solution.py:380
  375.0 26.8 %collective-permute-done.44.refs_3_ = bf16[4,4,32,256]{3,2,1,0:T(8,128)(2,1)S(1)} collective-permute-done((bf16[4,4,32,256]{3,2,1,0:T(8,128)(2,1)S(1)}, bf16[4,4,32,256]{3,2,1,0:T(8,128)(2,1)S(1)}, u32[]{:S(2)}, u32[]{:S(2)}) %collective-permute-start.44) | collective-permute-done | bytes 262176 | tf_op jit(solution)/shard_map/ppermute | solution.py:380
  402.5 7.3 %points.9 = (bf16[4,4,32,256]{3,2,1,0:T(8,128)(2,1)}, bf16[4,4,32,256]{3,2,1,0:T(8,128)(2,1)}, bf16[4,4,32,256]{3,2,1,0:T(8,128)(2,1)}, bf16[4,4,32,256]{3,2,1,0:T(8,128)(2,1)}, s32[2]{0:T(128)}) custom-call(s32[2]{0:T(128)} %get-tuple-element.148.pos, bf16[352,128]{1,0:T(8,128)(2,1)} %copy.16.basis, bf16[128,352]{1,0:T(8,128)(2,1)} %bitcast.9, ...), custom_call_target="tpu_custom_call" | custom-call | flops 1 | bytes 1 | tf_op jit(solution)/shard_map/points/pallas_call | solution.py:243
  410.9 4.6 settle.7
  416.7 34.1 %collect.8 = (bf16[32,2,32,256]{3,2,1,0:T(8,128)(2,1)}, s32[2]{0:T(128)}) custom-call(s32[2]{0:T(128)} %get-tuple-element.156.pos, bf16[8,4,32,256]{3,2,1,0:T(8,128)(2,1)} %get-tuple-element.157.refs_0_.refs_1_, bf16[8,4,32,256]{3,2,1,0:T(8,128)(2,1)} %copy-done.17, bf16[8,4,32,256]{3,2,1,0:T(8,128)(2,1)} %copy-done.18, bf16[8,4,32,256]{3,2,1,0:T(8,128)(2,1)} %copy-done.19), custom_call_target="tpu_custom_call" | custom-call | flops 1 | bytes 1 | tf_op jit(solution)/shard_map/collect/pallas_call | solution.py:274
  450.8 2.2 collective-permute-start.49
  454.8 22.0 %collective-permute-done.49.refs_5_ = bf16[32,2,32,256]{3,2,1,0:T(8,128)(2,1)S(1)} collective-permute-done((bf16[32,2,32,256]{3,2,1,0:T(8,128)(2,1)}, bf16[32,2,32,256]{3,2,1,0:T(8,128)(2,1)S(1)}, u32[]{:S(2)}, u32[]{:S(2)}) %collective-permute-start.49) | collective-permute-done | bytes 1048608 | tf_op jit(solution)/shard_map/ppermute | solution.py:372
  477.7 4.6 settle.8
  483.3 18.2 %collect.9 = (bf16[16,2,32,256]{3,2,1,0:T(8,128)(2,1)}, s32[2]{0:T(128)}) custom-call(s32[2]{0:T(128)} %get-tuple-element.164.pos, bf16[4,4,32,256]{3,2,1,0:T(8,128)(2,1)} %get-tuple-element.165.refs_0_.refs_1_, bf16[4,4,32,256]{3,2,1,0:T(8,128)(2,1)} %copy-done.25, bf16[4,4,32,256]{3,2,1,0:T(8,128)(2,1)} %copy-done.26, bf16[4,4,32,256]{3,2,1,0:T(8,128)(2,1)} %copy-done.27), custom_call_target="tpu_custom_call" | custom-call | flops 1 | bytes 1 | tf_op jit(solution)/shard_map/collect/pallas_call | solution.py:274
  503.3 12.1 %collective-permute-done.53.refs_5_ = bf16[16,2,32,256]{3,2,1,0:T(8,128)(2,1)S(1)} collective-permute-done((bf16[16,2,32,256]{3,2,1,0:T(8,128)(2,1)}, bf16[16,2,32,256]{3,2,1,0:T(8,128)(2,1)S(1)}, u32[]{:S(2)}, u32[]{:S(2)}) %collective-permute-start.53) | collective-permute-done | bytes 524320 | tf_op jit(solution)/shard_map/ppermute | solution.py:372
  516.2 4.0 settle.9
  (246 shorter events, 59.9 us)
Async XLA Ops:
  8.6 24.7 %collective-permute-start.4 = (bf16[18,2,32,256]{3,2,1,0:T(8,128)(2,1)}, bf16[18,2,32,256]{3,2,1,0:T(8,128)(2,1)}, u32[]{:S(2)}, u32[]{:S(2)}) collective-permute-start(bf16[18,2,32,256]{3,2,1,0:T(8,128)(2,1)} %get-tuple-element.93), channel_id=1, source_target_pairs={{0,4},{4,0},{8,12},{12,8},{16,20},{20,16},{24,28},{28,24},{1,5},{5... | collective-permute-start | bytes 1769480 | tf_op jit(solution)/shard_map/ppermute | solution.py:372
  11.7 20.3 %collective-permute-start.1 = (f32[2,130,256]{2,1,0:T(8,128)S(1)}, f32[2,130,256]{2,1,0:T(8,128)S(1)}, u32[]{:S(2)}, u32[]{:S(2)}) collective-permute-start(f32[2,130,256]{2,1,0:T(8,128)S(1)} %copy-done.21), channel_id=1, source_target_pairs={{0,4},{4,0},{8,12},{12,8},{16,20},{20,16},{24,28},{28,24},{1,5},{5... | collective-permute-start | bytes 798728 | tf_op jit(solution)/shard_map/ppermute | solution.py:372
  16.3 63.3 %collective-permute-start.11 = (bf16[32,2,32,256]{3,2,1,0:T(8,128)(2,1)}, bf16[32,2,32,256]{3,2,1,0:T(8,128)(2,1)}, u32[]{:S(2)}, u32[]{:S(2)}) collective-permute-start(bf16[32,2,32,256]{3,2,1,0:T(8,128)(2,1)} %get-tuple-element.103), channel_id=1, source_target_pairs={{0,4},{4,0},{8,12},{12,8},{16,20},{20,16},{24,28},{28,24},{1,5},{5... | collective-permute-start | bytes 3145736 | tf_op jit(solution)/shard_map/ppermute | solution.py:372
  22.9 58.6 %collective-permute-start.17 = (bf16[32,2,32,256]{3,2,1,0:T(8,128)(2,1)}, bf16[32,2,32,256]{3,2,1,0:T(8,128)(2,1)S(1)}, u32[]{:S(2)}, u32[]{:S(2)}) collective-permute-start(bf16[32,2,32,256]{3,2,1,0:T(8,128)(2,1)} %get-tuple-element.111), channel_id=1, source_target_pairs={{0,4},{4,0},{8,12},{12,8},{16,20},{20,16},{24,28},{28,24},{1,5},{5... | collective-permute-start | bytes 3145736 | tf_op jit(solution)/shard_map/ppermute | solution.py:372
  23.0 30.2 %collective-permute-start.3 = (bf16[18,2,32,256]{3,2,1,0:T(8,128)(2,1)S(1)}, bf16[18,2,32,256]{3,2,1,0:T(8,128)(2,1)S(1)}, u32[]{:S(2)}, u32[]{:S(2)}) collective-permute-start(bf16[18,2,32,256]{3,2,1,0:T(8,128)(2,1)S(1)} %copy-done.9), channel_id=1, source_target_pairs={{4,12},{8,0},{12,20},{16,8},{20,28},{24,16},{5,13},{9,1},{13,21},{... | collective-permute-start | bytes 1769480 | tf_op jit(solution)/shard_map/ppermute | solution.py:375
  32.0 10.4 %collective-permute-start = (f32[1,130,256]{2,1,0:T(8,128)}, f32[1,130,256]{2,1,0:T(8,128)S(1)}, u32[]{:S(2)}, u32[]{:S(2)}) collective-permute-start(f32[1,130,256]{2,1,0:T(8,128)} %slice.44), channel_id=1, source_target_pairs={{4,12},{8,0},{12,20},{16,8},{20,28},{24,16},{5,13},{9,1},{13,21},{... | collective-permute-start | bytes 399368 | tf_op jit(solution)/shard_map/ppermute | solution.py:375
  33.3 22.8 %collective-permute-start.5 = (bf16[18,2,32,256]{3,2,1,0:T(8,128)(2,1)}, bf16[18,2,32,256]{3,2,1,0:T(8,128)(2,1)}, u32[]{:S(2)}, u32[]{:S(2)}) collective-permute-start(bf16[18,2,32,256]{3,2,1,0:T(8,128)(2,1)} %collective-permute-done.4.refs_1_.refs_5_), channel_id=1, source_target_pairs={{12,4},{0,8},{20,12},{8,16},{28,20},{16,24},{13,5},{1,9},{21,13},{... | collective-permute-start | bytes 1769480 | tf_op jit(solution)/shard_map/ppermute | solution.py:375
  42.4 9.6 %collective-permute-start.2 = (f32[1,130,256]{2,1,0:T(8,128)S(1)}, f32[1,130,256]{2,1,0:T(8,128)S(1)}, u32[]{:S(2)}, u32[]{:S(2)}) collective-permute-start(f32[1,130,256]{2,1,0:T(8,128)S(1)} %slice.45), channel_id=1, source_target_pairs={{12,4},{0,8},{20,12},{8,16},{28,20},{16,24},{13,5},{1,9},{21,13},{... | collective-permute-start | bytes 399368 | tf_op jit(solution)/shard_map/ppermute | solution.py:375
  51.9 58.3 %collective-permute-start.10 = (bf16[32,2,32,256]{3,2,1,0:T(8,128)(2,1)}, bf16[32,2,32,256]{3,2,1,0:T(8,128)(2,1)}, u32[]{:S(2)}, u32[]{:S(2)}) collective-permute-start(bf16[32,2,32,256]{3,2,1,0:T(8,128)(2,1)} %get-tuple-element.102.refs_2_.refs_6_), channel_id=1, source_target_pairs={{4,12},{8,0},{12,20},{16,8},{20,28},{24,16},{5,13},{9,1},{13,21},{... | collective-permute-start | bytes 3145736 | tf_op jit(solution)/shard_map/ppermute | solution.py:375
  54.1 56.4 %collective-permute-start.16 = (bf16[32,2,32,256]{3,2,1,0:T(8,128)(2,1)}, bf16[32,2,32,256]{3,2,1,0:T(8,128)(2,1)S(1)}, u32[]{:S(2)}, u32[]{:S(2)}) collective-permute-start(bf16[32,2,32,256]{3,2,1,0:T(8,128)(2,1)} %get-tuple-element.110.refs_2_.refs_6_), channel_id=1, source_target_pairs={{4,12},{8,0},{12,20},{16,8},{20,28},{24,16},{5,13},{9,1},{13,21},{... | collective-permute-start | bytes 3145736 | tf_op jit(solution)/shard_map/ppermute | solution.py:375
  56.1 23.0 %collective-permute-start.6 = (bf16[2,128,256]{2,1,0:T(8,128)(2,1)S(1)}, bf16[2,128,256]{2,1,0:T(8,128)(2,1)}, u32[]{:S(2)}, u32[]{:S(2)}) collective-permute-start(bf16[2,128,256]{2,1,0:T(8,128)(2,1)S(1)} %select_convert_fusion), channel_id=1, source_target_pairs={{0,4},{4,0},{8,12},{12,8},{16,20},{20,16},{24,28},{28,24},{1,5},{5... | collective-permute-start | bytes 393224 | tf_op jit(solution)/shard_map/ppermute | solution.py:372
  79.6 12.1 %collective-permute-start.8 = (bf16[4,4,32,256]{3,2,1,0:T(8,128)(2,1)}, bf16[4,4,32,256]{3,2,1,0:T(8,128)(2,1)}, u32[]{:S(2)}, u32[]{:S(2)}) collective-permute-start(bf16[4,4,32,256]{3,2,1,0:T(8,128)(2,1)} %get-tuple-element.99), channel_id=1, source_target_pairs={{0,2},{1,3},{2,0},{3,1},{4,6},{5,7},{6,4},{7,5},{8,10},{9,11},{10,... | collective-permute-start | bytes 786440 | tf_op jit(solution)/shard_map/ppermute | solution.py:380
  81.4 13.0 %collective-permute-start.9 = (bf16[4,4,32,256]{3,2,1,0:T(8,128)(2,1)}, bf16[4,4,32,256]{3,2,1,0:T(8,128)(2,1)}, u32[]{:S(2)}, u32[]{:S(2)}) collective-permute-start(bf16[4,4,32,256]{3,2,1,0:T(8,128)(2,1)} %get-tuple-element.100), channel_id=1, source_target_pairs={{0,3},{1,2},{2,1},{3,0},{4,7},{5,6},{6,5},{7,4},{8,11},{9,10},{10,... | collective-permute-start | bytes 786440 | tf_op jit(solution)/shard_map/ppermute | solution.py:380
  82.5 37.6 %collective-permute-start.12 = (bf16[32,2,32,256]{3,2,1,0:T(8,128)(2,1)}, bf16[32,2,32,256]{3,2,1,0:T(8,128)(2,1)}, u32[]{:S(2)}, u32[]{:S(2)}) collective-permute-start(bf16[32,2,32,256]{3,2,1,0:T(8,128)(2,1)} %collective-permute-done.11.refs_1_.refs_5_), channel_id=1, source_target_pairs={{12,4},{0,8},{20,12},{8,16},{28,20},{16,24},{13,5},{1,9},{21,13},{... | collective-permute-start | bytes 3145736 | tf_op jit(solution)/shard_map/ppermute | solution.py:375
  91.7 45.4 %collective-permute-start.18 = (bf16[32,2,32,256]{3,2,1,0:T(8,128)(2,1)S(1)}, bf16[32,2,32,256]{3,2,1,0:T(8,128)(2,1)S(1)}, u32[]{:S(2)}, u32[]{:S(2)}) collective-permute-start(bf16[32,2,32,256]{3,2,1,0:T(8,128)(2,1)S(1)} %collective-permute-done.17.refs_1_.refs_5_), channel_id=1, source_target_pairs={{12,4},{0,8},{20,12},{8,16},{28,20},{16,24},{13,5},{1,9},{21,13},{... | collective-permute-start | bytes 3145736 | tf_op jit(solution)/shard_map/ppermute | solution.py:375
  94.5 43.6 %collective-permute-start.24 = (bf16[32,2,32,256]{3,2,1,0:T(8,128)(2,1)}, bf16[32,2,32,256]{3,2,1,0:T(8,128)(2,1)S(1)}, u32[]{:S(2)}, u32[]{:S(2)}) collective-permute-start(bf16[32,2,32,256]{3,2,1,0:T(8,128)(2,1)} %get-tuple-element.121), channel_id=1, source_target_pairs={{0,4},{4,0},{8,12},{12,8},{16,20},{20,16},{24,28},{28,24},{1,5},{5... | collective-permute-start | bytes 3145736 | tf_op jit(solution)/shard_map/ppermute | solution.py:372
  112.0 62.7 %collective-permute-start.23 = (bf16[32,2,32,256]{3,2,1,0:T(8,128)(2,1)S(1)}, bf16[32,2,32,256]{3,2,1,0:T(8,128)(2,1)}, u32[]{:S(2)}, u32[]{:S(2)}) collective-permute-start(bf16[32,2,32,256]{3,2,1,0:T(8,128)(2,1)S(1)} %copy-done.3), channel_id=1, source_target_pairs={{4,12},{8,0},{12,20},{16,8},{20,28},{24,16},{5,13},{9,1},{13,21},{... | collective-permute-start | bytes 3145736 | tf_op jit(solution)/shard_map/ppermute | solution.py:375
  119.2 17.4 %collective-permute-start.30 = (bf16[16,2,32,256]{3,2,1,0:T(8,128)(2,1)}, bf16[16,2,32,256]{3,2,1,0:T(8,128)(2,1)}, u32[]{:S(2)}, u32[]{:S(2)}) collective-permute-start(bf16[16,2,32,256]{3,2,1,0:T(8,128)(2,1)} %get-tuple-element.129), channel_id=1, source_target_pairs={{0,4},{4,0},{8,12},{12,8},{16,20},{20,16},{24,28},{28,24},{1,5},{5... | collective-permute-start | bytes 1572872 | tf_op jit(solution)/shard_map/ppermute | solution.py:372
  120.1 15.2 %collective-permute-start.15 = (bf16[4,4,32,256]{3,2,1,0:T(8,128)(2,1)}, bf16[4,4,32,256]{3,2,1,0:T(8,128)(2,1)S(1)}, u32[]{:S(2)}, u32[]{:S(2)}) collective-permute-start(bf16[4,4,32,256]{3,2,1,0:T(8,128)(2,1)} %get-tuple-element.108), channel_id=1, source_target_pairs={{0,3},{1,2},{2,1},{3,0},{4,7},{5,6},{6,5},{7,4},{8,11},{9,10},{10,... | collective-permute-start | bytes 786440 | tf_op jit(solution)/shard_map/ppermute | solution.py:380
  135.4 39.4 %collective-permute-start.19 = (bf16[8,4,32,256]{3,2,1,0:T(8,128)(2,1)}, bf16[8,4,32,256]{3,2,1,0:T(8,128)(2,1)}, u32[]{:S(2)}, u32[]{:S(2)}) collective-permute-start(bf16[8,4,32,256]{3,2,1,0:T(8,128)(2,1)} %get-tuple-element.114), channel_id=1, source_target_pairs={{0,1},{1,0},{2,3},{3,2},{4,5},{5,4},{6,7},{7,6},{8,9},{9,8},{10,11... | collective-permute-start | bytes 1572872 | tf_op jit(solution)/shard_map/ppermute | solution.py:380
  136.6 38.7 %collective-permute-start.20 = (bf16[8,4,32,256]{3,2,1,0:T(8,128)(2,1)}, bf16[8,4,32,256]{3,2,1,0:T(8,128)(2,1)}, u32[]{:S(2)}, u32[]{:S(2)}) collective-permute-start(bf16[8,4,32,256]{3,2,1,0:T(8,128)(2,1)} %get-tuple-element.115), channel_id=1, source_target_pairs={{0,2},{1,3},{2,0},{3,1},{4,6},{5,7},{6,4},{7,5},{8,10},{9,11},{10,... | collective-permute-start | bytes 1572872 | tf_op jit(solution)/shard_map/ppermute | solution.py:380
  137.1 38.7 %collective-permute-start.21 = (bf16[8,4,32,256]{3,2,1,0:T(8,128)(2,1)}, bf16[8,4,32,256]{3,2,1,0:T(8,128)(2,1)S(1)}, u32[]{:S(2)}, u32[]{:S(2)}) collective-permute-start(bf16[8,4,32,256]{3,2,1,0:T(8,128)(2,1)} %get-tuple-element.116), channel_id=1, source_target_pairs={{0,3},{1,2},{2,1},{3,0},{4,7},{5,6},{6,5},{7,4},{8,11},{9,10},{10,... | collective-permute-start | bytes 1572872 | tf_op jit(solution)/shard_map/ppermute | solution.py:380
  138.1 63.2 %collective-permute-start.25 = (bf16[32,2,32,256]{3,2,1,0:T(8,128)(2,1)S(1)}, bf16[32,2,32,256]{3,2,1,0:T(8,128)(2,1)S(1)}, u32[]{:S(2)}, u32[]{:S(2)}) collective-permute-start(bf16[32,2,32,256]{3,2,1,0:T(8,128)(2,1)S(1)} %collective-permute-done.24.refs_1_.refs_5_), channel_id=1, source_target_pairs={{12,4},{0,8},{20,12},{8,16},{28,20},{16,24},{13,5},{1,9},{21,13},{... | collective-permute-start | bytes 3145736 | tf_op jit(solution)/shard_map/ppermute | solution.py:375
  174.7 14.8 %collective-permute-start.22 = (bf16[16,2,32,256]{3,2,1,0:T(8,128)(2,1)}, bf16[16,2,32,256]{3,2,1,0:T(8,128)(2,1)S(1)}, u32[]{:S(2)}, u32[]{:S(2)}) collective-permute-start(bf16[16,2,32,256]{3,2,1,0:T(8,128)(2,1)} %get-tuple-element.118), channel_id=1, source_target_pairs={{0,4},{4,0},{8,12},{12,8},{16,20},{20,16},{24,28},{28,24},{1,5},{5... | collective-permute-start | bytes 1572872 | tf_op jit(solution)/shard_map/ppermute | solution.py:372
  174.8 16.0 %collective-permute-start.26 = (bf16[8,4,32,256]{3,2,1,0:T(8,128)(2,1)}, bf16[8,4,32,256]{3,2,1,0:T(8,128)(2,1)S(1)}, u32[]{:S(2)}, u32[]{:S(2)}) collective-permute-start(bf16[8,4,32,256]{3,2,1,0:T(8,128)(2,1)} %get-tuple-element.124), channel_id=1, source_target_pairs={{0,1},{1,0},{2,3},{3,2},{4,5},{5,4},{6,7},{7,6},{8,9},{9,8},{10,11... | collective-permute-start | bytes 1572872 | tf_op jit(solution)/shard_map/ppermute | solution.py:380
  175.3 20.1 %collective-permute-start.27 = (bf16[8,4,32,256]{3,2,1,0:T(8,128)(2,1)}, bf16[8,4,32,256]{3,2,1,0:T(8,128)(2,1)S(1)}, u32[]{:S(2)}, u32[]{:S(2)}) collective-permute-start(bf16[8,4,32,256]{3,2,1,0:T(8,128)(2,1)} %get-tuple-element.125), channel_id=1, source_target_pairs={{0,2},{1,3},{2,0},{3,1},{4,6},{5,7},{6,4},{7,5},{8,10},{9,11},{10,... | collective-permute-start | bytes 1572872 | tf_op jit(solution)/shard_map/ppermute | solution.py:380
  175.8 24.0 %collective-permute-start.28 = (bf16[8,4,32,256]{3,2,1,0:T(8,128)(2,1)}, bf16[8,4,32,256]{3,2,1,0:T(8,128)(2,1)S(1)}, u32[]{:S(2)}, u32[]{:S(2)}) collective-permute-start(bf16[8,4,32,256]{3,2,1,0:T(8,128)(2,1)} %get-tuple-element.126), channel_id=1, source_target_pairs={{0,3},{1,2},{2,1},{3,0},{4,7},{5,6},{6,5},{7,4},{8,11},{9,10},{10,... | collective-permute-start | bytes 1572872 | tf_op jit(solution)/shard_map/ppermute | solution.py:380
  189.5 45.7 %collective-permute-start.29 = (bf16[16,2,32,256]{3,2,1,0:T(8,128)(2,1)}, bf16[16,2,32,256]{3,2,1,0:T(8,128)(2,1)S(1)}, u32[]{:S(2)}, u32[]{:S(2)}) collective-permute-start(bf16[16,2,32,256]{3,2,1,0:T(8,128)(2,1)} %get-tuple-element.128.refs_2_), channel_id=1, source_target_pairs={{4,12},{8,0},{12,20},{16,8},{20,28},{24,16},{5,13},{9,1},{13,21},{... | collective-permute-start | bytes 1572872 | tf_op jit(solution)/shard_map/ppermute | solution.py:375
  190.9 44.4 %collective-permute-start.31 = (bf16[16,2,32,256]{3,2,1,0:T(8,128)(2,1)}, bf16[16,2,32,256]{3,2,1,0:T(8,128)(2,1)S(1)}, u32[]{:S(2)}, u32[]{:S(2)}) collective-permute-start(bf16[16,2,32,256]{3,2,1,0:T(8,128)(2,1)} %collective-permute-done.30.refs_1_), channel_id=1, source_target_pairs={{12,4},{0,8},{20,12},{8,16},{28,20},{16,24},{13,5},{1,9},{21,13},{... | collective-permute-start | bytes 1572872 | tf_op jit(solution)/shard_map/ppermute | solution.py:375
  195.5 50.2 %collective-permute-start.32 = (bf16[8,4,32,256]{3,2,1,0:T(8,128)(2,1)}, bf16[8,4,32,256]{3,2,1,0:T(8,128)(2,1)S(1)}, u32[]{:S(2)}, u32[]{:S(2)}) collective-permute-start(bf16[8,4,32,256]{3,2,1,0:T(8,128)(2,1)} %get-tuple-element.132), channel_id=1, source_target_pairs={{0,1},{1,0},{2,3},{3,2},{4,5},{5,4},{6,7},{7,6},{8,9},{9,8},{10,11... | collective-permute-start | bytes 1572872 | tf_op jit(solution)/shard_map/ppermute | solution.py:380
  200.6 45.1 %collective-permute-start.33 = (bf16[8,4,32,256]{3,2,1,0:T(8,128)(2,1)}, bf16[8,4,32,256]{3,2,1,0:T(8,128)(2,1)S(1)}, u32[]{:S(2)}, u32[]{:S(2)}) collective-permute-start(bf16[8,4,32,256]{3,2,1,0:T(8,128)(2,1)} %get-tuple-element.133), channel_id=1, source_target_pairs={{0,2},{1,3},{2,0},{3,1},{4,6},{5,7},{6,4},{7,5},{8,10},{9,11},{10,... | collective-permute-start | bytes 1572872 | tf_op jit(solution)/shard_map/ppermute | solution.py:380
  201.3 44.4 %collective-permute-start.34 = (bf16[8,4,32,256]{3,2,1,0:T(8,128)(2,1)}, bf16[8,4,32,256]{3,2,1,0:T(8,128)(2,1)S(1)}, u32[]{:S(2)}, u32[]{:S(2)}) collective-permute-start(bf16[8,4,32,256]{3,2,1,0:T(8,128)(2,1)} %get-tuple-element.134), channel_id=1, source_target_pairs={{0,3},{1,2},{2,1},{3,0},{4,7},{5,6},{6,5},{7,4},{8,11},{9,10},{10,... | collective-permute-start | bytes 1572872 | tf_op jit(solution)/shard_map/ppermute | solution.py:380
  280.9 40.8 %collective-permute-start.38 = (bf16[32,2,32,256]{3,2,1,0:T(8,128)(2,1)}, bf16[32,2,32,256]{3,2,1,0:T(8,128)(2,1)S(1)}, u32[]{:S(2)}, u32[]{:S(2)}) collective-permute-start(bf16[32,2,32,256]{3,2,1,0:T(8,128)(2,1)} %get-tuple-element.142), channel_id=1, source_target_pairs={{0,4},{4,0},{8,12},{12,8},{16,20},{20,16},{24,28},{28,24},{1,5},{5... | collective-permute-start | bytes 3145736 | tf_op jit(solution)/shard_map/ppermute | solution.py:372
  283.0 14.7 %collective-permute-start.36 = (bf16[8,4,32,256]{3,2,1,0:T(8,128)(2,1)S(1)}, bf16[8,4,32,256]{3,2,1,0:T(8,128)(2,1)S(1)}, u32[]{:S(2)}, u32[]{:S(2)}) collective-permute-start(bf16[8,4,32,256]{3,2,1,0:T(8,128)(2,1)S(1)} %copy-done.58), channel_id=1, source_target_pairs={{0,2},{1,3},{2,0},{3,1},{4,6},{5,7},{6,4},{7,5},{8,10},{9,11},{10,... | collective-permute-start | bytes 1572872 | tf_op jit(solution)/shard_map/ppermute | solution.py:380
  283.5 24.6 %collective-permute-start.37 = (bf16[8,4,32,256]{3,2,1,0:T(8,128)(2,1)}, bf16[8,4,32,256]{3,2,1,0:T(8,128)(2,1)S(1)}, u32[]{:S(2)}, u32[]{:S(2)}) collective-permute-start(bf16[8,4,32,256]{3,2,1,0:T(8,128)(2,1)} %get-tuple-element.139), channel_id=1, source_target_pairs={{0,3},{1,2},{2,1},{3,0},{4,7},{5,6},{6,5},{7,4},{8,11},{9,10},{10,... | collective-permute-start | bytes 1572872 | tf_op jit(solution)/shard_map/ppermute | solution.py:380
  284.8 42.5 %collective-permute-start.39 = (bf16[8,4,32,256]{3,2,1,0:T(8,128)(2,1)}, bf16[8,4,32,256]{3,2,1,0:T(8,128)(2,1)S(1)}, u32[]{:S(2)}, u32[]{:S(2)}) collective-permute-start(bf16[8,4,32,256]{3,2,1,0:T(8,128)(2,1)} %get-tuple-element.145), channel_id=1, source_target_pairs={{0,1},{1,0},{2,3},{3,2},{4,5},{5,4},{6,7},{7,6},{8,9},{9,8},{10,11... | collective-permute-start | bytes 1572872 | tf_op jit(solution)/shard_map/ppermute | solution.py:380
  285.1 42.3 %collective-permute-start.40 = (bf16[8,4,32,256]{3,2,1,0:T(8,128)(2,1)S(1)}, bf16[8,4,32,256]{3,2,1,0:T(8,128)(2,1)S(1)}, u32[]{:S(2)}, u32[]{:S(2)}) collective-permute-start(bf16[8,4,32,256]{3,2,1,0:T(8,128)(2,1)S(1)} %copy-done.55), channel_id=1, source_target_pairs={{0,2},{1,3},{2,0},{3,1},{4,6},{5,7},{6,4},{7,5},{8,10},{9,11},{10,... | collective-permute-start | bytes 1572872 | tf_op jit(solution)/shard_map/ppermute | solution.py:380
  297.7 32.9 %collective-permute-start.41 = (bf16[8,4,32,256]{3,2,1,0:T(8,128)(2,1)S(1)}, bf16[8,4,32,256]{3,2,1,0:T(8,128)(2,1)S(1)}, u32[]{:S(2)}, u32[]{:S(2)}) collective-permute-start(bf16[8,4,32,256]{3,2,1,0:T(8,128)(2,1)S(1)} %copy-done.54), channel_id=1, source_target_pairs={{0,3},{1,2},{2,1},{3,0},{4,7},{5,6},{6,5},{7,4},{8,11},{9,10},{10,... | collective-permute-start | bytes 1572872 | tf_op jit(solution)/shard_map/ppermute | solution.py:380
  365.5 44.4 %collective-permute-start.45 = (bf16[32,2,32,256]{3,2,1,0:T(8,128)(2,1)}, bf16[32,2,32,256]{3,2,1,0:T(8,128)(2,1)S(1)}, u32[]{:S(2)}, u32[]{:S(2)}) collective-permute-start(bf16[32,2,32,256]{3,2,1,0:T(8,128)(2,1)} %get-tuple-element.155), channel_id=1, source_target_pairs={{0,4},{4,0},{8,12},{12,8},{16,20},{20,16},{24,28},{28,24},{1,5},{5... | collective-permute-start | bytes 3145736 | tf_op jit(solution)/shard_map/ppermute | solution.py:372
  366.5 49.1 %collective-permute-start.46 = (bf16[8,4,32,256]{3,2,1,0:T(8,128)(2,1)}, bf16[8,4,32,256]{3,2,1,0:T(8,128)(2,1)S(1)}, u32[]{:S(2)}, u32[]{:S(2)}) collective-permute-start(bf16[8,4,32,256]{3,2,1,0:T(8,128)(2,1)} %get-tuple-element.158), channel_id=1, source_target_pairs={{0,1},{1,0},{2,3},{3,2},{4,5},{5,4},{6,7},{7,6},{8,9},{9,8},{10,11... | collective-permute-start | bytes 1572872 | tf_op jit(solution)/shard_map/ppermute | solution.py:380
  366.5 49.1 %collective-permute-start.47 = (bf16[8,4,32,256]{3,2,1,0:T(8,128)(2,1)S(1)}, bf16[8,4,32,256]{3,2,1,0:T(8,128)(2,1)S(1)}, u32[]{:S(2)}, u32[]{:S(2)}) collective-permute-start(bf16[8,4,32,256]{3,2,1,0:T(8,128)(2,1)S(1)} %copy-done.57), channel_id=1, source_target_pairs={{0,2},{1,3},{2,0},{3,1},{4,6},{5,7},{6,4},{7,5},{8,10},{9,11},{10,... | collective-permute-start | bytes 1572872 | tf_op jit(solution)/shard_map/ppermute | solution.py:380
  367.9 47.6 %collective-permute-start.48 = (bf16[8,4,32,256]{3,2,1,0:T(8,128)(2,1)S(1)}, bf16[8,4,32,256]{3,2,1,0:T(8,128)(2,1)S(1)}, u32[]{:S(2)}, u32[]{:S(2)}) collective-permute-start(bf16[8,4,32,256]{3,2,1,0:T(8,128)(2,1)S(1)} %copy-done.56), channel_id=1, source_target_pairs={{0,3},{1,2},{2,1},{3,0},{4,7},{5,6},{6,5},{7,4},{8,11},{9,10},{10,... | collective-permute-start | bytes 1572872 | tf_op jit(solution)/shard_map/ppermute | solution.py:380
  375.0 26.8 %collective-permute-start.44 = (bf16[4,4,32,256]{3,2,1,0:T(8,128)(2,1)S(1)}, bf16[4,4,32,256]{3,2,1,0:T(8,128)(2,1)S(1)}, u32[]{:S(2)}, u32[]{:S(2)}) collective-permute-start(bf16[4,4,32,256]{3,2,1,0:T(8,128)(2,1)S(1)} %copy-done.59), channel_id=1, source_target_pairs={{0,3},{1,2},{2,1},{3,0},{4,7},{5,6},{6,5},{7,4},{8,11},{9,10},{10,... | collective-permute-start | bytes 786440 | tf_op jit(solution)/shard_map/ppermute | solution.py:380
  450.8 26.0 %collective-permute-start.49 = (bf16[32,2,32,256]{3,2,1,0:T(8,128)(2,1)}, bf16[32,2,32,256]{3,2,1,0:T(8,128)(2,1)S(1)}, u32[]{:S(2)}, u32[]{:S(2)}) collective-permute-start(bf16[32,2,32,256]{3,2,1,0:T(8,128)(2,1)} %get-tuple-element.163), channel_id=1, source_target_pairs={{0,4},{4,0},{8,12},{12,8},{16,20},{20,16},{24,28},{28,24},{1,5},{5... | collective-permute-start | bytes 3145736 | tf_op jit(solution)/shard_map/ppermute | solution.py:372
  452.9 29.4 %collective-permute-start.50 = (bf16[4,4,32,256]{3,2,1,0:T(8,128)(2,1)S(1)}, bf16[4,4,32,256]{3,2,1,0:T(8,128)(2,1)S(1)}, u32[]{:S(2)}, u32[]{:S(2)}) collective-permute-start(bf16[4,4,32,256]{3,2,1,0:T(8,128)(2,1)S(1)} %copy-done.64), channel_id=1, source_target_pairs={{0,1},{1,0},{2,3},{3,2},{4,5},{5,4},{6,7},{7,6},{8,9},{9,8},{10,11... | collective-permute-start | bytes 786440 | tf_op jit(solution)/shard_map/ppermute | solution.py:380
  452.9 29.4 %collective-permute-start.51 = (bf16[4,4,32,256]{3,2,1,0:T(8,128)(2,1)S(1)}, bf16[4,4,32,256]{3,2,1,0:T(8,128)(2,1)S(1)}, u32[]{:S(2)}, u32[]{:S(2)}) collective-permute-start(bf16[4,4,32,256]{3,2,1,0:T(8,128)(2,1)S(1)} %copy-done.63), channel_id=1, source_target_pairs={{0,2},{1,3},{2,0},{3,1},{4,6},{5,7},{6,4},{7,5},{8,10},{9,11},{10,... | collective-permute-start | bytes 786440 | tf_op jit(solution)/shard_map/ppermute | solution.py:380
  453.6 28.8 %collective-permute-start.52 = (bf16[4,4,32,256]{3,2,1,0:T(8,128)(2,1)S(1)}, bf16[4,4,32,256]{3,2,1,0:T(8,128)(2,1)S(1)}, u32[]{:S(2)}, u32[]{:S(2)}) collective-permute-start(bf16[4,4,32,256]{3,2,1,0:T(8,128)(2,1)S(1)} %copy-done.62), channel_id=1, source_target_pairs={{0,3},{1,2},{2,1},{3,0},{4,7},{5,6},{6,5},{7,4},{8,11},{9,10},{10,... | collective-permute-start | bytes 786440 | tf_op jit(solution)/shard_map/ppermute | solution.py:380
  501.5 13.9 %collective-permute-start.53 = (bf16[16,2,32,256]{3,2,1,0:T(8,128)(2,1)}, bf16[16,2,32,256]{3,2,1,0:T(8,128)(2,1)S(1)}, u32[]{:S(2)}, u32[]{:S(2)}) collective-permute-start(bf16[16,2,32,256]{3,2,1,0:T(8,128)(2,1)} %get-tuple-element.171), channel_id=1, source_target_pairs={{0,4},{4,0},{8,12},{12,8},{16,20},{20,16},{24,28},{28,24},{1,5},{5... | collective-permute-start | bytes 1572872 | tf_op jit(solution)/shard_map/ppermute | solution.py:372
  (71 other events, 1554.3 us)

commit v3 on v2

--- a/solution.py
+++ b/solution.py
@@ -2,6 +2,7 @@
 
 import jax
 import jax.numpy as jnp
+import numpy as np
 from jax import lax
 from jax.experimental import pallas as pl
 from jax.experimental.pallas import tpu as pltpu
@@ -11,15 +12,14 @@
 ANY = pl.BlockSpec(memory_space=pl.ANY)
 VMEM = pl.BlockSpec(memory_space=pltpu.VMEM)
 SMEM = pl.BlockSpec(memory_space=pltpu.SMEM)
-VMEM_LIMIT = 58 * 1024 * 1024
 TOKEN = jax.ShapeDtypeStruct((2,), jnp.int32)
 COST = pl.CostEstimate(flops=1, bytes_accessed=1, transcendentals=0)
 EDGE = 2
 TILE = 16
 
 
-def params():
-    return pltpu.CompilerParams(vmem_limit_bytes=VMEM_LIMIT)
+def params(mebibytes):
+    return pltpu.CompilerParams(vmem_limit_bytes=mebibytes * 1024 * 1024)
 
 
 def from_rows(y, group):
@@ -83,7 +83,7 @@
             pltpu.VMEM((2, planes, modes, depth, cols), BF16),
             pltpu.SemaphoreType.DMA((2,)),
         ],
-        compiler_params=params(),
+        compiler_params=params(10),
         cost_estimate=COST,
         name="spread",
     )(pos, field, turn, *after)
@@ -93,99 +93,87 @@
     group = 4
     blocks, refs = refs[:group], refs[group:]
     tails, refs = refs[:heads], refs[heads:]
-    outs, (token, field, first, aside, final, sems) = refs[:count], refs[count:]
+    outs, (token, first, edge, sems) = refs[:count], refs[count:]
     token[0], token[1] = pos[0], pos[1]
-    _, stack, modes, cols = field.shape
-    planes = stack // group
-    mine = stack - 2 * planes
-    rows = final.shape[0]
+    planes, modes, cols = blocks[0].shape[1:]
+    mine = 2 * planes
+    part = outs[0].shape[0]
+    rows = part * count
     lead = 2 * EDGE if heads else EDGE
     copies = []
-    for g in range(group):
-        to = pl.ds(g * planes, planes)
+    for g in range(heads):
+        length = tails[g].shape[0]
         copies.append(
-            pltpu.make_async_copy(blocks[g], field.at[pl.ds(lead, rows + 2 * EDGE - lead), to], sems.at[g])
+            pltpu.make_async_copy(
+                tails[g].at[pl.ds(length - lead, lead)], edge.at[:, pl.ds(g * planes, planes)], sems.at[g]
+            )
         )
-        if heads:
-            length = tails[g].shape[0]
-            copies.append(
-                pltpu.make_async_copy(
-                    tails[g].at[pl.ds(length - lead, lead)], field.at[pl.ds(0, lead), to], sems.at[group + g]
-                )
-            )
     for copy in copies:
         copy.start()
-    if not heads:
-        field[pl.ds(0, lead)] = jnp.zeros((lead, stack, modes, cols), BF16)
     for copy in copies:
         copy.wait()
     low = planes - 1
     wide = mine + 2
     piece = min(modes, 16)
 
-    def beside(x):
+    def field(row, p, some):
+        if isinstance(row, int) and row < lead:
+            if heads:
+                return edge[row, p, some]
+            return jnp.zeros((some.size, cols), BF16)
+        return blocks[p // planes][row - lead, p % planes, some]
+
+    def beside(parts, number):
         return jnp.dot(
-            to_bf16_rows(x.reshape(-1, modes, cols)), shift[...], preferred_element_type=F32
-        ).reshape(x.shape[:2] + (modes, cols))
-
-    def look(j, slot):
-        aside[slot] = beside(field[pl.ds(2 * j + 1, 2), pl.ds(low, wide)])
-
-    look(0, 0)
-
-    def pair(j, _):
-        slot = j % 2
-        i = 2 * j
-
-        look(jnp.minimum(j + 1, (rows + 2) // 2 - 1), 1 - slot)
-        for a in range(2):
+            to_bf16_rows(jnp.stack(parts)), shift[...], preferred_element_type=F32
+        ).reshape(number, -1, modes, cols)
+
+    def once(i, number):
+        every = pl.ds(0, modes)
+        aside = beside([field(i + 1 + a, low + p, every) for a in range(number) for p in range(wide)], number)
+        for a in range(number):
             speeds = [rate[p, pl.ds(begin + i + a, 1), :] for p in range(wide)]
             for h in range(modes // piece):
                 some = pl.ds(h * piece, piece)
-                line = [field[i + 1 + a, low - 1 + p, some].astype(F32) for p in range(wide + 2)]
+                line = [field(i + 1 + a, low - 1 + p, some).astype(F32) for p in range(wide + 2)]
                 for p in range(wide):
                     centre = line[p + 1]
-                    around = aside[slot, a, p, some] + (line[p] + line[p + 2])
+                    around = aside[a, p, h * piece : (h + 1) * piece] + (line[p] + line[p + 2])
                     around = around + (
-                        field[i + a, low + p, some].astype(F32) + field[i + 2 + a, low + p, some].astype(F32)
+                        field(i + a, low + p, some).astype(F32) + field(i + 2 + a, low + p, some).astype(F32)
                     )
                     first[i + a, p, some] = centre + speeds[p] * (around - 6.0 * centre)
+
+    for i in range(0, lead, 2):
+        once(i, 2)
+
+    def pair(j, _):
+        once(lead + 2 * j, 2)
         return 0
 
-    lax.fori_loop(0, (rows + 2) // 2, pair, 0)
-
-    def look_again(j, slot):
-        aside[slot, :, pl.ds(0, mine)] = beside(first[pl.ds(2 * j + 1, 2), pl.ds(1, mine)])
-
-    look_again(0, 0)
-
-    def pair_again(j, _):
-        slot = j % 2
-        i = 2 * j
-
-        look_again(jnp.minimum(j + 1, rows // 2 - 1), 1 - slot)
-        for a in range(2):
-            speeds = [rate[p + 1, pl.ds(begin + i + a + 1, 1), :] for p in range(mine)]
-            for h in range(modes // piece):
-                some = pl.ds(h * piece, piece)
-                line = [first[i + 1 + a, p, some] for p in range(wide)]
-                for p in range(mine):
-                    centre = line[p + 1]
-                    around = aside[slot, a, p, some] + (line[p] + line[p + 2])
-                    around = around + (first[i + a, p + 1, some] + first[i + 2 + a, p + 1, some])
-                    final[i + a, p, some] = (centre + speeds[p] * (around - 6.0 * centre)).astype(BF16)
-        return 0
-
-    lax.fori_loop(0, rows // 2, pair_again, 0)
-    part = rows // count
-    copies = []
+    lax.fori_loop(0, (rows + 2 - lead) // 2, pair, 0)
+    number = 2 if part % 2 == 0 else 1
     for k in range(count):
         base = jnp.bitwise_xor(pos[1], k) * part
-        copies.append(pltpu.make_async_copy(final.at[pl.ds(base, part)], outs[k], sems.at[2 * group + k]))
-    for copy in copies:
-        copy.start()
-    for copy in copies:
-        copy.wait()
+
+        def again(j, _):
+            i = base + number * j
+            aside = beside([first[i + 1 + a, 1 + p] for a in range(number) for p in range(mine)], number)
+            for a in range(number):
+                speeds = [rate[p + 1, pl.ds(begin + i + a + 1, 1), :] for p in range(mine)]
+                for h in range(modes // piece):
+                    some = pl.ds(h * piece, piece)
+                    line = [first[i + 1 + a, p, some] for p in range(wide)]
+                    for p in range(mine):
+                        centre = line[p + 1]
+                        around = aside[a, p, h * piece : (h + 1) * piece] + (line[p] + line[p + 2])
+                        around = around + (first[i + a, p + 1, some] + first[i + 2 + a, p + 1, some])
+                        outs[k][number * j + a, p, some] = (
+                            centre + speeds[p] * (around - 6.0 * centre)
+                        ).astype(BF16)
+            return 0
+
+        lax.fori_loop(0, part // number, again, 0)
 
 
 def sweep(pos, rate, shift, blocks, tails, begin, rows, count):
@@ -195,16 +183,14 @@
     return pl.pallas_call(
         functools.partial(sweep_kernel, begin=begin, count=count, heads=len(tails)),
         out_shape=(piece,) * count + (TOKEN,),
-        in_specs=[SMEM, VMEM, VMEM] + [ANY] * (4 + len(tails)),
-        out_specs=(ANY,) * count + (SMEM,),
+        in_specs=[SMEM] + [VMEM] * 6 + [ANY] * len(tails),
+        out_specs=(VMEM,) * count + (SMEM,),
         scratch_shapes=[
-            pltpu.VMEM((rows + 2 * EDGE, 4 * planes, modes, cols), BF16),
             pltpu.VMEM((rows + 2, mine + 2, modes, cols), F32),
-            pltpu.VMEM((2, 2, mine + 2, modes, cols), F32),
-            pltpu.VMEM((rows, mine, modes, cols), BF16),
-            pltpu.SemaphoreType.DMA((8 + count,)),
+            pltpu.VMEM((2 * EDGE, 4 * planes, modes, cols), BF16),
+            pltpu.SemaphoreType.DMA((4,)),
         ],
-        compiler_params=params(),
+        compiler_params=params(22),
         cost_estimate=COST,
         name="sweep",
     )(pos, rate, shift, *blocks, *tails)
@@ -245,7 +231,7 @@
         out_shape=tuple(jax.ShapeDtypeStruct(block.shape, BF16) for block in blocks) + (TOKEN,),
         in_specs=[SMEM] + [VMEM] * (5 + count),
         out_specs=(VMEM,) * count + (SMEM,),
-        compiler_params=params(),
+        compiler_params=params(14),
         cost_estimate=COST,
         name="points",
     )(pos, basis, basis_t, flat, swing, load, *blocks)
@@ -275,9 +261,9 @@
         collect_kernel,
         out_shape=(jax.ShapeDtypeStruct(shape, BF16), TOKEN),
         in_specs=[SMEM] + [ANY] * count,
-        out_specs=(ANY, SMEM),
+        out_specs=(VMEM, SMEM),
         scratch_shapes=[pltpu.SemaphoreType.DMA((count,))],
-        compiler_params=params(),
+        compiler_params=params(6),
         cost_estimate=COST,
         name="collect",
     )(pos, *blocks)
@@ -341,7 +327,7 @@
             pltpu.SemaphoreType.DMA((count + 3,)),
         ],
         input_output_aliases={2: 0} if chained else {},
-        compiler_params=params(),
+        compiler_params=params(10),
         cost_estimate=COST,
         name="settle",
     )(pos, turn, *([result] if chained else []), *blocks, other)
@@ -352,7 +338,23 @@
     return [unit, 2 * unit, 2 * unit, 2 * unit, unit]
 
 
-ORDER = "T0 T1 T2 S0 T3 T4 P0 S1 C0 S2 P1 F0 S3 P2 S4 C1 P3 F1 C2 P4 F2 C3 F3 C4 F4".split()
+ORDER = (
+    ("T", 0), ("T", 1), ("T", 2), ("S", 0), ("T", 3),
+    ("T", 4), ("P", 0), ("S", 1), ("C", 0), ("S", 2),
+    ("P", 1), ("F", 0), ("S", 3), ("P", 2), ("S", 4),
+    ("C", 1), ("P", 3), ("F", 1), ("C", 2), ("P", 4),
+    ("F", 2), ("C", 3), ("F", 3), ("C", 4), ("F", 4),
+)
+
+
+def turns(group):
+    at = np.arange(group * TILE)
+    row, mode = at // group, at % group
+    same = mode[:, None] == (at // TILE)[None, :]
+    straight = same & (row[:, None] == (at % TILE)[None, :])
+    reverse = same & (row[:, None] == TILE - 1 - (at % TILE)[None, :])
+    to_rows = np.stack([straight, reverse])
+    return jnp.asarray(to_rows, BF16), jnp.asarray(to_rows.transpose(0, 2, 1), BF16)
 
 
 def on_device(field, diffusion, joule, basis, quad_weight, base_conductivity, thermal_slope):
@@ -386,24 +388,9 @@
         send = jnp.where(side == 1, planes_back, rows_back).astype(sent)
         return own, send
 
-    own_rate, send_rate = logical(diffusion, half + EDGE, side, F32)
-    other_rate = across(send_rate)
-    before, after = halo(own_rate[-1:], other_rate[:1])
-    rate = jnp.concatenate([before, other_rate, own_rate, after], axis=0)
-    rate = jnp.pad(rate, ((0, 0), (1, -(half + EDGE + 1) % 8), (0, 0)))
-
-    lane = jnp.arange(cols)
-    shift = (jnp.abs(lane[:, None] - lane[None, :]) == 1).astype(BF16)
-
-    group = min(modes, TILE)
-    at = jnp.arange(group * TILE)
-    row_first = (at // group, at % group)
-    mode_first = (at % TILE, at // TILE)
-    same = row_first[1][:, None] == mode_first[1][None, :]
-    straight = row_first[0][:, None] == mode_first[0][None, :]
-    reverse = row_first[0][:, None] == TILE - 1 - mode_first[0][None, :]
-    to_rows = jnp.stack([same & straight, same & reverse]).astype(BF16)
-    to_modes = jnp.stack([(same & straight).T, (same & reverse).T]).astype(BF16)
+    lane = np.arange(cols)
+    shift = jnp.asarray(np.abs(lane[:, None] - lane[None, :]) == 1, BF16)
+    to_rows, to_modes = turns(min(modes, TILE))
 
     points_count = basis.shape[0]
     extra = -points_count % 32
@@ -420,19 +407,26 @@
     begins = [sum(rows_of[:c]) for c in range(len(rows_of))]
     own, other, blocks, cells, home, theirs = {}, {}, {}, {}, {}, {}
     result = None
-    for step in ORDER:
-        kind, c = step[0], int(step[1:])
+    for kind, c in ORDER:
         begin, rows = begins[c], rows_of[c]
         if kind == "T":
             skip = EDGE if c else 0
-            after = () if c else (send_rate,)
+            after = ()
+            if c == 1:
+                own_rate, send_rate = logical(diffusion, half + EDGE, pos[0], F32)
+                own_load, send_load = logical(joule, half, pos[0], BF16)
+                other_rate, other_load = across(send_rate), across(send_load)
+                before, behind = halo(own_rate[-1:], other_rate[:1])
+                rate = jnp.concatenate([before, other_rate, own_rate, behind], axis=0)
+                rate = jnp.pad(rate, ((0, 0), (1, -(half + EDGE + 1) % 8), (0, 0)))
+                load = jnp.concatenate([other_load.astype(F32), own_load], axis=0)
+                after = (send_rate, send_load)
+            elif c == 2:
+                after = (blocks[0][0], other_load)
             own[c], send, pos = spread(pos, field, to_rows, after, begin, skip, rows + EDGE - skip, rows + TILE)
             other[c] = across(send)
             before, after = halo(own[c], other[c])
             blocks[c] = (before, other[c], own[c], after)
-            if c == 0:
-                own_load, send_load = logical(joule, half, pos[0], BF16)
-                load = jnp.concatenate([across(send_load).astype(F32), own_load], axis=0)
         elif kind == "S":
             *pieces, pos = sweep(pos, rate, shift, blocks[c], blocks.get(c - 1, ()), begin, rows, count)
             cells[c] = exchange(pieces)

time: 522 us -> 359 us (0.69)
  Pallas kernels: 298 us -> 120 us
  waiting for transfers between devices: 120 us -> 140 us
  other arithmetic: 8.35 us -> 2.55 us
    pallas_call x5, Pallas kernels: 139 us -> 6.47 us  [collect(): pl.pallas_call(collect_kernel, out_shape=(jax.ShapeDtypeStruct(shape, BF1...]
    pallas_call x5, Pallas kernels: 63 us -> 42.1 us  [sweep(): pl.pallas_call(functools.partial(sweep_kernel, begin=begin, count=count,...]
    ppermute x12, waiting for transfers between devices: 44.7 us -> 58.9 us  [across(): return lax.ppermute(x, 'space', swap)]
    ppermute x30, waiting for transfers between devices: 69.1 us -> 80 us  [exchange(): lax.ppermute(pieces[k], 'modes', [(j, j ^ k) for j in range(count)])]
    pallas_call x5, Pallas kernels: 21.3 us -> 11.8 us  [spread(): pl.pallas_call(functools.partial(spread_kernel, begin=begin, skip=skip),...]
    pallas_call x5, Pallas kernels: 52.9 us -> 44.1 us  [points(): pl.pallas_call(functools.partial(points_kernel, begin=begin), out_shape=t...]
    unnamed x134 -> x54, local copies, waits for them, and re-layouts: 12.2 us -> 19.1 us
    pallas_call x5, Pallas kernels: 21.8 us -> 15.2 us  [settle(): pl.pallas_call(functools.partial(settle_kernel, begin=begin, count=count,...]
  transfers between devices with their start and end apart: 54 -> 54, of which waited for: 12 -> 16; matrix products, arithmetic and copies ran while one was open for 2% -> 2% of each run, Pallas kernels for 33% -> 31%
where the time goes in v3:
time: 359 us; the launch traced here: 358 us
  waiting for transfers between devices  140 us (39%)
  Pallas kernels  120 us (33%)
  starting transfers between devices  71 us (20%)
  local copies, waits for them, and re-layouts  23.1 us (6%)
    ppermute x30, waiting for transfers between devices, exchange(): lax.ppermute(pieces[k], 'modes', [(j, j ^ k) for j in range(count)])  80 us
    ppermute x12, waiting for transfers between devices, across(): return lax.ppermute(x, 'space', swap)  58.9 us
    pallas_call x5, Pallas kernels, points(): pl.pallas_call(functools.partial(points_kernel, begin=begin), out_shape=t...  44.1 us
    pallas_call x5, Pallas kernels, sweep(): pl.pallas_call(functools.partial(sweep_kernel, begin=begin, count=count,...  42.1 us
    ppermute x6, starting transfers between devices, halo(): lax.ppermute(other, 'space', back)  25 us
    ppermute x30, starting transfers between devices, exchange(): lax.ppermute(pieces[k], 'modes', [(j, j ^ k) for j in range(count)])  21 us
    unnamed x54, local copies, waits for them, and re-layouts  19.1 us
    ppermute x12, starting transfers between devices, across(): return lax.ppermute(x, 'space', swap)  17.3 us
  transfers between devices with their start and end apart: 54, of which 16 were waited for; matrix products, arithmetic and copies ran while one was open for 2% of the time, Pallas kernels for 31%

profile of v3, /device:TPU:0, one launch (start us, length us, event | category | flops | bytes accessed | tf_op | source)
XLA Modules:
  0.0 357.6 jit_solution(6664889290524617748)
XLA Ops:
  0.1 3.4 copy-done
  4.4 1.9 spread.5
  7.6 5.2 %collective-permute-start.5 = (bf16[18,2,32,256]{3,2,1,0:T(8,128)(2,1)S(1)}, bf16[18,2,32,256]{3,2,1,0:T(8,128)(2,1)}, u32[]{:S(2)}, u32[]{:S(2)}) collective-permute-start(bf16[18,2,32,256]{3,2,1,0:T(8,128)(2,1)S(1)} %get-tuple-element.93), channel_id=1, source_target_pairs={{0,4},{4,0},{8,12},{12,8},{16,20},{20,16},{24,28},{28,24},{1,5},{5... | collective-permute-start | bytes 1769480 | tf_op jit(solution)/shard_map/ppermute | solution.py:374
  15.6 3.4 copy-done.1
  19.0 3.1 spread.6
  22.2 4.9 %collective-permute-done.5.refs_1_.refs_5_ = bf16[18,2,32,256]{3,2,1,0:T(8,128)(2,1)} collective-permute-done((bf16[18,2,32,256]{3,2,1,0:T(8,128)(2,1)S(1)}, bf16[18,2,32,256]{3,2,1,0:T(8,128)(2,1)}, u32[]{:S(2)}, u32[]{:S(2)}) %collective-permute-start.5) | collective-permute-done | bytes 589856 | tf_op jit(solution)/shard_map/ppermute | solution.py:374
  27.1 3.5 collective-permute-start.6
  30.7 2.0 collective-permute-start.3
  32.7 19.6 %collective-permute-done.1.refs_1_ = bf16[2,128,256]{2,1,0:T(8,128)(2,1)S(1)} collective-permute-done((bf16[2,128,256]{2,1,0:T(8,128)(2,1)S(1)}, bf16[2,128,256]{2,1,0:T(8,128)(2,1)S(1)}, u32[]{:S(2)}, u32[]{:S(2)}) %collective-permute-start.1) | collective-permute-done | bytes 131104 | tf_op jit(solution)/shard_map/ppermute | solution.py:374
  52.3 2.7 spread.7
  55.0 2.1 collective-permute-start.17
  58.5 4.6 %collective-permute-start.4 = (f32[1,130,256]{2,1,0:T(8,128)S(1)}, f32[1,130,256]{2,1,0:T(8,128)S(1)}, u32[]{:S(2)}, u32[]{:S(2)}) collective-permute-start(f32[1,130,256]{2,1,0:T(8,128)S(1)} %slice.46), channel_id=1, source_target_pairs={{12,4},{0,8},{20,12},{8,16},{28,20},{16,24},{13,5},{1,9},{21,13},{... | collective-permute-start | bytes 399368 | tf_op jit(solution)/shard_map/ppermute | solution.py:377
  67.0 6.0 %sweep.5 = (bf16[4,4,32,256]{3,2,1,0:T(8,128)(2,1)S(1)}, bf16[4,4,32,256]{3,2,1,0:T(8,128)(2,1)}, bf16[4,4,32,256]{3,2,1,0:T(8,128)(2,1)}, bf16[4,4,32,256]{3,2,1,0:T(8,128)(2,1)S(1)}, s32[2]{0:T(128)S(1)}) custom-call(s32[2]{0:T(128)S(1)} %get-tuple-element.92.pos, f32[6,136,256]{2,1,0:T(8,128)S(1)} %select_maximum_fusion.rate, ...), custom_call_target="tpu_custom_call" | custom-call | flops 1 | bytes 1 | tf_op jit(solution)/shard_map/sweep/pallas_call | solution.py:183
  82.8 5.0 %collective-permute-start.12 = (bf16[32,2,32,256]{3,2,1,0:T(8,128)(2,1)}, bf16[32,2,32,256]{3,2,1,0:T(8,128)(2,1)S(1)}, u32[]{:S(2)}, u32[]{:S(2)}) collective-permute-start(bf16[32,2,32,256]{3,2,1,0:T(8,128)(2,1)} %collective-permute-done.11.refs_1_.refs_5_), channel_id=1, source_target_pairs={{12,4},{0,8},{20,12},{8,16},{28,20},{16,24},{13,5},{1,9},{21,13},{... | collective-permute-start | bytes 3145736 | tf_op jit(solution)/shard_map/ppermute | solution.py:377
  88.6 3.4 copy-done.2
  92.7 2.2 spread.8
  96.4 4.6 %collective-permute-start.18 = (bf16[32,2,32,256]{3,2,1,0:T(8,128)(2,1)}, bf16[32,2,32,256]{3,2,1,0:T(8,128)(2,1)S(1)}, u32[]{:S(2)}, u32[]{:S(2)}) collective-permute-start(bf16[32,2,32,256]{3,2,1,0:T(8,128)(2,1)} %collective-permute-done.17.refs_1_.refs_5_), channel_id=1, source_target_pairs={{12,4},{0,8},{20,12},{8,16},{28,20},{16,24},{13,5},{1,9},{21,13},{... | collective-permute-start | bytes 3145736 | tf_op jit(solution)/shard_map/ppermute | solution.py:377
  101.2 3.4 copy-done.3
  104.5 1.9 spread.9
  106.7 6.4 %points.5 = (bf16[4,4,32,256]{3,2,1,0:T(8,128)(2,1)S(1)}, bf16[4,4,32,256]{3,2,1,0:T(8,128)(2,1)S(1)}, bf16[4,4,32,256]{3,2,1,0:T(8,128)(2,1)S(1)}, bf16[4,4,32,256]{3,2,1,0:T(8,128)(2,1)S(1)}, s32[2]{0:T(128)S(1)}) custom-call(s32[2]{0:T(128)S(1)} %get-tuple-element.96.pos, bf16[352,128]{1,0:T(8,128)(2,1)S(1)} %copy.19.basis, bf16[128,352]{1,0:T(8,128)(2,1)S(1)} %bitcast.5, ...), custom_call_target="tpu_custom_call" | custom-call | flops 1 | bytes 1 | tf_op jit(solution)/shard_map/points/pallas_call | solution.py:229
  116.1 5.8 %collective-permute-done.14.refs_2_ = bf16[4,4,32,256]{3,2,1,0:T(8,128)(2,1)S(1)} collective-permute-done((bf16[4,4,32,256]{3,2,1,0:T(8,128)(2,1)S(1)}, bf16[4,4,32,256]{3,2,1,0:T(8,128)(2,1)S(1)}, u32[]{:S(2)}, u32[]{:S(2)}) %collective-permute-start.14) | collective-permute-done | bytes 262176 | tf_op jit(solution)/shard_map/ppermute | solution.py:382
  122.7 10.9 %sweep.6 = (bf16[8,4,32,256]{3,2,1,0:T(8,128)(2,1)S(1)}, bf16[8,4,32,256]{3,2,1,0:T(8,128)(2,1)S(1)}, bf16[8,4,32,256]{3,2,1,0:T(8,128)(2,1)S(1)}, bf16[8,4,32,256]{3,2,1,0:T(8,128)(2,1)S(1)}, s32[2]{0:T(128)S(1)}) custom-call(s32[2]{0:T(128)S(1)} %get-tuple-element.101.pos, f32[6,136,256]{2,1,0:T(8,128)S(1)} %select_maximum_fusion.rate, ...), custom_call_target="tpu_custom_call" | custom-call | flops 1 | bytes 1 | tf_op jit(solution)/shard_map/sweep/pallas_call | solution.py:183
  136.9 2.7 collective-permute-start.25
  141.0 10.6 %sweep.7 = (bf16[8,4,32,256]{3,2,1,0:T(8,128)(2,1)S(1)}, bf16[8,4,32,256]{3,2,1,0:T(8,128)(2,1)S(1)}, bf16[8,4,32,256]{3,2,1,0:T(8,128)(2,1)S(1)}, bf16[8,4,32,256]{3,2,1,0:T(8,128)(2,1)S(1)}, s32[2]{0:T(128)S(1)}) custom-call(s32[2]{0:T(128)S(1)} %get-tuple-element.109.pos, f32[6,136,256]{2,1,0:T(8,128)S(1)} %select_maximum_fusion.rate, ...), custom_call_target="tpu_custom_call" | custom-call | flops 1 | bytes 1 | tf_op jit(solution)/shard_map/sweep/pallas_call | solution.py:183
  153.6 6.9 %collective-permute-done.21.refs_3_ = bf16[8,4,32,256]{3,2,1,0:T(8,128)(2,1)S(1)} collective-permute-done((bf16[8,4,32,256]{3,2,1,0:T(8,128)(2,1)S(1)}, bf16[8,4,32,256]{3,2,1,0:T(8,128)(2,1)S(1)}, u32[]{:S(2)}, u32[]{:S(2)}) %collective-permute-start.21) | collective-permute-done | bytes 524320 | tf_op jit(solution)/shard_map/ppermute | solution.py:382
  160.5 2.2 collective-permute-start.28
  162.7 10.6 %points.6 = (bf16[8,4,32,256]{3,2,1,0:T(8,128)(2,1)S(1)}, bf16[8,4,32,256]{3,2,1,0:T(8,128)(2,1)S(1)}, bf16[8,4,32,256]{3,2,1,0:T(8,128)(2,1)S(1)}, bf16[8,4,32,256]{3,2,1,0:T(8,128)(2,1)S(1)}, s32[2]{0:T(128)S(1)}) custom-call(s32[2]{0:T(128)S(1)} %get-tuple-element.112.pos, bf16[352,128]{1,0:T(8,128)(2,1)S(1)} %copy.19.basis, ...), custom_call_target="tpu_custom_call" | custom-call | flops 1 | bytes 1 | tf_op jit(solution)/shard_map/points/pallas_call | solution.py:229
  174.7 4.6 %collective-permute-start.31 = (bf16[16,2,32,256]{3,2,1,0:T(8,128)(2,1)S(1)}, bf16[16,2,32,256]{3,2,1,0:T(8,128)(2,1)S(1)}, u32[]{:S(2)}, u32[]{:S(2)}) collective-permute-start(bf16[16,2,32,256]{3,2,1,0:T(8,128)(2,1)S(1)} %collective-permute-done.30.refs_1_), channel_id=1, source_target_pairs={{12,4},{0,8},{20,12},{8,16},{28,20},{16,24},{13,5},{1,9},{21,13},{... | collective-permute-start | bytes 1572872 | tf_op jit(solution)/shard_map/ppermute | solution.py:377
  181.6 1.9 collective-permute-start.34
  183.6 2.8 settle.5
  186.4 9.6 %sweep.8 = (bf16[8,4,32,256]{3,2,1,0:T(8,128)(2,1)S(1)}, bf16[8,4,32,256]{3,2,1,0:T(8,128)(2,1)S(1)}, bf16[8,4,32,256]{3,2,1,0:T(8,128)(2,1)S(1)}, bf16[8,4,32,256]{3,2,1,0:T(8,128)(2,1)S(1)}, s32[2]{0:T(128)S(1)}) custom-call(s32[2]{0:T(128)S(1)} %get-tuple-element.119.pos, f32[6,136,256]{2,1,0:T(8,128)S(1)} %select_maximum_fusion.rate, ...), custom_call_target="tpu_custom_call" | custom-call | flops 1 | bytes 1 | tf_op jit(solution)/shard_map/sweep/pallas_call | solution.py:183
  196.0 10.6 %points.7 = (bf16[8,4,32,256]{3,2,1,0:T(8,128)(2,1)S(1)}, bf16[8,4,32,256]{3,2,1,0:T(8,128)(2,1)S(1)}, bf16[8,4,32,256]{3,2,1,0:T(8,128)(2,1)S(1)}, bf16[8,4,32,256]{3,2,1,0:T(8,128)(2,1)S(1)}, s32[2]{0:T(128)S(1)}) custom-call(s32[2]{0:T(128)S(1)} %get-tuple-element.122.pos, bf16[352,128]{1,0:T(8,128)(2,1)S(1)} %copy.19.basis, ...), custom_call_target="tpu_custom_call" | custom-call | flops 1 | bytes 1 | tf_op jit(solution)/shard_map/points/pallas_call | solution.py:229
  206.6 5.0 %sweep.9 = (bf16[4,4,32,256]{3,2,1,0:T(8,128)(2,1)S(1)}, bf16[4,4,32,256]{3,2,1,0:T(8,128)(2,1)S(1)}, bf16[4,4,32,256]{3,2,1,0:T(8,128)(2,1)S(1)}, bf16[4,4,32,256]{3,2,1,0:T(8,128)(2,1)S(1)}, s32[2]{0:T(128)S(1)}) custom-call(s32[2]{0:T(128)S(1)} %get-tuple-element.127.pos, f32[6,136,256]{2,1,0:T(8,128)S(1)} %select_maximum_fusion.rate, ...), custom_call_target="tpu_custom_call" | custom-call | flops 1 | bytes 1 | tf_op jit(solution)/shard_map/sweep/pallas_call | solution.py:183
  213.0 2.1 collective-permute-start.38
  217.7 12.1 %collective-permute-done.36.refs_2_ = bf16[8,4,32,256]{3,2,1,0:T(8,128)(2,1)S(1)} collective-permute-done((bf16[8,4,32,256]{3,2,1,0:T(8,128)(2,1)S(1)}, bf16[8,4,32,256]{3,2,1,0:T(8,128)(2,1)S(1)}, u32[]{:S(2)}, u32[]{:S(2)}) %collective-permute-start.36) | collective-permute-done | bytes 524320 | tf_op jit(solution)/shard_map/ppermute | solution.py:382
  229.8 10.5 %collective-permute-done.37.refs_3_ = bf16[8,4,32,256]{3,2,1,0:T(8,128)(2,1)S(1)} collective-permute-done((bf16[8,4,32,256]{3,2,1,0:T(8,128)(2,1)S(1)}, bf16[8,4,32,256]{3,2,1,0:T(8,128)(2,1)S(1)}, u32[]{:S(2)}, u32[]{:S(2)}) %collective-permute-start.37) | collective-permute-done | bytes 524320 | tf_op jit(solution)/shard_map/ppermute | solution.py:382
  240.2 10.6 %points.8 = (bf16[8,4,32,256]{3,2,1,0:T(8,128)(2,1)S(1)}, bf16[8,4,32,256]{3,2,1,0:T(8,128)(2,1)S(1)}, bf16[8,4,32,256]{3,2,1,0:T(8,128)(2,1)S(1)}, bf16[8,4,32,256]{3,2,1,0:T(8,128)(2,1)S(1)}, s32[2]{0:T(128)S(1)}) custom-call(s32[2]{0:T(128)S(1)} %get-tuple-element.135.pos, bf16[352,128]{1,0:T(8,128)(2,1)S(1)} %copy.19.basis, ...), custom_call_target="tpu_custom_call" | custom-call | flops 1 | bytes 1 | tf_op jit(solution)/shard_map/points/pallas_call | solution.py:229
  250.9 3.2 settle.6
  254.1 8.6 %collective-permute-done.41.refs_3_.refs_4_ = bf16[8,4,32,256]{3,2,1,0:T(8,128)(2,1)S(1)} collective-permute-done((bf16[8,4,32,256]{3,2,1,0:T(8,128)(2,1)S(1)}, bf16[8,4,32,256]{3,2,1,0:T(8,128)(2,1)S(1)}, u32[]{:S(2)}, u32[]{:S(2)}) %collective-permute-start.41) | collective-permute-done | bytes 524320 | tf_op jit(solution)/shard_map/ppermute | solution.py:382
  267.0 6.5 %collective-permute-done.43.refs_2_ = bf16[4,4,32,256]{3,2,1,0:T(8,128)(2,1)S(1)} collective-permute-done((bf16[4,4,32,256]{3,2,1,0:T(8,128)(2,1)S(1)}, bf16[4,4,32,256]{3,2,1,0:T(8,128)(2,1)S(1)}, u32[]{:S(2)}, u32[]{:S(2)}) %collective-permute-start.43) | collective-permute-done | bytes 262176 | tf_op jit(solution)/shard_map/ppermute | solution.py:382
  273.5 26.8 %collective-permute-done.44.refs_3_ = bf16[4,4,32,256]{3,2,1,0:T(8,128)(2,1)S(1)} collective-permute-done((bf16[4,4,32,256]{3,2,1,0:T(8,128)(2,1)S(1)}, bf16[4,4,32,256]{3,2,1,0:T(8,128)(2,1)S(1)}, u32[]{:S(2)}, u32[]{:S(2)}) %collective-permute-start.44) | collective-permute-done | bytes 262176 | tf_op jit(solution)/shard_map/ppermute | solution.py:382
  300.3 5.9 %points.9 = (bf16[4,4,32,256]{3,2,1,0:T(8,128)(2,1)S(1)}, bf16[4,4,32,256]{3,2,1,0:T(8,128)(2,1)S(1)}, bf16[4,4,32,256]{3,2,1,0:T(8,128)(2,1)S(1)}, bf16[4,4,32,256]{3,2,1,0:T(8,128)(2,1)S(1)}, s32[2]{0:T(128)S(1)}) custom-call(s32[2]{0:T(128)S(1)} %get-tuple-element.148.pos, bf16[352,128]{1,0:T(8,128)(2,1)S(1)} %copy.19.basis, ...), custom_call_target="tpu_custom_call" | custom-call | flops 1 | bytes 1 | tf_op jit(solution)/shard_map/points/pallas_call | solution.py:229
  306.2 3.2 settle.7
  310.7 2.3 collective-permute-start.49
  314.8 21.7 %collective-permute-done.49.refs_5_ = bf16[32,2,32,256]{3,2,1,0:T(8,128)(2,1)S(1)} collective-permute-done((bf16[32,2,32,256]{3,2,1,0:T(8,128)(2,1)S(1)}, bf16[32,2,32,256]{3,2,1,0:T(8,128)(2,1)S(1)}, u32[]{:S(2)}, u32[]{:S(2)}) %collective-permute-start.49) | collective-permute-done | bytes 1048608 | tf_op jit(solution)/shard_map/ppermute | solution.py:374
  336.5 3.2 settle.8
  342.9 11.8 %collective-permute-done.53.refs_5_ = bf16[16,2,32,256]{3,2,1,0:T(8,128)(2,1)S(1)} collective-permute-done((bf16[16,2,32,256]{3,2,1,0:T(8,128)(2,1)S(1)}, bf16[16,2,32,256]{3,2,1,0:T(8,128)(2,1)S(1)}, u32[]{:S(2)}, u32[]{:S(2)}) %collective-permute-start.53) | collective-permute-done | bytes 524320 | tf_op jit(solution)/shard_map/ppermute | solution.py:374
  354.7 2.7 settle.9
  (160 shorter events, 51.9 us)
Async XLA Ops:
  6.3 46.0 %collective-permute-start = (bf16[18,2,32,256]{3,2,1,0:T(8,128)(2,1)S(1)}, bf16[18,2,32,256]{3,2,1,0:T(8,128)(2,1)S(1)}, u32[]{:S(2)}, u32[]{:S(2)}) collective-permute-start(bf16[18,2,32,256]{3,2,1,0:T(8,128)(2,1)S(1)} %get-tuple-element.91.refs_2_.refs_6_), channel_id=1, source_target_pairs={{4,12},{8,0},{12,20},{16,8},{20,28},{24,16},{5,13},{9,1},{13,21},{... | collective-permute-start | bytes 1769480 | tf_op jit(solution)/shard_map/ppermute | solution.py:377
  7.6 19.5 %collective-permute-start.5 = (bf16[18,2,32,256]{3,2,1,0:T(8,128)(2,1)S(1)}, bf16[18,2,32,256]{3,2,1,0:T(8,128)(2,1)}, u32[]{:S(2)}, u32[]{:S(2)}) collective-permute-start(bf16[18,2,32,256]{3,2,1,0:T(8,128)(2,1)S(1)} %get-tuple-element.93), channel_id=1, source_target_pairs={{0,4},{4,0},{8,12},{12,8},{16,20},{20,16},{24,28},{28,24},{1,5},{5... | collective-permute-start | bytes 1769480 | tf_op jit(solution)/shard_map/ppermute | solution.py:374
  22.1 51.6 %collective-permute-start.11 = (bf16[32,2,32,256]{3,2,1,0:T(8,128)(2,1)S(1)}, bf16[32,2,32,256]{3,2,1,0:T(8,128)(2,1)}, u32[]{:S(2)}, u32[]{:S(2)}) collective-permute-start(bf16[32,2,32,256]{3,2,1,0:T(8,128)(2,1)S(1)} %get-tuple-element.103), channel_id=1, source_target_pairs={{0,4},{4,0},{8,12},{12,8},{16,20},{20,16},{24,28},{28,24},{1,5},{5... | collective-permute-start | bytes 3145736 | tf_op jit(solution)/shard_map/ppermute | solution.py:374
  27.1 39.9 %collective-permute-start.6 = (bf16[18,2,32,256]{3,2,1,0:T(8,128)(2,1)}, bf16[18,2,32,256]{3,2,1,0:T(8,128)(2,1)S(1)}, u32[]{:S(2)}, u32[]{:S(2)}) collective-permute-start(bf16[18,2,32,256]{3,2,1,0:T(8,128)(2,1)} %collective-permute-done.5.refs_1_.refs_5_), channel_id=1, source_target_pairs={{12,4},{0,8},{20,12},{8,16},{28,20},{16,24},{13,5},{1,9},{21,13},{... | collective-permute-start | bytes 1769480 | tf_op jit(solution)/shard_map/ppermute | solution.py:377
  30.6 21.7 %collective-permute-start.1 = (bf16[2,128,256]{2,1,0:T(8,128)(2,1)S(1)}, bf16[2,128,256]{2,1,0:T(8,128)(2,1)S(1)}, u32[]{:S(2)}, u32[]{:S(2)}) collective-permute-start(bf16[2,128,256]{2,1,0:T(8,128)(2,1)S(1)} %select_convert_fusion.refs_1_), channel_id=1, source_target_pairs={{0,4},{4,0},{8,12},{12,8},{16,20},{20,16},{24,28},{28,24},{1,5},{5... | collective-permute-start | bytes 393224 | tf_op jit(solution)/shard_map/ppermute | solution.py:374
  30.7 27.8 %collective-permute-start.3 = (f32[2,130,256]{2,1,0:T(8,128)S(1)}, f32[2,130,256]{2,1,0:T(8,128)S(1)}, u32[]{:S(2)}, u32[]{:S(2)}) collective-permute-start(f32[2,130,256]{2,1,0:T(8,128)S(1)} %get-tuple-element.176.refs_0_), channel_id=1, source_target_pairs={{0,4},{4,0},{8,12},{12,8},{16,20},{20,16},{24,28},{28,24},{1,5},{5... | collective-permute-start | bytes 798728 | tf_op jit(solution)/shard_map/ppermute | solution.py:374
  55.0 41.4 %collective-permute-start.17 = (bf16[32,2,32,256]{3,2,1,0:T(8,128)(2,1)}, bf16[32,2,32,256]{3,2,1,0:T(8,128)(2,1)}, u32[]{:S(2)}, u32[]{:S(2)}) collective-permute-start(bf16[32,2,32,256]{3,2,1,0:T(8,128)(2,1)} %get-tuple-element.111), channel_id=1, source_target_pairs={{0,4},{4,0},{8,12},{12,8},{16,20},{20,16},{24,28},{28,24},{1,5},{5... | collective-permute-start | bytes 3145736 | tf_op jit(solution)/shard_map/ppermute | solution.py:374
  64.1 48.9 %collective-permute-start.10 = (bf16[32,2,32,256]{3,2,1,0:T(8,128)(2,1)}, bf16[32,2,32,256]{3,2,1,0:T(8,128)(2,1)}, u32[]{:S(2)}, u32[]{:S(2)}) collective-permute-start(bf16[32,2,32,256]{3,2,1,0:T(8,128)(2,1)} %get-tuple-element.102.refs_2_.refs_6_), channel_id=1, source_target_pairs={{4,12},{8,0},{12,20},{16,8},{20,28},{24,16},{5,13},{9,1},{13,21},{... | collective-permute-start | bytes 3145736 | tf_op jit(solution)/shard_map/ppermute | solution.py:377
  65.6 47.5 %collective-permute-start.16 = (bf16[32,2,32,256]{3,2,1,0:T(8,128)(2,1)S(1)}, bf16[32,2,32,256]{3,2,1,0:T(8,128)(2,1)}, u32[]{:S(2)}, u32[]{:S(2)}) collective-permute-start(bf16[32,2,32,256]{3,2,1,0:T(8,128)(2,1)S(1)} %get-tuple-element.110.refs_2_.refs_6_), channel_id=1, source_target_pairs={{4,12},{8,0},{12,20},{16,8},{20,28},{24,16},{5,13},{9,1},{13,21},{... | collective-permute-start | bytes 3145736 | tf_op jit(solution)/shard_map/ppermute | solution.py:377
  74.5 8.3 %collective-permute-start.8 = (bf16[4,4,32,256]{3,2,1,0:T(8,128)(2,1)}, bf16[4,4,32,256]{3,2,1,0:T(8,128)(2,1)}, u32[]{:S(2)}, u32[]{:S(2)}) collective-permute-start(bf16[4,4,32,256]{3,2,1,0:T(8,128)(2,1)} %get-tuple-element.99), channel_id=1, source_target_pairs={{0,2},{1,3},{2,0},{3,1},{4,6},{5,7},{6,4},{7,5},{8,10},{9,11},{10,... | collective-permute-start | bytes 786440 | tf_op jit(solution)/shard_map/ppermute | solution.py:382
  80.3 14.6 %collective-permute-start.9 = (bf16[4,4,32,256]{3,2,1,0:T(8,128)(2,1)}, bf16[4,4,32,256]{3,2,1,0:T(8,128)(2,1)}, u32[]{:S(2)}, u32[]{:S(2)}) collective-permute-start(bf16[4,4,32,256]{3,2,1,0:T(8,128)(2,1)} %copy-done.18), channel_id=1, source_target_pairs={{0,3},{1,2},{2,1},{3,0},{4,7},{5,6},{6,5},{7,4},{8,11},{9,10},{10,... | collective-permute-start | bytes 786440 | tf_op jit(solution)/shard_map/ppermute | solution.py:382
  82.8 39.0 %collective-permute-start.12 = (bf16[32,2,32,256]{3,2,1,0:T(8,128)(2,1)}, bf16[32,2,32,256]{3,2,1,0:T(8,128)(2,1)S(1)}, u32[]{:S(2)}, u32[]{:S(2)}) collective-permute-start(bf16[32,2,32,256]{3,2,1,0:T(8,128)(2,1)} %collective-permute-done.11.refs_1_.refs_5_), channel_id=1, source_target_pairs={{12,4},{0,8},{20,12},{8,16},{28,20},{16,24},{13,5},{1,9},{21,13},{... | collective-permute-start | bytes 3145736 | tf_op jit(solution)/shard_map/ppermute | solution.py:377
  94.9 42.0 %collective-permute-start.24 = (bf16[32,2,32,256]{3,2,1,0:T(8,128)(2,1)S(1)}, bf16[32,2,32,256]{3,2,1,0:T(8,128)(2,1)S(1)}, u32[]{:S(2)}, u32[]{:S(2)}) collective-permute-start(bf16[32,2,32,256]{3,2,1,0:T(8,128)(2,1)S(1)} %get-tuple-element.121), channel_id=1, source_target_pairs={{0,4},{4,0},{8,12},{12,8},{16,20},{20,16},{24,28},{28,24},{1,5},{5... | collective-permute-start | bytes 3145736 | tf_op jit(solution)/shard_map/ppermute | solution.py:374
  96.4 40.5 %collective-permute-start.18 = (bf16[32,2,32,256]{3,2,1,0:T(8,128)(2,1)}, bf16[32,2,32,256]{3,2,1,0:T(8,128)(2,1)S(1)}, u32[]{:S(2)}, u32[]{:S(2)}) collective-permute-start(bf16[32,2,32,256]{3,2,1,0:T(8,128)(2,1)} %collective-permute-done.17.refs_1_.refs_5_), channel_id=1, source_target_pairs={{12,4},{0,8},{20,12},{8,16},{28,20},{16,24},{13,5},{1,9},{21,13},{... | collective-permute-start | bytes 3145736 | tf_op jit(solution)/shard_map/ppermute | solution.py:377
  113.1 8.7 %collective-permute-start.14 = (bf16[4,4,32,256]{3,2,1,0:T(8,128)(2,1)S(1)}, bf16[4,4,32,256]{3,2,1,0:T(8,128)(2,1)S(1)}, u32[]{:S(2)}, u32[]{:S(2)}) collective-permute-start(bf16[4,4,32,256]{3,2,1,0:T(8,128)(2,1)S(1)} %get-tuple-element.107), channel_id=1, source_target_pairs={{0,2},{1,3},{2,0},{3,1},{4,6},{5,7},{6,4},{7,5},{8,10},{9,11},{10,... | collective-permute-start | bytes 786440 | tf_op jit(solution)/shard_map/ppermute | solution.py:382
  114.8 36.8 %collective-permute-start.23 = (bf16[32,2,32,256]{3,2,1,0:T(8,128)(2,1)S(1)}, bf16[32,2,32,256]{3,2,1,0:T(8,128)(2,1)S(1)}, u32[]{:S(2)}, u32[]{:S(2)}) collective-permute-start(bf16[32,2,32,256]{3,2,1,0:T(8,128)(2,1)S(1)} %get-tuple-element.120.refs_2_.refs_6_), channel_id=1, source_target_pairs={{4,12},{8,0},{12,20},{16,8},{20,28},{24,16},{5,13},{9,1},{13,21},{... | collective-permute-start | bytes 3145736 | tf_op jit(solution)/shard_map/ppermute | solution.py:377
  121.8 13.5 %collective-permute-start.30 = (bf16[16,2,32,256]{3,2,1,0:T(8,128)(2,1)S(1)}, bf16[16,2,32,256]{3,2,1,0:T(8,128)(2,1)S(1)}, u32[]{:S(2)}, u32[]{:S(2)}) collective-permute-start(bf16[16,2,32,256]{3,2,1,0:T(8,128)(2,1)S(1)} %get-tuple-element.129), channel_id=1, source_target_pairs={{0,4},{4,0},{8,12},{12,8},{16,20},{20,16},{24,28},{28,24},{1,5},{5... | collective-permute-start | bytes 1572872 | tf_op jit(solution)/shard_map/ppermute | solution.py:374
  121.9 11.7 %collective-permute-start.15 = (bf16[4,4,32,256]{3,2,1,0:T(8,128)(2,1)S(1)}, bf16[4,4,32,256]{3,2,1,0:T(8,128)(2,1)S(1)}, u32[]{:S(2)}, u32[]{:S(2)}) collective-permute-start(bf16[4,4,32,256]{3,2,1,0:T(8,128)(2,1)S(1)} %get-tuple-element.108), channel_id=1, source_target_pairs={{0,3},{1,2},{2,1},{3,0},{4,7},{5,6},{6,5},{7,4},{8,11},{9,10},{10,... | collective-permute-start | bytes 786440 | tf_op jit(solution)/shard_map/ppermute | solution.py:382
  133.6 18.1 %collective-permute-start.19 = (bf16[8,4,32,256]{3,2,1,0:T(8,128)(2,1)S(1)}, bf16[8,4,32,256]{3,2,1,0:T(8,128)(2,1)S(1)}, u32[]{:S(2)}, u32[]{:S(2)}) collective-permute-start(bf16[8,4,32,256]{3,2,1,0:T(8,128)(2,1)S(1)} %get-tuple-element.114), channel_id=1, source_target_pairs={{0,1},{1,0},{2,3},{3,2},{4,5},{5,4},{6,7},{7,6},{8,9},{9,8},{10,11... | collective-permute-start | bytes 1572872 | tf_op jit(solution)/shard_map/ppermute | solution.py:382
  135.3 16.7 %collective-permute-start.20 = (bf16[8,4,32,256]{3,2,1,0:T(8,128)(2,1)S(1)}, bf16[8,4,32,256]{3,2,1,0:T(8,128)(2,1)S(1)}, u32[]{:S(2)}, u32[]{:S(2)}) collective-permute-start(bf16[8,4,32,256]{3,2,1,0:T(8,128)(2,1)S(1)} %get-tuple-element.115), channel_id=1, source_target_pairs={{0,2},{1,3},{2,0},{3,1},{4,6},{5,7},{6,4},{7,5},{8,10},{9,11},{10,... | collective-permute-start | bytes 1572872 | tf_op jit(solution)/shard_map/ppermute | solution.py:382
  136.9 23.6 %collective-permute-start.21 = (bf16[8,4,32,256]{3,2,1,0:T(8,128)(2,1)S(1)}, bf16[8,4,32,256]{3,2,1,0:T(8,128)(2,1)S(1)}, u32[]{:S(2)}, u32[]{:S(2)}) collective-permute-start(bf16[8,4,32,256]{3,2,1,0:T(8,128)(2,1)S(1)} %get-tuple-element.116), channel_id=1, source_target_pairs={{0,3},{1,2},{2,1},{3,0},{4,7},{5,6},{6,5},{7,4},{8,11},{9,10},{10,... | collective-permute-start | bytes 1572872 | tf_op jit(solution)/shard_map/ppermute | solution.py:382
  136.9 44.7 %collective-permute-start.25 = (bf16[32,2,32,256]{3,2,1,0:T(8,128)(2,1)S(1)}, bf16[32,2,32,256]{3,2,1,0:T(8,128)(2,1)S(1)}, u32[]{:S(2)}, u32[]{:S(2)}) collective-permute-start(bf16[32,2,32,256]{3,2,1,0:T(8,128)(2,1)S(1)} %collective-permute-done.24.refs_1_.refs_5_), channel_id=1, source_target_pairs={{12,4},{0,8},{20,12},{8,16},{28,20},{16,24},{13,5},{1,9},{21,13},{... | collective-permute-start | bytes 3145736 | tf_op jit(solution)/shard_map/ppermute | solution.py:377
  151.6 21.7 %collective-permute-start.22 = (bf16[16,2,32,256]{3,2,1,0:T(8,128)(2,1)S(1)}, bf16[16,2,32,256]{3,2,1,0:T(8,128)(2,1)S(1)}, u32[]{:S(2)}, u32[]{:S(2)}) collective-permute-start(bf16[16,2,32,256]{3,2,1,0:T(8,128)(2,1)S(1)} %get-tuple-element.118), channel_id=1, source_target_pairs={{0,4},{4,0},{8,12},{12,8},{16,20},{20,16},{24,28},{28,24},{1,5},{5... | collective-permute-start | bytes 1572872 | tf_op jit(solution)/shard_map/ppermute | solution.py:374
  151.7 23.0 %collective-permute-start.26 = (bf16[8,4,32,256]{3,2,1,0:T(8,128)(2,1)S(1)}, bf16[8,4,32,256]{3,2,1,0:T(8,128)(2,1)S(1)}, u32[]{:S(2)}, u32[]{:S(2)}) collective-permute-start(bf16[8,4,32,256]{3,2,1,0:T(8,128)(2,1)S(1)} %get-tuple-element.124), channel_id=1, source_target_pairs={{0,1},{1,0},{2,3},{3,2},{4,5},{5,4},{6,7},{7,6},{8,9},{9,8},{10,11... | collective-permute-start | bytes 1572872 | tf_op jit(solution)/shard_map/ppermute | solution.py:382
  152.0 27.3 %collective-permute-start.27 = (bf16[8,4,32,256]{3,2,1,0:T(8,128)(2,1)S(1)}, bf16[8,4,32,256]{3,2,1,0:T(8,128)(2,1)S(1)}, u32[]{:S(2)}, u32[]{:S(2)}) collective-permute-start(bf16[8,4,32,256]{3,2,1,0:T(8,128)(2,1)S(1)} %get-tuple-element.125), channel_id=1, source_target_pairs={{0,2},{1,3},{2,0},{3,1},{4,6},{5,7},{6,4},{7,5},{8,10},{9,11},{10,... | collective-permute-start | bytes 1572872 | tf_op jit(solution)/shard_map/ppermute | solution.py:382
  160.5 20.2 %collective-permute-start.28 = (bf16[8,4,32,256]{3,2,1,0:T(8,128)(2,1)S(1)}, bf16[8,4,32,256]{3,2,1,0:T(8,128)(2,1)S(1)}, u32[]{:S(2)}, u32[]{:S(2)}) collective-permute-start(bf16[8,4,32,256]{3,2,1,0:T(8,128)(2,1)S(1)} %get-tuple-element.126), channel_id=1, source_target_pairs={{0,3},{1,2},{2,1},{3,0},{4,7},{5,6},{6,5},{7,4},{8,11},{9,10},{10,... | collective-permute-start | bytes 1572872 | tf_op jit(solution)/shard_map/ppermute | solution.py:382
  173.4 33.2 %collective-permute-start.29 = (bf16[16,2,32,256]{3,2,1,0:T(8,128)(2,1)S(1)}, bf16[16,2,32,256]{3,2,1,0:T(8,128)(2,1)S(1)}, u32[]{:S(2)}, u32[]{:S(2)}) collective-permute-start(bf16[16,2,32,256]{3,2,1,0:T(8,128)(2,1)S(1)} %get-tuple-element.128.refs_2_), channel_id=1, source_target_pairs={{4,12},{8,0},{12,20},{16,8},{20,28},{24,16},{5,13},{9,1},{13,21},{... | collective-permute-start | bytes 1572872 | tf_op jit(solution)/shard_map/ppermute | solution.py:377
  174.7 31.9 %collective-permute-start.31 = (bf16[16,2,32,256]{3,2,1,0:T(8,128)(2,1)S(1)}, bf16[16,2,32,256]{3,2,1,0:T(8,128)(2,1)S(1)}, u32[]{:S(2)}, u32[]{:S(2)}) collective-permute-start(bf16[16,2,32,256]{3,2,1,0:T(8,128)(2,1)S(1)} %collective-permute-done.30.refs_1_), channel_id=1, source_target_pairs={{12,4},{0,8},{20,12},{8,16},{28,20},{16,24},{13,5},{1,9},{21,13},{... | collective-permute-start | bytes 1572872 | tf_op jit(solution)/shard_map/ppermute | solution.py:377
  179.3 32.4 %collective-permute-start.32 = (bf16[8,4,32,256]{3,2,1,0:T(8,128)(2,1)S(1)}, bf16[8,4,32,256]{3,2,1,0:T(8,128)(2,1)S(1)}, u32[]{:S(2)}, u32[]{:S(2)}) collective-permute-start(bf16[8,4,32,256]{3,2,1,0:T(8,128)(2,1)S(1)} %get-tuple-element.132), channel_id=1, source_target_pairs={{0,1},{1,0},{2,3},{3,2},{4,5},{5,4},{6,7},{7,6},{8,9},{9,8},{10,11... | collective-permute-start | bytes 1572872 | tf_op jit(solution)/shard_map/ppermute | solution.py:382
  180.7 31.0 %collective-permute-start.33 = (bf16[8,4,32,256]{3,2,1,0:T(8,128)(2,1)S(1)}, bf16[8,4,32,256]{3,2,1,0:T(8,128)(2,1)S(1)}, u32[]{:S(2)}, u32[]{:S(2)}) collective-permute-start(bf16[8,4,32,256]{3,2,1,0:T(8,128)(2,1)S(1)} %get-tuple-element.133), channel_id=1, source_target_pairs={{0,2},{1,3},{2,0},{3,1},{4,6},{5,7},{6,4},{7,5},{8,10},{9,11},{10,... | collective-permute-start | bytes 1572872 | tf_op jit(solution)/shard_map/ppermute | solution.py:382
  181.6 30.0 %collective-permute-start.34 = (bf16[8,4,32,256]{3,2,1,0:T(8,128)(2,1)S(1)}, bf16[8,4,32,256]{3,2,1,0:T(8,128)(2,1)S(1)}, u32[]{:S(2)}, u32[]{:S(2)}) collective-permute-start(bf16[8,4,32,256]{3,2,1,0:T(8,128)(2,1)S(1)} %get-tuple-element.134), channel_id=1, source_target_pairs={{0,3},{1,2},{2,1},{3,0},{4,7},{5,6},{6,5},{7,4},{8,11},{9,10},{10,... | collective-permute-start | bytes 1572872 | tf_op jit(solution)/shard_map/ppermute | solution.py:382
  213.0 37.9 %collective-permute-start.38 = (bf16[32,2,32,256]{3,2,1,0:T(8,128)(2,1)S(1)}, bf16[32,2,32,256]{3,2,1,0:T(8,128)(2,1)S(1)}, u32[]{:S(2)}, u32[]{:S(2)}) collective-permute-start(bf16[32,2,32,256]{3,2,1,0:T(8,128)(2,1)S(1)} %get-tuple-element.142), channel_id=1, source_target_pairs={{0,4},{4,0},{8,12},{12,8},{16,20},{20,16},{24,28},{28,24},{1,5},{5... | collective-permute-start | bytes 3145736 | tf_op jit(solution)/shard_map/ppermute | solution.py:374
  215.1 14.7 %collective-permute-start.36 = (bf16[8,4,32,256]{3,2,1,0:T(8,128)(2,1)S(1)}, bf16[8,4,32,256]{3,2,1,0:T(8,128)(2,1)S(1)}, u32[]{:S(2)}, u32[]{:S(2)}) collective-permute-start(bf16[8,4,32,256]{3,2,1,0:T(8,128)(2,1)S(1)} %get-tuple-element.138), channel_id=1, source_target_pairs={{0,2},{1,3},{2,0},{3,1},{4,6},{5,7},{6,4},{7,5},{8,10},{9,11},{10,... | collective-permute-start | bytes 1572872 | tf_op jit(solution)/shard_map/ppermute | solution.py:382
  215.5 24.7 %collective-permute-start.37 = (bf16[8,4,32,256]{3,2,1,0:T(8,128)(2,1)S(1)}, bf16[8,4,32,256]{3,2,1,0:T(8,128)(2,1)S(1)}, u32[]{:S(2)}, u32[]{:S(2)}) collective-permute-start(bf16[8,4,32,256]{3,2,1,0:T(8,128)(2,1)S(1)} %get-tuple-element.139), channel_id=1, source_target_pairs={{0,3},{1,2},{2,1},{3,0},{4,7},{5,6},{6,5},{7,4},{8,11},{9,10},{10,... | collective-permute-start | bytes 1572872 | tf_op jit(solution)/shard_map/ppermute | solution.py:382
  216.9 37.2 %collective-permute-start.39 = (bf16[8,4,32,256]{3,2,1,0:T(8,128)(2,1)S(1)}, bf16[8,4,32,256]{3,2,1,0:T(8,128)(2,1)S(1)}, u32[]{:S(2)}, u32[]{:S(2)}) collective-permute-start(bf16[8,4,32,256]{3,2,1,0:T(8,128)(2,1)S(1)} %get-tuple-element.145), channel_id=1, source_target_pairs={{0,1},{1,0},{2,3},{3,2},{4,5},{5,4},{6,7},{7,6},{8,9},{9,8},{10,11... | collective-permute-start | bytes 1572872 | tf_op jit(solution)/shard_map/ppermute | solution.py:382
  217.2 36.9 %collective-permute-start.40 = (bf16[8,4,32,256]{3,2,1,0:T(8,128)(2,1)S(1)}, bf16[8,4,32,256]{3,2,1,0:T(8,128)(2,1)S(1)}, u32[]{:S(2)}, u32[]{:S(2)}) collective-permute-start(bf16[8,4,32,256]{3,2,1,0:T(8,128)(2,1)S(1)} %get-tuple-element.146), channel_id=1, source_target_pairs={{0,2},{1,3},{2,0},{3,1},{4,6},{5,7},{6,4},{7,5},{8,10},{9,11},{10,... | collective-permute-start | bytes 1572872 | tf_op jit(solution)/shard_map/ppermute | solution.py:382
  229.8 32.9 %collective-permute-start.41 = (bf16[8,4,32,256]{3,2,1,0:T(8,128)(2,1)S(1)}, bf16[8,4,32,256]{3,2,1,0:T(8,128)(2,1)S(1)}, u32[]{:S(2)}, u32[]{:S(2)}) collective-permute-start(bf16[8,4,32,256]{3,2,1,0:T(8,128)(2,1)S(1)} %get-tuple-element.147), channel_id=1, source_target_pairs={{0,3},{1,2},{2,1},{3,0},{4,7},{5,6},{6,5},{7,4},{8,11},{9,10},{10,... | collective-permute-start | bytes 1572872 | tf_op jit(solution)/shard_map/ppermute | solution.py:382
  264.0 42.2 %collective-permute-start.45 = (bf16[32,2,32,256]{3,2,1,0:T(8,128)(2,1)S(1)}, bf16[32,2,32,256]{3,2,1,0:T(8,128)(2,1)S(1)}, u32[]{:S(2)}, u32[]{:S(2)}) collective-permute-start(bf16[32,2,32,256]{3,2,1,0:T(8,128)(2,1)S(1)} %get-tuple-element.155), channel_id=1, source_target_pairs={{0,4},{4,0},{8,12},{12,8},{16,20},{20,16},{24,28},{28,24},{1,5},{5... | collective-permute-start | bytes 3145736 | tf_op jit(solution)/shard_map/ppermute | solution.py:374
  264.3 9.1 %collective-permute-start.43 = (bf16[4,4,32,256]{3,2,1,0:T(8,128)(2,1)S(1)}, bf16[4,4,32,256]{3,2,1,0:T(8,128)(2,1)S(1)}, u32[]{:S(2)}, u32[]{:S(2)}) collective-permute-start(bf16[4,4,32,256]{3,2,1,0:T(8,128)(2,1)S(1)} %get-tuple-element.151), channel_id=1, source_target_pairs={{0,2},{1,3},{2,0},{3,1},{4,6},{5,7},{6,4},{7,5},{8,10},{9,11},{10,... | collective-permute-start | bytes 786440 | tf_op jit(solution)/shard_map/ppermute | solution.py:382
  265.1 44.3 %collective-permute-start.46 = (bf16[8,4,32,256]{3,2,1,0:T(8,128)(2,1)S(1)}, bf16[8,4,32,256]{3,2,1,0:T(8,128)(2,1)S(1)}, u32[]{:S(2)}, u32[]{:S(2)}) collective-permute-start(bf16[8,4,32,256]{3,2,1,0:T(8,128)(2,1)S(1)} %get-tuple-element.158), channel_id=1, source_target_pairs={{0,1},{1,0},{2,3},{3,2},{4,5},{5,4},{6,7},{7,6},{8,9},{9,8},{10,11... | collective-permute-start | bytes 1572872 | tf_op jit(solution)/shard_map/ppermute | solution.py:382
  265.3 44.1 %collective-permute-start.47 = (bf16[8,4,32,256]{3,2,1,0:T(8,128)(2,1)S(1)}, bf16[8,4,32,256]{3,2,1,0:T(8,128)(2,1)S(1)}, u32[]{:S(2)}, u32[]{:S(2)}) collective-permute-start(bf16[8,4,32,256]{3,2,1,0:T(8,128)(2,1)S(1)} %get-tuple-element.159), channel_id=1, source_target_pairs={{0,2},{1,3},{2,0},{3,1},{4,6},{5,7},{6,4},{7,5},{8,10},{9,11},{10,... | collective-permute-start | bytes 1572872 | tf_op jit(solution)/shard_map/ppermute | solution.py:382
  266.4 43.0 %collective-permute-start.48 = (bf16[8,4,32,256]{3,2,1,0:T(8,128)(2,1)S(1)}, bf16[8,4,32,256]{3,2,1,0:T(8,128)(2,1)S(1)}, u32[]{:S(2)}, u32[]{:S(2)}) collective-permute-start(bf16[8,4,32,256]{3,2,1,0:T(8,128)(2,1)S(1)} %get-tuple-element.160), channel_id=1, source_target_pairs={{0,3},{1,2},{2,1},{3,0},{4,7},{5,6},{6,5},{7,4},{8,11},{9,10},{10,... | collective-permute-start | bytes 1572872 | tf_op jit(solution)/shard_map/ppermute | solution.py:382
  273.5 26.8 %collective-permute-start.44 = (bf16[4,4,32,256]{3,2,1,0:T(8,128)(2,1)S(1)}, bf16[4,4,32,256]{3,2,1,0:T(8,128)(2,1)S(1)}, u32[]{:S(2)}, u32[]{:S(2)}) collective-permute-start(bf16[4,4,32,256]{3,2,1,0:T(8,128)(2,1)S(1)} %get-tuple-element.152), channel_id=1, source_target_pairs={{0,3},{1,2},{2,1},{3,0},{4,7},{5,6},{6,5},{7,4},{8,11},{9,10},{10,... | collective-permute-start | bytes 786440 | tf_op jit(solution)/shard_map/ppermute | solution.py:382
  310.7 25.8 %collective-permute-start.49 = (bf16[32,2,32,256]{3,2,1,0:T(8,128)(2,1)S(1)}, bf16[32,2,32,256]{3,2,1,0:T(8,128)(2,1)S(1)}, u32[]{:S(2)}, u32[]{:S(2)}) collective-permute-start(bf16[32,2,32,256]{3,2,1,0:T(8,128)(2,1)S(1)} %get-tuple-element.163), channel_id=1, source_target_pairs={{0,4},{4,0},{8,12},{12,8},{16,20},{20,16},{24,28},{28,24},{1,5},{5... | collective-permute-start | bytes 3145736 | tf_op jit(solution)/shard_map/ppermute | solution.py:374
  312.9 26.7 %collective-permute-start.50 = (bf16[4,4,32,256]{3,2,1,0:T(8,128)(2,1)S(1)}, bf16[4,4,32,256]{3,2,1,0:T(8,128)(2,1)S(1)}, u32[]{:S(2)}, u32[]{:S(2)}) collective-permute-start(bf16[4,4,32,256]{3,2,1,0:T(8,128)(2,1)S(1)} %get-tuple-element.166), channel_id=1, source_target_pairs={{0,1},{1,0},{2,3},{3,2},{4,5},{5,4},{6,7},{7,6},{8,9},{9,8},{10,11... | collective-permute-start | bytes 786440 | tf_op jit(solution)/shard_map/ppermute | solution.py:382
  313.0 26.8 %collective-permute-start.51 = (bf16[4,4,32,256]{3,2,1,0:T(8,128)(2,1)S(1)}, bf16[4,4,32,256]{3,2,1,0:T(8,128)(2,1)S(1)}, u32[]{:S(2)}, u32[]{:S(2)}) collective-permute-start(bf16[4,4,32,256]{3,2,1,0:T(8,128)(2,1)S(1)} %get-tuple-element.167), channel_id=1, source_target_pairs={{0,2},{1,3},{2,0},{3,1},{4,6},{5,7},{6,4},{7,5},{8,10},{9,11},{10,... | collective-permute-start | bytes 786440 | tf_op jit(solution)/shard_map/ppermute | solution.py:382
  313.4 26.3 %collective-permute-start.52 = (bf16[4,4,32,256]{3,2,1,0:T(8,128)(2,1)S(1)}, bf16[4,4,32,256]{3,2,1,0:T(8,128)(2,1)S(1)}, u32[]{:S(2)}, u32[]{:S(2)}) collective-permute-start(bf16[4,4,32,256]{3,2,1,0:T(8,128)(2,1)S(1)} %get-tuple-element.168), channel_id=1, source_target_pairs={{0,3},{1,2},{2,1},{3,0},{4,7},{5,6},{6,5},{7,4},{8,11},{9,10},{10,... | collective-permute-start | bytes 786440 | tf_op jit(solution)/shard_map/ppermute | solution.py:382
  341.1 13.6 %collective-permute-start.53 = (bf16[16,2,32,256]{3,2,1,0:T(8,128)(2,1)S(1)}, bf16[16,2,32,256]{3,2,1,0:T(8,128)(2,1)S(1)}, u32[]{:S(2)}, u32[]{:S(2)}) collective-permute-start(bf16[16,2,32,256]{3,2,1,0:T(8,128)(2,1)S(1)} %get-tuple-element.171), channel_id=1, source_target_pairs={{0,4},{4,0},{8,12},{12,8},{16,20},{20,16},{24,28},{28,24},{1,5},{5... | collective-permute-start | bytes 1572872 | tf_op jit(solution)/shard_map/ppermute | solution.py:374
  (31 other events, 480.0 us)

commit v4 on v3

v4 whole, which is shorter than its diff:
```python
import functools

import jax
import jax.numpy as jnp
import numpy as np
from jax import lax
from jax.experimental import pallas as pl
from jax.experimental.pallas import tpu as pltpu
from jax.sharding import PartitionSpec as P

F32, BF16 = jnp.float32, jnp.bfloat16
ANY = pl.BlockSpec(memory_space=pl.ANY)
VMEM = pl.BlockSpec(memory_space=pltpu.VMEM)
HBM = pl.BlockSpec(memory_space=pltpu.HBM)
SMEM = pl.BlockSpec(memory_space=pltpu.SMEM)
TOKEN = jax.ShapeDtypeStruct((2,), jnp.int32)
COST = pl.CostEstimate(flops=1, bytes_accessed=1, transcendentals=0)
EDGE = 2
TILE = 16


def params(mebibytes):
    return pltpu.CompilerParams(vmem_limit_bytes=mebibytes * 1024 * 1024)


def from_rows(y, group):
    if group % 16 == 0:
        return y.astype(BF16).reshape(-1, group, y.shape[1])
    return y.reshape(-1, group, y.shape[1]).astype(BF16)


def to_bf16_rows(x):
    a, m, y = x.shape
    if m % 16 == 0:
        return x.astype(BF16).reshape(a * m, y)
    return x.astype(F32).reshape(a * m, y).astype(BF16)


def spread_kernel(pos, field, turn, *refs, begin, skip):
    own, send, token, window, sems = refs[-5:]
    side = pos[0]
    token[0], token[1] = pos[0], pos[1]
    _, planes, modes, depth, cols = window.shape
    size = field.shape[2]
    rows = own.shape[0]
    group = turn.shape[1] // TILE
    copies = []
    for a in range(2):
        far = 1 - side if a == 0 else side
        start = jnp.where(far == 1, size - depth - begin, begin)
        start = pl.multiple_of(start, TILE)
        copy = pltpu.make_async_copy(
            field.at[:, :, pl.ds(start, depth), :], window.at[a], sems.at[a]
        )
        copy.start()
        copies.append(copy)
    for a, out in ((0, send), (1, own)):
        far = 1 - side if a == 0 else side
        copies[a].wait()
        for z in range(planes):
            to = jnp.where(far == 1, z, planes - 1 - z)
            for g in range(depth // TILE):
                block = jnp.where(far == 1, depth // TILE - 1 - g, g)
                low, high = max(0, skip - g * TILE), min(TILE, rows + skip - g * TILE)
                if high <= low:
                    continue
                for h in range(modes // group):
                    there = pl.ds(h * group, group)
                    x = window[a, z, there, pl.ds(pl.multiple_of(block * TILE, TILE), TILE), :]
                    y = jnp.dot(turn[far], x.reshape(group * TILE, cols), preferred_element_type=F32)
                    y = from_rows(y, group)
                    out[pl.ds(g * TILE + low - skip, high - low), to, there, :] = y[low:high]


def spread(pos, field, turn, after, begin, skip, rows, depth):
    planes, modes, _, cols = field.shape
    piece = jax.ShapeDtypeStruct((rows, planes, modes, cols), BF16)
    return pl.pallas_call(
        functools.partial(spread_kernel, begin=begin, skip=skip),
        out_shape=(piece, piece, TOKEN),
        in_specs=[SMEM, HBM, VMEM] + [ANY] * len(after),
        out_specs=(VMEM, VMEM, SMEM),
        scratch_shapes=[
            pltpu.VMEM((2, planes, modes, depth, cols), BF16),
            pltpu.SemaphoreType.DMA((2,)),
        ],
        compiler_params=params(10),
        cost_estimate=COST,
        name="spread",
    )(pos, field, turn, *after)


def relay_kernel(pos, *refs):
    token = refs[-1]
    token[0], token[1] = pos[0], pos[1]


def relay(pos, passed, after):
    count = len(passed)
    return pl.pallas_call(
        relay_kernel,
        out_shape=tuple(jax.ShapeDtypeStruct(x.shape, x.dtype) for x in passed) + (TOKEN,),
        in_specs=[SMEM] + [ANY] * (count + len(after)),
        out_specs=(ANY,) * count + (SMEM,),
        input_output_aliases={1 + i: i for i in range(count)},
        compiler_params=params(1),
        cost_estimate=COST,
        name="relay",
    )(pos, *passed, *after)


def sweep_kernel(pos, rate, shift, *refs, begin, heads):
    group = 4
    blocks, refs = refs[:group], refs[group:]
    tails, refs = refs[:heads], refs[heads:]
    out, token, first, edge, sems = refs
    token[0], token[1] = pos[0], pos[1]
    planes, modes, cols = blocks[0].shape[1:]
    rows, mine = out.shape[:2]
    lead = 2 * EDGE if heads else EDGE
    copies = []
    for g in range(heads):
        length = tails[g].shape[0]
        copies.append(
            pltpu.make_async_copy(
                tails[g].at[pl.ds(length - lead, lead)], edge.at[:, pl.ds(g * planes, planes)], sems.at[g]
            )
        )
    for copy in copies:
        copy.start()
    for copy in copies:
        copy.wait()
    low = planes - 1
    wide = mine + 2
    piece = min(modes, 16)

    def field(row, p, some):
        if isinstance(row, int) and row < lead:
            if heads:
                return edge[row, p, some]
            return jnp.zeros((some.size, cols), BF16)
        return blocks[p // planes][row - lead, p % planes, some]

    def beside(parts, number):
        return jnp.dot(
            to_bf16_rows(jnp.stack(parts)), shift[...], preferred_element_type=F32
        ).reshape(number, -1, modes, cols)

    def once(i, number):
        every = pl.ds(0, modes)
        aside = beside([field(i + 1 + a, low + p, every) for a in range(number) for p in range(wide)], number)
        for a in range(number):
            speeds = [rate[p, pl.ds(begin + i + a, 1), :] for p in range(wide)]
            for h in range(modes // piece):
                some = pl.ds(h * piece, piece)
                line = [field(i + 1 + a, low - 1 + p, some).astype(F32) for p in range(wide + 2)]
                for p in range(wide):
                    centre = line[p + 1]
                    around = aside[a, p, h * piece : (h + 1) * piece] + (line[p] + line[p + 2])
                    around = around + (
                        field(i + a, low + p, some).astype(F32) + field(i + 2 + a, low + p, some).astype(F32)
                    )
                    first[i + a, p, some] = centre + speeds[p] * (around - 6.0 * centre)

    for i in range(0, lead, 2):
        once(i, 2)

    def pair(j, _):
        once(lead + 2 * j, 2)
        return 0

    lax.fori_loop(0, (rows + 2 - lead) // 2, pair, 0)

    def again(j, _):
        i = 2 * j
        aside = beside([first[i + 1 + a, 1 + p] for a in range(2) for p in range(mine)], 2)
        for a in range(2):
            speeds = [rate[p + 1, pl.ds(begin + i + a + 1, 1), :] for p in range(mine)]
            for h in range(modes // piece):
                some = pl.ds(h * piece, piece)
                line = [first[i + 1 + a, p, some] for p in range(wide)]
                for p in range(mine):
                    centre = line[p + 1]
                    around = aside[a, p, h * piece : (h + 1) * piece] + (line[p] + line[p + 2])
                    around = around + (first[i + a, p + 1, some] + first[i + 2 + a, p + 1, some])
                    out[i + a, p, some] = (centre + speeds[p] * (around - 6.0 * centre)).astype(BF16)
        return 0

    lax.fori_loop(0, rows // 2, again, 0)


def sweep(pos, rate, shift, blocks, tails, begin, rows):
    _, planes, modes, cols = blocks[0].shape
    mine = 2 * planes
    return pl.pallas_call(
        functools.partial(sweep_kernel, begin=begin, heads=len(tails)),
        out_shape=(jax.ShapeDtypeStruct((rows, mine, modes, cols), BF16), TOKEN),
        in_specs=[SMEM] + [VMEM] * 6 + [ANY] * len(tails),
        out_specs=(VMEM, SMEM),
        scratch_shapes=[
            pltpu.VMEM((rows + 2, mine + 2, modes, cols), F32),
            pltpu.VMEM((2 * EDGE, 4 * planes, modes, cols), BF16),
            pltpu.SemaphoreType.DMA((4,)),
        ],
        compiler_params=params(22),
        cost_estimate=COST,
        name="sweep",
    )(pos, rate, shift, *blocks, *tails)


def points_kernel(pos, basis, basis_t, flat, swing, load, field, theirs, mine, token, *, begin):
    token[0], token[1] = pos[0], pos[1]
    rows, planes, modes, cols = field.shape
    count = basis.shape[1] // modes
    part = rows // count
    copies = cols // flat.shape[1]

    def row(i, _):
        place = begin + pos[1] * part + i
        for p in range(planes):
            cells = [field[k * part + i, p] for k in range(count)]
            cells = to_bf16_rows(jnp.stack(cells))
            heat = jnp.tanh(jnp.dot(basis[...], cells, preferred_element_type=F32))
            offset = jnp.concatenate([flat[...]] * copies, axis=1)
            slope = jnp.concatenate([swing[...]] * copies, axis=1)
            weighted = (offset + slope * heat).astype(BF16)
            source = jnp.dot(basis_t[...], weighted, preferred_element_type=F32).astype(BF16).astype(F32)
            done = cells.astype(F32) + load[p, pl.ds(place, 1), :] * source
            half = planes // 2
            for k in range(count):
                out = theirs if p < half else mine
                out[k * part + i, p % half] = done[k * modes : (k + 1) * modes].astype(BF16)
        return 0

    lax.fori_loop(0, part, row, 0)


def points(pos, basis, basis_t, flat, swing, load, field, begin):
    rows, planes, modes, cols = field.shape
    piece = jax.ShapeDtypeStruct((rows, planes // 2, modes, cols), BF16)
    return pl.pallas_call(
        functools.partial(points_kernel, begin=begin),
        out_shape=(piece, piece, TOKEN),
        in_specs=[SMEM] + [VMEM] * 6,
        out_specs=(VMEM, VMEM, SMEM),
        compiler_params=params(14),
        cost_estimate=COST,
        name="points",
    )(pos, basis, basis_t, flat, swing, load, field)


def settle_kernel(pos, turn, *refs, begin):
    mine, theirs, out, token, final, sems = refs[-6:]
    token[0], token[1] = pos[0], pos[1]
    side = pos[0]
    rows, planes, modes, cols = mine.shape
    size = out.shape[2]
    group = turn.shape[1] // TILE
    copies = []
    for a, source in ((0, mine), (1, theirs)):
        far = side if a == 0 else 1 - side
        for z in range(planes):
            to = jnp.where(far == 1, z, planes - 1 - z)
            for g in range(rows // TILE):
                block = jnp.where(far == 1, rows // TILE - 1 - g, g)
                for h in range(modes // group):
                    there = pl.ds(h * group, group)
                    x = source[pl.ds(g * TILE, TILE), z, there, :]
                    y = jnp.dot(turn[far], to_bf16_rows(x), preferred_element_type=F32).astype(BF16)
                    final[a, to, there, pl.ds(pl.multiple_of(block * TILE, TILE), TILE), :] = y.reshape(
                        group, TILE, cols
                    )
        start = pl.multiple_of(jnp.where(far == 1, size - rows - begin, begin), TILE)
        copy = pltpu.make_async_copy(final.at[a], out.at[:, :, pl.ds(start, rows), :], sems.at[a])
        copy.start()
        copies.append(copy)
    for copy in copies:
        copy.wait()


def settle(pos, turn, result, mine, theirs, begin, shape):
    rows, planes, modes, cols = mine.shape
    chained = result is not None
    return pl.pallas_call(
        functools.partial(settle_kernel, begin=begin),
        out_shape=(jax.ShapeDtypeStruct(shape, BF16), TOKEN),
        in_specs=[SMEM, VMEM] + [HBM] * chained + [VMEM, VMEM],
        out_specs=(HBM, SMEM),
        scratch_shapes=[
            pltpu.VMEM((2, planes, modes, rows, cols), BF16),
            pltpu.SemaphoreType.DMA((2,)),
        ],
        input_output_aliases={2: 0} if chained else {},
        compiler_params=params(10),
        cost_estimate=COST,
        name="settle",
    )(pos, turn, *([result] if chained else []), mine, theirs)


def chunk_rows(half):
    unit = half // 8
    return [unit, 2 * unit, 2 * unit, 2 * unit, unit]


def pipeline(chunks):
    stage = {"T": 0, "R": 1, "S": 2, "P": 3, "C": 4, "F": 5}
    for iteration in range(chunks + 5):
        for kind in "SPTRCF":
            c = iteration - stage[kind]
            if 0 <= c < chunks:
                yield kind, c


def turns(group):
    at = np.arange(group * TILE)
    row, mode = at // group, at % group
    same = mode[:, None] == (at // TILE)[None, :]
    straight = same & (row[:, None] == (at % TILE)[None, :])
    reverse = same & (row[:, None] == TILE - 1 - (at % TILE)[None, :])
    to_rows = np.stack([straight, reverse])
    return jnp.asarray(to_rows, BF16), jnp.asarray(to_rows.transpose(0, 2, 1), BF16)


def on_device(field, diffusion, joule, basis, quad_weight, base_conductivity, thermal_slope):
    planes, modes, size, cols = field.shape
    half = size // 2
    spaces = lax.axis_size("space")
    side = lax.axis_index("space") % 2
    me = lax.axis_index("modes")
    pos = jnp.stack([side, me]).astype(jnp.int32)

    swap = [(i, i ^ 1) for i in range(spaces)]
    ahead = [(i, i + 4 * (i % 2) - 2) for i in range(spaces)]
    ahead = [(i, j) for i, j in ahead if 0 <= j < spaces]
    back = [(j, i) for i, j in ahead]

    def across(x):
        return lax.ppermute(x, "space", swap)

    def ahead_of(x):
        return lax.ppermute(x, "space", ahead)

    def behind_of(x):
        return lax.ppermute(x, "space", back)

    def exchange(x):
        return lax.all_to_all(x, "modes", split_axis=0, concat_axis=0, tiled=True)

    def logical(x, length, side, sent):
        rows_back, planes_back = jnp.flip(x, 1)[:, :length], jnp.flip(x, 0)[:, :length]
        own = jnp.where(side == 1, rows_back, planes_back)
        send = jnp.where(side == 1, planes_back, rows_back).astype(sent)
        return own, send

    lane = np.arange(cols)
    shift = jnp.asarray(np.abs(lane[:, None] - lane[None, :]) == 1, BF16)
    to_rows, to_modes = turns(min(modes, TILE))

    points_count = basis.shape[0]
    extra = -points_count % 32
    basis = jnp.pad(basis, ((0, extra), (0, 0)))
    level = quad_weight * base_conductivity
    spread_out = lambda v: jnp.broadcast_to(jnp.pad(v, (0, extra))[:, None], (points_count + extra, 128))
    flat, swing = spread_out(level), spread_out(level * thermal_slope)

    rows_of = chunk_rows(half)
    begins = [sum(rows_of[:c]) for c in range(len(rows_of))]
    own, other, before, blocks, cells, home, theirs = {}, {}, {}, {}, {}, {}, {}
    result = None
    for kind, c in pipeline(len(rows_of)):
        begin, rows = begins[c], rows_of[c]
        if kind == "T":
            skip = EDGE if c else 0
            after = ()
            if c == 1:
                own_rate, send_rate = logical(diffusion, half + EDGE, pos[0], F32)
                own_load, send_load = logical(joule, half, pos[0], BF16)
                other_rate, other_load = across(send_rate), across(send_load)
                after = (send_rate, send_load)
            own[c], send, pos = spread(pos, field, to_rows, after, begin, skip, rows + EDGE - skip, rows + TILE)
            other[c] = across(send)
            before[c] = ahead_of(own[c])
        elif kind == "R":
            if c == 0:
                other[c], other_rate, other_load, pos = relay(pos, (other[c], other_rate, other_load), (before[c],))
                edges = ahead_of(own_rate[-1:]), behind_of(other_rate[:1])
                rate = jnp.concatenate([edges[0], other_rate, own_rate, edges[1]], axis=0)
                rate = jnp.pad(rate, ((0, 0), (1, -(half + EDGE + 1) % 8), (0, 0)))
                load = jnp.concatenate([other_load.astype(F32), own_load], axis=0)
            else:
                other[c], pos = relay(pos, (other[c],), (before[c],))
            blocks[c] = (before[c], other[c], own[c], behind_of(other[c]))
        elif kind == "S":
            settled, pos = sweep(pos, rate, shift, blocks[c], blocks.get(c - 1, ()), begin, rows)
            cells[c] = exchange(settled)
        elif kind == "P":
            away, near, pos = points(pos, basis, basis.T, flat, swing, load, cells[c], begin)
            theirs[c], home[c] = exchange(away), exchange(near)
        elif kind == "C":
            away, pos = relay(pos, (theirs[c],), ())
            theirs[c] = across(away)
        else:
            result, pos = settle(pos, to_modes, result, home[c], theirs[c], begin, field.shape)
    return result


def solution(mesh):
    return jax.shard_map(
        on_device,
        mesh=mesh,
        in_specs=(
            P("space", "modes", None, None),
            P("space", None, None),
            P("space", None, None),
            P(),
            P(),
            P(),
            P(),
        ),
        out_specs=P("space", "modes", None, None),
        check_vma=False,
    )
```

time: 359 us -> 539 us (1.50)
  blocking collectives: 0 us -> 49.6 us
  local copies, waits for them, and re-layouts: 23.1 us -> 71.9 us
  waiting for transfers between devices: 140 us -> 179 us
  starting transfers between devices: 71 us -> 105 us
  Pallas kernels: 120 us -> 128 us
    all_to_all x0 -> x3, blocking collectives: none -> 49.6 us  [exchange(): return lax.all_to_all(x, 'modes', split_axis=0, concat_axis=0, tiled=True)]
    unnamed x54 -> x190, local copies, waits for them, and re-layouts: 19.1 us -> 67.7 us
    all_to_all x0 -> x12, starting transfers between devices: none -> 48.5 us  [exchange(): return lax.all_to_all(x, 'modes', split_axis=0, concat_axis=0, tiled=True)]
    all_to_all x0 -> x12, waiting for transfers between devices: none -> 45.6 us  [exchange(): return lax.all_to_all(x, 'modes', split_axis=0, concat_axis=0, tiled=True)]
    ppermute x42 -> x12, waiting for transfers between devices: 81.4 us -> 52.4 us  [the longest x6 45 us: behind_of(): return lax.ppermute(x, 'space', back)]
    ppermute x12, waiting for transfers between devices: 58.9 us -> 80.7 us  [across(): return lax.ppermute(x, 'space', swap)]
    ppermute x42 -> x12, starting transfers between devices: 53.7 us -> 34 us  [the longest x6 26 us: behind_of(): return lax.ppermute(x, 'space', back)]
    pallas_call x20 -> x25, Pallas kernels: 108 us -> 117 us  [the longest x5 44.9 us: points(): pl.pallas_call(functools.partial(points_kernel, begin=begin), out_shape=(...]
  transfers between devices with their start and end apart: 54 -> 36, of which waited for: 16 -> 20; matrix products, arithmetic and copies ran while one was open for 2% -> 1% of each run, Pallas kernels for 31% -> 22%
where the time goes in v4:
time: 539 us; the launch traced here: 536 us
  waiting for transfers between devices  179 us (33%)
  Pallas kernels  128 us (24%)
  starting transfers between devices  105 us (19%)
  local copies, waits for them, and re-layouts  71.9 us (13%)
  blocking collectives  49.6 us (9%)
    ppermute x12, waiting for transfers between devices, across(): return lax.ppermute(x, 'space', swap)  80.7 us
    unnamed x190, local copies, waits for them, and re-layouts  67.7 us
    all_to_all x3, blocking collectives, exchange(): return lax.all_to_all(x, 'modes', split_axis=0, concat_axis=0, tiled=True)  49.6 us
    all_to_all x12, starting transfers between devices, exchange(): return lax.all_to_all(x, 'modes', split_axis=0, concat_axis=0, tiled=True)  48.5 us
    all_to_all x12, waiting for transfers between devices, exchange(): return lax.all_to_all(x, 'modes', split_axis=0, concat_axis=0, tiled=True)  45.6 us
    ppermute x6, waiting for transfers between devices, behind_of(): return lax.ppermute(x, 'space', back)  45 us
    pallas_call x5, Pallas kernels, points(): pl.pallas_call(functools.partial(points_kernel, begin=begin), out_shape=(...  44.9 us
    pallas_call x5, Pallas kernels, sweep(): pl.pallas_call(functools.partial(sweep_kernel, begin=begin, heads=len(tai...  43.5 us
  transfers between devices with their start and end apart: 36, of which 20 were waited for; matrix products, arithmetic and copies ran while one was open for 1% of the time, Pallas kernels for 22%

profile of v4, /device:TPU:0, one launch (start us, length us, event | category | flops | bytes accessed | tf_op | source)
XLA Modules:
  0.0 535.6 jit_solution(11304385381153023198)
XLA Ops:
  24.8 24.1 %collective-permute-done.2.refs_2_ = bf16[2,128,256]{2,1,0:T(8,128)(2,1)S(1)} collective-permute-done((bf16[2,128,256]{2,1,0:T(8,128)(2,1)S(1)}, bf16[2,128,256]{2,1,0:T(8,128)(2,1)S(1)}, u32[]{:S(2)}, u32[]{:S(2)}) %collective-permute-start.2) | collective-permute-done | bytes 131104 | tf_op jit(solution)/shard_map/ppermute | solution.py:338
  50.6 6.1 %collective-permute-done.1.refs_1_ = f32[2,130,256]{2,1,0:T(8,128)S(1)} collective-permute-done((f32[2,130,256]{2,1,0:T(8,128)S(1)}, f32[2,130,256]{2,1,0:T(8,128)S(1)}, u32[]{:S(2)}, u32[]{:S(2)}) %collective-permute-start.1) | collective-permute-done | bytes 266272 | tf_op jit(solution)/shard_map/ppermute | solution.py:338
  62.7 4.6 collective-permute-start.5
  68.3 7.0 %collective-permute-done.5 = f32[1,130,256]{2,1,0:T(8,128)S(1)} collective-permute-done((f32[1,130,256]{2,1,0:T(8,128)S(1)}, f32[1,130,256]{2,1,0:T(8,128)S(1)}, u32[]{:S(2)}, u32[]{:S(2)}) %collective-permute-start.5) | collective-permute-done | bytes 133152 | tf_op jit(solution)/shard_map/ppermute | solution.py:344
  76.7 5.6 %sweep.5 = (bf16[16,4,32,256]{3,2,1,0:T(8,128)(2,1)S(1)}, s32[2]{0:T(128)S(1)}) custom-call(s32[2]{0:T(128)S(1)} %get-tuple-element.80.pos, f32[6,136,256]{2,1,0:T(8,128)S(1)} %select_maximum_fusion.rate, bf16[256,256]{1,0:T(8,128)(2,1)S(1)} %copy-done.40, bf16[18,2,32,256]{3,2,1,0:T(8,128)(2,1)S(1)} %copy-done.26, ...), custom_call_target="tpu_custom_call" | custom-call | flops 1 | bytes 1 | tf_op jit(solution)/shard_map/sweep/pallas_call | solution.py:195
  82.3 3.8 copy-done.2
  89.6 5.4 collective-permute-start.9
  94.9 4.3 all-to-all-start
  103.3 10.3 %collective-permute-done.9.refs_3_.refs_7_ = bf16[32,2,32,256]{3,2,1,0:T(8,128)(2,1)} collective-permute-done((bf16[32,2,32,256]{3,2,1,0:T(8,128)(2,1)S(1)}, bf16[32,2,32,256]{3,2,1,0:T(8,128)(2,1)}, u32[]{:S(2)}, u32[]{:S(2)}) %collective-permute-start.9) | collective-permute-done | bytes 1048608 | tf_op jit(solution)/shard_map/ppermute | solution.py:344
  118.6 10.3 %sweep.6 = (bf16[32,4,32,256]{3,2,1,0:T(8,128)(2,1)S(1)}, s32[2]{0:T(128)S(1)}) custom-call(s32[2]{0:T(128)S(1)} %copy-done.83, f32[6,136,256]{2,1,0:T(8,128)S(1)} %select_maximum_fusion.rate, bf16[256,256]{1,0:T(8,128)(2,1)S(1)} %copy-done.41, bf16[32,2,32,256]{3,2,1,0:T(8,128)(2,1)S(1)} %collective-permute-done.8.refs_1_.refs_0_.refs_4_, ...), custom_call_target="tpu_custom_call" | custom-call | flops 1 | bytes 1 | tf_op jit(solution)/shard_map/sweep/pallas_call | solution.py:195
  133.9 6.0 %points.5 = (bf16[16,2,32,256]{3,2,1,0:T(8,128)(2,1)S(1)}, bf16[16,2,32,256]{3,2,1,0:T(8,128)(2,1)S(1)}, s32[2]{0:T(128)S(1)}) custom-call(s32[2]{0:T(128)S(1)} %copy-done.79, bf16[352,128]{1,0:T(8,128)(2,1)S(1)} %copy-done.45, bf16[128,352]{1,0:T(8,128)(2,1)S(1)} %pad_bitcast_fusion.basis_t, f32[352,128]{1,0:T(8,128)S(1)} %broadcast_in_dim.4.flat, ...), custom_call_target="tpu_custom_call" | custom-call | flops 1 | bytes 1 | tf_op jit(solution)/shard_map/points/pallas_call | solution.py:241
  142.1 4.2 all-to-all-start.2
  150.2 5.0 all-to-all-done.2.refs_0_
  155.1 4.5 all-to-all-start.1
  166.8 5.9 %collective-permute-done.10.refs_0_ = bf16[32,2,32,256]{3,2,1,0:T(8,128)(2,1)S(1)} collective-permute-done((bf16[32,2,32,256]{3,2,1,0:T(8,128)(2,1)}, bf16[32,2,32,256]{3,2,1,0:T(8,128)(2,1)S(1)}, u32[]{:S(2)}, u32[]{:S(2)}) %collective-permute-start.10) | collective-permute-done | bytes 1048608 | tf_op jit(solution)/shard_map/ppermute | solution.py:338
  177.8 4.4 collective-permute-start.12
  185.4 4.1 all-to-all-start.5
  189.5 13.5 %collective-permute-done.12.refs_3_.refs_7_ = bf16[32,2,32,256]{3,2,1,0:T(8,128)(2,1)} collective-permute-done((bf16[32,2,32,256]{3,2,1,0:T(8,128)(2,1)S(1)}, bf16[32,2,32,256]{3,2,1,0:T(8,128)(2,1)}, u32[]{:S(2)}, u32[]{:S(2)}) %collective-permute-start.12) | collective-permute-done | bytes 1048608 | tf_op jit(solution)/shard_map/ppermute | solution.py:344
  209.5 10.4 %sweep.7 = (bf16[32,4,32,256]{3,2,1,0:T(8,128)(2,1)S(1)}, s32[2]{0:T(128)S(1)}) custom-call(s32[2]{0:T(128)S(1)} %copy-done.77, f32[6,136,256]{2,1,0:T(8,128)S(1)} %select_maximum_fusion.rate, bf16[256,256]{1,0:T(8,128)(2,1)S(1)} %copy-done.42, bf16[32,2,32,256]{3,2,1,0:T(8,128)(2,1)S(1)} %collective-permute-done.11.refs_1_.refs_0_.refs_4_, ...), custom_call_target="tpu_custom_call" | custom-call | flops 1 | bytes 1 | tf_op jit(solution)/shard_map/sweep/pallas_call | solution.py:195
  221.2 11.1 %points.6 = (bf16[32,2,32,256]{3,2,1,0:T(8,128)(2,1)S(1)}, bf16[32,2,32,256]{3,2,1,0:T(8,128)(2,1)S(1)}, s32[2]{0:T(128)S(1)}) custom-call(s32[2]{0:T(128)S(1)} %get-tuple-element.98.pos, bf16[352,128]{1,0:T(8,128)(2,1)S(1)} %copy-done.46, bf16[128,352]{1,0:T(8,128)(2,1)S(1)} %pad_bitcast_fusion.basis_t, f32[352,128]{1,0:T(8,128)S(1)} %copy-done.18, ...), custom_call_target="tpu_custom_call" | custom-call | flops 1 | bytes 1 | tf_op jit(solution)/shard_map/points/pallas_call | solution.py:241
  234.8 18.8 %all_to_all.75.refs_0_ = bf16[32,2,32,256]{3,2,1,0:T(8,128)(2,1)} all-to-all(bf16[32,2,32,256]{3,2,1,0:T(8,128)(2,1)} %copy-done.60), channel_id=1, replica_groups=mesh['space'=8,'modes'=4] {'modes'}, dimensions={0} | all-to-all | bytes 2097152 | tf_op jit(solution)/shard_map/all_to_all | solution.py:347
  253.5 4.5 all-to-all-start.3
  268.8 15.1 %collective-permute-done.13.refs_0_ = bf16[32,2,32,256]{3,2,1,0:T(8,128)(2,1)} collective-permute-done((bf16[32,2,32,256]{3,2,1,0:T(8,128)(2,1)}, bf16[32,2,32,256]{3,2,1,0:T(8,128)(2,1)}, u32[]{:S(2)}, u32[]{:S(2)}) %collective-permute-start.13) | collective-permute-done | bytes 1048608 | tf_op jit(solution)/shard_map/ppermute | solution.py:338
  288.6 4.6 collective-permute-start.15
  293.2 4.3 all-to-all-start.8
  300.8 13.5 %collective-permute-done.15.refs_3_.refs_7_ = bf16[32,2,32,256]{3,2,1,0:T(8,128)(2,1)} collective-permute-done((bf16[32,2,32,256]{3,2,1,0:T(8,128)(2,1)}, bf16[32,2,32,256]{3,2,1,0:T(8,128)(2,1)}, u32[]{:S(2)}, u32[]{:S(2)}) %collective-permute-start.15) | collective-permute-done | bytes 1048608 | tf_op jit(solution)/shard_map/ppermute | solution.py:344
  318.9 10.6 %sweep.8 = (bf16[32,4,32,256]{3,2,1,0:T(8,128)(2,1)S(1)}, s32[2]{0:T(128)S(1)}) custom-call(s32[2]{0:T(128)S(1)} %get-tuple-element.106.pos, f32[6,136,256]{2,1,0:T(8,128)S(1)} %select_maximum_fusion.rate, bf16[256,256]{1,0:T(8,128)(2,1)S(1)} %copy-done.43, bf16[32,2,32,256]{3,2,1,0:T(8,128)(2,1)S(1)} %collective-permute-done.14.refs_1_.refs_0_.refs_4_, ...), custom_call_target="tpu_custom_call" | custom-call | flops 1 | bytes 1 | tf_op jit(solution)/shard_map/sweep/pallas_call | solution.py:195
  330.9 11.6 %points.7 = (bf16[32,2,32,256]{3,2,1,0:T(8,128)(2,1)}, bf16[32,2,32,256]{3,2,1,0:T(8,128)(2,1)S(1)}, s32[2]{0:T(128)S(1)}) custom-call(s32[2]{0:T(128)S(1)} %get-tuple-element.108.pos, bf16[352,128]{1,0:T(8,128)(2,1)S(1)} %copy-done.47, bf16[128,352]{1,0:T(8,128)(2,1)S(1)} %pad_bitcast_fusion.basis_t, f32[352,128]{1,0:T(8,128)S(1)} %copy-done.19, ...), custom_call_target="tpu_custom_call" | custom-call | flops 1 | bytes 1 | tf_op jit(solution)/shard_map/points/pallas_call | solution.py:241
  344.1 4.3 all-to-all-start.7
  352.4 3.6 collective-permute-start.19
  359.4 3.9 collective-permute-done.18.refs_1_
  370.9 6.5 %sweep.9 = (bf16[16,4,32,256]{3,2,1,0:T(8,128)(2,1)S(1)}, s32[2]{0:T(128)S(1)}) custom-call(s32[2]{0:T(128)S(1)} %get-tuple-element.118.pos, f32[6,136,256]{2,1,0:T(8,128)S(1)} %select_maximum_fusion.rate, bf16[256,256]{1,0:T(8,128)(2,1)S(1)} %copy-done.44, bf16[16,2,32,256]{3,2,1,0:T(8,128)(2,1)} %collective-permute-done.17.refs_1_.refs_0_, ...), custom_call_target="tpu_custom_call" | custom-call | flops 1 | bytes 1 | tf_op jit(solution)/shard_map/sweep/pallas_call | solution.py:195
  379.1 18.9 %all_to_all.76.field = bf16[16,4,32,256]{3,2,1,0:T(8,128)(2,1)} all-to-all(bf16[16,4,32,256]{3,2,1,0:T(8,128)(2,1)} %copy-done.59), channel_id=1, replica_groups=mesh['space'=8,'modes'=4] {'modes'}, dimensions={0} | all-to-all | bytes 2097152 | tf_op jit(solution)/shard_map/all_to_all | solution.py:347
  398.0 3.6 all-to-all-start.6
  402.9 24.3 %all-to-all-done.6.field = bf16[32,4,32,256]{3,2,1,0:T(8,128)(2,1)S(1)} async-done(((bf16[32,4,32,256]{3,2,1,0:T(8,128)(2,1)}), bf16[32,4,32,256]{3,2,1,0:T(8,128)(2,1)S(1)}, u32[]{:S(2)}, u32[]{:S(2)}) %all-to-all-start.6) | async-done | bytes 2097184 | tf_op jit(solution)/shard_map/all_to_all | solution.py:347
  427.2 4.4 all-to-all-start.11
  434.4 11.0 %points.8 = (bf16[32,2,32,256]{3,2,1,0:T(8,128)(2,1)}, bf16[32,2,32,256]{3,2,1,0:T(8,128)(2,1)S(1)}, s32[2]{0:T(128)S(1)}) custom-call(s32[2]{0:T(128)S(1)} %copy-done.81, bf16[352,128]{1,0:T(8,128)(2,1)S(1)} %copy-done.48, bf16[128,352]{1,0:T(8,128)(2,1)S(1)} %pad_bitcast_fusion.basis_t, f32[352,128]{1,0:T(8,128)S(1)} %copy-done.20, ...), custom_call_target="tpu_custom_call" | custom-call | flops 1 | bytes 1 | tf_op jit(solution)/shard_map/points/pallas_call | solution.py:241
  447.5 3.9 settle.6
  451.5 5.3 points.9
  457.6 11.9 %all_to_all.77.refs_0_ = bf16[16,2,32,256]{3,2,1,0:T(8,128)(2,1)S(1)} all-to-all(bf16[16,2,32,256]{3,2,1,0:T(8,128)(2,1)S(1)} %get-tuple-element.137), channel_id=1, replica_groups=mesh['space'=8,'modes'=4] {'modes'}, dimensions={0} | all-to-all | bytes 1048576 | tf_op jit(solution)/shard_map/all_to_all | solution.py:347
  469.5 3.5 all-to-all-start.10
  474.3 13.1 %all-to-all-done.10.refs_0_ = bf16[32,2,32,256]{3,2,1,0:T(8,128)(2,1)S(1)} async-done(((bf16[32,2,32,256]{3,2,1,0:T(8,128)(2,1)}), bf16[32,2,32,256]{3,2,1,0:T(8,128)(2,1)S(1)}, u32[]{:S(2)}, u32[]{:S(2)}) %all-to-all-start.10) | async-done | bytes 1048608 | tf_op jit(solution)/shard_map/all_to_all | solution.py:347
  487.4 3.5 all-to-all-start.13
  493.4 5.9 %collective-permute-done.21.refs_2_ = bf16[32,2,32,256]{3,2,1,0:T(8,128)(2,1)} collective-permute-done((bf16[32,2,32,256]{3,2,1,0:T(8,128)(2,1)}, bf16[32,2,32,256]{3,2,1,0:T(8,128)(2,1)}, u32[]{:S(2)}, u32[]{:S(2)}) %collective-permute-start.21) | collective-permute-done | bytes 1048608 | tf_op jit(solution)/shard_map/ppermute | solution.py:338
  499.3 3.9 settle.7
  509.2 12.6 %collective-permute-done.22.refs_2_ = bf16[32,2,32,256]{3,2,1,0:T(8,128)(2,1)} collective-permute-done((bf16[32,2,32,256]{3,2,1,0:T(8,128)(2,1)S(1)}, bf16[32,2,32,256]{3,2,1,0:T(8,128)(2,1)}, u32[]{:S(2)}, u32[]{:S(2)}) %collective-permute-start.22) | collective-permute-done | bytes 1048608 | tf_op jit(solution)/shard_map/ppermute | solution.py:338
  521.8 3.6 settle.8
  525.4 7.2 %collective-permute-done.23.refs_2_ = bf16[16,2,32,256]{3,2,1,0:T(8,128)(2,1)} collective-permute-done((bf16[16,2,32,256]{3,2,1,0:T(8,128)(2,1)S(1)}, bf16[16,2,32,256]{3,2,1,0:T(8,128)(2,1)}, u32[]{:S(2)}, u32[]{:S(2)}) %collective-permute-start.23) | collective-permute-done | bytes 524320 | tf_op jit(solution)/shard_map/ppermute | solution.py:338
  (267 shorter events, 146.1 us)
Async XLA Ops:
  7.0 49.7 %collective-permute-start = (bf16[18,2,32,256]{3,2,1,0:T(8,128)(2,1)}, bf16[18,2,32,256]{3,2,1,0:T(8,128)(2,1)}, u32[]{:S(2)}, u32[]{:S(2)}) collective-permute-start(bf16[18,2,32,256]{3,2,1,0:T(8,128)(2,1)} %get-tuple-element.78), channel_id=1, source_target_pairs={{0,4},{4,0},{8,12},{12,8},{16,20},{20,16},{24,28},{28,24},{1,5},{5... | collective-permute-start | bytes 1769480 | tf_op jit(solution)/shard_map/ppermute | solution.py:338
  10.0 46.7 %collective-permute-start.3 = (bf16[18,2,32,256]{3,2,1,0:T(8,128)(2,1)}, bf16[18,2,32,256]{3,2,1,0:T(8,128)(2,1)S(1)}, u32[]{:S(2)}, u32[]{:S(2)}) collective-permute-start(bf16[18,2,32,256]{3,2,1,0:T(8,128)(2,1)} %get-tuple-element.79.refs_2_.refs_6_), channel_id=1, source_target_pairs={{4,12},{8,0},{12,20},{16,8},{20,28},{24,16},{5,13},{9,1},{13,21},{... | collective-permute-start | bytes 1769480 | tf_op jit(solution)/shard_map/ppermute | solution.py:341
  11.4 64.0 %copy-start.40 = (bf16[256,256]{1,0:T(8,128)(2,1)S(1)}, bf16[256,256]{1,0:T(8,128)(2,1)}, u32[]{:S(2)}) copy-start(bf16[256,256]{1,0:T(8,128)(2,1)} %constant.36.clone.shift) | copy-start | bytes 393220
  18.0 71.5 %copy-start.37 = (bf16[32,2,32,256]{3,2,1,0:T(8,128)(2,1)}, bf16[32,2,32,256]{3,2,1,0:T(8,128)(2,1)S(1)}, u32[]{:S(2)}) copy-start(bf16[32,2,32,256]{3,2,1,0:T(8,128)(2,1)S(1)} %get-tuple-element.86.refs_2_.refs_6_) | copy-start | bytes 3145732
  18.0 70.4 %collective-permute-start.7 = (bf16[32,2,32,256]{3,2,1,0:T(8,128)(2,1)S(1)}, bf16[32,2,32,256]{3,2,1,0:T(8,128)(2,1)S(1)}, u32[]{:S(2)}, u32[]{:S(2)}) collective-permute-start(bf16[32,2,32,256]{3,2,1,0:T(8,128)(2,1)S(1)} %get-tuple-element.85), channel_id=1, source_target_pairs={{0,4},{4,0},{8,12},{12,8},{16,20},{20,16},{24,28},{28,24},{1,5},{5... | collective-permute-start | bytes 3145736 | tf_op jit(solution)/shard_map/ppermute | solution.py:338
  20.8 67.5 %collective-permute-start.8 = (bf16[32,2,32,256]{3,2,1,0:T(8,128)(2,1)S(1)}, bf16[32,2,32,256]{3,2,1,0:T(8,128)(2,1)S(1)}, u32[]{:S(2)}, u32[]{:S(2)}) collective-permute-start(bf16[32,2,32,256]{3,2,1,0:T(8,128)(2,1)S(1)} %get-tuple-element.86.refs_2_.refs_6_), channel_id=1, source_target_pairs={{4,12},{8,0},{12,20},{16,8},{20,28},{24,16},{5,13},{9,1},{13,21},{... | collective-permute-start | bytes 3145736 | tf_op jit(solution)/shard_map/ppermute | solution.py:341
  22.1 26.7 %collective-permute-start.2 = (bf16[2,128,256]{2,1,0:T(8,128)(2,1)S(1)}, bf16[2,128,256]{2,1,0:T(8,128)(2,1)S(1)}, u32[]{:S(2)}, u32[]{:S(2)}) collective-permute-start(bf16[2,128,256]{2,1,0:T(8,128)(2,1)S(1)} %select_convert_fusion.refs_1_), channel_id=1, source_target_pairs={{0,4},{4,0},{8,12},{12,8},{16,20},{20,16},{24,28},{28,24},{1,5},{5... | collective-permute-start | bytes 393224 | tf_op jit(solution)/shard_map/ppermute | solution.py:338
  48.9 7.8 %collective-permute-start.1 = (f32[2,130,256]{2,1,0:T(8,128)S(1)}, f32[2,130,256]{2,1,0:T(8,128)S(1)}, u32[]{:S(2)}, u32[]{:S(2)}) collective-permute-start(f32[2,130,256]{2,1,0:T(8,128)S(1)} %get-tuple-element.150.refs_0_), channel_id=1, source_target_pairs={{0,4},{4,0},{8,12},{12,8},{16,20},{20,16},{24,28},{28,24},{1,5},{5... | collective-permute-start | bytes 798728 | tf_op jit(solution)/shard_map/ppermute | solution.py:338
  57.9 17.5 %collective-permute-start.6 = (bf16[18,2,32,256]{3,2,1,0:T(8,128)(2,1)}, bf16[18,2,32,256]{3,2,1,0:T(8,128)(2,1)S(1)}, u32[]{:S(2)}, u32[]{:S(2)}) collective-permute-start(bf16[18,2,32,256]{3,2,1,0:T(8,128)(2,1)} %get-tuple-element.82.refs_1_.refs_5_), channel_id=1, source_target_pairs={{12,4},{0,8},{20,12},{8,16},{28,20},{16,24},{13,5},{1,9},{21,13},{... | collective-permute-start | bytes 1769480 | tf_op jit(solution)/shard_map/ppermute | solution.py:344
  61.3 6.9 %collective-permute-start.4 = (f32[1,130,256]{2,1,0:T(8,128)S(1)}, f32[1,130,256]{2,1,0:T(8,128)S(1)}, u32[]{:S(2)}, u32[]{:S(2)}) collective-permute-start(f32[1,130,256]{2,1,0:T(8,128)S(1)} %slice.45), channel_id=1, source_target_pairs={{4,12},{8,0},{12,20},{16,8},{20,28},{24,16},{5,13},{9,1},{13,21},{... | collective-permute-start | bytes 399368 | tf_op jit(solution)/shard_map/ppermute | solution.py:341
  62.7 12.6 %collective-permute-start.5 = (f32[1,130,256]{2,1,0:T(8,128)S(1)}, f32[1,130,256]{2,1,0:T(8,128)S(1)}, u32[]{:S(2)}, u32[]{:S(2)}) collective-permute-start(f32[1,130,256]{2,1,0:T(8,128)S(1)} %slice.44), channel_id=1, source_target_pairs={{12,4},{0,8},{20,12},{8,16},{28,20},{16,24},{13,5},{1,9},{21,13},{... | collective-permute-start | bytes 399368 | tf_op jit(solution)/shard_map/ppermute | solution.py:344
  76.7 26.6 %copy-start.64 = (bf16[2,128,256]{2,1,0:T(8,128)(2,1)S(1)}, bf16[2,128,256]{2,1,0:T(8,128)(2,1)}, u32[]{:S(2)}) copy-start(bf16[2,128,256]{2,1,0:T(8,128)(2,1)} %copy-done.63) | copy-start | bytes 393220
  88.4 51.5 %copy-start.7 = (bf16[32,2,32,256]{3,2,1,0:T(8,128)(2,1)}, bf16[32,2,32,256]{3,2,1,0:T(8,128)(2,1)S(1)}, u32[]{:S(2)}) copy-start(bf16[32,2,32,256]{3,2,1,0:T(8,128)(2,1)S(1)} %collective-permute-done.8.refs_1_.refs_0_.refs_4_) | copy-start | bytes 3145732
  89.6 56.7 %copy-start.9 = (bf16[32,2,32,256]{3,2,1,0:T(8,128)(2,1)}, bf16[32,2,32,256]{3,2,1,0:T(8,128)(2,1)S(1)}, u32[]{:S(2)}) copy-start(bf16[32,2,32,256]{3,2,1,0:T(8,128)(2,1)S(1)} %get-tuple-element.88.refs_1_.refs_5_) | copy-start | bytes 3145732
  89.6 24.1 %collective-permute-start.9 = (bf16[32,2,32,256]{3,2,1,0:T(8,128)(2,1)S(1)}, bf16[32,2,32,256]{3,2,1,0:T(8,128)(2,1)}, u32[]{:S(2)}, u32[]{:S(2)}) collective-permute-start(bf16[32,2,32,256]{3,2,1,0:T(8,128)(2,1)S(1)} %get-tuple-element.88.refs_1_.refs_5_), channel_id=1, source_target_pairs={{12,4},{0,8},{20,12},{8,16},{28,20},{16,24},{13,5},{1,9},{21,13},{... | collective-permute-start | bytes 3145736 | tf_op jit(solution)/shard_map/ppermute | solution.py:344
  94.9 35.8 %all-to-all-start = ((bf16[16,4,32,256]{3,2,1,0:T(8,128)(2,1)}), bf16[16,4,32,256]{3,2,1,0:T(8,128)(2,1)}, u32[]{:S(2)}, u32[]{:S(2)}) async-start(bf16[16,4,32,256]{3,2,1,0:T(8,128)(2,1)} %copy-done.58), calls=%async_computation | async-start | bytes 2097152 | tf_op jit(solution)/shard_map/all_to_all | solution.py:347
  142.1 13.1 %all-to-all-start.2 = ((bf16[16,2,32,256]{3,2,1,0:T(8,128)(2,1)}), bf16[16,2,32,256]{3,2,1,0:T(8,128)(2,1)}, u32[]{:S(2)}, u32[]{:S(2)}) async-start(bf16[16,2,32,256]{3,2,1,0:T(8,128)(2,1)} %copy-done.67), calls=%async_computation.2 | async-start | bytes 1048576 | tf_op jit(solution)/shard_map/all_to_all | solution.py:347
  146.3 26.5 %collective-permute-start.10 = (bf16[32,2,32,256]{3,2,1,0:T(8,128)(2,1)}, bf16[32,2,32,256]{3,2,1,0:T(8,128)(2,1)S(1)}, u32[]{:S(2)}, u32[]{:S(2)}) collective-permute-start(bf16[32,2,32,256]{3,2,1,0:T(8,128)(2,1)} %copy-done.84), channel_id=1, source_target_pairs={{0,4},{4,0},{8,12},{12,8},{16,20},{20,16},{24,28},{28,24},{1,5},{5... | collective-permute-start | bytes 3145736 | tf_op jit(solution)/shard_map/ppermute | solution.py:338
  148.9 27.2 %collective-permute-start.11 = (bf16[32,2,32,256]{3,2,1,0:T(8,128)(2,1)}, bf16[32,2,32,256]{3,2,1,0:T(8,128)(2,1)S(1)}, u32[]{:S(2)}, u32[]{:S(2)}) collective-permute-start(bf16[32,2,32,256]{3,2,1,0:T(8,128)(2,1)} %copy-done.28), channel_id=1, source_target_pairs={{4,12},{8,0},{12,20},{16,8},{20,28},{24,16},{5,13},{9,1},{13,21},{... | collective-permute-start | bytes 3145736 | tf_op jit(solution)/shard_map/ppermute | solution.py:341
  155.1 30.2 %all-to-all-start.1 = ((bf16[32,4,32,256]{3,2,1,0:T(8,128)(2,1)}), bf16[32,4,32,256]{3,2,1,0:T(8,128)(2,1)}, u32[]{:S(2)}, u32[]{:S(2)}) async-start(bf16[32,4,32,256]{3,2,1,0:T(8,128)(2,1)} %copy-done.53), calls=%async_computation.1 | async-start | bytes 4194304 | tf_op jit(solution)/shard_map/all_to_all | solution.py:347
  177.8 75.8 %copy-start.5 = (bf16[32,2,32,256]{3,2,1,0:T(8,128)(2,1)}, bf16[32,2,32,256]{3,2,1,0:T(8,128)(2,1)S(1)}, u32[]{:S(2)}) copy-start(bf16[32,2,32,256]{3,2,1,0:T(8,128)(2,1)S(1)} %get-tuple-element.97.refs_1_.refs_5_) | copy-start | bytes 3145732
  177.8 25.3 %collective-permute-start.12 = (bf16[32,2,32,256]{3,2,1,0:T(8,128)(2,1)S(1)}, bf16[32,2,32,256]{3,2,1,0:T(8,128)(2,1)}, u32[]{:S(2)}, u32[]{:S(2)}) collective-permute-start(bf16[32,2,32,256]{3,2,1,0:T(8,128)(2,1)S(1)} %get-tuple-element.97.refs_1_.refs_5_), channel_id=1, source_target_pairs={{12,4},{0,8},{20,12},{8,16},{28,20},{16,24},{13,5},{1,9},{21,13},{... | collective-permute-start | bytes 3145736 | tf_op jit(solution)/shard_map/ppermute | solution.py:344
  185.4 49.4 %all-to-all-start.5 = ((bf16[16,2,32,256]{3,2,1,0:T(8,128)(2,1)}), bf16[16,2,32,256]{3,2,1,0:T(8,128)(2,1)}, u32[]{:S(2)}, u32[]{:S(2)}) async-start(bf16[16,2,32,256]{3,2,1,0:T(8,128)(2,1)} %copy-done.66), calls=%async_computation.5 | async-start | bytes 1048576 | tf_op jit(solution)/shard_map/all_to_all | solution.py:347
  253.5 39.6 %all-to-all-start.3 = ((bf16[32,4,32,256]{3,2,1,0:T(8,128)(2,1)}), bf16[32,4,32,256]{3,2,1,0:T(8,128)(2,1)}, u32[]{:S(2)}, u32[]{:S(2)}) async-start(bf16[32,4,32,256]{3,2,1,0:T(8,128)(2,1)} %copy-done.54), calls=%async_computation.3 | async-start | bytes 4194304 | tf_op jit(solution)/shard_map/all_to_all | solution.py:347
  258.0 25.8 %collective-permute-start.13 = (bf16[32,2,32,256]{3,2,1,0:T(8,128)(2,1)}, bf16[32,2,32,256]{3,2,1,0:T(8,128)(2,1)}, u32[]{:S(2)}, u32[]{:S(2)}) collective-permute-start(bf16[32,2,32,256]{3,2,1,0:T(8,128)(2,1)} %copy-done.85), channel_id=1, source_target_pairs={{0,4},{4,0},{8,12},{12,8},{16,20},{20,16},{24,28},{28,24},{1,5},{5... | collective-permute-start | bytes 3145736 | tf_op jit(solution)/shard_map/ppermute | solution.py:338
  259.6 27.2 %collective-permute-start.14 = (bf16[32,2,32,256]{3,2,1,0:T(8,128)(2,1)}, bf16[32,2,32,256]{3,2,1,0:T(8,128)(2,1)S(1)}, u32[]{:S(2)}, u32[]{:S(2)}) collective-permute-start(bf16[32,2,32,256]{3,2,1,0:T(8,128)(2,1)} %copy-done.31), channel_id=1, source_target_pairs={{4,12},{8,0},{12,20},{16,8},{20,28},{24,16},{5,13},{9,1},{13,21},{... | collective-permute-start | bytes 3145736 | tf_op jit(solution)/shard_map/ppermute | solution.py:341
  288.6 25.8 %collective-permute-start.15 = (bf16[32,2,32,256]{3,2,1,0:T(8,128)(2,1)}, bf16[32,2,32,256]{3,2,1,0:T(8,128)(2,1)}, u32[]{:S(2)}, u32[]{:S(2)}) collective-permute-start(bf16[32,2,32,256]{3,2,1,0:T(8,128)(2,1)} %get-tuple-element.107.refs_1_.refs_5_), channel_id=1, source_target_pairs={{12,4},{0,8},{20,12},{8,16},{28,20},{16,24},{13,5},{1,9},{21,13},{... | collective-permute-start | bytes 3145736 | tf_op jit(solution)/shard_map/ppermute | solution.py:344
  293.2 50.9 %all-to-all-start.8 = ((bf16[32,2,32,256]{3,2,1,0:T(8,128)(2,1)}), bf16[32,2,32,256]{3,2,1,0:T(8,128)(2,1)}, u32[]{:S(2)}, u32[]{:S(2)}) async-start(bf16[32,2,32,256]{3,2,1,0:T(8,128)(2,1)} %copy-done.56), calls=%async_computation.8 | async-start | bytes 2097152 | tf_op jit(solution)/shard_map/all_to_all | solution.py:347
  297.4 33.5 %copy-start.19 = (f32[352,128]{1,0:T(8,128)S(1)}, f32[352,128]{1,0:T(8,128)}, u32[]{:S(2)}) copy-start(f32[352,128]{1,0:T(8,128)} %copy-done.17) | copy-start | bytes 540676
  297.5 33.5 %copy-start.23 = (f32[352,128]{1,0:T(8,128)S(1)}, f32[352,128]{1,0:T(8,128)}, u32[]{:S(2)}) copy-start(f32[352,128]{1,0:T(8,128)} %copy-done.21) | copy-start | bytes 540676
  297.5 33.4 %copy-start.47 = (bf16[352,128]{1,0:T(8,128)(2,1)S(1)}, bf16[352,128]{1,0:T(8,128)(2,1)}, u32[]{:S(2)}) copy-start(bf16[352,128]{1,0:T(8,128)(2,1)} %pad.16.clone.basis) | copy-start | bytes 270340
  297.5 53.1 %collective-permute-start.16 = (bf16[16,2,32,256]{3,2,1,0:T(8,128)(2,1)}, bf16[16,2,32,256]{3,2,1,0:T(8,128)(2,1)}, u32[]{:S(2)}, u32[]{:S(2)}) collective-permute-start(bf16[16,2,32,256]{3,2,1,0:T(8,128)(2,1)} %copy-done.86), channel_id=1, source_target_pairs={{0,4},{4,0},{8,12},{12,8},{16,20},{20,16},{24,28},{28,24},{1,5},{5... | collective-permute-start | bytes 1572872 | tf_op jit(solution)/shard_map/ppermute | solution.py:338
  297.6 53.0 %collective-permute-start.17 = (bf16[16,2,32,256]{3,2,1,0:T(8,128)(2,1)}, bf16[16,2,32,256]{3,2,1,0:T(8,128)(2,1)}, u32[]{:S(2)}, u32[]{:S(2)}) collective-permute-start(bf16[16,2,32,256]{3,2,1,0:T(8,128)(2,1)} %copy-done.61), channel_id=1, source_target_pairs={{4,12},{8,0},{12,20},{16,8},{20,28},{24,16},{5,13},{9,1},{13,21},{... | collective-permute-start | bytes 1572872 | tf_op jit(solution)/shard_map/ppermute | solution.py:341
  344.1 35.0 %all-to-all-start.7 = ((bf16[32,2,32,256]{3,2,1,0:T(8,128)(2,1)}), bf16[32,2,32,256]{3,2,1,0:T(8,128)(2,1)}, u32[]{:S(2)}, u32[]{:S(2)}) async-start(bf16[32,2,32,256]{3,2,1,0:T(8,128)(2,1)} %get-tuple-element.123), calls=%async_computation.7 | async-start | bytes 2097152 | tf_op jit(solution)/shard_map/all_to_all | solution.py:347
  348.3 14.9 %collective-permute-start.18 = (bf16[16,2,32,256]{3,2,1,0:T(8,128)(2,1)}, bf16[16,2,32,256]{3,2,1,0:T(8,128)(2,1)S(1)}, u32[]{:S(2)}, u32[]{:S(2)}) collective-permute-start(bf16[16,2,32,256]{3,2,1,0:T(8,128)(2,1)} %get-tuple-element.117), channel_id=1, source_target_pairs={{0,4},{4,0},{8,12},{12,8},{16,20},{20,16},{24,28},{28,24},{1,5},{5... | collective-permute-start | bytes 1572872 | tf_op jit(solution)/shard_map/ppermute | solution.py:338
  352.4 15.4 %collective-permute-start.19 = (bf16[16,2,32,256]{3,2,1,0:T(8,128)(2,1)}, bf16[16,2,32,256]{3,2,1,0:T(8,128)(2,1)S(1)}, u32[]{:S(2)}, u32[]{:S(2)}) collective-permute-start(bf16[16,2,32,256]{3,2,1,0:T(8,128)(2,1)} %get-tuple-element.119.refs_1_), channel_id=1, source_target_pairs={{12,4},{0,8},{20,12},{8,16},{28,20},{16,24},{13,5},{1,9},{21,13},{... | collective-permute-start | bytes 1572872 | tf_op jit(solution)/shard_map/ppermute | solution.py:344
  379.0 68.5 %copy-start.12 = (bf16[2,256,256]{2,1,0:T(8,128)(2,1)S(1)}, bf16[2,256,256]{2,1,0:T(8,128)(2,1)}, u32[]{:S(2)}) copy-start(bf16[2,256,256]{2,1,0:T(8,128)(2,1)} %constant.38.clone.turn) | copy-start | bytes 786436
  379.1 52.6 %copy-start.81 = (s32[2]{0:T(128)S(1)}, s32[2]{0:T(128)}, u32[]{:S(2)}) copy-start(s32[2]{0:T(128)} %copy-done.80) | copy-start | bytes 28
  398.0 29.3 %all-to-all-start.6 = ((bf16[32,4,32,256]{3,2,1,0:T(8,128)(2,1)}), bf16[32,4,32,256]{3,2,1,0:T(8,128)(2,1)S(1)}, u32[]{:S(2)}, u32[]{:S(2)}) async-start(bf16[32,4,32,256]{3,2,1,0:T(8,128)(2,1)} %copy-done.52), calls=%async_computation.6 | async-start | bytes 4194304 | tf_op jit(solution)/shard_map/all_to_all | solution.py:347
  401.6 45.9 %collective-permute-start.20 = (bf16[32,2,32,256]{3,2,1,0:T(8,128)(2,1)}, bf16[32,2,32,256]{3,2,1,0:T(8,128)(2,1)}, u32[]{:S(2)}, u32[]{:S(2)}) collective-permute-start(bf16[32,2,32,256]{3,2,1,0:T(8,128)(2,1)} %copy-done.36), channel_id=1, source_target_pairs={{0,4},{4,0},{8,12},{12,8},{16,20},{20,16},{24,28},{28,24},{1,5},{5... | collective-permute-start | bytes 3145736 | tf_op jit(solution)/shard_map/ppermute | solution.py:338
  427.2 24.2 %copy-start.49 = (bf16[352,128]{1,0:T(8,128)(2,1)S(1)}, bf16[352,128]{1,0:T(8,128)(2,1)}, u32[]{:S(2)}) copy-start(bf16[352,128]{1,0:T(8,128)(2,1)} %pad.16.clone.basis) | copy-start | bytes 270340
  427.2 30.3 %all-to-all-start.11 = ((bf16[32,2,32,256]{3,2,1,0:T(8,128)(2,1)}), bf16[32,2,32,256]{3,2,1,0:T(8,128)(2,1)}, u32[]{:S(2)}, u32[]{:S(2)}) async-start(bf16[32,2,32,256]{3,2,1,0:T(8,128)(2,1)} %copy-done.55), calls=%async_computation.11 | async-start | bytes 2097152 | tf_op jit(solution)/shard_map/all_to_all | solution.py:347
  469.5 18.0 %all-to-all-start.10 = ((bf16[32,2,32,256]{3,2,1,0:T(8,128)(2,1)}), bf16[32,2,32,256]{3,2,1,0:T(8,128)(2,1)S(1)}, u32[]{:S(2)}, u32[]{:S(2)}) async-start(bf16[32,2,32,256]{3,2,1,0:T(8,128)(2,1)} %get-tuple-element.131), calls=%async_computation.10 | async-start | bytes 2097152 | tf_op jit(solution)/shard_map/all_to_all | solution.py:347
  473.0 26.3 %collective-permute-start.21 = (bf16[32,2,32,256]{3,2,1,0:T(8,128)(2,1)}, bf16[32,2,32,256]{3,2,1,0:T(8,128)(2,1)}, u32[]{:S(2)}, u32[]{:S(2)}) collective-permute-start(bf16[32,2,32,256]{3,2,1,0:T(8,128)(2,1)} %get-tuple-element.135), channel_id=1, source_target_pairs={{0,4},{4,0},{8,12},{12,8},{16,20},{20,16},{24,28},{28,24},{1,5},{5... | collective-permute-start | bytes 3145736 | tf_op jit(solution)/shard_map/ppermute | solution.py:338
  487.4 18.3 %all-to-all-start.13 = ((bf16[32,2,32,256]{3,2,1,0:T(8,128)(2,1)}), bf16[32,2,32,256]{3,2,1,0:T(8,128)(2,1)S(1)}, u32[]{:S(2)}, u32[]{:S(2)}) async-start(bf16[32,2,32,256]{3,2,1,0:T(8,128)(2,1)} %copy-done.57), calls=%async_computation.13 | async-start | bytes 2097152 | tf_op jit(solution)/shard_map/all_to_all | solution.py:347
  492.1 29.7 %collective-permute-start.22 = (bf16[32,2,32,256]{3,2,1,0:T(8,128)(2,1)S(1)}, bf16[32,2,32,256]{3,2,1,0:T(8,128)(2,1)}, u32[]{:S(2)}, u32[]{:S(2)}) collective-permute-start(bf16[32,2,32,256]{3,2,1,0:T(8,128)(2,1)S(1)} %get-tuple-element.141), channel_id=1, source_target_pairs={{0,4},{4,0},{8,12},{12,8},{16,20},{20,16},{24,28},{28,24},{1,5},{5... | collective-permute-start | bytes 3145736 | tf_op jit(solution)/shard_map/ppermute | solution.py:338
  504.4 28.2 %collective-permute-start.23 = (bf16[16,2,32,256]{3,2,1,0:T(8,128)(2,1)S(1)}, bf16[16,2,32,256]{3,2,1,0:T(8,128)(2,1)}, u32[]{:S(2)}, u32[]{:S(2)}) collective-permute-start(bf16[16,2,32,256]{3,2,1,0:T(8,128)(2,1)S(1)} %get-tuple-element.145), channel_id=1, source_target_pairs={{0,4},{4,0},{8,12},{12,8},{16,20},{20,16},{24,28},{28,24},{1,5},{5... | collective-permute-start | bytes 1572872 | tf_op jit(solution)/shard_map/ppermute | solution.py:338
  505.8 19.7 %all-to-all-start.14 = ((bf16[16,2,32,256]{3,2,1,0:T(8,128)(2,1)}), bf16[16,2,32,256]{3,2,1,0:T(8,128)(2,1)S(1)}, u32[]{:S(2)}, u32[]{:S(2)}) async-start(bf16[16,2,32,256]{3,2,1,0:T(8,128)(2,1)} %copy-done.65), calls=%async_computation.14 | async-start | bytes 1048576 | tf_op jit(solution)/shard_map/all_to_all | solution.py:347
  (82 other events, 346.5 us)

commit v5 on v3

--- a/solution.py
+++ b/solution.py
@@ -11,6 +11,7 @@
 F32, BF16 = jnp.float32, jnp.bfloat16
 ANY = pl.BlockSpec(memory_space=pl.ANY)
 VMEM = pl.BlockSpec(memory_space=pltpu.VMEM)
+HBM = pl.BlockSpec(memory_space=pltpu.HBM)
 SMEM = pl.BlockSpec(memory_space=pltpu.SMEM)
 TOKEN = jax.ShapeDtypeStruct((2,), jnp.int32)
 COST = pl.CostEstimate(flops=1, bytes_accessed=1, transcendentals=0)
@@ -77,7 +78,7 @@
     return pl.pallas_call(
         functools.partial(spread_kernel, begin=begin, skip=skip),
         out_shape=(piece, piece, TOKEN),
-        in_specs=[SMEM, ANY, VMEM] + [ANY] * len(after),
+        in_specs=[SMEM, HBM, VMEM] + [ANY] * len(after),
         out_specs=(VMEM, VMEM, SMEM),
         scratch_shapes=[
             pltpu.VMEM((2, planes, modes, depth, cols), BF16),
@@ -87,6 +88,27 @@
         cost_estimate=COST,
         name="spread",
     )(pos, field, turn, *after)
+
+
+def take_kernel(pos, both, *refs):
+    out, token, sem = refs[-3:]
+    token[0], token[1] = pos[0], pos[1]
+    copy = pltpu.make_async_copy(both.at[1 - pos[0]], out, sem)
+    copy.start()
+    copy.wait()
+
+
+def take(pos, both, after):
+    return pl.pallas_call(
+        take_kernel,
+        out_shape=(jax.ShapeDtypeStruct(both.shape[1:], both.dtype), TOKEN),
+        in_specs=[SMEM, HBM] + [ANY] * len(after),
+        out_specs=(VMEM, SMEM),
+        scratch_shapes=[pltpu.SemaphoreType.DMA],
+        compiler_params=params(4),
+        cost_estimate=COST,
+        name="take",
+    )(pos, both, *after)
 
 
 def sweep_kernel(pos, rate, shift, *refs, begin, count, heads):
@@ -280,7 +302,7 @@
     _, rows, planes, modes, cols = both.shape
     size = out.shape[2]
     group = turn.shape[1] // TILE
-    incoming = [pltpu.make_async_copy(other, both.at[1], sems.at[count])]
+    incoming = [pltpu.make_async_copy(other.at[1 - side], both.at[1], sems.at[count])]
     for k in range(count):
         base = jnp.bitwise_xor(pos[1], k) * part
         incoming.append(
@@ -314,13 +336,13 @@
 
 def settle(pos, turn, result, blocks, other, begin, shape):
     count = len(blocks)
-    rows, planes, modes, cols = other.shape
+    rows, planes, modes, cols = other.shape[1:]
     chained = result is not None
     return pl.pallas_call(
         functools.partial(settle_kernel, begin=begin, count=count, chained=chained),
         out_shape=(jax.ShapeDtypeStruct(shape, BF16), TOKEN),
-        in_specs=[SMEM, VMEM] + [ANY] * (count + 1 + chained),
-        out_specs=(ANY, SMEM),
+        in_specs=[SMEM, VMEM] + [HBM] * chained + [ANY] * count + [HBM],
+        out_specs=(HBM, SMEM),
         scratch_shapes=[
             pltpu.VMEM((2, rows, planes, modes, cols), BF16),
             pltpu.VMEM((2, planes, modes, rows, cols), BF16),
@@ -338,13 +360,13 @@
     return [unit, 2 * unit, 2 * unit, 2 * unit, unit]
 
 
-ORDER = (
-    ("T", 0), ("T", 1), ("T", 2), ("S", 0), ("T", 3),
-    ("T", 4), ("P", 0), ("S", 1), ("C", 0), ("S", 2),
-    ("P", 1), ("F", 0), ("S", 3), ("P", 2), ("S", 4),
-    ("C", 1), ("P", 3), ("F", 1), ("C", 2), ("P", 4),
-    ("F", 2), ("C", 3), ("F", 3), ("C", 4), ("F", 4),
-)
+def pipeline(chunks):
+    stage = {"T": 0, "R": 1, "S": 2, "P": 3, "C": 4, "F": 5}
+    for iteration in range(chunks + 5):
+        for kind in "SPTRCF":
+            c = iteration - stage[kind]
+            if 0 <= c < chunks:
+                yield kind, c
 
 
 def turns(group):
@@ -373,8 +395,16 @@
     def across(x):
         return lax.ppermute(x, "space", swap)
 
-    def halo(own, other):
-        return lax.ppermute(own, "space", ahead), lax.ppermute(other, "space", back)
+    pairs = [[i, i + 1] for i in range(0, spaces, 2)]
+
+    def both_of(x):
+        return lax.all_gather(x, "space", axis_index_groups=pairs)
+
+    def ahead_of(x):
+        return lax.ppermute(x, "space", ahead)
+
+    def behind_of(x):
+        return lax.ppermute(x, "space", back)
 
     def exchange(pieces):
         moved = [pieces[0]]
@@ -405,9 +435,9 @@
 
     rows_of = chunk_rows(half)
     begins = [sum(rows_of[:c]) for c in range(len(rows_of))]
-    own, other, blocks, cells, home, theirs = {}, {}, {}, {}, {}, {}
+    own, other, before, blocks, cells, home, theirs = {}, {}, {}, {}, {}, {}, {}
     result = None
-    for kind, c in ORDER:
+    for kind, c in pipeline(len(rows_of)):
         begin, rows = begins[c], rows_of[c]
         if kind == "T":
             skip = EDGE if c else 0
@@ -416,17 +446,20 @@
                 own_rate, send_rate = logical(diffusion, half + EDGE, pos[0], F32)
                 own_load, send_load = logical(joule, half, pos[0], BF16)
                 other_rate, other_load = across(send_rate), across(send_load)
-                before, behind = halo(own_rate[-1:], other_rate[:1])
-                rate = jnp.concatenate([before, other_rate, own_rate, behind], axis=0)
+                after = (send_rate, send_load)
+            own[c], send, pos = spread(pos, field, to_rows, after, begin, skip, rows + EDGE - skip, rows + TILE)
+            other[c] = both_of(send)
+            before[c] = ahead_of(own[c])
+        elif kind == "R":
+            after = (before[c],)
+            if c == 0:
+                after = (before[c], other_rate, other_load)
+                edges = ahead_of(own_rate[-1:]), behind_of(other_rate[:1])
+                rate = jnp.concatenate([edges[0], other_rate, own_rate, edges[1]], axis=0)
                 rate = jnp.pad(rate, ((0, 0), (1, -(half + EDGE + 1) % 8), (0, 0)))
                 load = jnp.concatenate([other_load.astype(F32), own_load], axis=0)
-                after = (send_rate, send_load)
-            elif c == 2:
-                after = (blocks[0][0], other_load)
-            own[c], send, pos = spread(pos, field, to_rows, after, begin, skip, rows + EDGE - skip, rows + TILE)
-            other[c] = across(send)
-            before, after = halo(own[c], other[c])
-            blocks[c] = (before, other[c], own[c], after)
+            other[c], pos = take(pos, other[c], after)
+            blocks[c] = (before[c], other[c], own[c], behind_of(other[c]))
         elif kind == "S":
             *pieces, pos = sweep(pos, rate, shift, blocks[c], blocks.get(c - 1, ()), begin, rows, count)
             cells[c] = exchange(pieces)
@@ -435,7 +468,7 @@
             home[c] = exchange(stepped)
         elif kind == "C":
             out, pos = collect(pos, home[c])
-            theirs[c] = across(out)
+            theirs[c] = both_of(out)
         else:
             result, pos = settle(pos, to_modes, result, home[c], theirs[c], begin, field.shape)
     return result

time: 359 us -> 447 us (1.25)
  local copies, waits for them, and re-layouts: 23.1 us -> 76 us
  waiting for transfers between devices: 140 us -> 157 us
  Pallas kernels: 120 us -> 135 us
  between operations: 1.1 us -> 15.4 us
  starting transfers between devices: 71 us -> 59.5 us
    unnamed x54 -> x300, local copies, waits for them, and re-layouts: 19.1 us -> 72 us
    ppermute x12, waiting for transfers between devices: 1.31 us -> 50.9 us  [the longest x6 47.1 us: behind_of(): return lax.ppermute(x, 'space', back)]
    ppermute x12 -> x2, waiting for transfers between devices: 58.9 us -> 18.1 us  [across(): return lax.ppermute(x, 'space', swap)]
    all_gather x0 -> x10, waiting for transfers between devices: none -> 32.6 us  [both_of(): return lax.all_gather(x, 'space', axis_index_groups=pairs)]
    ppermute x30, waiting for transfers between devices: 80 us -> 55.3 us  [exchange(): lax.ppermute(pieces[k], 'modes', [(j, j ^ k) for j in range(count)])]
    ppermute x12 -> x2, starting transfers between devices: 17.3 us -> 5.31 us  [across(): return lax.ppermute(x, 'space', swap)]
    pallas_call x0 -> x5, Pallas kernels: none -> 6.91 us  [take(): pl.pallas_call(take_kernel, out_shape=(jax.ShapeDtypeStruct(both.shape[1:...]
  transfers between devices with their start and end apart: 54 -> 54, of which waited for: 16 -> 17; matrix products, arithmetic and copies ran while one was open for 2% -> 1% of each run, Pallas kernels for 31% -> 29%
where the time goes in v5:
time: 447 us; the launch traced here: 445 us
  waiting for transfers between devices  157 us (35%)
  Pallas kernels  135 us (30%)
  local copies, waits for them, and re-layouts  76 us (17%)
  starting transfers between devices  59.5 us (13%)
  between operations  15.4 us (3%)
    unnamed x300, local copies, waits for them, and re-layouts  72 us
    ppermute x30, waiting for transfers between devices, exchange(): lax.ppermute(pieces[k], 'modes', [(j, j ^ k) for j in range(count)])  55.3 us
    ppermute x6, waiting for transfers between devices, behind_of(): return lax.ppermute(x, 'space', back)  47.1 us
    pallas_call x5, Pallas kernels, points(): pl.pallas_call(functools.partial(points_kernel, begin=begin), out_shape=t...  46.4 us
    pallas_call x5, Pallas kernels, sweep(): pl.pallas_call(functools.partial(sweep_kernel, begin=begin, count=count,...  41.4 us
    all_gather x10, waiting for transfers between devices, both_of(): return lax.all_gather(x, 'space', axis_index_groups=pairs)  32.6 us
    ppermute x6, starting transfers between devices, behind_of(): return lax.ppermute(x, 'space', back)  24.9 us
    ppermute x30, starting transfers between devices, exchange(): lax.ppermute(pieces[k], 'modes', [(j, j ^ k) for j in range(count)])  20.8 us
  transfers between devices with their start and end apart: 54, of which 17 were waited for; matrix products, arithmetic and copies ran while one was open for 1% of the time, Pallas kernels for 29%

profile of v5, /device:TPU:0, one launch (start us, length us, event | category | flops | bytes accessed | tf_op | source)
XLA Modules:
  0.0 444.6 jit_solution(14653239832787315748)
XLA Ops:
  6.6 3.4 copy-done
  16.0 3.4 copy-done.1
  19.4 3.1 spread.6
  23.9 5.2 %collective-permute-start.1 = (f32[2,130,256]{2,1,0:T(8,128)S(1)}, f32[2,130,256]{2,1,0:T(8,128)S(1)}, u32[]{:S(2)}, u32[]{:S(2)}) collective-permute-start(f32[2,130,256]{2,1,0:T(8,128)S(1)} %get-tuple-element.196.refs_0_), channel_id=1, source_target_pairs={{0,4},{4,0},{8,12},{12,8},{16,20},{20,16},{24,28},{28,24},{1,5},{5... | collective-permute-start | bytes 798728 | tf_op jit(solution)/shard_map/ppermute | solution.py:396
  29.2 18.1 %collective-permute-done.2.refs_2_ = bf16[2,128,256]{2,1,0:T(8,128)(2,1)S(1)} collective-permute-done((bf16[2,128,256]{2,1,0:T(8,128)(2,1)S(1)}, bf16[2,128,256]{2,1,0:T(8,128)(2,1)S(1)}, u32[]{:S(2)}, u32[]{:S(2)}) %collective-permute-start.2) | collective-permute-done | bytes 131104 | tf_op jit(solution)/shard_map/ppermute | solution.py:396
  50.1 3.4 collective-permute-start.5
  55.8 4.6 %collective-permute-start.4 = (f32[1,130,256]{2,1,0:T(8,128)S(1)}, f32[1,130,256]{2,1,0:T(8,128)S(1)}, u32[]{:S(2)}, u32[]{:S(2)}) collective-permute-start(f32[1,130,256]{2,1,0:T(8,128)S(1)} %slice.46), channel_id=1, source_target_pairs={{12,4},{0,8},{20,12},{8,16},{28,20},{16,24},{13,5},{1,9},{21,13},{... | collective-permute-start | bytes 399368 | tf_op jit(solution)/shard_map/ppermute | solution.py:407
  61.7 7.2 %collective-permute-done.4 = f32[1,130,256]{2,1,0:T(8,128)S(1)} collective-permute-done((f32[1,130,256]{2,1,0:T(8,128)S(1)}, f32[1,130,256]{2,1,0:T(8,128)S(1)}, u32[]{:S(2)}, u32[]{:S(2)}) %collective-permute-start.4) | collective-permute-done | bytes 133152 | tf_op jit(solution)/shard_map/ppermute | solution.py:407
  70.0 5.3 %sweep.5 = (bf16[4,4,32,256]{3,2,1,0:T(8,128)(2,1)S(1)}, bf16[4,4,32,256]{3,2,1,0:T(8,128)(2,1)}, bf16[4,4,32,256]{3,2,1,0:T(8,128)(2,1)}, bf16[4,4,32,256]{3,2,1,0:T(8,128)(2,1)}, s32[2]{0:T(128)S(1)}) custom-call(s32[2]{0:T(128)S(1)} %get-tuple-element.103.pos, f32[6,136,256]{2,1,0:T(8,128)S(1)} %select_maximum_fusion.rate, ...), custom_call_target="tpu_custom_call" | custom-call | flops 1 | bytes 1 | tf_op jit(solution)/shard_map/sweep/pallas_call | solution.py:205
  75.3 3.5 copy-done.2
  78.8 2.7 spread.7
  82.6 3.8 collective-permute-done.6.refs_0_.refs_4_
  90.4 4.4 collective-permute-start.7
  100.6 14.0 %collective-permute-done.7.refs_3_.refs_7_ = bf16[32,2,32,256]{3,2,1,0:T(8,128)(2,1)} collective-permute-done((bf16[32,2,32,256]{3,2,1,0:T(8,128)(2,1)}, bf16[32,2,32,256]{3,2,1,0:T(8,128)(2,1)}, u32[]{:S(2)}, u32[]{:S(2)}) %collective-permute-start.7) | collective-permute-done | bytes 1048608 | tf_op jit(solution)/shard_map/ppermute | solution.py:407
  119.8 10.1 %sweep.6 = (bf16[8,4,32,256]{3,2,1,0:T(8,128)(2,1)S(1)}, bf16[8,4,32,256]{3,2,1,0:T(8,128)(2,1)S(1)}, bf16[8,4,32,256]{3,2,1,0:T(8,128)(2,1)S(1)}, bf16[8,4,32,256]{3,2,1,0:T(8,128)(2,1)S(1)}, s32[2]{0:T(128)S(1)}) custom-call(s32[2]{0:T(128)S(1)} %copy-done.105, f32[6,136,256]{2,1,0:T(8,128)S(1)} %select_maximum_fusion.rate, ...), custom_call_target="tpu_custom_call" | custom-call | flops 1 | bytes 1 | tf_op jit(solution)/shard_map/sweep/pallas_call | solution.py:205
  130.3 5.9 %points.5 = (bf16[4,4,32,256]{3,2,1,0:T(8,128)(2,1)S(1)}, bf16[4,4,32,256]{3,2,1,0:T(8,128)(2,1)S(1)}, bf16[4,4,32,256]{3,2,1,0:T(8,128)(2,1)S(1)}, bf16[4,4,32,256]{3,2,1,0:T(8,128)(2,1)S(1)}, s32[2]{0:T(128)S(1)}) custom-call(s32[2]{0:T(128)S(1)} %get-tuple-element.111.pos, bf16[352,128]{1,0:T(8,128)(2,1)S(1)} %copy-done.36, ...), custom_call_target="tpu_custom_call" | custom-call | flops 1 | bytes 1 | tf_op jit(solution)/shard_map/points/pallas_call | solution.py:251
  137.6 3.6 copy-done.3
  141.2 2.7 spread.8
  147.9 4.6 %collective-permute-start.12 = (bf16[32,2,32,256]{3,2,1,0:T(8,128)(2,1)S(1)}, bf16[32,2,32,256]{3,2,1,0:T(8,128)(2,1)S(1)}, u32[]{:S(2)}, u32[]{:S(2)}) collective-permute-start(bf16[32,2,32,256]{3,2,1,0:T(8,128)(2,1)S(1)} %get-tuple-element.121.refs_1_.refs_5_), channel_id=1, source_target_pairs={{12,4},{0,8},{20,12},{8,16},{28,20},{16,24},{13,5},{1,9},{21,13},{... | collective-permute-start | bytes 3145736 | tf_op jit(solution)/shard_map/ppermute | solution.py:407
  155.9 16.0 %collective-permute-done.12.refs_3_.refs_7_ = bf16[32,2,32,256]{3,2,1,0:T(8,128)(2,1)S(1)} collective-permute-done((bf16[32,2,32,256]{3,2,1,0:T(8,128)(2,1)S(1)}, bf16[32,2,32,256]{3,2,1,0:T(8,128)(2,1)S(1)}, u32[]{:S(2)}, u32[]{:S(2)}) %collective-permute-start.12) | collective-permute-done | bytes 1048608 | tf_op jit(solution)/shard_map/ppermute | solution.py:407
  175.7 10.3 %sweep.7 = (bf16[8,4,32,256]{3,2,1,0:T(8,128)(2,1)S(1)}, bf16[8,4,32,256]{3,2,1,0:T(8,128)(2,1)}, bf16[8,4,32,256]{3,2,1,0:T(8,128)(2,1)}, bf16[8,4,32,256]{3,2,1,0:T(8,128)(2,1)S(1)}, s32[2]{0:T(128)S(1)}) custom-call(s32[2]{0:T(128)S(1)} %get-tuple-element.120.pos, f32[6,136,256]{2,1,0:T(8,128)S(1)} %select_maximum_fusion.rate, ...), custom_call_target="tpu_custom_call" | custom-call | flops 1 | bytes 1 | tf_op jit(solution)/shard_map/sweep/pallas_call | solution.py:205
  186.1 10.6 %points.6 = (bf16[8,4,32,256]{3,2,1,0:T(8,128)(2,1)S(1)}, bf16[8,4,32,256]{3,2,1,0:T(8,128)(2,1)S(1)}, bf16[8,4,32,256]{3,2,1,0:T(8,128)(2,1)S(1)}, bf16[8,4,32,256]{3,2,1,0:T(8,128)(2,1)S(1)}, s32[2]{0:T(128)S(1)}) custom-call(s32[2]{0:T(128)S(1)} %get-tuple-element.122.pos, bf16[352,128]{1,0:T(8,128)(2,1)S(1)} %copy-done.37, ...), custom_call_target="tpu_custom_call" | custom-call | flops 1 | bytes 1 | tf_op jit(solution)/shard_map/points/pallas_call | solution.py:251
  205.0 5.3 %collective-permute-start.20 = (bf16[32,2,32,256]{3,2,1,0:T(8,128)(2,1)}, bf16[32,2,32,256]{3,2,1,0:T(8,128)(2,1)}, u32[]{:S(2)}, u32[]{:S(2)}) collective-permute-start(bf16[32,2,32,256]{3,2,1,0:T(8,128)(2,1)} %get-tuple-element.137.refs_1_.refs_5_), channel_id=1, source_target_pairs={{12,4},{0,8},{20,12},{8,16},{28,20},{16,24},{13,5},{1,9},{21,13},{... | collective-permute-start | bytes 3145736 | tf_op jit(solution)/shard_map/ppermute | solution.py:407
  214.2 5.4 %collective-permute-done.18.refs_2_ = bf16[4,4,32,256]{3,2,1,0:T(8,128)(2,1)S(1)} collective-permute-done((bf16[4,4,32,256]{3,2,1,0:T(8,128)(2,1)S(1)}, bf16[4,4,32,256]{3,2,1,0:T(8,128)(2,1)S(1)}, u32[]{:S(2)}, u32[]{:S(2)}) %collective-permute-start.18) | collective-permute-done | bytes 262176 | tf_op jit(solution)/shard_map/ppermute | solution.py:412
  219.5 4.7 %collective-permute-done.19.refs_3_ = bf16[4,4,32,256]{3,2,1,0:T(8,128)(2,1)S(1)} collective-permute-done((bf16[4,4,32,256]{3,2,1,0:T(8,128)(2,1)S(1)}, bf16[4,4,32,256]{3,2,1,0:T(8,128)(2,1)S(1)}, u32[]{:S(2)}, u32[]{:S(2)}) %collective-permute-start.19) | collective-permute-done | bytes 262176 | tf_op jit(solution)/shard_map/ppermute | solution.py:412
  230.5 6.0 %collective-permute-done.22.refs_2_ = bf16[8,4,32,256]{3,2,1,0:T(8,128)(2,1)} collective-permute-done((bf16[8,4,32,256]{3,2,1,0:T(8,128)(2,1)}, bf16[8,4,32,256]{3,2,1,0:T(8,128)(2,1)}, u32[]{:S(2)}, u32[]{:S(2)}) %collective-permute-start.22) | collective-permute-done | bytes 524320 | tf_op jit(solution)/shard_map/ppermute | solution.py:412
  244.6 9.8 %sweep.8 = (bf16[8,4,32,256]{3,2,1,0:T(8,128)(2,1)S(1)}, bf16[8,4,32,256]{3,2,1,0:T(8,128)(2,1)S(1)}, bf16[8,4,32,256]{3,2,1,0:T(8,128)(2,1)S(1)}, bf16[8,4,32,256]{3,2,1,0:T(8,128)(2,1)S(1)}, s32[2]{0:T(128)S(1)}) custom-call(s32[2]{0:T(128)S(1)} %copy-done.99, f32[6,136,256]{2,1,0:T(8,128)S(1)} %select_maximum_fusion.rate, ...), custom_call_target="tpu_custom_call" | custom-call | flops 1 | bytes 1 | tf_op jit(solution)/shard_map/sweep/pallas_call | solution.py:205
  254.5 11.9 %points.7 = (bf16[8,4,32,256]{3,2,1,0:T(8,128)(2,1)S(1)}, bf16[8,4,32,256]{3,2,1,0:T(8,128)(2,1)S(1)}, bf16[8,4,32,256]{3,2,1,0:T(8,128)(2,1)S(1)}, bf16[8,4,32,256]{3,2,1,0:T(8,128)(2,1)S(1)}, s32[2]{0:T(128)S(1)}) custom-call(s32[2]{0:T(128)S(1)} %get-tuple-element.138.pos, bf16[352,128]{1,0:T(8,128)(2,1)S(1)} %copy-done.38, ...), custom_call_target="tpu_custom_call" | custom-call | flops 1 | bytes 1 | tf_op jit(solution)/shard_map/points/pallas_call | solution.py:251
  276.0 2.3 collect.6
  279.8 2.5 collective-permute-start.28
  284.8 9.9 %collective-permute-done.28.refs_3_ = bf16[16,2,32,256]{3,2,1,0:T(8,128)(2,1)S(1)} collective-permute-done((bf16[16,2,32,256]{3,2,1,0:T(8,128)(2,1)}, bf16[16,2,32,256]{3,2,1,0:T(8,128)(2,1)S(1)}, u32[]{:S(2)}, u32[]{:S(2)}) %collective-permute-start.28) | collective-permute-done | bytes 524320 | tf_op jit(solution)/shard_map/ppermute | solution.py:407
  302.3 2.8 settle.5
  307.3 5.9 %sweep.9 = (bf16[4,4,32,256]{3,2,1,0:T(8,128)(2,1)S(1)}, bf16[4,4,32,256]{3,2,1,0:T(8,128)(2,1)S(1)}, bf16[4,4,32,256]{3,2,1,0:T(8,128)(2,1)S(1)}, bf16[4,4,32,256]{3,2,1,0:T(8,128)(2,1)S(1)}, s32[2]{0:T(128)S(1)}) custom-call(s32[2]{0:T(128)S(1)} %get-tuple-element.153.pos, f32[6,136,256]{2,1,0:T(8,128)S(1)} %select_maximum_fusion.rate, ...), custom_call_target="tpu_custom_call" | custom-call | flops 1 | bytes 1 | tf_op jit(solution)/shard_map/sweep/pallas_call | solution.py:205
  313.3 11.6 %points.8 = (bf16[8,4,32,256]{3,2,1,0:T(8,128)(2,1)S(1)}, bf16[8,4,32,256]{3,2,1,0:T(8,128)(2,1)S(1)}, bf16[8,4,32,256]{3,2,1,0:T(8,128)(2,1)S(1)}, bf16[8,4,32,256]{3,2,1,0:T(8,128)(2,1)S(1)}, s32[2]{0:T(128)S(1)}) custom-call(s32[2]{0:T(128)S(1)} %get-tuple-element.155.pos, bf16[352,128]{1,0:T(8,128)(2,1)S(1)} %copy-done.39, ...), custom_call_target="tpu_custom_call" | custom-call | flops 1 | bytes 1 | tf_op jit(solution)/shard_map/points/pallas_call | solution.py:251
  325.0 5.8 %collective-permute-done.34.refs_3_.refs_4_ = bf16[8,4,32,256]{3,2,1,0:T(8,128)(2,1)} collective-permute-done((bf16[8,4,32,256]{3,2,1,0:T(8,128)(2,1)}, bf16[8,4,32,256]{3,2,1,0:T(8,128)(2,1)}, u32[]{:S(2)}, u32[]{:S(2)}) %collective-permute-start.34) | collective-permute-done | bytes 524320 | tf_op jit(solution)/shard_map/ppermute | solution.py:412
  330.8 2.3 collect.7
  340.4 3.8 settle.6
  344.2 22.8 %collective-permute-done.36.refs_2_ = bf16[4,4,32,256]{3,2,1,0:T(8,128)(2,1)} collective-permute-done((bf16[4,4,32,256]{3,2,1,0:T(8,128)(2,1)}, bf16[4,4,32,256]{3,2,1,0:T(8,128)(2,1)}, u32[]{:S(2)}, u32[]{:S(2)}) %collective-permute-start.36) | collective-permute-done | bytes 262176 | tf_op jit(solution)/shard_map/ppermute | solution.py:412
  367.0 4.4 collective-permute-done.37.refs_3_
  371.4 6.3 %points.9 = (bf16[4,4,32,256]{3,2,1,0:T(8,128)(2,1)S(1)}, bf16[4,4,32,256]{3,2,1,0:T(8,128)(2,1)S(1)}, bf16[4,4,32,256]{3,2,1,0:T(8,128)(2,1)S(1)}, bf16[4,4,32,256]{3,2,1,0:T(8,128)(2,1)S(1)}, s32[2]{0:T(128)S(1)}) custom-call(s32[2]{0:T(128)S(1)} %get-tuple-element.168.pos, bf16[352,128]{1,0:T(8,128)(2,1)S(1)} %copy-done.39, ...), custom_call_target="tpu_custom_call" | custom-call | flops 1 | bytes 1 | tf_op jit(solution)/shard_map/points/pallas_call | solution.py:251
  377.8 2.7 collect.8
  384.3 3.9 settle.7
  388.2 2.3 collective-permute-done.42.refs_2_.refs_3_
  390.5 3.9 collective-permute-done.43.refs_3_.refs_4_
  395.9 15.1 %all-gather.37.cloned.1.call-done = bf16[64,2,32,256]{3,2,1,0:T(8,128)(2,1)} async-done(((bf16[32,2,32,256]{3,2,1,0:T(8,128)(2,1)}), bf16[64,2,32,256]{3,2,1,0:T(8,128)(2,1)}) %all-gather.37.cloned.1.call-update) | async-done | bytes 2097168 | tf_op jit(solution)/shard_map/all_gather | solution.py:401
  412.7 3.8 settle.8
  416.5 17.3 %all-gather.39.cloned.1.call-done = bf16[32,2,32,256]{3,2,1,0:T(8,128)(2,1)} async-done(((bf16[16,2,32,256]{3,2,1,0:T(8,128)(2,1)}), bf16[32,2,32,256]{3,2,1,0:T(8,128)(2,1)}) %all-gather.39.cloned.1.call-update) | async-done | bytes 1048592 | tf_op jit(solution)/shard_map/all_gather | solution.py:401
  435.0 2.7 settle.9
  (422 shorter events, 108.0 us)
Async XLA Ops:
  6.5 40.9 %all-gather.21.cloned.1.call-start = ((), (), s32[]{:S(2)}) async-start(), calls=%async_computation | async-start | bytes 1769472 | tf_op jit(solution)/shard_map/all_gather | solution.py:401
  13.2 73.1 %all-gather.23.cloned.1.call-start = ((), (), s32[]{:S(2)}) async-start(), calls=%async_computation.1 | async-start | bytes 3145728 | tf_op jit(solution)/shard_map/all_gather | solution.py:401
  22.5 122.5 %all-gather.25.cloned.1.call-start = ((), (), s32[]{:S(2)}) async-start(), calls=%async_computation.2 | async-start | bytes 3145728 | tf_op jit(solution)/shard_map/all_gather | solution.py:401
  22.6 24.8 %collective-permute-start = (bf16[18,2,32,256]{3,2,1,0:T(8,128)(2,1)S(1)}, bf16[18,2,32,256]{3,2,1,0:T(8,128)(2,1)S(1)}, u32[]{:S(2)}, u32[]{:S(2)}) collective-permute-start(bf16[18,2,32,256]{3,2,1,0:T(8,128)(2,1)S(1)} %get-tuple-element.102.refs_2_.refs_6_), channel_id=1, source_target_pairs={{4,12},{8,0},{12,20},{16,8},{20,28},{24,16},{5,13},{9,1},{13,21},{... | collective-permute-start | bytes 1769480 | tf_op jit(solution)/shard_map/ppermute | solution.py:404
  23.9 23.4 %collective-permute-start.1 = (f32[2,130,256]{2,1,0:T(8,128)S(1)}, f32[2,130,256]{2,1,0:T(8,128)S(1)}, u32[]{:S(2)}, u32[]{:S(2)}) collective-permute-start(f32[2,130,256]{2,1,0:T(8,128)S(1)} %get-tuple-element.196.refs_0_), channel_id=1, source_target_pairs={{0,4},{4,0},{8,12},{12,8},{16,20},{20,16},{24,28},{28,24},{1,5},{5... | collective-permute-start | bytes 798728 | tf_op jit(solution)/shard_map/ppermute | solution.py:396
  29.1 18.2 %collective-permute-start.2 = (bf16[2,128,256]{2,1,0:T(8,128)(2,1)S(1)}, bf16[2,128,256]{2,1,0:T(8,128)(2,1)S(1)}, u32[]{:S(2)}, u32[]{:S(2)}) collective-permute-start(bf16[2,128,256]{2,1,0:T(8,128)(2,1)S(1)} %select_convert_fusion.refs_1_), channel_id=1, source_target_pairs={{0,4},{4,0},{8,12},{12,8},{16,20},{20,16},{24,28},{28,24},{1,5},{5... | collective-permute-start | bytes 393224 | tf_op jit(solution)/shard_map/ppermute | solution.py:396
  50.1 19.8 %collective-permute-start.5 = (bf16[18,2,32,256]{3,2,1,0:T(8,128)(2,1)S(1)}, bf16[18,2,32,256]{3,2,1,0:T(8,128)(2,1)S(1)}, u32[]{:S(2)}, u32[]{:S(2)}) collective-permute-start(bf16[18,2,32,256]{3,2,1,0:T(8,128)(2,1)S(1)} %get-tuple-element.104.refs_1_.refs_5_), channel_id=1, source_target_pairs={{12,4},{0,8},{20,12},{8,16},{28,20},{16,24},{13,5},{1,9},{21,13},{... | collective-permute-start | bytes 1769480 | tf_op jit(solution)/shard_map/ppermute | solution.py:407
  55.8 13.1 %collective-permute-start.4 = (f32[1,130,256]{2,1,0:T(8,128)S(1)}, f32[1,130,256]{2,1,0:T(8,128)S(1)}, u32[]{:S(2)}, u32[]{:S(2)}) collective-permute-start(f32[1,130,256]{2,1,0:T(8,128)S(1)} %slice.46), channel_id=1, source_target_pairs={{12,4},{0,8},{20,12},{8,16},{28,20},{16,24},{13,5},{1,9},{21,13},{... | collective-permute-start | bytes 399368 | tf_op jit(solution)/shard_map/ppermute | solution.py:407
  60.4 25.9 %collective-permute-start.6 = (bf16[32,2,32,256]{3,2,1,0:T(8,128)(2,1)}, bf16[32,2,32,256]{3,2,1,0:T(8,128)(2,1)S(1)}, u32[]{:S(2)}, u32[]{:S(2)}) collective-permute-start(bf16[32,2,32,256]{3,2,1,0:T(8,128)(2,1)} %get-tuple-element.108.refs_2_.refs_6_), channel_id=1, source_target_pairs={{4,12},{8,0},{12,20},{16,8},{20,28},{24,16},{5,13},{9,1},{13,21},{... | collective-permute-start | bytes 3145736 | tf_op jit(solution)/shard_map/ppermute | solution.py:404
  82.5 118.6 %all-gather.27.cloned.1.call-start = ((), (), s32[]{:S(2)}) async-start(), calls=%async_computation.3 | async-start | bytes 3145728 | tf_op jit(solution)/shard_map/all_gather | solution.py:401
  90.4 24.2 %collective-permute-start.7 = (bf16[32,2,32,256]{3,2,1,0:T(8,128)(2,1)}, bf16[32,2,32,256]{3,2,1,0:T(8,128)(2,1)}, u32[]{:S(2)}, u32[]{:S(2)}) collective-permute-start(bf16[32,2,32,256]{3,2,1,0:T(8,128)(2,1)} %get-tuple-element.110.refs_1_.refs_5_), channel_id=1, source_target_pairs={{12,4},{0,8},{20,12},{8,16},{28,20},{16,24},{13,5},{1,9},{21,13},{... | collective-permute-start | bytes 3145736 | tf_op jit(solution)/shard_map/ppermute | solution.py:407
  97.3 32.6 %collective-permute-start.8 = (bf16[4,4,32,256]{3,2,1,0:T(8,128)(2,1)}, bf16[4,4,32,256]{3,2,1,0:T(8,128)(2,1)S(1)}, u32[]{:S(2)}, u32[]{:S(2)}) collective-permute-start(bf16[4,4,32,256]{3,2,1,0:T(8,128)(2,1)} %get-tuple-element.113), channel_id=1, source_target_pairs={{0,1},{1,0},{2,3},{3,2},{4,5},{5,4},{6,7},{7,6},{8,9},{9,8},{10,11... | collective-permute-start | bytes 786440 | tf_op jit(solution)/shard_map/ppermute | solution.py:412
  97.3 32.6 %collective-permute-start.9 = (bf16[4,4,32,256]{3,2,1,0:T(8,128)(2,1)}, bf16[4,4,32,256]{3,2,1,0:T(8,128)(2,1)S(1)}, u32[]{:S(2)}, u32[]{:S(2)}) collective-permute-start(bf16[4,4,32,256]{3,2,1,0:T(8,128)(2,1)} %get-tuple-element.114), channel_id=1, source_target_pairs={{0,2},{1,3},{2,0},{3,1},{4,6},{5,7},{6,4},{7,5},{8,10},{9,11},{10,... | collective-permute-start | bytes 786440 | tf_op jit(solution)/shard_map/ppermute | solution.py:412
  98.8 31.1 %collective-permute-start.10 = (bf16[4,4,32,256]{3,2,1,0:T(8,128)(2,1)}, bf16[4,4,32,256]{3,2,1,0:T(8,128)(2,1)S(1)}, u32[]{:S(2)}, u32[]{:S(2)}) collective-permute-start(bf16[4,4,32,256]{3,2,1,0:T(8,128)(2,1)} %get-tuple-element.115), channel_id=1, source_target_pairs={{0,3},{1,2},{2,1},{3,0},{4,7},{5,6},{6,5},{7,4},{8,11},{9,10},{10,... | collective-permute-start | bytes 786440 | tf_op jit(solution)/shard_map/ppermute | solution.py:412
  99.3 45.8 %collective-permute-start.11 = (bf16[32,2,32,256]{3,2,1,0:T(8,128)(2,1)}, bf16[32,2,32,256]{3,2,1,0:T(8,128)(2,1)S(1)}, u32[]{:S(2)}, u32[]{:S(2)}) collective-permute-start(bf16[32,2,32,256]{3,2,1,0:T(8,128)(2,1)} %copy-done.21), channel_id=1, source_target_pairs={{4,12},{8,0},{12,20},{16,8},{20,28},{24,16},{5,13},{9,1},{13,21},{... | collective-permute-start | bytes 3145736 | tf_op jit(solution)/shard_map/ppermute | solution.py:404
  145.0 126.1 %all-gather.29.cloned.1.call-start = ((), (), s32[]{:S(2)}) async-start(), calls=%async_computation.4 | async-start | bytes 1572864 | tf_op jit(solution)/shard_map/all_gather | solution.py:401
  147.9 24.1 %collective-permute-start.12 = (bf16[32,2,32,256]{3,2,1,0:T(8,128)(2,1)S(1)}, bf16[32,2,32,256]{3,2,1,0:T(8,128)(2,1)S(1)}, u32[]{:S(2)}, u32[]{:S(2)}) collective-permute-start(bf16[32,2,32,256]{3,2,1,0:T(8,128)(2,1)S(1)} %get-tuple-element.121.refs_1_.refs_5_), channel_id=1, source_target_pairs={{12,4},{0,8},{20,12},{8,16},{28,20},{16,24},{13,5},{1,9},{21,13},{... | collective-permute-start | bytes 3145736 | tf_op jit(solution)/shard_map/ppermute | solution.py:407
  152.5 48.6 %collective-permute-start.16 = (bf16[32,2,32,256]{3,2,1,0:T(8,128)(2,1)}, bf16[32,2,32,256]{3,2,1,0:T(8,128)(2,1)S(1)}, u32[]{:S(2)}, u32[]{:S(2)}) collective-permute-start(bf16[32,2,32,256]{3,2,1,0:T(8,128)(2,1)} %copy-done.24), channel_id=1, source_target_pairs={{4,12},{8,0},{12,20},{16,8},{20,28},{24,16},{5,13},{9,1},{13,21},{... | collective-permute-start | bytes 3145736 | tf_op jit(solution)/shard_map/ppermute | solution.py:404
  154.0 32.1 %collective-permute-start.13 = (bf16[8,4,32,256]{3,2,1,0:T(8,128)(2,1)}, bf16[8,4,32,256]{3,2,1,0:T(8,128)(2,1)S(1)}, u32[]{:S(2)}, u32[]{:S(2)}) collective-permute-start(bf16[8,4,32,256]{3,2,1,0:T(8,128)(2,1)} %copy-done.120), channel_id=1, source_target_pairs={{0,1},{1,0},{2,3},{3,2},{4,5},{5,4},{6,7},{7,6},{8,9},{9,8},{10,11... | collective-permute-start | bytes 1572872 | tf_op jit(solution)/shard_map/ppermute | solution.py:412
  154.1 32.0 %collective-permute-start.14 = (bf16[8,4,32,256]{3,2,1,0:T(8,128)(2,1)}, bf16[8,4,32,256]{3,2,1,0:T(8,128)(2,1)S(1)}, u32[]{:S(2)}, u32[]{:S(2)}) collective-permute-start(bf16[8,4,32,256]{3,2,1,0:T(8,128)(2,1)} %copy-done.119), channel_id=1, source_target_pairs={{0,2},{1,3},{2,0},{3,1},{4,6},{5,7},{6,4},{7,5},{8,10},{9,11},{10,... | collective-permute-start | bytes 1572872 | tf_op jit(solution)/shard_map/ppermute | solution.py:412
  155.7 30.4 %collective-permute-start.15 = (bf16[8,4,32,256]{3,2,1,0:T(8,128)(2,1)}, bf16[8,4,32,256]{3,2,1,0:T(8,128)(2,1)S(1)}, u32[]{:S(2)}, u32[]{:S(2)}) collective-permute-start(bf16[8,4,32,256]{3,2,1,0:T(8,128)(2,1)} %copy-done.117), channel_id=1, source_target_pairs={{0,3},{1,2},{2,1},{3,0},{4,7},{5,6},{6,5},{7,4},{8,11},{9,10},{10,... | collective-permute-start | bytes 1572872 | tf_op jit(solution)/shard_map/ppermute | solution.py:412
  201.0 96.5 %all-gather.31.cloned.1.call-start = ((), (), s32[]{:S(2)}) async-start(), calls=%async_computation.5 | async-start | bytes 1572864 | tf_op jit(solution)/shard_map/all_gather | solution.py:401
  205.0 33.1 %collective-permute-start.20 = (bf16[32,2,32,256]{3,2,1,0:T(8,128)(2,1)}, bf16[32,2,32,256]{3,2,1,0:T(8,128)(2,1)}, u32[]{:S(2)}, u32[]{:S(2)}) collective-permute-start(bf16[32,2,32,256]{3,2,1,0:T(8,128)(2,1)} %get-tuple-element.137.refs_1_.refs_5_), channel_id=1, source_target_pairs={{12,4},{0,8},{20,12},{8,16},{28,20},{16,24},{13,5},{1,9},{21,13},{... | collective-permute-start | bytes 3145736 | tf_op jit(solution)/shard_map/ppermute | solution.py:407
  212.0 12.2 %collective-permute-start.19 = (bf16[4,4,32,256]{3,2,1,0:T(8,128)(2,1)S(1)}, bf16[4,4,32,256]{3,2,1,0:T(8,128)(2,1)S(1)}, u32[]{:S(2)}, u32[]{:S(2)}) collective-permute-start(bf16[4,4,32,256]{3,2,1,0:T(8,128)(2,1)S(1)} %copy-done.123), channel_id=1, source_target_pairs={{0,3},{1,2},{2,1},{3,0},{4,7},{5,6},{6,5},{7,4},{8,11},{9,10},{10,... | collective-permute-start | bytes 786440 | tf_op jit(solution)/shard_map/ppermute | solution.py:412
  212.2 18.2 %collective-permute-start.21 = (bf16[8,4,32,256]{3,2,1,0:T(8,128)(2,1)}, bf16[8,4,32,256]{3,2,1,0:T(8,128)(2,1)}, u32[]{:S(2)}, u32[]{:S(2)}) collective-permute-start(bf16[8,4,32,256]{3,2,1,0:T(8,128)(2,1)} %get-tuple-element.140), channel_id=1, source_target_pairs={{0,1},{1,0},{2,3},{3,2},{4,5},{5,4},{6,7},{7,6},{8,9},{9,8},{10,11... | collective-permute-start | bytes 1572872 | tf_op jit(solution)/shard_map/ppermute | solution.py:412
  212.6 23.9 %collective-permute-start.22 = (bf16[8,4,32,256]{3,2,1,0:T(8,128)(2,1)}, bf16[8,4,32,256]{3,2,1,0:T(8,128)(2,1)}, u32[]{:S(2)}, u32[]{:S(2)}) collective-permute-start(bf16[8,4,32,256]{3,2,1,0:T(8,128)(2,1)} %get-tuple-element.141), channel_id=1, source_target_pairs={{0,2},{1,3},{2,0},{3,1},{4,6},{5,7},{6,4},{7,5},{8,10},{9,11},{10,... | collective-permute-start | bytes 1572872 | tf_op jit(solution)/shard_map/ppermute | solution.py:412
  227.1 111.5 %all-gather.33.cloned.1.call-start = ((), (), s32[]{:S(2)}) async-start(), calls=%async_computation.6 | async-start | bytes 3145728 | tf_op jit(solution)/shard_map/all_gather | solution.py:401
  227.1 27.3 %collective-permute-start.23 = (bf16[8,4,32,256]{3,2,1,0:T(8,128)(2,1)}, bf16[8,4,32,256]{3,2,1,0:T(8,128)(2,1)S(1)}, u32[]{:S(2)}, u32[]{:S(2)}) collective-permute-start(bf16[8,4,32,256]{3,2,1,0:T(8,128)(2,1)} %copy-done.109), channel_id=1, source_target_pairs={{0,3},{1,2},{2,1},{3,0},{4,7},{5,6},{6,5},{7,4},{8,11},{9,10},{10,... | collective-permute-start | bytes 1572872 | tf_op jit(solution)/shard_map/ppermute | solution.py:412
  229.1 41.1 %collective-permute-start.24 = (bf16[16,2,32,256]{3,2,1,0:T(8,128)(2,1)}, bf16[16,2,32,256]{3,2,1,0:T(8,128)(2,1)S(1)}, u32[]{:S(2)}, u32[]{:S(2)}) collective-permute-start(bf16[16,2,32,256]{3,2,1,0:T(8,128)(2,1)} %copy-done.76), channel_id=1, source_target_pairs={{4,12},{8,0},{12,20},{16,8},{20,28},{24,16},{5,13},{9,1},{13,21},{... | collective-permute-start | bytes 1572872 | tf_op jit(solution)/shard_map/ppermute | solution.py:404
  230.4 45.6 %collective-permute-start.25 = (bf16[8,4,32,256]{3,2,1,0:T(8,128)(2,1)}, bf16[8,4,32,256]{3,2,1,0:T(8,128)(2,1)}, u32[]{:S(2)}, u32[]{:S(2)}) collective-permute-start(bf16[8,4,32,256]{3,2,1,0:T(8,128)(2,1)} %copy-done.108), channel_id=1, source_target_pairs={{0,1},{1,0},{2,3},{3,2},{4,5},{5,4},{6,7},{7,6},{8,9},{9,8},{10,11... | collective-permute-start | bytes 1572872 | tf_op jit(solution)/shard_map/ppermute | solution.py:412
  236.5 39.5 %collective-permute-start.26 = (bf16[8,4,32,256]{3,2,1,0:T(8,128)(2,1)}, bf16[8,4,32,256]{3,2,1,0:T(8,128)(2,1)}, u32[]{:S(2)}, u32[]{:S(2)}) collective-permute-start(bf16[8,4,32,256]{3,2,1,0:T(8,128)(2,1)} %copy-done.107), channel_id=1, source_target_pairs={{0,2},{1,3},{2,0},{3,1},{4,6},{5,7},{6,4},{7,5},{8,10},{9,11},{10,... | collective-permute-start | bytes 1572872 | tf_op jit(solution)/shard_map/ppermute | solution.py:412
  238.1 37.9 %collective-permute-start.27 = (bf16[8,4,32,256]{3,2,1,0:T(8,128)(2,1)}, bf16[8,4,32,256]{3,2,1,0:T(8,128)(2,1)}, u32[]{:S(2)}, u32[]{:S(2)}) collective-permute-start(bf16[8,4,32,256]{3,2,1,0:T(8,128)(2,1)} %copy-done.106), channel_id=1, source_target_pairs={{0,3},{1,2},{2,1},{3,0},{4,7},{5,6},{6,5},{7,4},{8,11},{9,10},{10,... | collective-permute-start | bytes 1572872 | tf_op jit(solution)/shard_map/ppermute | solution.py:412
  279.8 102.8 %all-gather.35.cloned.1.call-start = ((), (), s32[]{:S(2)}) async-start(), calls=%async_computation.7 | async-start | bytes 3145728 | tf_op jit(solution)/shard_map/all_gather | solution.py:401
  279.8 14.9 %collective-permute-start.28 = (bf16[16,2,32,256]{3,2,1,0:T(8,128)(2,1)}, bf16[16,2,32,256]{3,2,1,0:T(8,128)(2,1)S(1)}, u32[]{:S(2)}, u32[]{:S(2)}) collective-permute-start(bf16[16,2,32,256]{3,2,1,0:T(8,128)(2,1)} %copy-done.78), channel_id=1, source_target_pairs={{12,4},{0,8},{20,12},{8,16},{28,20},{16,24},{13,5},{1,9},{21,13},{... | collective-permute-start | bytes 1572872 | tf_op jit(solution)/shard_map/ppermute | solution.py:407
  282.4 13.4 %collective-permute-start.29 = (bf16[8,4,32,256]{3,2,1,0:T(8,128)(2,1)}, bf16[8,4,32,256]{3,2,1,0:T(8,128)(2,1)S(1)}, u32[]{:S(2)}, u32[]{:S(2)}) collective-permute-start(bf16[8,4,32,256]{3,2,1,0:T(8,128)(2,1)} %copy-done.121), channel_id=1, source_target_pairs={{0,1},{1,0},{2,3},{3,2},{4,5},{5,4},{6,7},{7,6},{8,9},{9,8},{10,11... | collective-permute-start | bytes 1572872 | tf_op jit(solution)/shard_map/ppermute | solution.py:412
  282.9 42.1 %collective-permute-start.32 = (bf16[8,4,32,256]{3,2,1,0:T(8,128)(2,1)}, bf16[8,4,32,256]{3,2,1,0:T(8,128)(2,1)}, u32[]{:S(2)}, u32[]{:S(2)}) collective-permute-start(bf16[8,4,32,256]{3,2,1,0:T(8,128)(2,1)} %copy-done.112), channel_id=1, source_target_pairs={{0,1},{1,0},{2,3},{3,2},{4,5},{5,4},{6,7},{7,6},{8,9},{9,8},{10,11... | collective-permute-start | bytes 1572872 | tf_op jit(solution)/shard_map/ppermute | solution.py:412
  283.0 30.3 %collective-permute-start.30 = (bf16[8,4,32,256]{3,2,1,0:T(8,128)(2,1)}, bf16[8,4,32,256]{3,2,1,0:T(8,128)(2,1)}, u32[]{:S(2)}, u32[]{:S(2)}) collective-permute-start(bf16[8,4,32,256]{3,2,1,0:T(8,128)(2,1)} %copy-done.114), channel_id=1, source_target_pairs={{0,2},{1,3},{2,0},{3,1},{4,6},{5,7},{6,4},{7,5},{8,10},{9,11},{10,... | collective-permute-start | bytes 1572872 | tf_op jit(solution)/shard_map/ppermute | solution.py:412
  284.4 28.9 %collective-permute-start.31 = (bf16[8,4,32,256]{3,2,1,0:T(8,128)(2,1)}, bf16[8,4,32,256]{3,2,1,0:T(8,128)(2,1)}, u32[]{:S(2)}, u32[]{:S(2)}) collective-permute-start(bf16[8,4,32,256]{3,2,1,0:T(8,128)(2,1)} %copy-done.113), channel_id=1, source_target_pairs={{0,3},{1,2},{2,1},{3,0},{4,7},{5,6},{6,5},{7,4},{8,11},{9,10},{10,... | collective-permute-start | bytes 1572872 | tf_op jit(solution)/shard_map/ppermute | solution.py:412
  295.5 29.5 %collective-permute-start.33 = (bf16[8,4,32,256]{3,2,1,0:T(8,128)(2,1)}, bf16[8,4,32,256]{3,2,1,0:T(8,128)(2,1)}, u32[]{:S(2)}, u32[]{:S(2)}) collective-permute-start(bf16[8,4,32,256]{3,2,1,0:T(8,128)(2,1)} %copy-done.111), channel_id=1, source_target_pairs={{0,2},{1,3},{2,0},{3,1},{4,6},{5,7},{6,4},{7,5},{8,10},{9,11},{10,... | collective-permute-start | bytes 1572872 | tf_op jit(solution)/shard_map/ppermute | solution.py:412
  296.7 34.1 %collective-permute-start.34 = (bf16[8,4,32,256]{3,2,1,0:T(8,128)(2,1)}, bf16[8,4,32,256]{3,2,1,0:T(8,128)(2,1)}, u32[]{:S(2)}, u32[]{:S(2)}) collective-permute-start(bf16[8,4,32,256]{3,2,1,0:T(8,128)(2,1)} %copy-done.110), channel_id=1, source_target_pairs={{0,3},{1,2},{2,1},{3,0},{4,7},{5,6},{6,5},{7,4},{8,11},{9,10},{10,... | collective-permute-start | bytes 1572872 | tf_op jit(solution)/shard_map/ppermute | solution.py:412
  334.2 76.8 %all-gather.37.cloned.1.call-start = ((), (), s32[]{:S(2)}) async-start(), calls=%async_computation.8 | async-start | bytes 3145728 | tf_op jit(solution)/shard_map/all_gather | solution.py:401
  334.9 42.9 %collective-permute-start.38 = (bf16[8,4,32,256]{3,2,1,0:T(8,128)(2,1)}, bf16[8,4,32,256]{3,2,1,0:T(8,128)(2,1)}, u32[]{:S(2)}, u32[]{:S(2)}) collective-permute-start(bf16[8,4,32,256]{3,2,1,0:T(8,128)(2,1)} %copy-done.118), channel_id=1, source_target_pairs={{0,1},{1,0},{2,3},{3,2},{4,5},{5,4},{6,7},{7,6},{8,9},{9,8},{10,11... | collective-permute-start | bytes 1572872 | tf_op jit(solution)/shard_map/ppermute | solution.py:412
  335.1 42.7 %collective-permute-start.39 = (bf16[8,4,32,256]{3,2,1,0:T(8,128)(2,1)}, bf16[8,4,32,256]{3,2,1,0:T(8,128)(2,1)}, u32[]{:S(2)}, u32[]{:S(2)}) collective-permute-start(bf16[8,4,32,256]{3,2,1,0:T(8,128)(2,1)} %copy-done.116), channel_id=1, source_target_pairs={{0,2},{1,3},{2,0},{3,1},{4,6},{5,7},{6,4},{7,5},{8,10},{9,11},{10,... | collective-permute-start | bytes 1572872 | tf_op jit(solution)/shard_map/ppermute | solution.py:412
  336.5 41.3 %collective-permute-start.40 = (bf16[8,4,32,256]{3,2,1,0:T(8,128)(2,1)}, bf16[8,4,32,256]{3,2,1,0:T(8,128)(2,1)}, u32[]{:S(2)}, u32[]{:S(2)}) collective-permute-start(bf16[8,4,32,256]{3,2,1,0:T(8,128)(2,1)} %copy-done.115), channel_id=1, source_target_pairs={{0,3},{1,2},{2,1},{3,0},{4,7},{5,6},{6,5},{7,4},{8,11},{9,10},{10,... | collective-permute-start | bytes 1572872 | tf_op jit(solution)/shard_map/ppermute | solution.py:412
  336.8 30.2 %collective-permute-start.36 = (bf16[4,4,32,256]{3,2,1,0:T(8,128)(2,1)}, bf16[4,4,32,256]{3,2,1,0:T(8,128)(2,1)}, u32[]{:S(2)}, u32[]{:S(2)}) collective-permute-start(bf16[4,4,32,256]{3,2,1,0:T(8,128)(2,1)} %copy-done.129), channel_id=1, source_target_pairs={{0,2},{1,3},{2,0},{3,1},{4,6},{5,7},{6,4},{7,5},{8,10},{9,11},{10,... | collective-permute-start | bytes 786440 | tf_op jit(solution)/shard_map/ppermute | solution.py:412
  338.2 33.2 %collective-permute-start.37 = (bf16[4,4,32,256]{3,2,1,0:T(8,128)(2,1)}, bf16[4,4,32,256]{3,2,1,0:T(8,128)(2,1)}, u32[]{:S(2)}, u32[]{:S(2)}) collective-permute-start(bf16[4,4,32,256]{3,2,1,0:T(8,128)(2,1)} %copy-done.128), channel_id=1, source_target_pairs={{0,3},{1,2},{2,1},{3,0},{4,7},{5,6},{6,5},{7,4},{8,11},{9,10},{10,... | collective-permute-start | bytes 786440 | tf_op jit(solution)/shard_map/ppermute | solution.py:412
  380.6 53.3 %all-gather.39.cloned.1.call-start = ((), (), s32[]{:S(2)}) async-start(), calls=%async_computation.9 | async-start | bytes 1572864 | tf_op jit(solution)/shard_map/all_gather | solution.py:401
  382.5 11.8 %collective-permute-start.43 = (bf16[4,4,32,256]{3,2,1,0:T(8,128)(2,1)}, bf16[4,4,32,256]{3,2,1,0:T(8,128)(2,1)S(1)}, u32[]{:S(2)}, u32[]{:S(2)}) collective-permute-start(bf16[4,4,32,256]{3,2,1,0:T(8,128)(2,1)} %copy-done.131), channel_id=1, source_target_pairs={{0,3},{1,2},{2,1},{3,0},{4,7},{5,6},{6,5},{7,4},{8,11},{9,10},{10,... | collective-permute-start | bytes 786440 | tf_op jit(solution)/shard_map/ppermute | solution.py:412
  (154 other events, 1156.7 us)
Sparse Core Ops, SparseCore 0:
  13.3 34.1 all-gather.20
  49.0 33.2 all-gather.22
  83.8 33.1 all-gather.24
  145.1 33.2 all-gather.26
  201.2 21.4 all-gather.28
  227.2 19.7 all-gather.30
  279.9 31.4 all-gather.32
  334.4 30.2 all-gather.34
  380.7 30.3 all-gather.36
  412.5 21.2 all-gather.38

commit v6 on v3

--- a/solution.py
+++ b/solution.py
@@ -11,6 +11,7 @@
 F32, BF16 = jnp.float32, jnp.bfloat16
 ANY = pl.BlockSpec(memory_space=pl.ANY)
 VMEM = pl.BlockSpec(memory_space=pltpu.VMEM)
+HBM = pl.BlockSpec(memory_space=pltpu.HBM)
 SMEM = pl.BlockSpec(memory_space=pltpu.SMEM)
 TOKEN = jax.ShapeDtypeStruct((2,), jnp.int32)
 COST = pl.CostEstimate(flops=1, bytes_accessed=1, transcendentals=0)
@@ -77,7 +78,7 @@
     return pl.pallas_call(
         functools.partial(spread_kernel, begin=begin, skip=skip),
         out_shape=(piece, piece, TOKEN),
-        in_specs=[SMEM, ANY, VMEM] + [ANY] * len(after),
+        in_specs=[SMEM, HBM, VMEM] + [ANY] * len(after),
         out_specs=(VMEM, VMEM, SMEM),
         scratch_shapes=[
             pltpu.VMEM((2, planes, modes, depth, cols), BF16),
@@ -87,6 +88,25 @@
         cost_estimate=COST,
         name="spread",
     )(pos, field, turn, *after)
+
+
+def relay_kernel(pos, *refs):
+    token = refs[-1]
+    token[0], token[1] = pos[0], pos[1]
+
+
+def relay(pos, passed, after):
+    count = len(passed)
+    return pl.pallas_call(
+        relay_kernel,
+        out_shape=tuple(jax.ShapeDtypeStruct(x.shape, x.dtype) for x in passed) + (TOKEN,),
+        in_specs=[SMEM] + [ANY] * (count + len(after)),
+        out_specs=(ANY,) * count + (SMEM,),
+        input_output_aliases={1 + i: i for i in range(count)},
+        compiler_params=params(1),
+        cost_estimate=COST,
+        name="relay",
+    )(pos, *passed, *after)
 
 
 def sweep_kernel(pos, rate, shift, *refs, begin, count, heads):
@@ -319,8 +339,8 @@
     return pl.pallas_call(
         functools.partial(settle_kernel, begin=begin, count=count, chained=chained),
         out_shape=(jax.ShapeDtypeStruct(shape, BF16), TOKEN),
-        in_specs=[SMEM, VMEM] + [ANY] * (count + 1 + chained),
-        out_specs=(ANY, SMEM),
+        in_specs=[SMEM, VMEM] + [HBM] * chained + [ANY] * (count + 1),
+        out_specs=(HBM, SMEM),
         scratch_shapes=[
             pltpu.VMEM((2, rows, planes, modes, cols), BF16),
             pltpu.VMEM((2, planes, modes, rows, cols), BF16),
@@ -333,17 +353,18 @@
     )(pos, turn, *([result] if chained else []), *blocks, other)
 
 
+SIZES = (1, 1, 2, 2, 2)
+
+
 def chunk_rows(half):
     unit = half // 8
-    return [unit, 2 * unit, 2 * unit, 2 * unit, unit]
+    return [n * unit for n in SIZES]
 
 
 ORDER = (
-    ("T", 0), ("T", 1), ("T", 2), ("S", 0), ("T", 3),
-    ("T", 4), ("P", 0), ("S", 1), ("C", 0), ("S", 2),
-    ("P", 1), ("F", 0), ("S", 3), ("P", 2), ("S", 4),
-    ("C", 1), ("P", 3), ("F", 1), ("C", 2), ("P", 4),
-    ("F", 2), ("C", 3), ("F", 3), ("C", 4), ("F", 4),
+    ("T", 0), ("T", 1), ("R", 0), ("T", 2), ("R", 1), ("S", 0), ("T", 3), ("R", 2), ("S", 1), ("P", 0),
+    ("T", 4), ("R", 3), ("S", 2), ("P", 1), ("C", 0), ("R", 4), ("S", 3), ("P", 2), ("C", 1), ("F", 0),
+    ("S", 4), ("P", 3), ("C", 2), ("F", 1), ("P", 4), ("C", 3), ("F", 2), ("C", 4), ("F", 3), ("F", 4),
 )
 
 
@@ -373,8 +394,11 @@
     def across(x):
         return lax.ppermute(x, "space", swap)
 
-    def halo(own, other):
-        return lax.ppermute(own, "space", ahead), lax.ppermute(other, "space", back)
+    def ahead_of(x):
+        return lax.ppermute(x, "space", ahead)
+
+    def behind_of(x):
+        return lax.ppermute(x, "space", back)
 
     def exchange(pieces):
         moved = [pieces[0]]
@@ -403,9 +427,17 @@
     spread_out = lambda v: jnp.broadcast_to(jnp.pad(v, (0, extra))[:, None], (points_count + extra, 128))
     flat, swing = spread_out(level), spread_out(level * thermal_slope)
 
+    sent = []
+
+    def coefficients(side):
+        own_rate, send_rate = logical(diffusion, half + EDGE, side, F32)
+        own_load, send_load = logical(joule, half, side, BF16)
+        sent.extend((own_rate, own_load, across(send_rate), across(send_load)))
+        return send_rate, send_load
+
     rows_of = chunk_rows(half)
     begins = [sum(rows_of[:c]) for c in range(len(rows_of))]
-    own, other, blocks, cells, home, theirs = {}, {}, {}, {}, {}, {}
+    own, other, before, blocks, cells, home, theirs = {}, {}, {}, {}, {}, {}, {}
     result = None
     for kind, c in ORDER:
         begin, rows = begins[c], rows_of[c]
@@ -413,20 +445,23 @@
             skip = EDGE if c else 0
             after = ()
             if c == 1:
-                own_rate, send_rate = logical(diffusion, half + EDGE, pos[0], F32)
-                own_load, send_load = logical(joule, half, pos[0], BF16)
-                other_rate, other_load = across(send_rate), across(send_load)
-                before, behind = halo(own_rate[-1:], other_rate[:1])
-                rate = jnp.concatenate([before, other_rate, own_rate, behind], axis=0)
+                after = coefficients(pos[0])
+            own[c], send, pos = spread(pos, field, to_rows, after, begin, skip, rows + EDGE - skip, rows + TILE)
+            other[c] = across(send)
+            before[c] = ahead_of(own[c])
+        elif kind == "R":
+            if c == 0:
+                if not sent:
+                    coefficients(pos[0])
+                own_rate, own_load, other_rate, other_load = sent
+                other[c], other_rate, other_load, pos = relay(pos, (other[c], other_rate, other_load), (before[c],))
+                edges = ahead_of(own_rate[-1:]), behind_of(other_rate[:1])
+                rate = jnp.concatenate([edges[0], other_rate, own_rate, edges[1]], axis=0)
                 rate = jnp.pad(rate, ((0, 0), (1, -(half + EDGE + 1) % 8), (0, 0)))
                 load = jnp.concatenate([other_load.astype(F32), own_load], axis=0)
-                after = (send_rate, send_load)
-            elif c == 2:
-                after = (blocks[0][0], other_load)
-            own[c], send, pos = spread(pos, field, to_rows, after, begin, skip, rows + EDGE - skip, rows + TILE)
-            other[c] = across(send)
-            before, after = halo(own[c], other[c])
-            blocks[c] = (before, other[c], own[c], after)
+            else:
+                other[c], pos = relay(pos, (other[c],), (before[c],))
+            blocks[c] = (before[c], other[c], own[c], behind_of(other[c]))
         elif kind == "S":
             *pieces, pos = sweep(pos, rate, shift, blocks[c], blocks.get(c - 1, ()), begin, rows, count)
             cells[c] = exchange(pieces)

time: 359 us -> 346 us (0.964)
  waiting for transfers between devices: 140 us -> 104 us
  starting transfers between devices: 71 us -> 82.1 us
  local copies, waits for them, and re-layouts: 23.1 us -> 28.7 us
  Pallas kernels: 120 us -> 124 us
    ppermute x12, waiting for transfers between devices: 58.9 us -> 32 us  [across(): return lax.ppermute(x, 'space', swap)]
    ppermute x30, waiting for transfers between devices: 80 us -> 59.5 us  [exchange(): lax.ppermute(pieces[k], 'modes', [(j, j ^ k) for j in range(count)])]
    ppermute x12, waiting for transfers between devices: 1.31 us -> 12.4 us  [the longest x6 12.4 us: ahead_of(): return lax.ppermute(x, 'space', ahead)]
    ppermute x12, starting transfers between devices: 17.3 us -> 23.4 us  [across(): return lax.ppermute(x, 'space', swap)]
    pallas_call x0 -> x5, Pallas kernels: none -> 5.69 us  [relay(): pl.pallas_call(relay_kernel, out_shape=tuple((jax.ShapeDtypeStruct(x.shap...]
  transfers between devices with their start and end apart: 54 -> 54, of which waited for: 16 -> 16; matrix products, arithmetic and copies ran while one was open for 2% -> 5% of each run, Pallas kernels for 31% -> 34%
where the time goes in v6:
time: 346 us; the launch traced here: 344 us
  Pallas kernels  124 us (36%)
  waiting for transfers between devices  104 us (30%)
  starting transfers between devices  82.1 us (24%)
  local copies, waits for them, and re-layouts  28.7 us (8%)
  other arithmetic  4.63 us (1%)
    ppermute x30, waiting for transfers between devices, exchange(): lax.ppermute(pieces[k], 'modes', [(j, j ^ k) for j in range(count)])  59.5 us
    pallas_call x5, Pallas kernels, points(): pl.pallas_call(functools.partial(points_kernel, begin=begin), out_shape=t...  43.6 us
    pallas_call x5, Pallas kernels, sweep(): pl.pallas_call(functools.partial(sweep_kernel, begin=begin, count=count,...  41 us
    ppermute x12, waiting for transfers between devices, across(): return lax.ppermute(x, 'space', swap)  32 us
    ppermute x6, starting transfers between devices, behind_of(): return lax.ppermute(x, 'space', back)  27.5 us
    ppermute x30, starting transfers between devices, exchange(): lax.ppermute(pieces[k], 'modes', [(j, j ^ k) for j in range(count)])  23.4 us
    ppermute x12, starting transfers between devices, across(): return lax.ppermute(x, 'space', swap)  23.4 us
    unnamed x54, local copies, waits for them, and re-layouts  20.7 us
  transfers between devices with their start and end apart: 54, of which 16 were waited for; matrix products, arithmetic and copies ran while one was open for 5% of the time, Pallas kernels for 34%

profile of v6, /device:TPU:0, one launch (start us, length us, event | category | flops | bytes accessed | tf_op | source)
XLA Modules:
  0.0 344.5 jit_solution(298437620136896603)
XLA Ops:
  1.8 3.4 copy-done
  6.2 2.1 spread.5
  9.3 2.9 collective-permute-start.1
  14.5 4.2 %collective-permute-start.2 = (bf16[2,128,256]{2,1,0:T(8,128)(2,1)S(1)}, bf16[2,128,256]{2,1,0:T(8,128)(2,1)S(1)}, u32[]{:S(2)}, u32[]{:S(2)}) collective-permute-start(bf16[2,128,256]{2,1,0:T(8,128)(2,1)S(1)} %select_convert_fusion.refs_1_), channel_id=1, source_target_pairs={{0,4},{4,0},{8,12},{12,8},{16,20},{20,16},{24,28},{28,24},{1,5},{5... | collective-permute-start | bytes 393224 | tf_op jit(solution)/shard_map/ppermute | solution.py:395
  18.7 3.4 copy-done.1
  22.1 2.5 spread.6
  24.7 10.7 %collective-permute-done.2.refs_2_ = bf16[2,128,256]{2,1,0:T(8,128)(2,1)S(1)} collective-permute-done((bf16[2,128,256]{2,1,0:T(8,128)(2,1)S(1)}, bf16[2,128,256]{2,1,0:T(8,128)(2,1)S(1)}, u32[]{:S(2)}, u32[]{:S(2)}) %collective-permute-start.2) | collective-permute-done | bytes 131104 | tf_op jit(solution)/shard_map/ppermute | solution.py:395
  38.5 3.1 spread.7
  41.6 5.1 %collective-permute-start.9 = (bf16[32,2,32,256]{3,2,1,0:T(8,128)(2,1)}, bf16[32,2,32,256]{3,2,1,0:T(8,128)(2,1)S(1)}, u32[]{:S(2)}, u32[]{:S(2)}) collective-permute-start(bf16[32,2,32,256]{3,2,1,0:T(8,128)(2,1)} %get-tuple-element.114), channel_id=1, source_target_pairs={{0,4},{4,0},{8,12},{12,8},{16,20},{20,16},{24,28},{28,24},{1,5},{5... | collective-permute-start | bytes 3145736 | tf_op jit(solution)/shard_map/ppermute | solution.py:395
  50.0 6.0 %collective-permute-start.8 = (bf16[18,2,32,256]{3,2,1,0:T(8,128)(2,1)S(1)}, bf16[18,2,32,256]{3,2,1,0:T(8,128)(2,1)}, u32[]{:S(2)}, u32[]{:S(2)}) collective-permute-start(bf16[18,2,32,256]{3,2,1,0:T(8,128)(2,1)S(1)} %get-tuple-element.111.refs_1_.refs_5_), channel_id=1, source_target_pairs={{12,4},{0,8},{20,12},{8,16},{28,20},{16,24},{13,5},{1,9},{21,13},{... | collective-permute-start | bytes 1769480 | tf_op jit(solution)/shard_map/ppermute | solution.py:401
  57.1 3.9 %collective-permute-start.11 = (bf16[16,2,32,256]{3,2,1,0:T(8,128)(2,1)}, bf16[16,2,32,256]{3,2,1,0:T(8,128)(2,1)}, u32[]{:S(2)}, u32[]{:S(2)}) collective-permute-start(bf16[16,2,32,256]{3,2,1,0:T(8,128)(2,1)} %get-tuple-element.117.refs_1_.refs_5_), channel_id=1, source_target_pairs={{12,4},{0,8},{20,12},{8,16},{28,20},{16,24},{13,5},{1,9},{21,13},{... | collective-permute-start | bytes 1572872 | tf_op jit(solution)/shard_map/ppermute | solution.py:401
  63.3 12.0 %collective-permute-done.6 = f32[1,130,256]{2,1,0:T(8,128)} collective-permute-done((f32[1,130,256]{2,1,0:T(8,128)}, f32[1,130,256]{2,1,0:T(8,128)}, u32[]{:S(2)}, u32[]{:S(2)}) %collective-permute-start.6) | collective-permute-done | bytes 133152 | tf_op jit(solution)/shard_map/ppermute | solution.py:398
  75.3 4.1 %collective-permute-start.7 = (f32[1,130,256]{2,1,0:T(8,128)}, f32[1,130,256]{2,1,0:T(8,128)}, u32[]{:S(2)}, u32[]{:S(2)}) collective-permute-start(f32[1,130,256]{2,1,0:T(8,128)} %slice.43), channel_id=1, source_target_pairs={{12,4},{0,8},{20,12},{8,16},{28,20},{16,24},{13,5},{1,9},{21,13},{... | collective-permute-start | bytes 399368 | tf_op jit(solution)/shard_map/ppermute | solution.py:401
  79.4 2.0 constant_dynamic-slice_fusion.3
  94.1 5.4 %sweep.5 = (bf16[4,4,32,256]{3,2,1,0:T(8,128)(2,1)S(1)}, bf16[4,4,32,256]{3,2,1,0:T(8,128)(2,1)S(1)}, bf16[4,4,32,256]{3,2,1,0:T(8,128)(2,1)S(1)}, bf16[4,4,32,256]{3,2,1,0:T(8,128)(2,1)S(1)}, s32[2]{0:T(128)S(1)}) custom-call(s32[2]{0:T(128)S(1)} %get-tuple-element.109.pos, f32[6,136,256]{2,1,0:T(8,128)S(1)} %select_maximum_fusion.rate, ...), custom_call_target="tpu_custom_call" | custom-call | flops 1 | bytes 1 | tf_op jit(solution)/shard_map/sweep/pallas_call | solution.py:203
  101.2 3.4 copy-done.2
  104.6 2.2 spread.8
  109.8 6.9 %sweep.6 = (bf16[4,4,32,256]{3,2,1,0:T(8,128)(2,1)S(1)}, bf16[4,4,32,256]{3,2,1,0:T(8,128)(2,1)S(1)}, bf16[4,4,32,256]{3,2,1,0:T(8,128)(2,1)S(1)}, bf16[4,4,32,256]{3,2,1,0:T(8,128)(2,1)S(1)}, s32[2]{0:T(128)S(1)}) custom-call(s32[2]{0:T(128)S(1)} %get-tuple-element.116.pos, f32[6,136,256]{2,1,0:T(8,128)S(1)} %select_maximum_fusion.rate, ...), custom_call_target="tpu_custom_call" | custom-call | flops 1 | bytes 1 | tf_op jit(solution)/shard_map/sweep/pallas_call | solution.py:203
  116.7 4.6 %collective-permute-start.17 = (bf16[32,2,32,256]{3,2,1,0:T(8,128)(2,1)S(1)}, bf16[32,2,32,256]{3,2,1,0:T(8,128)(2,1)S(1)}, u32[]{:S(2)}, u32[]{:S(2)}) collective-permute-start(bf16[32,2,32,256]{3,2,1,0:T(8,128)(2,1)S(1)} %get-tuple-element.129.refs_1_.refs_5_), channel_id=1, source_target_pairs={{12,4},{0,8},{20,12},{8,16},{28,20},{16,24},{13,5},{1,9},{21,13},{... | collective-permute-start | bytes 3145736 | tf_op jit(solution)/shard_map/ppermute | solution.py:401
  121.6 5.9 %points.5 = (bf16[4,4,32,256]{3,2,1,0:T(8,128)(2,1)S(1)}, bf16[4,4,32,256]{3,2,1,0:T(8,128)(2,1)S(1)}, bf16[4,4,32,256]{3,2,1,0:T(8,128)(2,1)S(1)}, bf16[4,4,32,256]{3,2,1,0:T(8,128)(2,1)S(1)}, s32[2]{0:T(128)S(1)}) custom-call(s32[2]{0:T(128)S(1)} %get-tuple-element.118.pos, bf16[352,128]{1,0:T(8,128)(2,1)S(1)} %copy-done.9, bf16[128,352]{1,0:T(8,128)(2,1)S(1)} %bitcast.7, ...), custom_call_target="tpu_custom_call" | custom-call | flops 1 | bytes 1 | tf_op jit(solution)/shard_map/points/pallas_call | solution.py:249
  128.1 2.2 spread.9
  136.3 5.5 %collective-permute-done.19.refs_2_ = bf16[4,4,32,256]{3,2,1,0:T(8,128)(2,1)S(1)} collective-permute-done((bf16[4,4,32,256]{3,2,1,0:T(8,128)(2,1)S(1)}, bf16[4,4,32,256]{3,2,1,0:T(8,128)(2,1)S(1)}, u32[]{:S(2)}, u32[]{:S(2)}) %collective-permute-start.19) | collective-permute-done | bytes 262176 | tf_op jit(solution)/shard_map/ppermute | solution.py:406
  141.8 4.9 %collective-permute-start.26 = (bf16[32,2,32,256]{3,2,1,0:T(8,128)(2,1)S(1)}, bf16[32,2,32,256]{3,2,1,0:T(8,128)(2,1)S(1)}, u32[]{:S(2)}, u32[]{:S(2)}) collective-permute-start(bf16[32,2,32,256]{3,2,1,0:T(8,128)(2,1)S(1)} %get-tuple-element.144.refs_1_.refs_5_), channel_id=1, source_target_pairs={{12,4},{0,8},{20,12},{8,16},{28,20},{16,24},{13,5},{1,9},{21,13},{... | collective-permute-start | bytes 3145736 | tf_op jit(solution)/shard_map/ppermute | solution.py:401
  148.3 10.4 %sweep.7 = (bf16[8,4,32,256]{3,2,1,0:T(8,128)(2,1)S(1)}, bf16[8,4,32,256]{3,2,1,0:T(8,128)(2,1)S(1)}, bf16[8,4,32,256]{3,2,1,0:T(8,128)(2,1)S(1)}, bf16[8,4,32,256]{3,2,1,0:T(8,128)(2,1)S(1)}, s32[2]{0:T(128)S(1)}) custom-call(s32[2]{0:T(128)S(1)} %get-tuple-element.128.pos, f32[6,136,256]{2,1,0:T(8,128)S(1)} %select_maximum_fusion.rate, ...), custom_call_target="tpu_custom_call" | custom-call | flops 1 | bytes 1 | tf_op jit(solution)/shard_map/sweep/pallas_call | solution.py:203
  158.7 5.9 %points.6 = (bf16[4,4,32,256]{3,2,1,0:T(8,128)(2,1)S(1)}, bf16[4,4,32,256]{3,2,1,0:T(8,128)(2,1)S(1)}, bf16[4,4,32,256]{3,2,1,0:T(8,128)(2,1)S(1)}, bf16[4,4,32,256]{3,2,1,0:T(8,128)(2,1)S(1)}, s32[2]{0:T(128)S(1)}) custom-call(s32[2]{0:T(128)S(1)} %get-tuple-element.130.pos, bf16[352,128]{1,0:T(8,128)(2,1)S(1)} %copy-done.9, bf16[128,352]{1,0:T(8,128)(2,1)S(1)} %bitcast.8, ...), custom_call_target="tpu_custom_call" | custom-call | flops 1 | bytes 1 | tf_op jit(solution)/shard_map/points/pallas_call | solution.py:249
  169.3 4.0 %collective-permute-start.34 = (bf16[32,2,32,256]{3,2,1,0:T(8,128)(2,1)S(1)}, bf16[32,2,32,256]{3,2,1,0:T(8,128)(2,1)S(1)}, u32[]{:S(2)}, u32[]{:S(2)}) collective-permute-start(bf16[32,2,32,256]{3,2,1,0:T(8,128)(2,1)S(1)} %get-tuple-element.158.refs_1_), channel_id=1, source_target_pairs={{12,4},{0,8},{20,12},{8,16},{28,20},{16,24},{13,5},{1,9},{21,13},{... | collective-permute-start | bytes 3145736 | tf_op jit(solution)/shard_map/ppermute | solution.py:401
  176.0 3.1 collective-permute-done.32.refs_3_.refs_4_
  181.0 2.1 collective-permute-start.33
  183.2 9.6 %sweep.8 = (bf16[8,4,32,256]{3,2,1,0:T(8,128)(2,1)S(1)}, bf16[8,4,32,256]{3,2,1,0:T(8,128)(2,1)S(1)}, bf16[8,4,32,256]{3,2,1,0:T(8,128)(2,1)S(1)}, bf16[8,4,32,256]{3,2,1,0:T(8,128)(2,1)S(1)}, s32[2]{0:T(128)S(1)}) custom-call(s32[2]{0:T(128)S(1)} %get-tuple-element.143.pos, f32[6,136,256]{2,1,0:T(8,128)S(1)} %select_maximum_fusion.rate, ...), custom_call_target="tpu_custom_call" | custom-call | flops 1 | bytes 1 | tf_op jit(solution)/shard_map/sweep/pallas_call | solution.py:203
  193.4 8.2 %collective-permute-done.29.refs_3_ = bf16[8,4,32,256]{3,2,1,0:T(8,128)(2,1)S(1)} collective-permute-done((bf16[8,4,32,256]{3,2,1,0:T(8,128)(2,1)S(1)}, bf16[8,4,32,256]{3,2,1,0:T(8,128)(2,1)S(1)}, u32[]{:S(2)}, u32[]{:S(2)}) %collective-permute-start.29) | collective-permute-done | bytes 524320 | tf_op jit(solution)/shard_map/ppermute | solution.py:406
  203.5 10.6 %points.7 = (bf16[8,4,32,256]{3,2,1,0:T(8,128)(2,1)S(1)}, bf16[8,4,32,256]{3,2,1,0:T(8,128)(2,1)S(1)}, bf16[8,4,32,256]{3,2,1,0:T(8,128)(2,1)S(1)}, bf16[8,4,32,256]{3,2,1,0:T(8,128)(2,1)S(1)}, s32[2]{0:T(128)S(1)}) custom-call(s32[2]{0:T(128)S(1)} %get-tuple-element.145.pos, bf16[352,128]{1,0:T(8,128)(2,1)S(1)} %copy-done.9, bf16[128,352]{1,0:T(8,128)(2,1)S(1)} %bitcast.9, ...), custom_call_target="tpu_custom_call" | custom-call | flops 1 | bytes 1 | tf_op jit(solution)/shard_map/points/pallas_call | solution.py:249
  217.4 2.8 settle.5
  220.3 8.8 %sweep.9 = (bf16[8,4,32,256]{3,2,1,0:T(8,128)(2,1)S(1)}, bf16[8,4,32,256]{3,2,1,0:T(8,128)(2,1)S(1)}, bf16[8,4,32,256]{3,2,1,0:T(8,128)(2,1)S(1)}, bf16[8,4,32,256]{3,2,1,0:T(8,128)(2,1)S(1)}, s32[2]{0:T(128)S(1)}) custom-call(s32[2]{0:T(128)S(1)} %get-tuple-element.157.pos, f32[6,136,256]{2,1,0:T(8,128)S(1)} %select_maximum_fusion.rate, ...), custom_call_target="tpu_custom_call" | custom-call | flops 1 | bytes 1 | tf_op jit(solution)/shard_map/sweep/pallas_call | solution.py:203
  231.0 10.6 %points.8 = (bf16[8,4,32,256]{3,2,1,0:T(8,128)(2,1)S(1)}, bf16[8,4,32,256]{3,2,1,0:T(8,128)(2,1)S(1)}, bf16[8,4,32,256]{3,2,1,0:T(8,128)(2,1)S(1)}, bf16[8,4,32,256]{3,2,1,0:T(8,128)(2,1)S(1)}, s32[2]{0:T(128)S(1)}) custom-call(s32[2]{0:T(128)S(1)} %get-tuple-element.159.pos, bf16[352,128]{1,0:T(8,128)(2,1)S(1)} %copy-done.9, bf16[128,352]{1,0:T(8,128)(2,1)S(1)} %bitcast.10, ...), custom_call_target="tpu_custom_call" | custom-call | flops 1 | bytes 1 | tf_op jit(solution)/shard_map/points/pallas_call | solution.py:249
  243.5 3.0 collective-permute-done.40.refs_3_.refs_4_
  247.8 1.9 collective-permute-start.48
  251.7 2.8 settle.6
  254.5 4.2 %collective-permute-done.43.refs_2_ = bf16[8,4,32,256]{3,2,1,0:T(8,128)(2,1)S(1)} collective-permute-done((bf16[8,4,32,256]{3,2,1,0:T(8,128)(2,1)S(1)}, bf16[8,4,32,256]{3,2,1,0:T(8,128)(2,1)S(1)}, u32[]{:S(2)}, u32[]{:S(2)}) %collective-permute-start.43) | collective-permute-done | bytes 524320 | tf_op jit(solution)/shard_map/ppermute | solution.py:406
  258.8 10.3 %collective-permute-done.44.refs_3_ = bf16[8,4,32,256]{3,2,1,0:T(8,128)(2,1)S(1)} collective-permute-done((bf16[8,4,32,256]{3,2,1,0:T(8,128)(2,1)S(1)}, bf16[8,4,32,256]{3,2,1,0:T(8,128)(2,1)S(1)}, u32[]{:S(2)}, u32[]{:S(2)}) %collective-permute-start.44) | collective-permute-done | bytes 524320 | tf_op jit(solution)/shard_map/ppermute | solution.py:406
  269.0 10.6 %points.9 = (bf16[8,4,32,256]{3,2,1,0:T(8,128)(2,1)S(1)}, bf16[8,4,32,256]{3,2,1,0:T(8,128)(2,1)S(1)}, bf16[8,4,32,256]{3,2,1,0:T(8,128)(2,1)S(1)}, bf16[8,4,32,256]{3,2,1,0:T(8,128)(2,1)S(1)}, s32[2]{0:T(128)S(1)}) custom-call(s32[2]{0:T(128)S(1)} %get-tuple-element.172.pos, bf16[352,128]{1,0:T(8,128)(2,1)S(1)} %copy-done.9, bf16[128,352]{1,0:T(8,128)(2,1)S(1)} %bitcast.11, ...), custom_call_target="tpu_custom_call" | custom-call | flops 1 | bytes 1 | tf_op jit(solution)/shard_map/points/pallas_call | solution.py:249
  282.3 9.2 %collective-permute-done.47.refs_3_.refs_4_ = bf16[8,4,32,256]{3,2,1,0:T(8,128)(2,1)S(1)} collective-permute-done((bf16[8,4,32,256]{3,2,1,0:T(8,128)(2,1)S(1)}, bf16[8,4,32,256]{3,2,1,0:T(8,128)(2,1)S(1)}, u32[]{:S(2)}, u32[]{:S(2)}) %collective-permute-start.47) | collective-permute-done | bytes 524320 | tf_op jit(solution)/shard_map/ppermute | solution.py:406
  294.7 3.2 settle.7
  297.9 5.8 %collective-permute-done.50.refs_2_.refs_3_ = bf16[8,4,32,256]{3,2,1,0:T(8,128)(2,1)S(1)} collective-permute-done((bf16[8,4,32,256]{3,2,1,0:T(8,128)(2,1)S(1)}, bf16[8,4,32,256]{3,2,1,0:T(8,128)(2,1)S(1)}, u32[]{:S(2)}, u32[]{:S(2)}) %collective-permute-start.50) | collective-permute-done | bytes 524320 | tf_op jit(solution)/shard_map/ppermute | solution.py:406
  303.7 9.5 %collective-permute-done.51.refs_3_.refs_4_ = bf16[8,4,32,256]{3,2,1,0:T(8,128)(2,1)S(1)} collective-permute-done((bf16[8,4,32,256]{3,2,1,0:T(8,128)(2,1)S(1)}, bf16[8,4,32,256]{3,2,1,0:T(8,128)(2,1)S(1)}, u32[]{:S(2)}, u32[]{:S(2)}) %collective-permute-start.51) | collective-permute-done | bytes 524320 | tf_op jit(solution)/shard_map/ppermute | solution.py:406
  314.5 2.7 collective-permute-start.53
  318.8 3.2 settle.8
  322.0 19.2 %collective-permute-done.53.refs_5_ = bf16[32,2,32,256]{3,2,1,0:T(8,128)(2,1)S(1)} collective-permute-done((bf16[32,2,32,256]{3,2,1,0:T(8,128)(2,1)S(1)}, bf16[32,2,32,256]{3,2,1,0:T(8,128)(2,1)S(1)}, u32[]{:S(2)}, u32[]{:S(2)}) %collective-permute-start.53) | collective-permute-done | bytes 1048608 | tf_op jit(solution)/shard_map/ppermute | solution.py:395
  341.2 3.1 settle.9
  (166 shorter events, 72.2 us)
Async XLA Ops:
  9.3 27.4 %collective-permute-start.1 = (f32[2,130,256]{2,1,0:T(8,128)}, f32[2,130,256]{2,1,0:T(8,128)}, u32[]{:S(2)}, u32[]{:S(2)}) collective-permute-start(f32[2,130,256]{2,1,0:T(8,128)} %get-tuple-element.200.refs_0_), channel_id=1, source_target_pairs={{0,4},{4,0},{8,12},{12,8},{16,20},{20,16},{24,28},{28,24},{1,5},{5... | collective-permute-start | bytes 798728 | tf_op jit(solution)/shard_map/ppermute | solution.py:395
  12.3 24.4 %collective-permute-start = (bf16[18,2,32,256]{3,2,1,0:T(8,128)(2,1)}, bf16[18,2,32,256]{3,2,1,0:T(8,128)(2,1)S(1)}, u32[]{:S(2)}, u32[]{:S(2)}) collective-permute-start(bf16[18,2,32,256]{3,2,1,0:T(8,128)(2,1)} %get-tuple-element.103), channel_id=1, source_target_pairs={{0,4},{4,0},{8,12},{12,8},{16,20},{20,16},{24,28},{28,24},{1,5},{5... | collective-permute-start | bytes 1769480 | tf_op jit(solution)/shard_map/ppermute | solution.py:395
  12.3 24.4 %collective-permute-start.3 = (bf16[18,2,32,256]{3,2,1,0:T(8,128)(2,1)S(1)}, bf16[18,2,32,256]{3,2,1,0:T(8,128)(2,1)S(1)}, u32[]{:S(2)}, u32[]{:S(2)}) collective-permute-start(bf16[18,2,32,256]{3,2,1,0:T(8,128)(2,1)S(1)} %get-tuple-element.104.refs_2_.refs_6_), channel_id=1, source_target_pairs={{4,12},{8,0},{12,20},{16,8},{20,28},{24,16},{5,13},{9,1},{13,21},{... | collective-permute-start | bytes 1769480 | tf_op jit(solution)/shard_map/ppermute | solution.py:398
  14.5 20.9 %collective-permute-start.2 = (bf16[2,128,256]{2,1,0:T(8,128)(2,1)S(1)}, bf16[2,128,256]{2,1,0:T(8,128)(2,1)S(1)}, u32[]{:S(2)}, u32[]{:S(2)}) collective-permute-start(bf16[2,128,256]{2,1,0:T(8,128)(2,1)S(1)} %select_convert_fusion.refs_1_), channel_id=1, source_target_pairs={{0,4},{4,0},{8,12},{12,8},{16,20},{20,16},{24,28},{28,24},{1,5},{5... | collective-permute-start | bytes 393224 | tf_op jit(solution)/shard_map/ppermute | solution.py:395
  24.6 25.4 %collective-permute-start.4 = (bf16[16,2,32,256]{3,2,1,0:T(8,128)(2,1)}, bf16[16,2,32,256]{3,2,1,0:T(8,128)(2,1)}, u32[]{:S(2)}, u32[]{:S(2)}) collective-permute-start(bf16[16,2,32,256]{3,2,1,0:T(8,128)(2,1)} %get-tuple-element.107), channel_id=1, source_target_pairs={{0,4},{4,0},{8,12},{12,8},{16,20},{20,16},{24,28},{28,24},{1,5},{5... | collective-permute-start | bytes 1572872 | tf_op jit(solution)/shard_map/ppermute | solution.py:395
  35.4 20.6 %collective-permute-start.5 = (bf16[16,2,32,256]{3,2,1,0:T(8,128)(2,1)}, bf16[16,2,32,256]{3,2,1,0:T(8,128)(2,1)}, u32[]{:S(2)}, u32[]{:S(2)}) collective-permute-start(bf16[16,2,32,256]{3,2,1,0:T(8,128)(2,1)} %get-tuple-element.108.refs_2_.refs_6_), channel_id=1, source_target_pairs={{4,12},{8,0},{12,20},{16,8},{20,28},{24,16},{5,13},{9,1},{13,21},{... | collective-permute-start | bytes 1572872 | tf_op jit(solution)/shard_map/ppermute | solution.py:398
  41.6 65.6 %collective-permute-start.9 = (bf16[32,2,32,256]{3,2,1,0:T(8,128)(2,1)}, bf16[32,2,32,256]{3,2,1,0:T(8,128)(2,1)S(1)}, u32[]{:S(2)}, u32[]{:S(2)}) collective-permute-start(bf16[32,2,32,256]{3,2,1,0:T(8,128)(2,1)} %get-tuple-element.114), channel_id=1, source_target_pairs={{0,4},{4,0},{8,12},{12,8},{16,20},{20,16},{24,28},{28,24},{1,5},{5... | collective-permute-start | bytes 3145736 | tf_op jit(solution)/shard_map/ppermute | solution.py:395
  46.7 60.5 %collective-permute-start.10 = (bf16[32,2,32,256]{3,2,1,0:T(8,128)(2,1)}, bf16[32,2,32,256]{3,2,1,0:T(8,128)(2,1)S(1)}, u32[]{:S(2)}, u32[]{:S(2)}) collective-permute-start(bf16[32,2,32,256]{3,2,1,0:T(8,128)(2,1)} %get-tuple-element.115.refs_2_.refs_6_), channel_id=1, source_target_pairs={{4,12},{8,0},{12,20},{16,8},{20,28},{24,16},{5,13},{9,1},{13,21},{... | collective-permute-start | bytes 3145736 | tf_op jit(solution)/shard_map/ppermute | solution.py:398
  48.6 26.7 %collective-permute-start.6 = (f32[1,130,256]{2,1,0:T(8,128)}, f32[1,130,256]{2,1,0:T(8,128)}, u32[]{:S(2)}, u32[]{:S(2)}) collective-permute-start(f32[1,130,256]{2,1,0:T(8,128)} %slice.44), channel_id=1, source_target_pairs={{4,12},{8,0},{12,20},{16,8},{20,28},{24,16},{5,13},{9,1},{13,21},{... | collective-permute-start | bytes 399368 | tf_op jit(solution)/shard_map/ppermute | solution.py:398
  50.0 42.2 %collective-permute-start.8 = (bf16[18,2,32,256]{3,2,1,0:T(8,128)(2,1)S(1)}, bf16[18,2,32,256]{3,2,1,0:T(8,128)(2,1)}, u32[]{:S(2)}, u32[]{:S(2)}) collective-permute-start(bf16[18,2,32,256]{3,2,1,0:T(8,128)(2,1)S(1)} %get-tuple-element.111.refs_1_.refs_5_), channel_id=1, source_target_pairs={{12,4},{0,8},{20,12},{8,16},{28,20},{16,24},{13,5},{1,9},{21,13},{... | collective-permute-start | bytes 1769480 | tf_op jit(solution)/shard_map/ppermute | solution.py:401
  57.1 49.7 %collective-permute-start.11 = (bf16[16,2,32,256]{3,2,1,0:T(8,128)(2,1)}, bf16[16,2,32,256]{3,2,1,0:T(8,128)(2,1)}, u32[]{:S(2)}, u32[]{:S(2)}) collective-permute-start(bf16[16,2,32,256]{3,2,1,0:T(8,128)(2,1)} %get-tuple-element.117.refs_1_.refs_5_), channel_id=1, source_target_pairs={{12,4},{0,8},{20,12},{8,16},{28,20},{16,24},{13,5},{1,9},{21,13},{... | collective-permute-start | bytes 1572872 | tf_op jit(solution)/shard_map/ppermute | solution.py:401
  75.3 15.4 %collective-permute-start.7 = (f32[1,130,256]{2,1,0:T(8,128)}, f32[1,130,256]{2,1,0:T(8,128)}, u32[]{:S(2)}, u32[]{:S(2)}) collective-permute-start(f32[1,130,256]{2,1,0:T(8,128)} %slice.43), channel_id=1, source_target_pairs={{12,4},{0,8},{20,12},{8,16},{28,20},{16,24},{13,5},{1,9},{21,13},{... | collective-permute-start | bytes 399368 | tf_op jit(solution)/shard_map/ppermute | solution.py:401
  99.5 17.2 %collective-permute-start.12 = (bf16[4,4,32,256]{3,2,1,0:T(8,128)(2,1)S(1)}, bf16[4,4,32,256]{3,2,1,0:T(8,128)(2,1)S(1)}, u32[]{:S(2)}, u32[]{:S(2)}) collective-permute-start(bf16[4,4,32,256]{3,2,1,0:T(8,128)(2,1)S(1)} %get-tuple-element.121), channel_id=1, source_target_pairs={{0,1},{1,0},{2,3},{3,2},{4,5},{5,4},{6,7},{7,6},{8,9},{9,8},{10,11... | collective-permute-start | bytes 786440 | tf_op jit(solution)/shard_map/ppermute | solution.py:406
  99.6 21.8 %collective-permute-start.13 = (bf16[4,4,32,256]{3,2,1,0:T(8,128)(2,1)S(1)}, bf16[4,4,32,256]{3,2,1,0:T(8,128)(2,1)S(1)}, u32[]{:S(2)}, u32[]{:S(2)}) collective-permute-start(bf16[4,4,32,256]{3,2,1,0:T(8,128)(2,1)S(1)} %get-tuple-element.122), channel_id=1, source_target_pairs={{0,2},{1,3},{2,0},{3,1},{4,6},{5,7},{6,4},{7,5},{8,10},{9,11},{10,... | collective-permute-start | bytes 786440 | tf_op jit(solution)/shard_map/ppermute | solution.py:406
  106.8 14.5 %collective-permute-start.14 = (bf16[4,4,32,256]{3,2,1,0:T(8,128)(2,1)S(1)}, bf16[4,4,32,256]{3,2,1,0:T(8,128)(2,1)S(1)}, u32[]{:S(2)}, u32[]{:S(2)}) collective-permute-start(bf16[4,4,32,256]{3,2,1,0:T(8,128)(2,1)S(1)} %get-tuple-element.123), channel_id=1, source_target_pairs={{0,3},{1,2},{2,1},{3,0},{4,7},{5,6},{6,5},{7,4},{8,11},{9,10},{10,... | collective-permute-start | bytes 786440 | tf_op jit(solution)/shard_map/ppermute | solution.py:406
  107.2 25.4 %collective-permute-start.15 = (bf16[32,2,32,256]{3,2,1,0:T(8,128)(2,1)S(1)}, bf16[32,2,32,256]{3,2,1,0:T(8,128)(2,1)S(1)}, u32[]{:S(2)}, u32[]{:S(2)}) collective-permute-start(bf16[32,2,32,256]{3,2,1,0:T(8,128)(2,1)S(1)} %get-tuple-element.126), channel_id=1, source_target_pairs={{0,4},{4,0},{8,12},{12,8},{16,20},{20,16},{24,28},{28,24},{1,5},{5... | collective-permute-start | bytes 3145736 | tf_op jit(solution)/shard_map/ppermute | solution.py:395
  107.2 27.3 %collective-permute-start.16 = (bf16[32,2,32,256]{3,2,1,0:T(8,128)(2,1)S(1)}, bf16[32,2,32,256]{3,2,1,0:T(8,128)(2,1)S(1)}, u32[]{:S(2)}, u32[]{:S(2)}) collective-permute-start(bf16[32,2,32,256]{3,2,1,0:T(8,128)(2,1)S(1)} %get-tuple-element.127.refs_2_.refs_6_), channel_id=1, source_target_pairs={{4,12},{8,0},{12,20},{16,8},{20,28},{24,16},{5,13},{9,1},{13,21},{... | collective-permute-start | bytes 3145736 | tf_op jit(solution)/shard_map/ppermute | solution.py:398
  116.7 31.6 %collective-permute-start.17 = (bf16[32,2,32,256]{3,2,1,0:T(8,128)(2,1)S(1)}, bf16[32,2,32,256]{3,2,1,0:T(8,128)(2,1)S(1)}, u32[]{:S(2)}, u32[]{:S(2)}) collective-permute-start(bf16[32,2,32,256]{3,2,1,0:T(8,128)(2,1)S(1)} %get-tuple-element.129.refs_1_.refs_5_), channel_id=1, source_target_pairs={{12,4},{0,8},{20,12},{8,16},{28,20},{16,24},{13,5},{1,9},{21,13},{... | collective-permute-start | bytes 3145736 | tf_op jit(solution)/shard_map/ppermute | solution.py:401
  130.3 36.5 %collective-permute-start.24 = (bf16[32,2,32,256]{3,2,1,0:T(8,128)(2,1)S(1)}, bf16[32,2,32,256]{3,2,1,0:T(8,128)(2,1)S(1)}, u32[]{:S(2)}, u32[]{:S(2)}) collective-permute-start(bf16[32,2,32,256]{3,2,1,0:T(8,128)(2,1)S(1)} %get-tuple-element.141), channel_id=1, source_target_pairs={{0,4},{4,0},{8,12},{12,8},{16,20},{20,16},{24,28},{28,24},{1,5},{5... | collective-permute-start | bytes 3145736 | tf_op jit(solution)/shard_map/ppermute | solution.py:395
  130.8 37.4 %collective-permute-start.25 = (bf16[32,2,32,256]{3,2,1,0:T(8,128)(2,1)S(1)}, bf16[32,2,32,256]{3,2,1,0:T(8,128)(2,1)S(1)}, u32[]{:S(2)}, u32[]{:S(2)}) collective-permute-start(bf16[32,2,32,256]{3,2,1,0:T(8,128)(2,1)S(1)} %get-tuple-element.142.refs_2_), channel_id=1, source_target_pairs={{4,12},{8,0},{12,20},{16,8},{20,28},{24,16},{5,13},{9,1},{13,21},{... | collective-permute-start | bytes 3145736 | tf_op jit(solution)/shard_map/ppermute | solution.py:398
  141.8 39.2 %collective-permute-start.26 = (bf16[32,2,32,256]{3,2,1,0:T(8,128)(2,1)S(1)}, bf16[32,2,32,256]{3,2,1,0:T(8,128)(2,1)S(1)}, u32[]{:S(2)}, u32[]{:S(2)}) collective-permute-start(bf16[32,2,32,256]{3,2,1,0:T(8,128)(2,1)S(1)} %get-tuple-element.144.refs_1_.refs_5_), channel_id=1, source_target_pairs={{12,4},{0,8},{20,12},{8,16},{28,20},{16,24},{13,5},{1,9},{21,13},{... | collective-permute-start | bytes 3145736 | tf_op jit(solution)/shard_map/ppermute | solution.py:401
  146.7 17.9 %collective-permute-start.22 = (bf16[4,4,32,256]{3,2,1,0:T(8,128)(2,1)S(1)}, bf16[4,4,32,256]{3,2,1,0:T(8,128)(2,1)S(1)}, u32[]{:S(2)}, u32[]{:S(2)}) collective-permute-start(bf16[4,4,32,256]{3,2,1,0:T(8,128)(2,1)S(1)} %get-tuple-element.138), channel_id=1, source_target_pairs={{0,2},{1,3},{2,0},{3,1},{4,6},{5,7},{6,4},{7,5},{8,10},{9,11},{10,... | collective-permute-start | bytes 786440 | tf_op jit(solution)/shard_map/ppermute | solution.py:406
  148.3 17.0 %collective-permute-start.23 = (bf16[4,4,32,256]{3,2,1,0:T(8,128)(2,1)S(1)}, bf16[4,4,32,256]{3,2,1,0:T(8,128)(2,1)S(1)}, u32[]{:S(2)}, u32[]{:S(2)}) collective-permute-start(bf16[4,4,32,256]{3,2,1,0:T(8,128)(2,1)S(1)} %get-tuple-element.139), channel_id=1, source_target_pairs={{0,3},{1,2},{2,1},{3,0},{4,7},{5,6},{6,5},{7,4},{8,11},{9,10},{10,... | collective-permute-start | bytes 786440 | tf_op jit(solution)/shard_map/ppermute | solution.py:406
  166.8 12.3 %collective-permute-start.32 = (bf16[4,4,32,256]{3,2,1,0:T(8,128)(2,1)S(1)}, bf16[4,4,32,256]{3,2,1,0:T(8,128)(2,1)S(1)}, u32[]{:S(2)}, u32[]{:S(2)}) collective-permute-start(bf16[4,4,32,256]{3,2,1,0:T(8,128)(2,1)S(1)} %get-tuple-element.154), channel_id=1, source_target_pairs={{0,3},{1,2},{2,1},{3,0},{4,7},{5,6},{6,5},{7,4},{8,11},{9,10},{10,... | collective-permute-start | bytes 786440 | tf_op jit(solution)/shard_map/ppermute | solution.py:406
  169.3 46.2 %collective-permute-start.34 = (bf16[32,2,32,256]{3,2,1,0:T(8,128)(2,1)S(1)}, bf16[32,2,32,256]{3,2,1,0:T(8,128)(2,1)S(1)}, u32[]{:S(2)}, u32[]{:S(2)}) collective-permute-start(bf16[32,2,32,256]{3,2,1,0:T(8,128)(2,1)S(1)} %get-tuple-element.158.refs_1_), channel_id=1, source_target_pairs={{12,4},{0,8},{20,12},{8,16},{28,20},{16,24},{13,5},{1,9},{21,13},{... | collective-permute-start | bytes 3145736 | tf_op jit(solution)/shard_map/ppermute | solution.py:401
  173.4 19.4 %collective-permute-start.27 = (bf16[8,4,32,256]{3,2,1,0:T(8,128)(2,1)S(1)}, bf16[8,4,32,256]{3,2,1,0:T(8,128)(2,1)S(1)}, u32[]{:S(2)}, u32[]{:S(2)}) collective-permute-start(bf16[8,4,32,256]{3,2,1,0:T(8,128)(2,1)S(1)} %get-tuple-element.147), channel_id=1, source_target_pairs={{0,1},{1,0},{2,3},{3,2},{4,5},{5,4},{6,7},{7,6},{8,9},{9,8},{10,11... | collective-permute-start | bytes 1572872 | tf_op jit(solution)/shard_map/ppermute | solution.py:406
  174.5 18.4 %collective-permute-start.28 = (bf16[8,4,32,256]{3,2,1,0:T(8,128)(2,1)S(1)}, bf16[8,4,32,256]{3,2,1,0:T(8,128)(2,1)S(1)}, u32[]{:S(2)}, u32[]{:S(2)}) collective-permute-start(bf16[8,4,32,256]{3,2,1,0:T(8,128)(2,1)S(1)} %get-tuple-element.148), channel_id=1, source_target_pairs={{0,2},{1,3},{2,0},{3,1},{4,6},{5,7},{6,4},{7,5},{8,10},{9,11},{10,... | collective-permute-start | bytes 1572872 | tf_op jit(solution)/shard_map/ppermute | solution.py:406
  179.1 22.5 %collective-permute-start.29 = (bf16[8,4,32,256]{3,2,1,0:T(8,128)(2,1)S(1)}, bf16[8,4,32,256]{3,2,1,0:T(8,128)(2,1)S(1)}, u32[]{:S(2)}, u32[]{:S(2)}) collective-permute-start(bf16[8,4,32,256]{3,2,1,0:T(8,128)(2,1)S(1)} %get-tuple-element.149), channel_id=1, source_target_pairs={{0,3},{1,2},{2,1},{3,0},{4,7},{5,6},{6,5},{7,4},{8,11},{9,10},{10,... | collective-permute-start | bytes 1572872 | tf_op jit(solution)/shard_map/ppermute | solution.py:406
  181.0 34.5 %collective-permute-start.33 = (bf16[16,2,32,256]{3,2,1,0:T(8,128)(2,1)S(1)}, bf16[16,2,32,256]{3,2,1,0:T(8,128)(2,1)S(1)}, u32[]{:S(2)}, u32[]{:S(2)}) collective-permute-start(bf16[16,2,32,256]{3,2,1,0:T(8,128)(2,1)S(1)} %get-tuple-element.156), channel_id=1, source_target_pairs={{0,4},{4,0},{8,12},{12,8},{16,20},{20,16},{24,28},{28,24},{1,5},{5... | collective-permute-start | bytes 1572872 | tf_op jit(solution)/shard_map/ppermute | solution.py:395
  192.8 23.4 %collective-permute-start.35 = (bf16[8,4,32,256]{3,2,1,0:T(8,128)(2,1)S(1)}, bf16[8,4,32,256]{3,2,1,0:T(8,128)(2,1)S(1)}, u32[]{:S(2)}, u32[]{:S(2)}) collective-permute-start(bf16[8,4,32,256]{3,2,1,0:T(8,128)(2,1)S(1)} %get-tuple-element.161), channel_id=1, source_target_pairs={{0,1},{1,0},{2,3},{3,2},{4,5},{5,4},{6,7},{7,6},{8,9},{9,8},{10,11... | collective-permute-start | bytes 1572872 | tf_op jit(solution)/shard_map/ppermute | solution.py:406
  192.8 36.2 %collective-permute-start.36 = (bf16[8,4,32,256]{3,2,1,0:T(8,128)(2,1)S(1)}, bf16[8,4,32,256]{3,2,1,0:T(8,128)(2,1)S(1)}, u32[]{:S(2)}, u32[]{:S(2)}) collective-permute-start(bf16[8,4,32,256]{3,2,1,0:T(8,128)(2,1)S(1)} %get-tuple-element.162), channel_id=1, source_target_pairs={{0,2},{1,3},{2,0},{3,1},{4,6},{5,7},{6,4},{7,5},{8,10},{9,11},{10,... | collective-permute-start | bytes 1572872 | tf_op jit(solution)/shard_map/ppermute | solution.py:406
  201.6 29.4 %collective-permute-start.37 = (bf16[8,4,32,256]{3,2,1,0:T(8,128)(2,1)S(1)}, bf16[8,4,32,256]{3,2,1,0:T(8,128)(2,1)S(1)}, u32[]{:S(2)}, u32[]{:S(2)}) collective-permute-start(bf16[8,4,32,256]{3,2,1,0:T(8,128)(2,1)S(1)} %get-tuple-element.163), channel_id=1, source_target_pairs={{0,3},{1,2},{2,1},{3,0},{4,7},{5,6},{6,5},{7,4},{8,11},{9,10},{10,... | collective-permute-start | bytes 1572872 | tf_op jit(solution)/shard_map/ppermute | solution.py:406
  215.5 26.2 %collective-permute-start.38 = (bf16[8,4,32,256]{3,2,1,0:T(8,128)(2,1)S(1)}, bf16[8,4,32,256]{3,2,1,0:T(8,128)(2,1)S(1)}, u32[]{:S(2)}, u32[]{:S(2)}) collective-permute-start(bf16[8,4,32,256]{3,2,1,0:T(8,128)(2,1)S(1)} %get-tuple-element.166), channel_id=1, source_target_pairs={{0,1},{1,0},{2,3},{3,2},{4,5},{5,4},{6,7},{7,6},{8,9},{9,8},{10,11... | collective-permute-start | bytes 1572872 | tf_op jit(solution)/shard_map/ppermute | solution.py:406
  215.6 26.7 %collective-permute-start.39 = (bf16[8,4,32,256]{3,2,1,0:T(8,128)(2,1)S(1)}, bf16[8,4,32,256]{3,2,1,0:T(8,128)(2,1)S(1)}, u32[]{:S(2)}, u32[]{:S(2)}) collective-permute-start(bf16[8,4,32,256]{3,2,1,0:T(8,128)(2,1)S(1)} %get-tuple-element.167), channel_id=1, source_target_pairs={{0,2},{1,3},{2,0},{3,1},{4,6},{5,7},{6,4},{7,5},{8,10},{9,11},{10,... | collective-permute-start | bytes 1572872 | tf_op jit(solution)/shard_map/ppermute | solution.py:406
  216.2 30.4 %collective-permute-start.40 = (bf16[8,4,32,256]{3,2,1,0:T(8,128)(2,1)S(1)}, bf16[8,4,32,256]{3,2,1,0:T(8,128)(2,1)S(1)}, u32[]{:S(2)}, u32[]{:S(2)}) collective-permute-start(bf16[8,4,32,256]{3,2,1,0:T(8,128)(2,1)S(1)} %get-tuple-element.168), channel_id=1, source_target_pairs={{0,3},{1,2},{2,1},{3,0},{4,7},{5,6},{6,5},{7,4},{8,11},{9,10},{10,... | collective-permute-start | bytes 1572872 | tf_op jit(solution)/shard_map/ppermute | solution.py:406
  229.1 20.7 %collective-permute-start.41 = (bf16[16,2,32,256]{3,2,1,0:T(8,128)(2,1)S(1)}, bf16[16,2,32,256]{3,2,1,0:T(8,128)(2,1)S(1)}, u32[]{:S(2)}, u32[]{:S(2)}) collective-permute-start(bf16[16,2,32,256]{3,2,1,0:T(8,128)(2,1)S(1)} %get-tuple-element.171), channel_id=1, source_target_pairs={{0,4},{4,0},{8,12},{12,8},{16,20},{20,16},{24,28},{28,24},{1,5},{5... | collective-permute-start | bytes 1572872 | tf_op jit(solution)/shard_map/ppermute | solution.py:395
  231.0 19.2 %collective-permute-start.42 = (bf16[8,4,32,256]{3,2,1,0:T(8,128)(2,1)S(1)}, bf16[8,4,32,256]{3,2,1,0:T(8,128)(2,1)S(1)}, u32[]{:S(2)}, u32[]{:S(2)}) collective-permute-start(bf16[8,4,32,256]{3,2,1,0:T(8,128)(2,1)S(1)} %get-tuple-element.174), channel_id=1, source_target_pairs={{0,1},{1,0},{2,3},{3,2},{4,5},{5,4},{6,7},{7,6},{8,9},{9,8},{10,11... | collective-permute-start | bytes 1572872 | tf_op jit(solution)/shard_map/ppermute | solution.py:406
  241.7 17.1 %collective-permute-start.43 = (bf16[8,4,32,256]{3,2,1,0:T(8,128)(2,1)S(1)}, bf16[8,4,32,256]{3,2,1,0:T(8,128)(2,1)S(1)}, u32[]{:S(2)}, u32[]{:S(2)}) collective-permute-start(bf16[8,4,32,256]{3,2,1,0:T(8,128)(2,1)S(1)} %get-tuple-element.175), channel_id=1, source_target_pairs={{0,2},{1,3},{2,0},{3,1},{4,6},{5,7},{6,4},{7,5},{8,10},{9,11},{10,... | collective-permute-start | bytes 1572872 | tf_op jit(solution)/shard_map/ppermute | solution.py:406
  242.2 26.8 %collective-permute-start.44 = (bf16[8,4,32,256]{3,2,1,0:T(8,128)(2,1)S(1)}, bf16[8,4,32,256]{3,2,1,0:T(8,128)(2,1)S(1)}, u32[]{:S(2)}, u32[]{:S(2)}) collective-permute-start(bf16[8,4,32,256]{3,2,1,0:T(8,128)(2,1)S(1)} %get-tuple-element.176), channel_id=1, source_target_pairs={{0,3},{1,2},{2,1},{3,0},{4,7},{5,6},{6,5},{7,4},{8,11},{9,10},{10,... | collective-permute-start | bytes 1572872 | tf_op jit(solution)/shard_map/ppermute | solution.py:406
  247.8 46.9 %collective-permute-start.48 = (bf16[32,2,32,256]{3,2,1,0:T(8,128)(2,1)S(1)}, bf16[32,2,32,256]{3,2,1,0:T(8,128)(2,1)S(1)}, u32[]{:S(2)}, u32[]{:S(2)}) collective-permute-start(bf16[32,2,32,256]{3,2,1,0:T(8,128)(2,1)S(1)} %get-tuple-element.184), channel_id=1, source_target_pairs={{0,4},{4,0},{8,12},{12,8},{16,20},{20,16},{24,28},{28,24},{1,5},{5... | collective-permute-start | bytes 3145736 | tf_op jit(solution)/shard_map/ppermute | solution.py:395
  249.7 31.1 %collective-permute-start.45 = (bf16[8,4,32,256]{3,2,1,0:T(8,128)(2,1)S(1)}, bf16[8,4,32,256]{3,2,1,0:T(8,128)(2,1)S(1)}, u32[]{:S(2)}, u32[]{:S(2)}) collective-permute-start(bf16[8,4,32,256]{3,2,1,0:T(8,128)(2,1)S(1)} %get-tuple-element.179), channel_id=1, source_target_pairs={{0,1},{1,0},{2,3},{3,2},{4,5},{5,4},{6,7},{7,6},{8,9},{9,8},{10,11... | collective-permute-start | bytes 1572872 | tf_op jit(solution)/shard_map/ppermute | solution.py:406
  250.2 32.1 %collective-permute-start.46 = (bf16[8,4,32,256]{3,2,1,0:T(8,128)(2,1)S(1)}, bf16[8,4,32,256]{3,2,1,0:T(8,128)(2,1)S(1)}, u32[]{:S(2)}, u32[]{:S(2)}) collective-permute-start(bf16[8,4,32,256]{3,2,1,0:T(8,128)(2,1)S(1)} %get-tuple-element.180), channel_id=1, source_target_pairs={{0,2},{1,3},{2,0},{3,1},{4,6},{5,7},{6,4},{7,5},{8,10},{9,11},{10,... | collective-permute-start | bytes 1572872 | tf_op jit(solution)/shard_map/ppermute | solution.py:406
  258.8 32.7 %collective-permute-start.47 = (bf16[8,4,32,256]{3,2,1,0:T(8,128)(2,1)S(1)}, bf16[8,4,32,256]{3,2,1,0:T(8,128)(2,1)S(1)}, u32[]{:S(2)}, u32[]{:S(2)}) collective-permute-start(bf16[8,4,32,256]{3,2,1,0:T(8,128)(2,1)S(1)} %get-tuple-element.181), channel_id=1, source_target_pairs={{0,3},{1,2},{2,1},{3,0},{4,7},{5,6},{6,5},{7,4},{8,11},{9,10},{10,... | collective-permute-start | bytes 1572872 | tf_op jit(solution)/shard_map/ppermute | solution.py:406
  279.6 18.3 %collective-permute-start.49 = (bf16[8,4,32,256]{3,2,1,0:T(8,128)(2,1)S(1)}, bf16[8,4,32,256]{3,2,1,0:T(8,128)(2,1)S(1)}, u32[]{:S(2)}, u32[]{:S(2)}) collective-permute-start(bf16[8,4,32,256]{3,2,1,0:T(8,128)(2,1)S(1)} %get-tuple-element.187), channel_id=1, source_target_pairs={{0,1},{1,0},{2,3},{3,2},{4,5},{5,4},{6,7},{7,6},{8,9},{9,8},{10,11... | collective-permute-start | bytes 1572872 | tf_op jit(solution)/shard_map/ppermute | solution.py:406
  280.8 22.9 %collective-permute-start.50 = (bf16[8,4,32,256]{3,2,1,0:T(8,128)(2,1)S(1)}, bf16[8,4,32,256]{3,2,1,0:T(8,128)(2,1)S(1)}, u32[]{:S(2)}, u32[]{:S(2)}) collective-permute-start(bf16[8,4,32,256]{3,2,1,0:T(8,128)(2,1)S(1)} %get-tuple-element.188), channel_id=1, source_target_pairs={{0,2},{1,3},{2,0},{3,1},{4,6},{5,7},{6,4},{7,5},{8,10},{9,11},{10,... | collective-permute-start | bytes 1572872 | tf_op jit(solution)/shard_map/ppermute | solution.py:406
  282.3 30.9 %collective-permute-start.51 = (bf16[8,4,32,256]{3,2,1,0:T(8,128)(2,1)S(1)}, bf16[8,4,32,256]{3,2,1,0:T(8,128)(2,1)S(1)}, u32[]{:S(2)}, u32[]{:S(2)}) collective-permute-start(bf16[8,4,32,256]{3,2,1,0:T(8,128)(2,1)S(1)} %get-tuple-element.189), channel_id=1, source_target_pairs={{0,3},{1,2},{2,1},{3,0},{4,7},{5,6},{6,5},{7,4},{8,11},{9,10},{10,... | collective-permute-start | bytes 1572872 | tf_op jit(solution)/shard_map/ppermute | solution.py:406
  292.7 26.1 %collective-permute-start.52 = (bf16[32,2,32,256]{3,2,1,0:T(8,128)(2,1)S(1)}, bf16[32,2,32,256]{3,2,1,0:T(8,128)(2,1)S(1)}, u32[]{:S(2)}, u32[]{:S(2)}) collective-permute-start(bf16[32,2,32,256]{3,2,1,0:T(8,128)(2,1)S(1)} %get-tuple-element.192), channel_id=1, source_target_pairs={{0,4},{4,0},{8,12},{12,8},{16,20},{20,16},{24,28},{28,24},{1,5},{5... | collective-permute-start | bytes 3145736 | tf_op jit(solution)/shard_map/ppermute | solution.py:395
  314.5 26.8 %collective-permute-start.53 = (bf16[32,2,32,256]{3,2,1,0:T(8,128)(2,1)S(1)}, bf16[32,2,32,256]{3,2,1,0:T(8,128)(2,1)S(1)}, u32[]{:S(2)}, u32[]{:S(2)}) collective-permute-start(bf16[32,2,32,256]{3,2,1,0:T(8,128)(2,1)S(1)} %get-tuple-element.195), channel_id=1, source_target_pairs={{0,4},{4,0},{8,12},{12,8},{16,20},{20,16},{24,28},{28,24},{1,5},{5... | collective-permute-start | bytes 3145736 | tf_op jit(solution)/shard_map/ppermute | solution.py:395
  (31 other events, 447.5 us)

commit v7 on v6

--- a/solution.py
+++ b/solution.py
@@ -17,6 +17,7 @@
 COST = pl.CostEstimate(flops=1, bytes_accessed=1, transcendentals=0)
 EDGE = 2
 TILE = 16
+LANES = 128
 
 
 def params(mebibytes):
@@ -36,55 +37,57 @@
     return x.astype(F32).reshape(a * m, y).astype(BF16)
 
 
-def spread_kernel(pos, field, turn, *refs, begin, skip):
-    own, send, token, window, sems = refs[-5:]
+def spread_kernel(pos, field, turn, *refs, spans):
+    outs, (token, window, sems) = refs[-3 - 2 * len(spans) : -3], refs[-3:]
     side = pos[0]
     token[0], token[1] = pos[0], pos[1]
-    _, planes, modes, depth, cols = window.shape
+    blocks, _, planes, modes, _, cols = window.shape
+    base = spans[0][0] // TILE
     size = field.shape[2]
-    rows = own.shape[0]
     group = turn.shape[1] // TILE
-    copies = []
-    for a in range(2):
-        far = 1 - side if a == 0 else side
-        start = jnp.where(far == 1, size - depth - begin, begin)
-        start = pl.multiple_of(start, TILE)
-        copy = pltpu.make_async_copy(
-            field.at[:, :, pl.ds(start, depth), :], window.at[a], sems.at[a]
-        )
-        copy.start()
-        copies.append(copy)
-    for a, out in ((0, send), (1, own)):
-        far = 1 - side if a == 0 else side
-        copies[a].wait()
-        for z in range(planes):
-            to = jnp.where(far == 1, z, planes - 1 - z)
-            for g in range(depth // TILE):
-                block = jnp.where(far == 1, depth // TILE - 1 - g, g)
-                low, high = max(0, skip - g * TILE), min(TILE, rows + skip - g * TILE)
-                if high <= low:
-                    continue
+    copies = {}
+    for g in range(blocks):
+        for a in range(2):
+            far = 1 - side if a == 0 else side
+            begin = (base + g) * TILE
+            start = pl.multiple_of(jnp.where(far == 1, size - TILE - begin, begin), TILE)
+            copies[g, a] = pltpu.make_async_copy(
+                field.at[:, :, pl.ds(start, TILE), :], window.at[g, a], sems.at[g, a]
+            )
+            copies[g, a].start()
+    for g in range(blocks):
+        for a in range(2):
+            far = 1 - side if a == 0 else side
+            copies[g, a].wait()
+            for z in range(planes):
+                to = jnp.where(far == 1, z, planes - 1 - z)
                 for h in range(modes // group):
                     there = pl.ds(h * group, group)
-                    x = window[a, z, there, pl.ds(pl.multiple_of(block * TILE, TILE), TILE), :]
+                    x = window[g, a, z, there]
                     y = jnp.dot(turn[far], x.reshape(group * TILE, cols), preferred_element_type=F32)
                     y = from_rows(y, group)
-                    out[pl.ds(g * TILE + low - skip, high - low), to, there, :] = y[low:high]
-
-
-def spread(pos, field, turn, after, begin, skip, rows, depth):
+                    for n, (first, last) in enumerate(spans):
+                        low, high = (min(max(r - (base + g) * TILE, 0), TILE) for r in (first, last))
+                        if low < high:
+                            at = (base + g) * TILE + low - first
+                            outs[2 * n + a][pl.ds(at, high - low), to, there, :] = y[low:high]
+
+
+def spread(pos, field, turn, after, spans):
     planes, modes, _, cols = field.shape
-    piece = jax.ShapeDtypeStruct((rows, planes, modes, cols), BF16)
+    pieces = [jax.ShapeDtypeStruct((last - first, planes, modes, cols), BF16) for first, last in spans]
+    pieces = [piece for piece in pieces for _ in range(2)]
+    blocks = -(-spans[-1][1] // TILE) - spans[0][0] // TILE
     return pl.pallas_call(
-        functools.partial(spread_kernel, begin=begin, skip=skip),
-        out_shape=(piece, piece, TOKEN),
+        functools.partial(spread_kernel, spans=spans),
+        out_shape=(*pieces, TOKEN),
         in_specs=[SMEM, HBM, VMEM] + [ANY] * len(after),
-        out_specs=(VMEM, VMEM, SMEM),
+        out_specs=(VMEM,) * len(pieces) + (SMEM,),
         scratch_shapes=[
-            pltpu.VMEM((2, planes, modes, depth, cols), BF16),
-            pltpu.SemaphoreType.DMA((2,)),
+            pltpu.VMEM((blocks, 2, planes, modes, TILE, cols), BF16),
+            pltpu.SemaphoreType.DMA((blocks, 2)),
         ],
-        compiler_params=params(10),
+        compiler_params=params(48),
         cost_estimate=COST,
         name="spread",
     )(pos, field, turn, *after)
@@ -109,7 +112,7 @@
     )(pos, *passed, *after)
 
 
-def sweep_kernel(pos, rate, shift, *refs, begin, count, heads):
+def sweep_kernel(pos, rate, *refs, begin, count, heads):
     group = 4
     blocks, refs = refs[:group], refs[group:]
     tails, refs = refs[:heads], refs[heads:]
@@ -143,14 +146,20 @@
             return jnp.zeros((some.size, cols), BF16)
         return blocks[p // planes][row - lead, p % planes, some]
 
-    def beside(parts, number):
-        return jnp.dot(
-            to_bf16_rows(jnp.stack(parts)), shift[...], preferred_element_type=F32
-        ).reshape(number, -1, modes, cols)
+    def beside(x):
+        parts = [x[:, h * LANES : (h + 1) * LANES] for h in range(cols // LANES)]
+        up = [pltpu.roll(part, 1, 1) for part in parts]
+        down = [pltpu.roll(part, LANES - 1, 1) for part in parts]
+        lane = lax.broadcasted_iota(jnp.int32, parts[0].shape, 1)
+        nothing = jnp.zeros_like(parts[0])
+        sums = []
+        for h in range(len(parts)):
+            left = jnp.where(lane == 0, up[h - 1] if h else nothing, up[h])
+            right = jnp.where(lane == LANES - 1, down[h + 1] if h + 1 < len(parts) else nothing, down[h])
+            sums.append(left + right)
+        return jnp.concatenate(sums, axis=1)
 
     def once(i, number):
-        every = pl.ds(0, modes)
-        aside = beside([field(i + 1 + a, low + p, every) for a in range(number) for p in range(wide)], number)
         for a in range(number):
             speeds = [rate[p, pl.ds(begin + i + a, 1), :] for p in range(wide)]
             for h in range(modes // piece):
@@ -158,7 +167,7 @@
                 line = [field(i + 1 + a, low - 1 + p, some).astype(F32) for p in range(wide + 2)]
                 for p in range(wide):
                     centre = line[p + 1]
-                    around = aside[a, p, h * piece : (h + 1) * piece] + (line[p] + line[p + 2])
+                    around = beside(centre) + (line[p] + line[p + 2])
                     around = around + (
                         field(i + a, low + p, some).astype(F32) + field(i + 2 + a, low + p, some).astype(F32)
                     )
@@ -178,7 +187,6 @@
 
         def again(j, _):
             i = base + number * j
-            aside = beside([first[i + 1 + a, 1 + p] for a in range(number) for p in range(mine)], number)
             for a in range(number):
                 speeds = [rate[p + 1, pl.ds(begin + i + a + 1, 1), :] for p in range(mine)]
                 for h in range(modes // piece):
@@ -186,7 +194,7 @@
                     line = [first[i + 1 + a, p, some] for p in range(wide)]
                     for p in range(mine):
                         centre = line[p + 1]
-                        around = aside[a, p, h * piece : (h + 1) * piece] + (line[p] + line[p + 2])
+                        around = beside(centre) + (line[p] + line[p + 2])
                         around = around + (first[i + a, p + 1, some] + first[i + 2 + a, p + 1, some])
                         outs[k][number * j + a, p, some] = (
                             centre + speeds[p] * (around - 6.0 * centre)
@@ -196,14 +204,14 @@
         lax.fori_loop(0, part // number, again, 0)
 
 
-def sweep(pos, rate, shift, blocks, tails, begin, rows, count):
+def sweep(pos, rate, blocks, tails, begin, rows, count):
     _, planes, modes, cols = blocks[0].shape
     mine = 2 * planes
     piece = jax.ShapeDtypeStruct((rows // count, mine, modes, cols), BF16)
     return pl.pallas_call(
         functools.partial(sweep_kernel, begin=begin, count=count, heads=len(tails)),
         out_shape=(piece,) * count + (TOKEN,),
-        in_specs=[SMEM] + [VMEM] * 6 + [ANY] * len(tails),
+        in_specs=[SMEM] + [VMEM] * 5 + [ANY] * len(tails),
         out_specs=(VMEM,) * count + (SMEM,),
         scratch_shapes=[
             pltpu.VMEM((rows + 2, mine + 2, modes, cols), F32),
@@ -213,32 +221,33 @@
         compiler_params=params(22),
         cost_estimate=COST,
         name="sweep",
-    )(pos, rate, shift, *blocks, *tails)
+    )(pos, rate, *blocks, *tails)
 
 
 def points_kernel(pos, basis, basis_t, flat, swing, load, *refs, begin):
-    *refs, token = refs
+    *refs, token, gathered, stepped = refs
     token[0], token[1] = pos[0], pos[1]
     count = len(refs) // 2
     blocks, outs = refs[:count], refs[count:]
     part, planes, modes, cols = blocks[0].shape
     copies = cols // flat.shape[1]
+    places = [pl.multiple_of(jnp.bitwise_xor(pos[1], k) * modes, modes) for k in range(count)]
 
     def row(i, _):
         place = begin + pos[1] * part + i
         for p in range(planes):
-            if modes % 16 == 0:
-                cells = jnp.concatenate([block[i, p] for block in blocks], axis=0)
-            else:
-                cells = jnp.concatenate([block[i, p].astype(F32) for block in blocks], axis=0).astype(BF16)
+            for k in range(count):
+                gathered[p, pl.ds(places[k], modes)] = blocks[k][i, p].astype(gathered.dtype)
+            cells = gathered[p].astype(BF16)
             heat = jnp.tanh(jnp.dot(basis[...], cells, preferred_element_type=F32))
             offset = jnp.concatenate([flat[...]] * copies, axis=1)
             slope = jnp.concatenate([swing[...]] * copies, axis=1)
             weighted = (offset + slope * heat).astype(BF16)
             source = jnp.dot(basis_t[...], weighted, preferred_element_type=F32).astype(BF16).astype(F32)
             done = cells.astype(F32) + load[p, pl.ds(place, 1), :] * source
+            stepped[p] = done.astype(stepped.dtype)
             for k in range(count):
-                outs[k][i, p] = done[k * modes : (k + 1) * modes].astype(BF16)
+                outs[k][i, p] = stepped[p, pl.ds(places[k], modes)].astype(BF16)
         return 0
 
     lax.fori_loop(0, part, row, 0)
@@ -246,11 +255,14 @@
 
 def points(pos, basis, basis_t, flat, swing, load, blocks, begin):
     count = len(blocks)
+    _, planes, modes, cols = blocks[0].shape
+    kept = BF16 if modes % 16 == 0 else F32
     return pl.pallas_call(
         functools.partial(points_kernel, begin=begin),
         out_shape=tuple(jax.ShapeDtypeStruct(block.shape, BF16) for block in blocks) + (TOKEN,),
         in_specs=[SMEM] + [VMEM] * (5 + count),
         out_specs=(VMEM,) * count + (SMEM,),
+        scratch_shapes=[pltpu.VMEM((planes, modes * count, cols), kept)] * 2,
         compiler_params=params(14),
         cost_estimate=COST,
         name="points",
@@ -362,8 +374,8 @@
 
 
 ORDER = (
-    ("T", 0), ("T", 1), ("R", 0), ("T", 2), ("R", 1), ("S", 0), ("T", 3), ("R", 2), ("S", 1), ("P", 0),
-    ("T", 4), ("R", 3), ("S", 2), ("P", 1), ("C", 0), ("R", 4), ("S", 3), ("P", 2), ("C", 1), ("F", 0),
+    ("T", 0), ("T", 1), ("R", 0), ("R", 1), ("S", 0), ("R", 2), ("S", 1), ("P", 0),
+    ("R", 3), ("S", 2), ("P", 1), ("C", 0), ("R", 4), ("S", 3), ("P", 2), ("C", 1), ("F", 0),
     ("S", 4), ("P", 3), ("C", 2), ("F", 1), ("P", 4), ("C", 3), ("F", 2), ("C", 4), ("F", 3), ("F", 4),
 )
 
@@ -391,6 +403,9 @@
     ahead = [(i, j) for i, j in ahead if 0 <= j < spaces]
     back = [(j, i) for i, j in ahead]
 
+    beyond = [(i, i - 1 if i % 2 == 0 else i + 1) for i in range(spaces)]
+    beyond = [(i, j) for i, j in beyond if 0 <= j < spaces]
+
     def across(x):
         return lax.ppermute(x, "space", swap)
 
@@ -412,61 +427,58 @@
         send = jnp.where(side == 1, planes_back, rows_back).astype(sent)
         return own, send
 
-    lane = np.arange(cols)
-    shift = jnp.asarray(np.abs(lane[:, None] - lane[None, :]) == 1, BF16)
     to_rows, to_modes = turns(min(modes, TILE))
 
     points_count = basis.shape[0]
     extra = -points_count % 32
-    turned = jnp.concatenate(
-        [lax.dynamic_slice_in_dim(basis, (me ^ k) * modes, modes, axis=1) for k in range(count)], axis=1
-    )
-    turned = jnp.pad(turned, ((0, extra), (0, 0)))
-    turned_t = turned.T
+    basis = jnp.pad(basis, ((0, extra), (0, 0)))
+    basis_t = basis.T
     level = quad_weight * base_conductivity
     spread_out = lambda v: jnp.broadcast_to(jnp.pad(v, (0, extra))[:, None], (points_count + extra, 128))
     flat, swing = spread_out(level), spread_out(level * thermal_slope)
 
-    sent = []
-
     def coefficients(side):
         own_rate, send_rate = logical(diffusion, half + EDGE, side, F32)
         own_load, send_load = logical(joule, half, side, BF16)
-        sent.extend((own_rate, own_load, across(send_rate), across(send_load)))
-        return send_rate, send_load
+        edge_rate = lax.ppermute(send_rate[:1], "space", beyond)
+        rates = ahead_of(own_rate[-1:]), across(send_rate), edge_rate
+        return own_rate, own_load, rates, across(send_load), (send_rate, send_load)
 
     rows_of = chunk_rows(half)
     begins = [sum(rows_of[:c]) for c in range(len(rows_of))]
+    edges = [(begin + EDGE * (begin > 0), begin + rows + EDGE) for begin, rows in zip(begins, rows_of)]
     own, other, before, blocks, cells, home, theirs = {}, {}, {}, {}, {}, {}, {}
     result = None
     for kind, c in ORDER:
         begin, rows = begins[c], rows_of[c]
         if kind == "T":
-            skip = EDGE if c else 0
             after = ()
-            if c == 1:
-                after = coefficients(pos[0])
-            own[c], send, pos = spread(pos, field, to_rows, after, begin, skip, rows + EDGE - skip, rows + TILE)
-            other[c] = across(send)
-            before[c] = ahead_of(own[c])
+            if c:
+                after = (*[rates[n] for n in (1,)], basis, basis_t, flat, swing)
+            else:
+                own_rate, own_load, rates, other_load, after = coefficients(pos[0])
+            those = range(1, len(rows_of)) if c else (0,)
+            *pieces, pos = spread(pos, field, to_rows, after, [edges[n] for n in those])
+            for n in those:
+                send, own[n], *pieces = pieces
+                other[n], before[n] = across(send), ahead_of(own[n])
         elif kind == "R":
             if c == 0:
-                if not sent:
-                    coefficients(pos[0])
-                own_rate, own_load, other_rate, other_load = sent
-                other[c], other_rate, other_load, pos = relay(pos, (other[c], other_rate, other_load), (before[c],))
-                edges = ahead_of(own_rate[-1:]), behind_of(other_rate[:1])
-                rate = jnp.concatenate([edges[0], other_rate, own_rate, edges[1]], axis=0)
+                after = (before[c], *[rates[n] for n in (0, 2)])
+                other[c], pos = relay(pos, (other[c],), after)
+                rate = jnp.concatenate([rates[0], rates[1], own_rate, rates[2]], axis=0)
                 rate = jnp.pad(rate, ((0, 0), (1, -(half + EDGE + 1) % 8), (0, 0)))
+            elif c == 1:
+                other[c], other_load, pos = relay(pos, (other[c], other_load), (before[c],))
                 load = jnp.concatenate([other_load.astype(F32), own_load], axis=0)
             else:
                 other[c], pos = relay(pos, (other[c],), (before[c],))
             blocks[c] = (before[c], other[c], own[c], behind_of(other[c]))
         elif kind == "S":
-            *pieces, pos = sweep(pos, rate, shift, blocks[c], blocks.get(c - 1, ()), begin, rows, count)
+            *pieces, pos = sweep(pos, rate, blocks[c], blocks.get(c - 1, ()), begin, rows, count)
             cells[c] = exchange(pieces)
         elif kind == "P":
-            *stepped, pos = points(pos, turned, turned_t, flat, swing, load, cells[c], begin)
+            *stepped, pos = points(pos, basis, basis_t, flat, swing, load, cells[c], begin)
             home[c] = exchange(stepped)
         elif kind == "C":
             out, pos = collect(pos, home[c])

time: 346 us -> 321 us (0.928)
  local copies, waits for them, and re-layouts: 28.7 us -> 10.6 us
  waiting for transfers between devices: 104 us -> 120 us
  starting transfers between devices: 82.1 us -> 69.1 us
  Pallas kernels: 124 us -> 119 us
  other arithmetic: 4.63 us -> 0.34 us
    unnamed x54 -> x24, local copies, waits for them, and re-layouts: 20.7 us -> 4.35 us
    ppermute x30, waiting for transfers between devices: 59.5 us -> 70.1 us  [exchange(): lax.ppermute(pieces[k], 'modes', [(j, j ^ k) for j in range(count)])]
    ppermute x6 -> x5, waiting for transfers between devices: 0.02 us -> 8.73 us  [behind_of(): return lax.ppermute(x, 'space', back)]
    ppermute x6, waiting for transfers between devices: 12.4 us -> 3.73 us  [ahead_of(): return lax.ppermute(x, 'space', ahead)]
    ppermute x12, starting transfers between devices: 23.4 us -> 17.1 us  [across(): return lax.ppermute(x, 'space', swap)]
    ppermute x6 -> x5, starting transfers between devices: 27.5 us -> 21.6 us  [behind_of(): return lax.ppermute(x, 'space', back)]
    ppermute x12, waiting for transfers between devices: 32 us -> 37.7 us  [across(): return lax.ppermute(x, 'space', swap)]
    pallas_call x5, Pallas kernels: 41 us -> 36.5 us  [sweep(): pl.pallas_call(functools.partial(sweep_kernel, begin=begin, count=count,...]
  transfers between devices with their start and end apart: 54 -> 54, of which waited for: 16 -> 21; matrix products, arithmetic and copies ran while one was open for 5% -> 2% of each run, Pallas kernels for 34% -> 35%
where the time goes in v7:
time: 321 us
  waiting for transfers between devices  120 us (37%)
  Pallas kernels  119 us (37%)
  starting transfers between devices  69.1 us (22%)
  local copies, waits for them, and re-layouts  10.6 us (3%)
    ppermute x30, waiting for transfers between devices, exchange(): lax.ppermute(pieces[k], 'modes', [(j, j ^ k) for j in range(count)])  70.1 us
    pallas_call x5, Pallas kernels, points(): pl.pallas_call(functools.partial(points_kernel, begin=begin), out_shape=t...  44.2 us
    ppermute x12, waiting for transfers between devices, across(): return lax.ppermute(x, 'space', swap)  37.7 us
    pallas_call x5, Pallas kernels, sweep(): pl.pallas_call(functools.partial(sweep_kernel, begin=begin, count=count,...  36.5 us
    ppermute x30, starting transfers between devices, exchange(): lax.ppermute(pieces[k], 'modes', [(j, j ^ k) for j in range(count)])  22.1 us
    ppermute x5, starting transfers between devices, behind_of(): return lax.ppermute(x, 'space', back)  21.6 us
    ppermute x12, starting transfers between devices, across(): return lax.ppermute(x, 'space', swap)  17.1 us
    pallas_call x5, Pallas kernels, settle(): pl.pallas_call(functools.partial(settle_kernel, begin=begin, count=count,...  15.1 us
  transfers between devices with their start and end apart: 54, of which 21 were waited for; matrix products, arithmetic and copies ran while one was open for 2% of the time, Pallas kernels for 35%

profile of v7, /device:TPU:0, one launch (start us, length us, event | category | flops | bytes accessed | tf_op | source)
XLA Modules:
  0.0 320.7 jit_solution(1506664371750093316)
XLA Ops:
  4.2 3.4 %spread.2 = (bf16[18,2,32,256]{3,2,1,0:T(8,128)(2,1)}, bf16[18,2,32,256]{3,2,1,0:T(8,128)(2,1)S(1)}, s32[2]{0:T(128)S(1)}) custom-call(s32[2]{0:T(128)S(1)} %pad_add_fusion.pos, bf16[2,32,256,256]{3,2,1,0:T(8,128)(2,1)} %field.3, bf16[2,256,256]{2,1,0:T(8,128)(2,1)S(1)} %copy-done.3, f32[2,130,256]{2,1,0:T(8,128)S(1)} %get-tuple-element.192.refs_0_, ...), custom_call_target="tpu_custom_call" | custom-call | flops 1 | bytes 1 | tf_op jit(solution)/shard_map/spread/pallas_call | solution.py:81
  7.6 3.0 collective-permute-start.1
  11.9 2.8 collective-permute-start
  18.1 1.6 copy.20
  19.7 1.6 copy.27
  22.3 10.1 %collective-permute-done.refs_0_ = f32[2,130,256]{2,1,0:T(8,128)S(1)} collective-permute-done((f32[2,130,256]{2,1,0:T(8,128)S(1)}, f32[2,130,256]{2,1,0:T(8,128)S(1)}, u32[]{:S(2)}, u32[]{:S(2)}) %collective-permute-start) | collective-permute-done | bytes 266272 | tf_op jit(solution)/shard_map/ppermute | solution.py:410
  32.3 2.5 collective-permute-start.6
  36.0 8.0 %spread.3 = (bf16[16,2,32,256]{3,2,1,0:T(8,128)(2,1)S(1)}, bf16[16,2,32,256]{3,2,1,0:T(8,128)(2,1)S(1)}, bf16[32,2,32,256]{3,2,1,0:T(8,128)(2,1)S(1)}, bf16[32,2...) custom-call(s32[2]{0:T(128)S(1)} %get-tuple-element.97.pos, ...), custom_call_target="tpu_custom_call" | custom-call | flops 1 | bytes 1 | tf_op jit(solution)/shard_map/spread/pallas_call | solution.py:81
  45.4 4.3 %collective-permute-start.9 = (bf16[32,2,32,256]{3,2,1,0:T(8,128)(2,1)S(1)}, bf16[32,2,32,256]{3,2,1,0:T(8,128)(2,1)S(1)}, u32[]{:S(2)}, u32[]{:S(2)}) collective-permute-start(bf16[32,2,32,256]{3,2,1,0:T(8,128)(2,1)S(1)} %get-tuple-element.107), channel_id=1, source_target_pairs={{0,4},{4,0},{8,12},{12,8},{16,20},{20,16},{24,28},{28,24},{1,5},{5... | collective-permute-start | bytes 3145736 | tf_op jit(solution)/shard_map/ppermute | solution.py:410
  52.1 4.6 %collective-permute-start.8 = (bf16[18,2,32,256]{3,2,1,0:T(8,128)(2,1)S(1)}, bf16[18,2,32,256]{3,2,1,0:T(8,128)(2,1)S(1)}, u32[]{:S(2)}, u32[]{:S(2)}) collective-permute-start(bf16[18,2,32,256]{3,2,1,0:T(8,128)(2,1)S(1)} %get-tuple-element.105.refs_1_.refs_5_), channel_id=1, source_target_pairs={{12,4},{0,8},{20,12},{8,16},{28,20},{16,24},{13,5},{1,9},{21,13},{... | collective-permute-start | bytes 1769480 | tf_op jit(solution)/shard_map/ppermute | solution.py:416
  56.7 2.2 collective-permute-done.5.refs_0_
  58.9 2.0 collective-permute-done.7.refs_2_.refs_0_.refs_4_
  62.1 4.1 %collective-permute-start.11 = (bf16[16,2,32,256]{3,2,1,0:T(8,128)(2,1)S(1)}, bf16[16,2,32,256]{3,2,1,0:T(8,128)(2,1)S(1)}, u32[]{:S(2)}, u32[]{:S(2)}) collective-permute-start(bf16[16,2,32,256]{3,2,1,0:T(8,128)(2,1)S(1)} %get-tuple-element.110.refs_1_.refs_5_), channel_id=1, source_target_pairs={{12,4},{0,8},{20,12},{8,16},{28,20},{16,24},{13,5},{1,9},{21,13},{... | collective-permute-start | bytes 1572872 | tf_op jit(solution)/shard_map/ppermute | solution.py:416
  66.3 4.2 %collective-permute-done.8.refs_3_.refs_7_ = bf16[18,2,32,256]{3,2,1,0:T(8,128)(2,1)S(1)} collective-permute-done((bf16[18,2,32,256]{3,2,1,0:T(8,128)(2,1)S(1)}, bf16[18,2,32,256]{3,2,1,0:T(8,128)(2,1)S(1)}, u32[]{:S(2)}, u32[]{:S(2)}) %collective-permute-start.8) | collective-permute-done | bytes 589856 | tf_op jit(solution)/shard_map/ppermute | solution.py:416
  71.9 4.9 %sweep.5 = (bf16[4,4,32,256]{3,2,1,0:T(8,128)(2,1)S(1)}, bf16[4,4,32,256]{3,2,1,0:T(8,128)(2,1)S(1)}, bf16[4,4,32,256]{3,2,1,0:T(8,128)(2,1)S(1)}, bf16[4,4,32,256]{3,2,1,0:T(8,128)(2,1)S(1)}, s32[2]{0:T(128)S(1)}) custom-call(s32[2]{0:T(128)S(1)} %get-tuple-element.104.pos, f32[6,136,256]{2,1,0:T(8,128)S(1)} %select_maximum_fusion.rate, ...), custom_call_target="tpu_custom_call" | custom-call | flops 1 | bytes 1 | tf_op jit(solution)/shard_map/sweep/pallas_call | solution.py:211
  78.2 3.2 collective-permute-done.9.refs_0_
  84.5 5.2 %sweep.6 = (bf16[4,4,32,256]{3,2,1,0:T(8,128)(2,1)S(1)}, bf16[4,4,32,256]{3,2,1,0:T(8,128)(2,1)S(1)}, bf16[4,4,32,256]{3,2,1,0:T(8,128)(2,1)S(1)}, bf16[4,4,32,256]{3,2,1,0:T(8,128)(2,1)S(1)}, s32[2]{0:T(128)S(1)}) custom-call(s32[2]{0:T(128)S(1)} %get-tuple-element.109.pos, f32[6,136,256]{2,1,0:T(8,128)S(1)} %select_maximum_fusion.rate, ...), custom_call_target="tpu_custom_call" | custom-call | flops 1 | bytes 1 | tf_op jit(solution)/shard_map/sweep/pallas_call | solution.py:211
  89.7 1.7 collective-permute-start.18
  92.7 3.4 %collective-permute-start.17 = (bf16[32,2,32,256]{3,2,1,0:T(8,128)(2,1)S(1)}, bf16[32,2,32,256]{3,2,1,0:T(8,128)(2,1)S(1)}, u32[]{:S(2)}, u32[]{:S(2)}) collective-permute-start(bf16[32,2,32,256]{3,2,1,0:T(8,128)(2,1)S(1)} %get-tuple-element.121.refs_1_.refs_5_), channel_id=1, source_target_pairs={{12,4},{0,8},{20,12},{8,16},{28,20},{16,24},{13,5},{1,9},{21,13},{... | collective-permute-start | bytes 3145736 | tf_op jit(solution)/shard_map/ppermute | solution.py:416
  96.2 5.9 %points.5 = (bf16[4,4,32,256]{3,2,1,0:T(8,128)(2,1)S(1)}, bf16[4,4,32,256]{3,2,1,0:T(8,128)(2,1)S(1)}, bf16[4,4,32,256]{3,2,1,0:T(8,128)(2,1)S(1)}, bf16[4,4,32,256]{3,2,1,0:T(8,128)(2,1)S(1)}, s32[2]{0:T(128)S(1)}) custom-call(s32[2]{0:T(128)S(1)} %get-tuple-element.111.pos, bf16[352,128]{1,0:T(8,128)(2,1)S(1)} %pad.15.clone.refs_1_.basis, ...), custom_call_target="tpu_custom_call" | custom-call | flops 1 | bytes 1 | tf_op jit(solution)/shard_map/points/pallas_call | solution.py:260
  106.7 5.1 %collective-permute-start.26 = (bf16[32,2,32,256]{3,2,1,0:T(8,128)(2,1)S(1)}, bf16[32,2,32,256]{3,2,1,0:T(8,128)(2,1)S(1)}, u32[]{:S(2)}, u32[]{:S(2)}) collective-permute-start(bf16[32,2,32,256]{3,2,1,0:T(8,128)(2,1)S(1)} %get-tuple-element.136.refs_1_.refs_5_), channel_id=1, source_target_pairs={{12,4},{0,8},{20,12},{8,16},{28,20},{16,24},{13,5},{1,9},{21,13},{... | collective-permute-start | bytes 3145736 | tf_op jit(solution)/shard_map/ppermute | solution.py:416
  111.8 1.6 collective-permute-done.20.refs_3_
  116.3 3.1 collective-permute-done.17.refs_3_.refs_7_
  120.9 8.8 %sweep.7 = (bf16[8,4,32,256]{3,2,1,0:T(8,128)(2,1)S(1)}, bf16[8,4,32,256]{3,2,1,0:T(8,128)(2,1)S(1)}, bf16[8,4,32,256]{3,2,1,0:T(8,128)(2,1)S(1)}, bf16[8,4,32,256]{3,2,1,0:T(8,128)(2,1)S(1)}, s32[2]{0:T(128)S(1)}) custom-call(s32[2]{0:T(128)S(1)} %get-tuple-element.120.pos, f32[6,136,256]{2,1,0:T(8,128)S(1)} %select_maximum_fusion.rate, ...), custom_call_target="tpu_custom_call" | custom-call | flops 1 | bytes 1 | tf_op jit(solution)/shard_map/sweep/pallas_call | solution.py:211
  129.7 6.0 %points.6 = (bf16[4,4,32,256]{3,2,1,0:T(8,128)(2,1)S(1)}, bf16[4,4,32,256]{3,2,1,0:T(8,128)(2,1)S(1)}, bf16[4,4,32,256]{3,2,1,0:T(8,128)(2,1)S(1)}, bf16[4,4,32,256]{3,2,1,0:T(8,128)(2,1)S(1)}, s32[2]{0:T(128)S(1)}) custom-call(s32[2]{0:T(128)S(1)} %get-tuple-element.122.pos, bf16[352,128]{1,0:T(8,128)(2,1)S(1)} %pad.15.clone.refs_1_.basis, ...), custom_call_target="tpu_custom_call" | custom-call | flops 1 | bytes 1 | tf_op jit(solution)/shard_map/points/pallas_call | solution.py:260
  139.1 4.4 %collective-permute-start.34 = (bf16[32,2,32,256]{3,2,1,0:T(8,128)(2,1)S(1)}, bf16[32,2,32,256]{3,2,1,0:T(8,128)(2,1)S(1)}, u32[]{:S(2)}, u32[]{:S(2)}) collective-permute-start(bf16[32,2,32,256]{3,2,1,0:T(8,128)(2,1)S(1)} %get-tuple-element.150.refs_1_), channel_id=1, source_target_pairs={{12,4},{0,8},{20,12},{8,16},{28,20},{16,24},{13,5},{1,9},{21,13},{... | collective-permute-start | bytes 3145736 | tf_op jit(solution)/shard_map/ppermute | solution.py:416
  143.5 1.6 collective-permute-start.28
  145.2 1.7 collective-permute-start.32
  146.9 8.8 %sweep.8 = (bf16[8,4,32,256]{3,2,1,0:T(8,128)(2,1)S(1)}, bf16[8,4,32,256]{3,2,1,0:T(8,128)(2,1)S(1)}, bf16[8,4,32,256]{3,2,1,0:T(8,128)(2,1)S(1)}, bf16[8,4,32,256]{3,2,1,0:T(8,128)(2,1)S(1)}, s32[2]{0:T(128)S(1)}) custom-call(s32[2]{0:T(128)S(1)} %get-tuple-element.135.pos, f32[6,136,256]{2,1,0:T(8,128)S(1)} %select_maximum_fusion.rate, ...), custom_call_target="tpu_custom_call" | custom-call | flops 1 | bytes 1 | tf_op jit(solution)/shard_map/sweep/pallas_call | solution.py:211
  155.7 18.1 %collective-permute-done.32.refs_3_.refs_4_ = bf16[4,4,32,256]{3,2,1,0:T(8,128)(2,1)S(1)} collective-permute-done((bf16[4,4,32,256]{3,2,1,0:T(8,128)(2,1)S(1)}, bf16[4,4,32,256]{3,2,1,0:T(8,128)(2,1)S(1)}, u32[]{:S(2)}, u32[]{:S(2)}) %collective-permute-start.32) | collective-permute-done | bytes 262176 | tf_op jit(solution)/shard_map/ppermute | solution.py:421
  177.1 10.8 %points.7 = (bf16[8,4,32,256]{3,2,1,0:T(8,128)(2,1)S(1)}, bf16[8,4,32,256]{3,2,1,0:T(8,128)(2,1)S(1)}, bf16[8,4,32,256]{3,2,1,0:T(8,128)(2,1)S(1)}, bf16[8,4,32,256]{3,2,1,0:T(8,128)(2,1)S(1)}, s32[2]{0:T(128)S(1)}) custom-call(s32[2]{0:T(128)S(1)} %get-tuple-element.137.pos, bf16[352,128]{1,0:T(8,128)(2,1)S(1)} %pad.15.clone.refs_1_.basis, ...), custom_call_target="tpu_custom_call" | custom-call | flops 1 | bytes 1 | tf_op jit(solution)/shard_map/points/pallas_call | solution.py:260
  191.2 2.8 settle.5
  194.0 8.8 %sweep.9 = (bf16[8,4,32,256]{3,2,1,0:T(8,128)(2,1)S(1)}, bf16[8,4,32,256]{3,2,1,0:T(8,128)(2,1)S(1)}, bf16[8,4,32,256]{3,2,1,0:T(8,128)(2,1)S(1)}, bf16[8,4,32,256]{3,2,1,0:T(8,128)(2,1)S(1)}, s32[2]{0:T(128)S(1)}) custom-call(s32[2]{0:T(128)S(1)} %get-tuple-element.149.pos, f32[6,136,256]{2,1,0:T(8,128)S(1)} %select_maximum_fusion.rate, ...), custom_call_target="tpu_custom_call" | custom-call | flops 1 | bytes 1 | tf_op jit(solution)/shard_map/sweep/pallas_call | solution.py:211
  204.0 10.8 %points.8 = (bf16[8,4,32,256]{3,2,1,0:T(8,128)(2,1)S(1)}, bf16[8,4,32,256]{3,2,1,0:T(8,128)(2,1)S(1)}, bf16[8,4,32,256]{3,2,1,0:T(8,128)(2,1)S(1)}, bf16[8,4,32,256]{3,2,1,0:T(8,128)(2,1)S(1)}, s32[2]{0:T(128)S(1)}) custom-call(s32[2]{0:T(128)S(1)} %get-tuple-element.151.pos, bf16[352,128]{1,0:T(8,128)(2,1)S(1)} %pad.15.clone.refs_1_.basis, ...), custom_call_target="tpu_custom_call" | custom-call | flops 1 | bytes 1 | tf_op jit(solution)/shard_map/points/pallas_call | solution.py:260
  214.8 1.7 collective-permute-start.43
  216.5 6.4 %collective-permute-done.40.refs_3_.refs_4_ = bf16[8,4,32,256]{3,2,1,0:T(8,128)(2,1)S(1)} collective-permute-done((bf16[8,4,32,256]{3,2,1,0:T(8,128)(2,1)S(1)}, bf16[8,4,32,256]{3,2,1,0:T(8,128)(2,1)S(1)}, u32[]{:S(2)}, u32[]{:S(2)}) %collective-permute-start.40) | collective-permute-done | bytes 524320 | tf_op jit(solution)/shard_map/ppermute | solution.py:421
  226.9 2.8 settle.6
  229.7 5.3 %collective-permute-done.43.refs_2_ = bf16[8,4,32,256]{3,2,1,0:T(8,128)(2,1)S(1)} collective-permute-done((bf16[8,4,32,256]{3,2,1,0:T(8,128)(2,1)S(1)}, bf16[8,4,32,256]{3,2,1,0:T(8,128)(2,1)S(1)}, u32[]{:S(2)}, u32[]{:S(2)}) %collective-permute-start.43) | collective-permute-done | bytes 524320 | tf_op jit(solution)/shard_map/ppermute | solution.py:421
  235.0 10.3 %collective-permute-done.44.refs_3_ = bf16[8,4,32,256]{3,2,1,0:T(8,128)(2,1)S(1)} collective-permute-done((bf16[8,4,32,256]{3,2,1,0:T(8,128)(2,1)S(1)}, bf16[8,4,32,256]{3,2,1,0:T(8,128)(2,1)S(1)}, u32[]{:S(2)}, u32[]{:S(2)}) %collective-permute-start.44) | collective-permute-done | bytes 524320 | tf_op jit(solution)/shard_map/ppermute | solution.py:421
  245.3 10.8 %points.9 = (bf16[8,4,32,256]{3,2,1,0:T(8,128)(2,1)S(1)}, bf16[8,4,32,256]{3,2,1,0:T(8,128)(2,1)S(1)}, bf16[8,4,32,256]{3,2,1,0:T(8,128)(2,1)S(1)}, bf16[8,4,32,256]{3,2,1,0:T(8,128)(2,1)S(1)}, s32[2]{0:T(128)S(1)}) custom-call(s32[2]{0:T(128)S(1)} %get-tuple-element.164.pos, bf16[352,128]{1,0:T(8,128)(2,1)S(1)} %pad.15.clone.refs_1_.basis, ...), custom_call_target="tpu_custom_call" | custom-call | flops 1 | bytes 1 | tf_op jit(solution)/shard_map/points/pallas_call | solution.py:260
  258.6 9.1 %collective-permute-done.47.refs_3_.refs_4_ = bf16[8,4,32,256]{3,2,1,0:T(8,128)(2,1)S(1)} collective-permute-done((bf16[8,4,32,256]{3,2,1,0:T(8,128)(2,1)S(1)}, bf16[8,4,32,256]{3,2,1,0:T(8,128)(2,1)S(1)}, u32[]{:S(2)}, u32[]{:S(2)}) %collective-permute-start.47) | collective-permute-done | bytes 524320 | tf_op jit(solution)/shard_map/ppermute | solution.py:421
  269.8 3.2 settle.7
  273.0 6.9 %collective-permute-done.50.refs_2_.refs_3_ = bf16[8,4,32,256]{3,2,1,0:T(8,128)(2,1)S(1)} collective-permute-done((bf16[8,4,32,256]{3,2,1,0:T(8,128)(2,1)S(1)}, bf16[8,4,32,256]{3,2,1,0:T(8,128)(2,1)S(1)}, u32[]{:S(2)}, u32[]{:S(2)}) %collective-permute-start.50) | collective-permute-done | bytes 524320 | tf_op jit(solution)/shard_map/ppermute | solution.py:421
  279.9 10.3 %collective-permute-done.51.refs_3_.refs_4_ = bf16[8,4,32,256]{3,2,1,0:T(8,128)(2,1)S(1)} collective-permute-done((bf16[8,4,32,256]{3,2,1,0:T(8,128)(2,1)S(1)}, bf16[8,4,32,256]{3,2,1,0:T(8,128)(2,1)S(1)}, u32[]{:S(2)}, u32[]{:S(2)}) %collective-permute-start.51) | collective-permute-done | bytes 524320 | tf_op jit(solution)/shard_map/ppermute | solution.py:421
  291.9 3.1 collective-permute-done.52.refs_5_
  295.0 3.2 settle.8
  298.2 19.2 %collective-permute-done.53.refs_5_ = bf16[32,2,32,256]{3,2,1,0:T(8,128)(2,1)S(1)} collective-permute-done((bf16[32,2,32,256]{3,2,1,0:T(8,128)(2,1)S(1)}, bf16[32,2,32,256]{3,2,1,0:T(8,128)(2,1)S(1)}, u32[]{:S(2)}, u32[]{:S(2)}) %collective-permute-start.53) | collective-permute-done | bytes 1048608 | tf_op jit(solution)/shard_map/ppermute | solution.py:410
  317.4 3.1 settle.9
  (131 shorter events, 53.4 us)
Async XLA Ops:
  7.6 37.8 %collective-permute-start.1 = (bf16[18,2,32,256]{3,2,1,0:T(8,128)(2,1)}, bf16[18,2,32,256]{3,2,1,0:T(8,128)(2,1)S(1)}, u32[]{:S(2)}, u32[]{:S(2)}) collective-permute-start(bf16[18,2,32,256]{3,2,1,0:T(8,128)(2,1)} %get-tuple-element.99), channel_id=1, source_target_pairs={{0,4},{4,0},{8,12},{12,8},{16,20},{20,16},{24,28},{28,24},{1,5},{5... | collective-permute-start | bytes 1769480 | tf_op jit(solution)/shard_map/ppermute | solution.py:410
  10.6 39.1 %collective-permute-start.2 = (bf16[18,2,32,256]{3,2,1,0:T(8,128)(2,1)S(1)}, bf16[18,2,32,256]{3,2,1,0:T(8,128)(2,1)S(1)}, u32[]{:S(2)}, u32[]{:S(2)}) collective-permute-start(bf16[18,2,32,256]{3,2,1,0:T(8,128)(2,1)S(1)} %get-tuple-element.100.refs_2_.refs_6_), channel_id=1, source_target_pairs={{4,12},{8,0},{12,20},{16,8},{20,28},{24,16},{5,13},{9,1},{13,21},{... | collective-permute-start | bytes 1769480 | tf_op jit(solution)/shard_map/ppermute | solution.py:413
  11.9 20.5 %collective-permute-start = (f32[2,130,256]{2,1,0:T(8,128)S(1)}, f32[2,130,256]{2,1,0:T(8,128)S(1)}, u32[]{:S(2)}, u32[]{:S(2)}) collective-permute-start(f32[2,130,256]{2,1,0:T(8,128)S(1)} %get-tuple-element.192.refs_0_), channel_id=1, source_target_pairs={{0,4},{4,0},{8,12},{12,8},{16,20},{20,16},{24,28},{28,24},{1,5},{5... | collective-permute-start | bytes 798728 | tf_op jit(solution)/shard_map/ppermute | solution.py:410
  15.4 28.6 %collective-permute-start.4 = (f32[1,130,256]{2,1,0:T(8,128)}, f32[1,130,256]{2,1,0:T(8,128)S(1)}, u32[]{:S(2)}, u32[]{:S(2)}) collective-permute-start(f32[1,130,256]{2,1,0:T(8,128)} %slice.41), channel_id=1, source_target_pairs={{4,8},{8,4},{12,16},{16,12},{20,24},{24,20},{5,9},{9,5},{13,17},{1... | collective-permute-start | bytes 399368 | tf_op jit(solution)/shard_map/ppermute | solution.py:443
  16.7 27.4 %collective-permute-start.3 = (f32[1,130,256]{2,1,0:T(8,128)}, f32[1,130,256]{2,1,0:T(8,128)S(1)}, u32[]{:S(2)}, u32[]{:S(2)}) collective-permute-start(f32[1,130,256]{2,1,0:T(8,128)} %slice.40), channel_id=1, source_target_pairs={{4,12},{8,0},{12,20},{16,8},{20,28},{24,16},{5,13},{9,1},{13,21},{... | collective-permute-start | bytes 399368 | tf_op jit(solution)/shard_map/ppermute | solution.py:413
  32.3 19.8 %collective-permute-start.6 = (bf16[2,128,256]{2,1,0:T(8,128)(2,1)S(1)}, bf16[2,128,256]{2,1,0:T(8,128)(2,1)S(1)}, u32[]{:S(2)}, u32[]{:S(2)}) collective-permute-start(bf16[2,128,256]{2,1,0:T(8,128)(2,1)S(1)} %select_convert_fusion.refs_1_), channel_id=1, source_target_pairs={{0,4},{4,0},{8,12},{12,8},{16,20},{20,16},{24,28},{28,24},{1,5},{5... | collective-permute-start | bytes 393224 | tf_op jit(solution)/shard_map/ppermute | solution.py:410
  44.0 14.9 %collective-permute-start.5 = (bf16[16,2,32,256]{3,2,1,0:T(8,128)(2,1)S(1)}, bf16[16,2,32,256]{3,2,1,0:T(8,128)(2,1)S(1)}, u32[]{:S(2)}, u32[]{:S(2)}) collective-permute-start(bf16[16,2,32,256]{3,2,1,0:T(8,128)(2,1)S(1)} %get-tuple-element.102), channel_id=1, source_target_pairs={{0,4},{4,0},{8,12},{12,8},{16,20},{20,16},{24,28},{28,24},{1,5},{5... | collective-permute-start | bytes 1572872 | tf_op jit(solution)/shard_map/ppermute | solution.py:410
  44.1 16.8 %collective-permute-start.7 = (bf16[16,2,32,256]{3,2,1,0:T(8,128)(2,1)S(1)}, bf16[16,2,32,256]{3,2,1,0:T(8,128)(2,1)S(1)}, u32[]{:S(2)}, u32[]{:S(2)}) collective-permute-start(bf16[16,2,32,256]{3,2,1,0:T(8,128)(2,1)S(1)} %get-tuple-element.103.refs_2_.refs_6_), channel_id=1, source_target_pairs={{4,12},{8,0},{12,20},{16,8},{20,28},{24,16},{5,13},{9,1},{13,21},{... | collective-permute-start | bytes 1572872 | tf_op jit(solution)/shard_map/ppermute | solution.py:413
  45.4 36.0 %collective-permute-start.9 = (bf16[32,2,32,256]{3,2,1,0:T(8,128)(2,1)S(1)}, bf16[32,2,32,256]{3,2,1,0:T(8,128)(2,1)S(1)}, u32[]{:S(2)}, u32[]{:S(2)}) collective-permute-start(bf16[32,2,32,256]{3,2,1,0:T(8,128)(2,1)S(1)} %get-tuple-element.107), channel_id=1, source_target_pairs={{0,4},{4,0},{8,12},{12,8},{16,20},{20,16},{24,28},{28,24},{1,5},{5... | collective-permute-start | bytes 3145736 | tf_op jit(solution)/shard_map/ppermute | solution.py:410
  49.7 33.7 %collective-permute-start.10 = (bf16[32,2,32,256]{3,2,1,0:T(8,128)(2,1)S(1)}, bf16[32,2,32,256]{3,2,1,0:T(8,128)(2,1)S(1)}, u32[]{:S(2)}, u32[]{:S(2)}) collective-permute-start(bf16[32,2,32,256]{3,2,1,0:T(8,128)(2,1)S(1)} %get-tuple-element.108.refs_2_.refs_6_), channel_id=1, source_target_pairs={{4,12},{8,0},{12,20},{16,8},{20,28},{24,16},{5,13},{9,1},{13,21},{... | collective-permute-start | bytes 3145736 | tf_op jit(solution)/shard_map/ppermute | solution.py:413
  52.1 18.3 %collective-permute-start.8 = (bf16[18,2,32,256]{3,2,1,0:T(8,128)(2,1)S(1)}, bf16[18,2,32,256]{3,2,1,0:T(8,128)(2,1)S(1)}, u32[]{:S(2)}, u32[]{:S(2)}) collective-permute-start(bf16[18,2,32,256]{3,2,1,0:T(8,128)(2,1)S(1)} %get-tuple-element.105.refs_1_.refs_5_), channel_id=1, source_target_pairs={{12,4},{0,8},{20,12},{8,16},{28,20},{16,24},{13,5},{1,9},{21,13},{... | collective-permute-start | bytes 1769480 | tf_op jit(solution)/shard_map/ppermute | solution.py:416
  62.1 16.1 %collective-permute-start.11 = (bf16[16,2,32,256]{3,2,1,0:T(8,128)(2,1)S(1)}, bf16[16,2,32,256]{3,2,1,0:T(8,128)(2,1)S(1)}, u32[]{:S(2)}, u32[]{:S(2)}) collective-permute-start(bf16[16,2,32,256]{3,2,1,0:T(8,128)(2,1)S(1)} %get-tuple-element.110.refs_1_.refs_5_), channel_id=1, source_target_pairs={{12,4},{0,8},{20,12},{8,16},{28,20},{16,24},{13,5},{1,9},{21,13},{... | collective-permute-start | bytes 1572872 | tf_op jit(solution)/shard_map/ppermute | solution.py:416
  66.2 36.0 %collective-permute-start.15 = (bf16[32,2,32,256]{3,2,1,0:T(8,128)(2,1)S(1)}, bf16[32,2,32,256]{3,2,1,0:T(8,128)(2,1)S(1)}, u32[]{:S(2)}, u32[]{:S(2)}) collective-permute-start(bf16[32,2,32,256]{3,2,1,0:T(8,128)(2,1)S(1)} %get-tuple-element.118), channel_id=1, source_target_pairs={{0,4},{4,0},{8,12},{12,8},{16,20},{20,16},{24,28},{28,24},{1,5},{5... | collective-permute-start | bytes 3145736 | tf_op jit(solution)/shard_map/ppermute | solution.py:410
  70.5 33.0 %collective-permute-start.16 = (bf16[32,2,32,256]{3,2,1,0:T(8,128)(2,1)}, bf16[32,2,32,256]{3,2,1,0:T(8,128)(2,1)S(1)}, u32[]{:S(2)}, u32[]{:S(2)}) collective-permute-start(bf16[32,2,32,256]{3,2,1,0:T(8,128)(2,1)} %get-tuple-element.119.refs_2_.refs_6_), channel_id=1, source_target_pairs={{4,12},{8,0},{12,20},{16,8},{20,28},{24,16},{5,13},{9,1},{13,21},{... | collective-permute-start | bytes 3145736 | tf_op jit(solution)/shard_map/ppermute | solution.py:413
  78.2 11.5 %collective-permute-start.12 = (bf16[4,4,32,256]{3,2,1,0:T(8,128)(2,1)S(1)}, bf16[4,4,32,256]{3,2,1,0:T(8,128)(2,1)S(1)}, u32[]{:S(2)}, u32[]{:S(2)}) collective-permute-start(bf16[4,4,32,256]{3,2,1,0:T(8,128)(2,1)S(1)} %get-tuple-element.114), channel_id=1, source_target_pairs={{0,1},{1,0},{2,3},{3,2},{4,5},{5,4},{6,7},{7,6},{8,9},{9,8},{10,11... | collective-permute-start | bytes 786440 | tf_op jit(solution)/shard_map/ppermute | solution.py:421
  89.7 15.1 %collective-permute-start.18 = (bf16[4,4,32,256]{3,2,1,0:T(8,128)(2,1)S(1)}, bf16[4,4,32,256]{3,2,1,0:T(8,128)(2,1)S(1)}, u32[]{:S(2)}, u32[]{:S(2)}) collective-permute-start(bf16[4,4,32,256]{3,2,1,0:T(8,128)(2,1)S(1)} %get-tuple-element.124), channel_id=1, source_target_pairs={{0,1},{1,0},{2,3},{3,2},{4,5},{5,4},{6,7},{7,6},{8,9},{9,8},{10,11... | collective-permute-start | bytes 786440 | tf_op jit(solution)/shard_map/ppermute | solution.py:421
  91.4 15.3 %collective-permute-start.19 = (bf16[4,4,32,256]{3,2,1,0:T(8,128)(2,1)S(1)}, bf16[4,4,32,256]{3,2,1,0:T(8,128)(2,1)S(1)}, u32[]{:S(2)}, u32[]{:S(2)}) collective-permute-start(bf16[4,4,32,256]{3,2,1,0:T(8,128)(2,1)S(1)} %get-tuple-element.125), channel_id=1, source_target_pairs={{0,2},{1,3},{2,0},{3,1},{4,6},{5,7},{6,4},{7,5},{8,10},{9,11},{10,... | collective-permute-start | bytes 786440 | tf_op jit(solution)/shard_map/ppermute | solution.py:421
  92.7 26.8 %collective-permute-start.17 = (bf16[32,2,32,256]{3,2,1,0:T(8,128)(2,1)S(1)}, bf16[32,2,32,256]{3,2,1,0:T(8,128)(2,1)S(1)}, u32[]{:S(2)}, u32[]{:S(2)}) collective-permute-start(bf16[32,2,32,256]{3,2,1,0:T(8,128)(2,1)S(1)} %get-tuple-element.121.refs_1_.refs_5_), channel_id=1, source_target_pairs={{12,4},{0,8},{20,12},{8,16},{28,20},{16,24},{13,5},{1,9},{21,13},{... | collective-permute-start | bytes 3145736 | tf_op jit(solution)/shard_map/ppermute | solution.py:416
  102.2 35.7 %collective-permute-start.24 = (bf16[32,2,32,256]{3,2,1,0:T(8,128)(2,1)S(1)}, bf16[32,2,32,256]{3,2,1,0:T(8,128)(2,1)S(1)}, u32[]{:S(2)}, u32[]{:S(2)}) collective-permute-start(bf16[32,2,32,256]{3,2,1,0:T(8,128)(2,1)S(1)} %copy-done.10), channel_id=1, source_target_pairs={{0,4},{4,0},{8,12},{12,8},{16,20},{20,16},{24,28},{28,24},{1,5},{5... | collective-permute-start | bytes 3145736 | tf_op jit(solution)/shard_map/ppermute | solution.py:410
  103.5 34.4 %collective-permute-start.25 = (bf16[32,2,32,256]{3,2,1,0:T(8,128)(2,1)S(1)}, bf16[32,2,32,256]{3,2,1,0:T(8,128)(2,1)S(1)}, u32[]{:S(2)}, u32[]{:S(2)}) collective-permute-start(bf16[32,2,32,256]{3,2,1,0:T(8,128)(2,1)S(1)} %copy-done.2), channel_id=1, source_target_pairs={{4,12},{8,0},{12,20},{16,8},{20,28},{24,16},{5,13},{9,1},{13,21},{... | collective-permute-start | bytes 3145736 | tf_op jit(solution)/shard_map/ppermute | solution.py:413
  106.7 36.8 %collective-permute-start.26 = (bf16[32,2,32,256]{3,2,1,0:T(8,128)(2,1)S(1)}, bf16[32,2,32,256]{3,2,1,0:T(8,128)(2,1)S(1)}, u32[]{:S(2)}, u32[]{:S(2)}) collective-permute-start(bf16[32,2,32,256]{3,2,1,0:T(8,128)(2,1)S(1)} %get-tuple-element.136.refs_1_.refs_5_), channel_id=1, source_target_pairs={{12,4},{0,8},{20,12},{8,16},{28,20},{16,24},{13,5},{1,9},{21,13},{... | collective-permute-start | bytes 3145736 | tf_op jit(solution)/shard_map/ppermute | solution.py:416
  114.9 20.7 %collective-permute-start.22 = (bf16[4,4,32,256]{3,2,1,0:T(8,128)(2,1)S(1)}, bf16[4,4,32,256]{3,2,1,0:T(8,128)(2,1)S(1)}, u32[]{:S(2)}, u32[]{:S(2)}) collective-permute-start(bf16[4,4,32,256]{3,2,1,0:T(8,128)(2,1)S(1)} %get-tuple-element.130), channel_id=1, source_target_pairs={{0,2},{1,3},{2,0},{3,1},{4,6},{5,7},{6,4},{7,5},{8,10},{9,11},{10,... | collective-permute-start | bytes 786440 | tf_op jit(solution)/shard_map/ppermute | solution.py:421
  119.4 16.5 %collective-permute-start.23 = (bf16[4,4,32,256]{3,2,1,0:T(8,128)(2,1)S(1)}, bf16[4,4,32,256]{3,2,1,0:T(8,128)(2,1)S(1)}, u32[]{:S(2)}, u32[]{:S(2)}) collective-permute-start(bf16[4,4,32,256]{3,2,1,0:T(8,128)(2,1)S(1)} %get-tuple-element.131), channel_id=1, source_target_pairs={{0,3},{1,2},{2,1},{3,0},{4,7},{5,6},{6,5},{7,4},{8,11},{9,10},{10,... | collective-permute-start | bytes 786440 | tf_op jit(solution)/shard_map/ppermute | solution.py:421
  137.8 37.4 %collective-permute-start.27 = (bf16[8,4,32,256]{3,2,1,0:T(8,128)(2,1)S(1)}, bf16[8,4,32,256]{3,2,1,0:T(8,128)(2,1)S(1)}, u32[]{:S(2)}, u32[]{:S(2)}) collective-permute-start(bf16[8,4,32,256]{3,2,1,0:T(8,128)(2,1)S(1)} %get-tuple-element.139), channel_id=1, source_target_pairs={{0,1},{1,0},{2,3},{3,2},{4,5},{5,4},{6,7},{7,6},{8,9},{9,8},{10,11... | collective-permute-start | bytes 1572872 | tf_op jit(solution)/shard_map/ppermute | solution.py:421
  139.1 51.4 %collective-permute-start.34 = (bf16[32,2,32,256]{3,2,1,0:T(8,128)(2,1)S(1)}, bf16[32,2,32,256]{3,2,1,0:T(8,128)(2,1)S(1)}, u32[]{:S(2)}, u32[]{:S(2)}) collective-permute-start(bf16[32,2,32,256]{3,2,1,0:T(8,128)(2,1)S(1)} %get-tuple-element.150.refs_1_), channel_id=1, source_target_pairs={{12,4},{0,8},{20,12},{8,16},{28,20},{16,24},{13,5},{1,9},{21,13},{... | collective-permute-start | bytes 3145736 | tf_op jit(solution)/shard_map/ppermute | solution.py:416
  143.5 31.7 %collective-permute-start.28 = (bf16[8,4,32,256]{3,2,1,0:T(8,128)(2,1)S(1)}, bf16[8,4,32,256]{3,2,1,0:T(8,128)(2,1)S(1)}, u32[]{:S(2)}, u32[]{:S(2)}) collective-permute-start(bf16[8,4,32,256]{3,2,1,0:T(8,128)(2,1)S(1)} %get-tuple-element.140), channel_id=1, source_target_pairs={{0,2},{1,3},{2,0},{3,1},{4,6},{5,7},{6,4},{7,5},{8,10},{9,11},{10,... | collective-permute-start | bytes 1572872 | tf_op jit(solution)/shard_map/ppermute | solution.py:421
  145.1 31.0 %collective-permute-start.29 = (bf16[8,4,32,256]{3,2,1,0:T(8,128)(2,1)S(1)}, bf16[8,4,32,256]{3,2,1,0:T(8,128)(2,1)S(1)}, u32[]{:S(2)}, u32[]{:S(2)}) collective-permute-start(bf16[8,4,32,256]{3,2,1,0:T(8,128)(2,1)S(1)} %get-tuple-element.141), channel_id=1, source_target_pairs={{0,3},{1,2},{2,1},{3,0},{4,7},{5,6},{6,5},{7,4},{8,11},{9,10},{10,... | collective-permute-start | bytes 1572872 | tf_op jit(solution)/shard_map/ppermute | solution.py:421
  145.2 28.6 %collective-permute-start.32 = (bf16[4,4,32,256]{3,2,1,0:T(8,128)(2,1)S(1)}, bf16[4,4,32,256]{3,2,1,0:T(8,128)(2,1)S(1)}, u32[]{:S(2)}, u32[]{:S(2)}) collective-permute-start(bf16[4,4,32,256]{3,2,1,0:T(8,128)(2,1)S(1)} %get-tuple-element.146), channel_id=1, source_target_pairs={{0,3},{1,2},{2,1},{3,0},{4,7},{5,6},{6,5},{7,4},{8,11},{9,10},{10,... | collective-permute-start | bytes 786440 | tf_op jit(solution)/shard_map/ppermute | solution.py:421
  173.8 15.5 %collective-permute-start.33 = (bf16[16,2,32,256]{3,2,1,0:T(8,128)(2,1)S(1)}, bf16[16,2,32,256]{3,2,1,0:T(8,128)(2,1)S(1)}, u32[]{:S(2)}, u32[]{:S(2)}) collective-permute-start(bf16[16,2,32,256]{3,2,1,0:T(8,128)(2,1)S(1)} %get-tuple-element.148), channel_id=1, source_target_pairs={{0,4},{4,0},{8,12},{12,8},{16,20},{20,16},{24,28},{28,24},{1,5},{5... | collective-permute-start | bytes 1572872 | tf_op jit(solution)/shard_map/ppermute | solution.py:410
  175.3 14.4 %collective-permute-start.35 = (bf16[8,4,32,256]{3,2,1,0:T(8,128)(2,1)S(1)}, bf16[8,4,32,256]{3,2,1,0:T(8,128)(2,1)S(1)}, u32[]{:S(2)}, u32[]{:S(2)}) collective-permute-start(bf16[8,4,32,256]{3,2,1,0:T(8,128)(2,1)S(1)} %get-tuple-element.153), channel_id=1, source_target_pairs={{0,1},{1,0},{2,3},{3,2},{4,5},{5,4},{6,7},{7,6},{8,9},{9,8},{10,11... | collective-permute-start | bytes 1572872 | tf_op jit(solution)/shard_map/ppermute | solution.py:421
  175.3 27.6 %collective-permute-start.36 = (bf16[8,4,32,256]{3,2,1,0:T(8,128)(2,1)S(1)}, bf16[8,4,32,256]{3,2,1,0:T(8,128)(2,1)S(1)}, u32[]{:S(2)}, u32[]{:S(2)}) collective-permute-start(bf16[8,4,32,256]{3,2,1,0:T(8,128)(2,1)S(1)} %get-tuple-element.154), channel_id=1, source_target_pairs={{0,2},{1,3},{2,0},{3,1},{4,6},{5,7},{6,4},{7,5},{8,10},{9,11},{10,... | collective-permute-start | bytes 1572872 | tf_op jit(solution)/shard_map/ppermute | solution.py:421
  176.1 27.6 %collective-permute-start.37 = (bf16[8,4,32,256]{3,2,1,0:T(8,128)(2,1)S(1)}, bf16[8,4,32,256]{3,2,1,0:T(8,128)(2,1)S(1)}, u32[]{:S(2)}, u32[]{:S(2)}) collective-permute-start(bf16[8,4,32,256]{3,2,1,0:T(8,128)(2,1)S(1)} %get-tuple-element.155), channel_id=1, source_target_pairs={{0,3},{1,2},{2,1},{3,0},{4,7},{5,6},{6,5},{7,4},{8,11},{9,10},{10,... | collective-permute-start | bytes 1572872 | tf_op jit(solution)/shard_map/ppermute | solution.py:421
  189.3 25.5 %collective-permute-start.38 = (bf16[8,4,32,256]{3,2,1,0:T(8,128)(2,1)S(1)}, bf16[8,4,32,256]{3,2,1,0:T(8,128)(2,1)S(1)}, u32[]{:S(2)}, u32[]{:S(2)}) collective-permute-start(bf16[8,4,32,256]{3,2,1,0:T(8,128)(2,1)S(1)} %get-tuple-element.158), channel_id=1, source_target_pairs={{0,1},{1,0},{2,3},{3,2},{4,5},{5,4},{6,7},{7,6},{8,9},{9,8},{10,11... | collective-permute-start | bytes 1572872 | tf_op jit(solution)/shard_map/ppermute | solution.py:421
  189.7 26.8 %collective-permute-start.39 = (bf16[8,4,32,256]{3,2,1,0:T(8,128)(2,1)S(1)}, bf16[8,4,32,256]{3,2,1,0:T(8,128)(2,1)S(1)}, u32[]{:S(2)}, u32[]{:S(2)}) collective-permute-start(bf16[8,4,32,256]{3,2,1,0:T(8,128)(2,1)S(1)} %get-tuple-element.159), channel_id=1, source_target_pairs={{0,2},{1,3},{2,0},{3,1},{4,6},{5,7},{6,4},{7,5},{8,10},{9,11},{10,... | collective-permute-start | bytes 1572872 | tf_op jit(solution)/shard_map/ppermute | solution.py:421
  190.5 32.3 %collective-permute-start.40 = (bf16[8,4,32,256]{3,2,1,0:T(8,128)(2,1)S(1)}, bf16[8,4,32,256]{3,2,1,0:T(8,128)(2,1)S(1)}, u32[]{:S(2)}, u32[]{:S(2)}) collective-permute-start(bf16[8,4,32,256]{3,2,1,0:T(8,128)(2,1)S(1)} %get-tuple-element.160), channel_id=1, source_target_pairs={{0,3},{1,2},{2,1},{3,0},{4,7},{5,6},{6,5},{7,4},{8,11},{9,10},{10,... | collective-permute-start | bytes 1572872 | tf_op jit(solution)/shard_map/ppermute | solution.py:421
  202.9 22.0 %collective-permute-start.41 = (bf16[16,2,32,256]{3,2,1,0:T(8,128)(2,1)S(1)}, bf16[16,2,32,256]{3,2,1,0:T(8,128)(2,1)S(1)}, u32[]{:S(2)}, u32[]{:S(2)}) collective-permute-start(bf16[16,2,32,256]{3,2,1,0:T(8,128)(2,1)S(1)} %get-tuple-element.163), channel_id=1, source_target_pairs={{0,4},{4,0},{8,12},{12,8},{16,20},{20,16},{24,28},{28,24},{1,5},{5... | collective-permute-start | bytes 1572872 | tf_op jit(solution)/shard_map/ppermute | solution.py:410
  203.7 21.7 %collective-permute-start.42 = (bf16[8,4,32,256]{3,2,1,0:T(8,128)(2,1)S(1)}, bf16[8,4,32,256]{3,2,1,0:T(8,128)(2,1)S(1)}, u32[]{:S(2)}, u32[]{:S(2)}) collective-permute-start(bf16[8,4,32,256]{3,2,1,0:T(8,128)(2,1)S(1)} %get-tuple-element.166), channel_id=1, source_target_pairs={{0,1},{1,0},{2,3},{3,2},{4,5},{5,4},{6,7},{7,6},{8,9},{9,8},{10,11... | collective-permute-start | bytes 1572872 | tf_op jit(solution)/shard_map/ppermute | solution.py:421
  214.8 20.2 %collective-permute-start.43 = (bf16[8,4,32,256]{3,2,1,0:T(8,128)(2,1)S(1)}, bf16[8,4,32,256]{3,2,1,0:T(8,128)(2,1)S(1)}, u32[]{:S(2)}, u32[]{:S(2)}) collective-permute-start(bf16[8,4,32,256]{3,2,1,0:T(8,128)(2,1)S(1)} %get-tuple-element.167), channel_id=1, source_target_pairs={{0,2},{1,3},{2,0},{3,1},{4,6},{5,7},{6,4},{7,5},{8,10},{9,11},{10,... | collective-permute-start | bytes 1572872 | tf_op jit(solution)/shard_map/ppermute | solution.py:421
  216.5 28.8 %collective-permute-start.44 = (bf16[8,4,32,256]{3,2,1,0:T(8,128)(2,1)S(1)}, bf16[8,4,32,256]{3,2,1,0:T(8,128)(2,1)S(1)}, u32[]{:S(2)}, u32[]{:S(2)}) collective-permute-start(bf16[8,4,32,256]{3,2,1,0:T(8,128)(2,1)S(1)} %get-tuple-element.168), channel_id=1, source_target_pairs={{0,3},{1,2},{2,1},{3,0},{4,7},{5,6},{6,5},{7,4},{8,11},{9,10},{10,... | collective-permute-start | bytes 1572872 | tf_op jit(solution)/shard_map/ppermute | solution.py:421
  224.1 45.7 %collective-permute-start.48 = (bf16[32,2,32,256]{3,2,1,0:T(8,128)(2,1)S(1)}, bf16[32,2,32,256]{3,2,1,0:T(8,128)(2,1)S(1)}, u32[]{:S(2)}, u32[]{:S(2)}) collective-permute-start(bf16[32,2,32,256]{3,2,1,0:T(8,128)(2,1)S(1)} %get-tuple-element.176), channel_id=1, source_target_pairs={{0,4},{4,0},{8,12},{12,8},{16,20},{20,16},{24,28},{28,24},{1,5},{5... | collective-permute-start | bytes 3145736 | tf_op jit(solution)/shard_map/ppermute | solution.py:410
  224.9 32.3 %collective-permute-start.45 = (bf16[8,4,32,256]{3,2,1,0:T(8,128)(2,1)S(1)}, bf16[8,4,32,256]{3,2,1,0:T(8,128)(2,1)S(1)}, u32[]{:S(2)}, u32[]{:S(2)}) collective-permute-start(bf16[8,4,32,256]{3,2,1,0:T(8,128)(2,1)S(1)} %get-tuple-element.171), channel_id=1, source_target_pairs={{0,1},{1,0},{2,3},{3,2},{4,5},{5,4},{6,7},{7,6},{8,9},{9,8},{10,11... | collective-permute-start | bytes 1572872 | tf_op jit(solution)/shard_map/ppermute | solution.py:421
  225.4 32.6 %collective-permute-start.46 = (bf16[8,4,32,256]{3,2,1,0:T(8,128)(2,1)S(1)}, bf16[8,4,32,256]{3,2,1,0:T(8,128)(2,1)S(1)}, u32[]{:S(2)}, u32[]{:S(2)}) collective-permute-start(bf16[8,4,32,256]{3,2,1,0:T(8,128)(2,1)S(1)} %get-tuple-element.172), channel_id=1, source_target_pairs={{0,2},{1,3},{2,0},{3,1},{4,6},{5,7},{6,4},{7,5},{8,10},{9,11},{10,... | collective-permute-start | bytes 1572872 | tf_op jit(solution)/shard_map/ppermute | solution.py:421
  235.0 32.8 %collective-permute-start.47 = (bf16[8,4,32,256]{3,2,1,0:T(8,128)(2,1)S(1)}, bf16[8,4,32,256]{3,2,1,0:T(8,128)(2,1)S(1)}, u32[]{:S(2)}, u32[]{:S(2)}) collective-permute-start(bf16[8,4,32,256]{3,2,1,0:T(8,128)(2,1)S(1)} %get-tuple-element.173), channel_id=1, source_target_pairs={{0,3},{1,2},{2,1},{3,0},{4,7},{5,6},{6,5},{7,4},{8,11},{9,10},{10,... | collective-permute-start | bytes 1572872 | tf_op jit(solution)/shard_map/ppermute | solution.py:421
  256.1 16.9 %collective-permute-start.49 = (bf16[8,4,32,256]{3,2,1,0:T(8,128)(2,1)S(1)}, bf16[8,4,32,256]{3,2,1,0:T(8,128)(2,1)S(1)}, u32[]{:S(2)}, u32[]{:S(2)}) collective-permute-start(bf16[8,4,32,256]{3,2,1,0:T(8,128)(2,1)S(1)} %get-tuple-element.179), channel_id=1, source_target_pairs={{0,1},{1,0},{2,3},{3,2},{4,5},{5,4},{6,7},{7,6},{8,9},{9,8},{10,11... | collective-permute-start | bytes 1572872 | tf_op jit(solution)/shard_map/ppermute | solution.py:421
  257.2 22.7 %collective-permute-start.50 = (bf16[8,4,32,256]{3,2,1,0:T(8,128)(2,1)S(1)}, bf16[8,4,32,256]{3,2,1,0:T(8,128)(2,1)S(1)}, u32[]{:S(2)}, u32[]{:S(2)}) collective-permute-start(bf16[8,4,32,256]{3,2,1,0:T(8,128)(2,1)S(1)} %get-tuple-element.180), channel_id=1, source_target_pairs={{0,2},{1,3},{2,0},{3,1},{4,6},{5,7},{6,4},{7,5},{8,10},{9,11},{10,... | collective-permute-start | bytes 1572872 | tf_op jit(solution)/shard_map/ppermute | solution.py:421
  258.0 32.2 %collective-permute-start.51 = (bf16[8,4,32,256]{3,2,1,0:T(8,128)(2,1)S(1)}, bf16[8,4,32,256]{3,2,1,0:T(8,128)(2,1)S(1)}, u32[]{:S(2)}, u32[]{:S(2)}) collective-permute-start(bf16[8,4,32,256]{3,2,1,0:T(8,128)(2,1)S(1)} %get-tuple-element.181), channel_id=1, source_target_pairs={{0,3},{1,2},{2,1},{3,0},{4,7},{5,6},{6,5},{7,4},{8,11},{9,10},{10,... | collective-permute-start | bytes 1572872 | tf_op jit(solution)/shard_map/ppermute | solution.py:421
  269.0 26.0 %collective-permute-start.52 = (bf16[32,2,32,256]{3,2,1,0:T(8,128)(2,1)S(1)}, bf16[32,2,32,256]{3,2,1,0:T(8,128)(2,1)S(1)}, u32[]{:S(2)}, u32[]{:S(2)}) collective-permute-start(bf16[32,2,32,256]{3,2,1,0:T(8,128)(2,1)S(1)} %get-tuple-element.184), channel_id=1, source_target_pairs={{0,4},{4,0},{8,12},{12,8},{16,20},{20,16},{24,28},{28,24},{1,5},{5... | collective-permute-start | bytes 3145736 | tf_op jit(solution)/shard_map/ppermute | solution.py:410
  291.5 25.9 %collective-permute-start.53 = (bf16[32,2,32,256]{3,2,1,0:T(8,128)(2,1)S(1)}, bf16[32,2,32,256]{3,2,1,0:T(8,128)(2,1)S(1)}, u32[]{:S(2)}, u32[]{:S(2)}) collective-permute-start(bf16[32,2,32,256]{3,2,1,0:T(8,128)(2,1)S(1)} %get-tuple-element.187), channel_id=1, source_target_pairs={{0,4},{4,0},{8,12},{12,8},{16,20},{20,16},{24,28},{28,24},{1,5},{5... | collective-permute-start | bytes 3145736 | tf_op jit(solution)/shard_map/ppermute | solution.py:410
  (17 other events, 390.3 us)

commit v8 on v7

--- a/solution.py
+++ b/solution.py
@@ -13,7 +13,7 @@
 VMEM = pl.BlockSpec(memory_space=pltpu.VMEM)
 HBM = pl.BlockSpec(memory_space=pltpu.HBM)
 SMEM = pl.BlockSpec(memory_space=pltpu.SMEM)
-TOKEN = jax.ShapeDtypeStruct((2,), jnp.int32)
+TOKEN = jax.ShapeDtypeStruct((3,), jnp.int32)
 COST = pl.CostEstimate(flops=1, bytes_accessed=1, transcendentals=0)
 EDGE = 2
 TILE = 16
@@ -28,6 +28,11 @@
     if group % 16 == 0:
         return y.astype(BF16).reshape(-1, group, y.shape[1])
     return y.reshape(-1, group, y.shape[1]).astype(BF16)
+
+
+def hand_on(pos, token):
+    for n in range(3):
+        token[n] = pos[n]
 
 
 def to_bf16_rows(x):
@@ -37,34 +42,53 @@
     return x.astype(F32).reshape(a * m, y).astype(BF16)
 
 
-def spread_kernel(pos, field, turn, *refs, spans):
+def spread_kernel(pos, field, raw, turn, *refs, spans, base):
     outs, (token, window, sems) = refs[-3 - 2 * len(spans) : -3], refs[-3:]
-    side = pos[0]
-    token[0], token[1] = pos[0], pos[1]
+    side, core = pos[0], pos[2]
+    hand_on(pos, token)
     blocks, _, planes, modes, _, cols = window.shape
-    base = spans[0][0] // TILE
+    modes = modes // 2
     size = field.shape[2]
+    quarter = size // 4
+    depth = raw.shape[3]
     group = turn.shape[1] // TILE
     copies = {}
     for g in range(blocks):
         for a in range(2):
             far = 1 - side if a == 0 else side
-            begin = (base + g) * TILE
+            begin = core * quarter + (base + g) * TILE
+            there = g if base >= 0 else g - 1 + core
+            if base + g < 0:
+                begin, there = jnp.maximum(begin, 0), jnp.maximum(there, 0)
             start = pl.multiple_of(jnp.where(far == 1, size - TILE - begin, begin), TILE)
-            copies[g, a] = pltpu.make_async_copy(
-                field.at[:, :, pl.ds(start, TILE), :], window.at[g, a], sems.at[g, a]
+            place = pl.multiple_of(jnp.where(far == 1, depth - TILE * (there + 1), TILE * there), TILE)
+            copies[g, a] = (
+                pltpu.make_async_copy(
+                    field.at[:, :, pl.ds(start, TILE), :],
+                    window.at[g, a, :, pl.ds(core * modes, modes)],
+                    sems.at[g, a, 0],
+                ),
+                pltpu.make_async_copy(
+                    raw.at[a, :, :, pl.ds(place, TILE), :],
+                    window.at[g, a, :, pl.ds((1 - core) * modes, modes)],
+                    sems.at[g, a, 1],
+                ),
             )
-            copies[g, a].start()
+            for copy in copies[g, a]:
+                copy.start()
     for g in range(blocks):
         for a in range(2):
             far = 1 - side if a == 0 else side
-            copies[g, a].wait()
+            for copy in copies[g, a]:
+                copy.wait()
             for z in range(planes):
                 to = jnp.where(far == 1, z, planes - 1 - z)
-                for h in range(modes // group):
+                for h in range(2 * modes // group):
                     there = pl.ds(h * group, group)
                     x = window[g, a, z, there]
                     y = jnp.dot(turn[far], x.reshape(group * TILE, cols), preferred_element_type=F32)
+                    if base + g < 0:
+                        y = jnp.where(core == 1, y, 0.0)
                     y = from_rows(y, group)
                     for n, (first, last) in enumerate(spans):
                         low, high = (min(max(r - (base + g) * TILE, 0), TILE) for r in (first, last))
@@ -73,29 +97,34 @@
                             outs[2 * n + a][pl.ds(at, high - low), to, there, :] = y[low:high]
 
 
-def spread(pos, field, turn, after, spans):
+def blocks_of(spans):
+    base = spans[0][0] // TILE
+    return base, -(-spans[-1][1] // TILE) - base
+
+
+def spread(pos, field, raw, turn, after, spans):
     planes, modes, _, cols = field.shape
-    pieces = [jax.ShapeDtypeStruct((last - first, planes, modes, cols), BF16) for first, last in spans]
+    pieces = [jax.ShapeDtypeStruct((last - first, planes, 2 * modes, cols), BF16) for first, last in spans]
     pieces = [piece for piece in pieces for _ in range(2)]
-    blocks = -(-spans[-1][1] // TILE) - spans[0][0] // TILE
+    base, blocks = blocks_of(spans)
     return pl.pallas_call(
-        functools.partial(spread_kernel, spans=spans),
+        functools.partial(spread_kernel, spans=spans, base=base),
         out_shape=(*pieces, TOKEN),
-        in_specs=[SMEM, HBM, VMEM] + [ANY] * len(after),
+        in_specs=[SMEM, HBM, ANY, VMEM] + [ANY] * len(after),
         out_specs=(VMEM,) * len(pieces) + (SMEM,),
         scratch_shapes=[
-            pltpu.VMEM((blocks, 2, planes, modes, TILE, cols), BF16),
-            pltpu.SemaphoreType.DMA((blocks, 2)),
+            pltpu.VMEM((blocks, 2, planes, 2 * modes, TILE, cols), BF16),
+            pltpu.SemaphoreType.DMA((blocks, 2, 2)),
         ],
         compiler_params=params(48),
         cost_estimate=COST,
         name="spread",
-    )(pos, field, turn, *after)
+    )(pos, field, raw, turn, *after)
 
 
 def relay_kernel(pos, *refs):
     token = refs[-1]
-    token[0], token[1] = pos[0], pos[1]
+    hand_on(pos, token)
 
 
 def relay(pos, passed, after):
@@ -117,12 +146,12 @@
     blocks, refs = refs[:group], refs[group:]
     tails, refs = refs[:heads], refs[heads:]
     outs, (token, first, edge, sems) = refs[:count], refs[count:]
-    token[0], token[1] = pos[0], pos[1]
+    hand_on(pos, token)
     planes, modes, cols = blocks[0].shape[1:]
     mine = 2 * planes
     part = outs[0].shape[0]
     rows = part * count
-    lead = 2 * EDGE if heads else EDGE
+    lead = 2 * EDGE if heads else 0
     copies = []
     for g in range(heads):
         length = tails[g].shape[0]
@@ -141,9 +170,7 @@
 
     def field(row, p, some):
         if isinstance(row, int) and row < lead:
-            if heads:
-                return edge[row, p, some]
-            return jnp.zeros((some.size, cols), BF16)
+            return edge[row, p, some]
         return blocks[p // planes][row - lead, p % planes, some]
 
     def beside(x):
@@ -226,7 +253,7 @@
 
 def points_kernel(pos, basis, basis_t, flat, swing, load, *refs, begin):
     *refs, token, gathered, stepped = refs
-    token[0], token[1] = pos[0], pos[1]
+    hand_on(pos, token)
     count = len(refs) // 2
     blocks, outs = refs[:count], refs[count:]
     part, planes, modes, cols = blocks[0].shape
@@ -271,7 +298,7 @@
 
 def collect_kernel(pos, *refs):
     *blocks, out, token, sems = refs
-    token[0], token[1] = pos[0], pos[1]
+    hand_on(pos, token)
     part, planes = blocks[0].shape[0], out.shape[1]
     copies = []
     for k, block in enumerate(blocks):
@@ -301,82 +328,125 @@
     )(pos, *blocks)
 
 
-def settle_kernel(pos, turn, *refs, begin, count, chained):
-    if chained:
-        refs = refs[1:]
-    blocks, other = refs[:count], refs[count]
-    out, token, both, final, sems = refs[count + 1 :]
-    token[0], token[1] = pos[0], pos[1]
-    side = pos[0]
-    part = blocks[0].shape[0]
+def put(out, source, side, core, begin, sems):
+    rows, size = source.shape[3], out.shape[2]
+    begin = core * (size // 4) + begin
+    copies = []
+    for a in range(2):
+        far = side if a == 0 else 1 - side
+        start = pl.multiple_of(jnp.where(far == 1, size - rows - begin, begin), TILE)
+        copies.append(pltpu.make_async_copy(source.at[a], out.at[:, :, pl.ds(start, rows), :], sems.at[a]))
+    for copy in copies:
+        copy.start()
+    return copies
+
+
+def settle_kernel(pos, turn, *refs, begin, old_begin, parts, arrivals):
+    refs = refs[-len(parts) - 7 - arrivals :]
+    pieces, arrived, refs = refs[: len(parts)], refs[len(parts) : len(parts) + arrivals], refs[-7:]
+    away, out, token, both, final, sems, out_sems = refs
+    hand_on(pos, token)
+    side, core = pos[0], pos[2]
     _, rows, planes, modes, cols = both.shape
-    size = out.shape[2]
+    modes = modes // 2
     group = turn.shape[1] // TILE
-    incoming = [pltpu.make_async_copy(other, both.at[1], sems.at[count])]
-    for k in range(count):
-        base = jnp.bitwise_xor(pos[1], k) * part
-        incoming.append(
-            pltpu.make_async_copy(blocks[k].at[:, pl.ds(planes, planes)], both.at[0, pl.ds(base, part)], sems.at[k])
+    outgoing = put(out, arrived[0], side, 1 - core, old_begin, out_sems.at[0]) if arrivals else []
+    incoming = []
+    for n, (piece, (a, at, xor, low)) in enumerate(zip(pieces, parts)):
+        length = piece.shape[0]
+        if xor is not None:
+            at = at + jnp.bitwise_xor(pos[1], xor) * length
+        copy = pltpu.make_async_copy(
+            piece.at[:, pl.ds(low, planes)], both.at[a, pl.ds(at, length)], sems.at[n]
         )
-    for copy in incoming:
         copy.start()
-    outgoing = []
-    for a in (1, 0):
-        for copy in incoming[:1] if a else incoming[1:]:
-            copy.wait()
+        incoming.append(copy)
+    for a in (0, 1):
+        for copy, part in zip(incoming, parts):
+            if part[0] == a:
+                copy.wait()
         far = side if a == 0 else 1 - side
         for z in range(planes):
             to = jnp.where(far == 1, z, planes - 1 - z)
             for g in range(rows // TILE):
                 block = jnp.where(far == 1, rows // TILE - 1 - g, g)
-                for h in range(modes // group):
+                for h in range(2 * modes // group):
                     there = pl.ds(h * group, group)
                     x = both[a, pl.ds(g * TILE, TILE), z, there, :]
                     y = jnp.dot(turn[far], to_bf16_rows(x), preferred_element_type=F32).astype(BF16)
                     final[a, to, there, pl.ds(pl.multiple_of(block * TILE, TILE), TILE), :] = y.reshape(
                         group, TILE, cols
                     )
-        start = pl.multiple_of(jnp.where(far == 1, size - rows - begin, begin), TILE)
-        copy = pltpu.make_async_copy(final.at[a], out.at[:, :, pl.ds(start, rows), :], sems.at[count + 1 + a])
-        copy.start()
-        outgoing.append(copy)
+    copy = pltpu.make_async_copy(final.at[:, :, pl.ds((1 - core) * modes, modes)], away, sems.at[len(parts)])
+    copy.start()
+    outgoing.append(copy)
+    outgoing += put(out, final.at[:, :, pl.ds(core * modes, modes)], side, core, begin, out_sems.at[1])
     for copy in outgoing:
         copy.wait()
 
 
-def settle(pos, turn, result, blocks, other, begin, shape):
-    count = len(blocks)
-    rows, planes, modes, cols = other.shape
+def settle(pos, turn, result, pieces, parts, arrived, begin, old_begin, rows, shape):
+    planes, modes, _, cols = shape
     chained = result is not None
+    given = ([result] if chained else []) + list(pieces) + list(arrived)
     return pl.pallas_call(
-        functools.partial(settle_kernel, begin=begin, count=count, chained=chained),
-        out_shape=(jax.ShapeDtypeStruct(shape, BF16), TOKEN),
-        in_specs=[SMEM, VMEM] + [HBM] * chained + [ANY] * (count + 1),
-        out_specs=(HBM, SMEM),
+        functools.partial(
+            settle_kernel, begin=begin, old_begin=old_begin, parts=tuple(parts), arrivals=len(arrived)
+        ),
+        out_shape=(
+            jax.ShapeDtypeStruct((2, planes, modes, rows, cols), BF16),
+            jax.ShapeDtypeStruct(shape, BF16),
+            TOKEN,
+        ),
+        in_specs=[SMEM, VMEM] + [HBM] * chained + [ANY] * len(pieces) + [VMEM] * len(arrived),
+        out_specs=(ANY, HBM, SMEM),
         scratch_shapes=[
-            pltpu.VMEM((2, rows, planes, modes, cols), BF16),
-            pltpu.VMEM((2, planes, modes, rows, cols), BF16),
-            pltpu.SemaphoreType.DMA((count + 3,)),
+            pltpu.VMEM((2, rows, planes, 2 * modes, cols), BF16),
+            pltpu.VMEM((2, planes, 2 * modes, rows, cols), BF16),
+            pltpu.SemaphoreType.DMA((len(pieces) + 1,)),
+            pltpu.SemaphoreType.DMA((2, 2)),
         ],
-        input_output_aliases={2: 0} if chained else {},
+        input_output_aliases={2: 1} if chained else {},
         compiler_params=params(10),
         cost_estimate=COST,
         name="settle",
-    )(pos, turn, *([result] if chained else []), *blocks, other)
-
-
-SIZES = (1, 1, 2, 2, 2)
-
-
-def chunk_rows(half):
-    unit = half // 8
-    return [n * unit for n in SIZES]
+    )(pos, turn, *given)
+
+
+def last_kernel(pos, result, arrived, out, sems, *, begin):
+    for copy in put(out, arrived, pos[0], 1 - pos[2], begin, sems):
+        copy.wait()
+
+
+def last(pos, result, arrived, begin):
+    return pl.pallas_call(
+        functools.partial(last_kernel, begin=begin),
+        out_shape=jax.ShapeDtypeStruct(result.shape, BF16),
+        in_specs=[SMEM, HBM, VMEM],
+        out_specs=HBM,
+        scratch_shapes=[pltpu.SemaphoreType.DMA((2,))],
+        input_output_aliases={1: 0},
+        compiler_params=params(6),
+        cost_estimate=COST,
+        name="settle_last",
+    )(pos, result, arrived)
+
+
+SIZES = (1, 1, 2, 2, 1, 1)
+GROUPS = ((0,), (1, 2, 3, 4, 5))
+ENDS = ((0, 1), (2,), (3,), (4, 5))
+EARLY = (1,)
+
+
+def chunk_rows(quarter):
+    return [n * (quarter // 8) for n in SIZES]
 
 
 ORDER = (
     ("T", 0), ("T", 1), ("R", 0), ("R", 1), ("S", 0), ("R", 2), ("S", 1), ("P", 0),
-    ("R", 3), ("S", 2), ("P", 1), ("C", 0), ("R", 4), ("S", 3), ("P", 2), ("C", 1), ("F", 0),
-    ("S", 4), ("P", 3), ("C", 2), ("F", 1), ("P", 4), ("C", 3), ("F", 2), ("C", 4), ("F", 3), ("F", 4),
+    ("R", 3), ("S", 2), ("P", 1), ("C", 0), ("R", 4), ("S", 3), ("P", 2), ("C", 1), ("R", 5),
+    ("S", 4), ("P", 3), ("C", 2), ("F", 0), ("S", 5), ("P", 4), ("C", 3), ("F", 1), ("P", 5), ("C", 4),
+    ("F", 2), ("C", 5), ("F", 3),
 )
 
 
@@ -392,17 +462,16 @@
 
 def on_device(field, diffusion, joule, basis, quad_weight, base_conductivity, thermal_slope):
     planes, modes, size, cols = field.shape
-    half = size // 2
-    spaces, count = lax.axis_size("space"), lax.axis_size("modes")
-    side = lax.axis_index("space") % 2
-    me = lax.axis_index("modes")
-    pos = jnp.stack([side, me]).astype(jnp.int32)
+    half, quarter = size // 2, size // 4
+    spaces, devices = lax.axis_size("space"), lax.axis_size("modes")
+    chips = devices // 2
+    pos = jnp.stack([lax.axis_index("space") % 2, lax.axis_index("modes") // 2, lax.axis_index("modes") % 2])
+    pos = pos.astype(jnp.int32)
 
     swap = [(i, i ^ 1) for i in range(spaces)]
     ahead = [(i, i + 4 * (i % 2) - 2) for i in range(spaces)]
     ahead = [(i, j) for i, j in ahead if 0 <= j < spaces]
     back = [(j, i) for i, j in ahead]
-
     beyond = [(i, i - 1 if i % 2 == 0 else i + 1) for i in range(spaces)]
     beyond = [(i, j) for i, j in beyond if 0 <= j < spaces]
 
@@ -415,59 +484,83 @@
     def behind_of(x):
         return lax.ppermute(x, "space", back)
 
+    def by_core(x):
+        return lax.ppermute(x, "modes", [(j, j ^ 1) for j in range(devices)])
+
     def exchange(pieces):
         moved = [pieces[0]]
-        for k in range(1, count):
-            moved.append(lax.ppermute(pieces[k], "modes", [(j, j ^ k) for j in range(count)]))
+        for k in range(1, chips):
+            moved.append(lax.ppermute(pieces[k], "modes", [(j, j ^ (2 * k)) for j in range(devices)]))
         return moved
 
-    def logical(x, length, side, sent):
-        rows_back, planes_back = jnp.flip(x, 1)[:, :length], jnp.flip(x, 0)[:, :length]
-        own = jnp.where(side == 1, rows_back, planes_back)
-        send = jnp.where(side == 1, planes_back, rows_back).astype(sent)
-        return own, send
-
-    to_rows, to_modes = turns(min(modes, TILE))
+    def raw_rows(spans, pos):
+        side, core = pos[0], pos[2]
+        base, blocks = blocks_of(spans)
+        begin = (1 - core) * (quarter + base * TILE if base < 0 else quarter)
+        depth = blocks * TILE
+        starts = [jnp.where(far == 1, size - depth - begin, begin) for far in (1 - side, side)]
+        return jnp.stack(
+            [lax.dynamic_slice(field, (0, 0, start, 0), (planes, modes, depth, cols)) for start in starts]
+        )
+
+    def logical(x, length, pos, sent):
+        begin = pos[2] * quarter
+        rows_back, planes_back = (
+            lax.dynamic_slice_in_dim(y, begin, length, axis=1) for y in (jnp.flip(x, 1), jnp.flip(x, 0))
+        )
+        own = jnp.where(pos[0] == 1, rows_back, planes_back)
+        return own, jnp.where(pos[0] == 1, planes_back, rows_back).astype(sent)
+
+    def coefficients(pos):
+        length = quarter + EDGE + 1
+        length += -length % 8
+        nothing = jnp.zeros((planes, 1, cols), F32)
+        rows_back = jnp.concatenate([nothing, jnp.flip(diffusion, 1)], axis=1)
+        planes_back = jnp.concatenate([nothing, jnp.flip(diffusion, 0)], axis=1)
+        rows_back, planes_back = (
+            lax.dynamic_slice_in_dim(x, pos[2] * quarter, length, axis=1) for x in (rows_back, planes_back)
+        )
+        own_rate = jnp.where(pos[0] == 1, rows_back, planes_back)
+        send_rate = jnp.where(pos[0] == 1, planes_back, rows_back)
+        own_load, send_load = logical(joule, quarter, pos, BF16)
+        edge_rate = lax.ppermute(send_rate[:1], "space", beyond)
+        rates = ahead_of(own_rate[-1:]), across(send_rate), edge_rate
+        return own_rate, own_load, rates, across(send_load), (send_rate, send_load)
+
+    to_rows, _ = turns(min(2 * modes, TILE))
+    _, to_modes = turns(min(2 * modes, TILE))
 
     points_count = basis.shape[0]
     extra = -points_count % 32
     basis = jnp.pad(basis, ((0, extra), (0, 0)))
     basis_t = basis.T
     level = quad_weight * base_conductivity
-    spread_out = lambda v: jnp.broadcast_to(jnp.pad(v, (0, extra))[:, None], (points_count + extra, 128))
+    spread_out = lambda v: jnp.broadcast_to(jnp.pad(v, (0, extra))[:, None], (points_count + extra, LANES))
     flat, swing = spread_out(level), spread_out(level * thermal_slope)
 
-    def coefficients(side):
-        own_rate, send_rate = logical(diffusion, half + EDGE, side, F32)
-        own_load, send_load = logical(joule, half, side, BF16)
-        edge_rate = lax.ppermute(send_rate[:1], "space", beyond)
-        rates = ahead_of(own_rate[-1:]), across(send_rate), edge_rate
-        return own_rate, own_load, rates, across(send_load), (send_rate, send_load)
-
-    rows_of = chunk_rows(half)
+    rows_of = chunk_rows(quarter)
     begins = [sum(rows_of[:c]) for c in range(len(rows_of))]
-    edges = [(begin + EDGE * (begin > 0), begin + rows + EDGE) for begin, rows in zip(begins, rows_of)]
+    edges = [(begin + EDGE if begin else -EDGE, begin + rows + EDGE) for begin, rows in zip(begins, rows_of)]
+    groups = [[edges[n] for n in those] for those in GROUPS]
+    raws = [by_core(raw_rows(spans, pos)) for spans in groups]
     own, other, before, blocks, cells, home, theirs = {}, {}, {}, {}, {}, {}, {}
-    result = None
+    result, arrived, old_begin = None, (), 0
     for kind, c in ORDER:
-        begin, rows = begins[c], rows_of[c]
         if kind == "T":
             after = ()
-            if c:
-                after = (*[rates[n] for n in (1,)], basis, basis_t, flat, swing)
-            else:
-                own_rate, own_load, rates, other_load, after = coefficients(pos[0])
-            those = range(1, len(rows_of)) if c else (0,)
-            *pieces, pos = spread(pos, field, to_rows, after, [edges[n] for n in those])
-            for n in those:
+            if c == 0:
+                own_rate, own_load, rates, other_load, after = coefficients(pos)
+            elif c == 1:
+                after = (*[rates[n] for n in EARLY], basis, basis_t, flat, swing)
+            *pieces, pos = spread(pos, field, raws[c], to_rows, after, groups[c])
+            for n in GROUPS[c]:
                 send, own[n], *pieces = pieces
                 other[n], before[n] = across(send), ahead_of(own[n])
         elif kind == "R":
             if c == 0:
-                after = (before[c], *[rates[n] for n in (0, 2)])
+                after = (before[c], *[rates[n] for n in range(3) if n not in EARLY])
                 other[c], pos = relay(pos, (other[c],), after)
                 rate = jnp.concatenate([rates[0], rates[1], own_rate, rates[2]], axis=0)
-                rate = jnp.pad(rate, ((0, 0), (1, -(half + EDGE + 1) % 8), (0, 0)))
             elif c == 1:
                 other[c], other_load, pos = relay(pos, (other[c], other_load), (before[c],))
                 load = jnp.concatenate([other_load.astype(F32), own_load], axis=0)
@@ -475,17 +568,26 @@
                 other[c], pos = relay(pos, (other[c],), (before[c],))
             blocks[c] = (before[c], other[c], own[c], behind_of(other[c]))
         elif kind == "S":
-            *pieces, pos = sweep(pos, rate, blocks[c], blocks.get(c - 1, ()), begin, rows, count)
+            *pieces, pos = sweep(pos, rate, blocks[c], blocks.get(c - 1, ()), begins[c], rows_of[c], chips)
             cells[c] = exchange(pieces)
         elif kind == "P":
-            *stepped, pos = points(pos, basis, basis_t, flat, swing, load, cells[c], begin)
+            *stepped, pos = points(pos, basis, basis_t, flat, swing, load, cells[c], begins[c])
             home[c] = exchange(stepped)
         elif kind == "C":
             out, pos = collect(pos, home[c])
             theirs[c] = across(out)
         else:
-            result, pos = settle(pos, to_modes, result, home[c], theirs[c], begin, field.shape)
-    return result
+            begin, rows = begins[ENDS[c][0]], sum(rows_of[n] for n in ENDS[c])
+            pieces, parts = [], []
+            for n in ENDS[c]:
+                at = begins[n] - begin
+                pieces += [*home[n], theirs[n]]
+                parts += [(0, at, k, planes) for k in range(chips)] + [(1, at, None, 0)]
+            away, result, pos = settle(
+                pos, to_modes, result, pieces, parts, arrived, begin, old_begin, rows, field.shape
+            )
+            arrived, old_begin = (by_core(away),), begin
+    return last(pos, result, arrived[0], old_begin)
 
 
 def solution(mesh):

time: 321 us -> 380 us (1.18)
  waiting for transfers between devices: 120 us -> 169 us
  other arithmetic: 0.34 us -> 8.23 us
  starting transfers between devices: 69.1 us -> 62.3 us
  local copies, waits for them, and re-layouts: 10.6 us -> 16.9 us
    ppermute x6 -> x7, waiting for transfers between devices: 3.73 us -> 35.7 us  [ahead_of(): return lax.ppermute(x, 'space', ahead)]
    ppermute x5 -> x6, waiting for transfers between devices: 8.73 us -> 30.8 us  [behind_of(): return lax.ppermute(x, 'space', back)]
    ppermute x30 -> x18, waiting for transfers between devices: 70.1 us -> 56.1 us  [the longest x12 53.4 us: exchange(): lax.ppermute(pieces[k], 'modes', [(j, j ^ 2 * k) for j in range(devices)])]
    ppermute x30 -> x18, starting transfers between devices: 22.1 us -> 13.2 us  [the longest x12 12.3 us: exchange(): lax.ppermute(pieces[k], 'modes', [(j, j ^ 2 * k) for j in range(devices)])]
    ppermute x12 -> x14, waiting for transfers between devices: 37.7 us -> 46.6 us  [across(): return lax.ppermute(x, 'space', swap)]
    rev x0 -> x4, local copies, waits for them, and re-layouts: none -> 8.77 us  [the longest x1 3.43 us: coefficients(): rows_back = jnp.concatenate([nothing, jnp.flip(diffusion, 1)], axis=1)]
    another operation x0 -> x2, local copies, waits for them, and re-layouts: none -> 4.6 us  [raw_rows(): jnp.stack([lax.dynamic_slice(field, (0, 0, start, 0), (planes, modes, dep...]
    another operation x1 -> x3, other arithmetic: 0.08 us -> 4.47 us  [the longest x2 4.39 us: raw_rows(): jnp.stack([lax.dynamic_slice(field, (0, 0, start, 0), (planes, modes, dep...]
  transfers between devices with their start and end apart: 54 -> 46, of which waited for: 21 -> 17; matrix products, arithmetic and copies ran while one was open for 2% -> 4% of each run, Pallas kernels for 35% -> 31%
where the time goes in v8:
time: 380 us; the launch traced here: 379 us
  waiting for transfers between devices  169 us (44%)
  Pallas kernels  121 us (32%)
  starting transfers between devices  62.3 us (16%)
  local copies, waits for them, and re-layouts  16.9 us (4%)
  other arithmetic  8.23 us (2%)
    ppermute x12, waiting for transfers between devices, exchange(): lax.ppermute(pieces[k], 'modes', [(j, j ^ 2 * k) for j in range(devices)])  53.4 us
    ppermute x14, waiting for transfers between devices, across(): return lax.ppermute(x, 'space', swap)  46.6 us
    pallas_call x6, Pallas kernels, points(): pl.pallas_call(functools.partial(points_kernel, begin=begin), out_shape=t...  45.4 us
    ppermute x7, waiting for transfers between devices, ahead_of(): return lax.ppermute(x, 'space', ahead)  35.7 us
    pallas_call x6, Pallas kernels, sweep(): pl.pallas_call(functools.partial(sweep_kernel, begin=begin, count=count,...  35.7 us
    ppermute x6, waiting for transfers between devices, behind_of(): return lax.ppermute(x, 'space', back)  30.8 us
    ppermute x6, starting transfers between devices, behind_of(): return lax.ppermute(x, 'space', back)  25.6 us
    ppermute x14, starting transfers between devices, across(): return lax.ppermute(x, 'space', swap)  13.9 us
  transfers between devices with their start and end apart: 46, of which 17 were waited for; matrix products, arithmetic and copies ran while one was open for 4% of the time, Pallas kernels for 31%

profile of v8, /device:TPU:0, one launch (start us, length us, event | category | flops | bytes accessed | tf_op | source)
XLA Modules:
  0.0 378.9 jit_solution(6703044431839942680)
XLA Ops:
  0.0 2.9 dynamic-slice_bitcast_fusion.1
  2.9 2.8 pad_maximum_fusion
  9.6 2.6 rev.17
  13.0 3.4 rev.15
  24.1 4.0 %spread.2 = (bf16[12,2,64,256]{3,2,1,0:T(8,128)(2,1)}, bf16[12,2,64,256]{3,2,1,0:T(8,128)(2,1)S(1)}, s32[3]{0:T(128)S(1)}) custom-call(s32[3]{0:T(128)S(1)} %pad_add_fusion.pos, bf16[2,32,256,256]{3,2,1,0:T(8,128)(2,1)} %field.3, bf16[2,2,32,32,256]{4,3,2,1,0:T(8,128)(2,1)S(1)} %copy-done.3, bf16[2,256,256]{2,1,0:T(8,128)(2,1)S(1)} %copy-done.4, ...), custom_call_target="tpu_custom_call" | custom-call | flops 1 | bytes 1 | tf_op jit(solution)/shard_map/spread/pallas_call | solution.py:110
  28.2 3.0 collective-permute-start.3
  32.4 2.8 collective-permute-start.2
  35.6 16.7 %collective-permute-done.2.refs_0_ = f32[2,72,256]{2,1,0:T(8,128)S(1)} collective-permute-done((f32[2,72,256]{2,1,0:T(8,128)S(1)}, f32[2,72,256]{2,1,0:T(8,128)S(1)}, u32[]{:S(2)}, u32[]{:S(2)}) %collective-permute-start.2) | collective-permute-done | bytes 147488 | tf_op jit(solution)/shard_map/ppermute | solution.py:479
  52.5 7.3 %spread.3 = (bf16[8,2,64,256]{3,2,1,0:T(8,128)(2,1)S(1)}, bf16[8,2,64,256]{3,2,1,0:T(8,128)(2,1)S(1)}, bf16[16,2,64,256]{3,2,1,0:T(8,128)(2,1)S(1)}, bf16[16,2,6...) custom-call(s32[3]{0:T(128)S(1)} %get-tuple-element.92.pos, ...), custom_call_target="tpu_custom_call" | custom-call | flops 1 | bytes 1 | tf_op jit(solution)/shard_map/spread/pallas_call | solution.py:110
  65.0 29.9 %collective-permute-done.5.refs_2_ = f32[1,72,256]{2,1,0:T(8,128)S(1)} collective-permute-done((f32[1,72,256]{2,1,0:T(8,128)S(1)}, f32[1,72,256]{2,1,0:T(8,128)S(1)}, u32[]{:S(2)}, u32[]{:S(2)}) %collective-permute-start.5) | collective-permute-done | bytes 73760 | tf_op jit(solution)/shard_map/ppermute | solution.py:482
  96.0 4.0 %collective-permute-start.10 = (bf16[12,2,64,256]{3,2,1,0:T(8,128)(2,1)S(1)}, bf16[12,2,64,256]{3,2,1,0:T(8,128)(2,1)S(1)}, u32[]{:S(2)}, u32[]{:S(2)}) collective-permute-start(bf16[12,2,64,256]{3,2,1,0:T(8,128)(2,1)S(1)} %get-tuple-element.100.refs_1_.refs_5_), channel_id=1, source_target_pairs={{12,4},{0,8},{20,12},{8,16},{28,20},{16,24},{13,5},{1,9},{21,13},{... | collective-permute-start | bytes 2359304 | tf_op jit(solution)/shard_map/ppermute | solution.py:485
  102.1 3.0 collective-permute-done.8.refs_1_
  106.4 6.9 %collective-permute-done.7.refs_0_ = bf16[8,2,64,256]{3,2,1,0:T(8,128)(2,1)S(1)} collective-permute-done((bf16[8,2,64,256]{3,2,1,0:T(8,128)(2,1)S(1)}, bf16[8,2,64,256]{3,2,1,0:T(8,128)(2,1)S(1)}, u32[]{:S(2)}, u32[]{:S(2)}) %collective-permute-start.7) | collective-permute-done | bytes 524320 | tf_op jit(solution)/shard_map/ppermute | solution.py:479
  114.0 3.9 %collective-permute-done.9.refs_2_.refs_0_.refs_4_ = bf16[8,2,64,256]{3,2,1,0:T(8,128)(2,1)S(1)} collective-permute-done((bf16[8,2,64,256]{3,2,1,0:T(8,128)(2,1)S(1)}, bf16[8,2,64,256]{3,2,1,0:T(8,128)(2,1)S(1)}, u32[]{:S(2)}, u32[]{:S(2)}) %collective-permute-start.9) | collective-permute-done | bytes 524320 | tf_op jit(solution)/shard_map/ppermute | solution.py:482
  120.3 4.9 %sweep.6 = (bf16[4,4,64,256]{3,2,1,0:T(8,128)(2,1)S(1)}, bf16[4,4,64,256]{3,2,1,0:T(8,128)(2,1)S(1)}, s32[3]{0:T(128)S(1)}) custom-call(s32[3]{0:T(128)S(1)} %get-tuple-element.99.pos, f32[6,72,256]{2,1,0:T(8,128)S(1)} %pad_maximum_fusion.2.rate, bf16[12,2,64,256]{3,2,1,0:T(8,128)(2,1)S(1)} %collective-permute-done.4.refs_1_.refs_0_.refs_4_, ...), custom_call_target="tpu_custom_call" | custom-call | flops 1 | bytes 1 | tf_op jit(solution)/shard_map/sweep/pallas_call | solution.py:238
  126.4 4.6 %collective-permute-start.17 = (bf16[16,2,64,256]{3,2,1,0:T(8,128)(2,1)S(1)}, bf16[16,2,64,256]{3,2,1,0:T(8,128)(2,1)S(1)}, u32[]{:S(2)}, u32[]{:S(2)}) collective-permute-start(bf16[16,2,64,256]{3,2,1,0:T(8,128)(2,1)S(1)} %get-tuple-element.114.refs_1_.refs_5_), channel_id=1, source_target_pairs={{12,4},{0,8},{20,12},{8,16},{28,20},{16,24},{13,5},{1,9},{21,13},{... | collective-permute-start | bytes 3145736 | tf_op jit(solution)/shard_map/ppermute | solution.py:485
  131.0 3.6 collective-permute-start.13
  137.2 19.1 %collective-permute-done.13.refs_3_.refs_7_ = bf16[8,2,64,256]{3,2,1,0:T(8,128)(2,1)S(1)} collective-permute-done((bf16[8,2,64,256]{3,2,1,0:T(8,128)(2,1)S(1)}, bf16[8,2,64,256]{3,2,1,0:T(8,128)(2,1)S(1)}, u32[]{:S(2)}, u32[]{:S(2)}) %collective-permute-start.13) | collective-permute-done | bytes 524320 | tf_op jit(solution)/shard_map/ppermute | solution.py:485
  156.3 4.9 %sweep.7 = (bf16[4,4,64,256]{3,2,1,0:T(8,128)(2,1)S(1)}, bf16[4,4,64,256]{3,2,1,0:T(8,128)(2,1)S(1)}, s32[3]{0:T(128)S(1)}) custom-call(s32[3]{0:T(128)S(1)} %get-tuple-element.104.pos, f32[6,72,256]{2,1,0:T(8,128)S(1)} %pad_maximum_fusion.2.rate, bf16[8,2,64,256]{3,2,1,0:T(8,128)(2,1)S(1)} %collective-permute-done.9.refs_2_.refs_0_.refs_4_, ...), custom_call_target="tpu_custom_call" | custom-call | flops 1 | bytes 1 | tf_op jit(solution)/shard_map/sweep/pallas_call | solution.py:238
  162.8 6.0 %points.6 = (bf16[4,4,64,256]{3,2,1,0:T(8,128)(2,1)S(1)}, bf16[4,4,64,256]{3,2,1,0:T(8,128)(2,1)S(1)}, s32[3]{0:T(128)S(1)}) custom-call(s32[3]{0:T(128)S(1)} %get-tuple-element.106.pos, bf16[352,128]{1,0:T(8,128)(2,1)S(1)} %pad.13.clone.refs_1_.basis, bf16[128,352]{1,0:T(8,128)(2,1)S(1)} %pad_bitcast_fusion.refs_2_.basis_t, ...), custom_call_target="tpu_custom_call" | custom-call | flops 1 | bytes 1 | tf_op jit(solution)/shard_map/points/pallas_call | solution.py:287
  169.9 4.5 %collective-permute-start.22 = (bf16[16,2,64,256]{3,2,1,0:T(8,128)(2,1)S(1)}, bf16[16,2,64,256]{3,2,1,0:T(8,128)(2,1)S(1)}, u32[]{:S(2)}, u32[]{:S(2)}) collective-permute-start(bf16[16,2,64,256]{3,2,1,0:T(8,128)(2,1)S(1)} %get-tuple-element.125.refs_1_.refs_5_), channel_id=1, source_target_pairs={{12,4},{0,8},{20,12},{8,16},{28,20},{16,24},{13,5},{1,9},{21,13},{... | collective-permute-start | bytes 3145736 | tf_op jit(solution)/shard_map/ppermute | solution.py:485
  174.4 8.1 %sweep.8 = (bf16[8,4,64,256]{3,2,1,0:T(8,128)(2,1)S(1)}, bf16[8,4,64,256]{3,2,1,0:T(8,128)(2,1)S(1)}, s32[3]{0:T(128)S(1)}) custom-call(s32[3]{0:T(128)S(1)} %get-tuple-element.113.pos, f32[6,72,256]{2,1,0:T(8,128)S(1)} %pad_maximum_fusion.2.rate, bf16[16,2,64,256]{3,2,1,0:T(8,128)(2,1)S(1)} %collective-permute-done.12.refs_1_.refs_0_.refs_4_, ...), custom_call_target="tpu_custom_call" | custom-call | flops 1 | bytes 1 | tf_op jit(solution)/shard_map/sweep/pallas_call | solution.py:238
  185.9 6.0 %points.7 = (bf16[4,4,64,256]{3,2,1,0:T(8,128)(2,1)S(1)}, bf16[4,4,64,256]{3,2,1,0:T(8,128)(2,1)S(1)}, s32[3]{0:T(128)S(1)}) custom-call(s32[3]{0:T(128)S(1)} %get-tuple-element.115.pos, bf16[352,128]{1,0:T(8,128)(2,1)S(1)} %pad.13.clone.refs_1_.basis, bf16[128,352]{1,0:T(8,128)(2,1)S(1)} %pad_bitcast_fusion.refs_2_.basis_t, ...), custom_call_target="tpu_custom_call" | custom-call | flops 1 | bytes 1 | tf_op jit(solution)/shard_map/points/pallas_call | solution.py:287
  191.8 25.3 %collective-permute-done.19.refs_1_ = bf16[4,4,64,256]{3,2,1,0:T(8,128)(2,1)S(1)} collective-permute-done((bf16[4,4,64,256]{3,2,1,0:T(8,128)(2,1)S(1)}, bf16[4,4,64,256]{3,2,1,0:T(8,128)(2,1)S(1)}, u32[]{:S(2)}, u32[]{:S(2)}) %collective-permute-start.19) | collective-permute-done | bytes 524320 | tf_op jit(solution)/shard_map/ppermute | solution.py:493
  219.5 8.1 %sweep.9 = (bf16[8,4,64,256]{3,2,1,0:T(8,128)(2,1)S(1)}, bf16[8,4,64,256]{3,2,1,0:T(8,128)(2,1)S(1)}, s32[3]{0:T(128)S(1)}) custom-call(s32[3]{0:T(128)S(1)} %get-tuple-element.124.pos, f32[6,72,256]{2,1,0:T(8,128)S(1)} %pad_maximum_fusion.2.rate, bf16[16,2,64,256]{3,2,1,0:T(8,128)(2,1)S(1)} %collective-permute-done.16.refs_1_.refs_0_.refs_4_, ...), custom_call_target="tpu_custom_call" | custom-call | flops 1 | bytes 1 | tf_op jit(solution)/shard_map/sweep/pallas_call | solution.py:238
  227.6 2.1 collective-permute-start.28
  229.7 10.8 %points.8 = (bf16[8,4,64,256]{3,2,1,0:T(8,128)(2,1)S(1)}, bf16[8,4,64,256]{3,2,1,0:T(8,128)(2,1)S(1)}, s32[3]{0:T(128)S(1)}) custom-call(s32[3]{0:T(128)S(1)} %get-tuple-element.126.pos, bf16[352,128]{1,0:T(8,128)(2,1)S(1)} %pad.13.clone.refs_1_.basis, bf16[128,352]{1,0:T(8,128)(2,1)S(1)} %pad_bitcast_fusion.refs_2_.basis_t, ...), custom_call_target="tpu_custom_call" | custom-call | flops 1 | bytes 1 | tf_op jit(solution)/shard_map/points/pallas_call | solution.py:287
  241.9 4.8 %collective-permute-start.27 = (bf16[8,2,64,256]{3,2,1,0:T(8,128)(2,1)S(1)}, bf16[8,2,64,256]{3,2,1,0:T(8,128)(2,1)S(1)}, u32[]{:S(2)}, u32[]{:S(2)}) collective-permute-start(bf16[8,2,64,256]{3,2,1,0:T(8,128)(2,1)S(1)} %get-tuple-element.136.refs_1_.refs_5_), channel_id=1, source_target_pairs={{12,4},{0,8},{20,12},{8,16},{28,20},{16,24},{13,5},{1,9},{21,13},{... | collective-permute-start | bytes 1572872 | tf_op jit(solution)/shard_map/ppermute | solution.py:485
  253.9 4.9 %sweep.10 = (bf16[4,4,64,256]{3,2,1,0:T(8,128)(2,1)S(1)}, bf16[4,4,64,256]{3,2,1,0:T(8,128)(2,1)S(1)}, s32[3]{0:T(128)S(1)}) custom-call(s32[3]{0:T(128)S(1)} %get-tuple-element.135.pos, f32[6,72,256]{2,1,0:T(8,128)S(1)} %pad_maximum_fusion.2.rate, bf16[8,2,64,256]{3,2,1,0:T(8,128)(2,1)S(1)} %collective-permute-done.21.refs_1_.refs_0_.refs_4_, ...), custom_call_target="tpu_custom_call" | custom-call | flops 1 | bytes 1 | tf_op jit(solution)/shard_map/sweep/pallas_call | solution.py:238
  258.8 10.8 %points.9 = (bf16[8,4,64,256]{3,2,1,0:T(8,128)(2,1)S(1)}, bf16[8,4,64,256]{3,2,1,0:T(8,128)(2,1)S(1)}, s32[3]{0:T(128)S(1)}) custom-call(s32[3]{0:T(128)S(1)} %get-tuple-element.137.pos, bf16[352,128]{1,0:T(8,128)(2,1)S(1)} %pad.13.clone.refs_1_.basis, bf16[128,352]{1,0:T(8,128)(2,1)S(1)} %pad_bitcast_fusion.refs_2_.basis_t, ...), custom_call_target="tpu_custom_call" | custom-call | flops 1 | bytes 1 | tf_op jit(solution)/shard_map/points/pallas_call | solution.py:287
  269.6 2.0 collective-permute-start.34
  271.6 4.7 %collective-permute-done.29.refs_1_.refs_2_ = bf16[8,4,64,256]{3,2,1,0:T(8,128)(2,1)S(1)} collective-permute-done((bf16[8,4,64,256]{3,2,1,0:T(8,128)(2,1)S(1)}, bf16[8,4,64,256]{3,2,1,0:T(8,128)(2,1)S(1)}, u32[]{:S(2)}, u32[]{:S(2)}) %collective-permute-start.29) | collective-permute-done | bytes 1048608 | tf_op jit(solution)/shard_map/ppermute | solution.py:493
  277.7 3.3 settle.4
  281.1 4.1 %collective-permute-start.32 = (bf16[8,2,64,256]{3,2,1,0:T(8,128)(2,1)S(1)}, bf16[8,2,64,256]{3,2,1,0:T(8,128)(2,1)S(1)}, u32[]{:S(2)}, u32[]{:S(2)}) collective-permute-start(bf16[8,2,64,256]{3,2,1,0:T(8,128)(2,1)S(1)} %get-tuple-element.147.refs_1_), channel_id=1, source_target_pairs={{12,4},{0,8},{20,12},{8,16},{28,20},{16,24},{13,5},{1,9},{21,13},{... | collective-permute-start | bytes 1572872 | tf_op jit(solution)/shard_map/ppermute | solution.py:485
  285.3 11.7 %collective-permute-done.32.refs_3_ = bf16[8,2,64,256]{3,2,1,0:T(8,128)(2,1)S(1)} collective-permute-done((bf16[8,2,64,256]{3,2,1,0:T(8,128)(2,1)S(1)}, bf16[8,2,64,256]{3,2,1,0:T(8,128)(2,1)S(1)}, u32[]{:S(2)}, u32[]{:S(2)}) %collective-permute-start.32) | collective-permute-done | bytes 524320 | tf_op jit(solution)/shard_map/ppermute | solution.py:485
  297.0 4.9 %sweep.11 = (bf16[4,4,64,256]{3,2,1,0:T(8,128)(2,1)S(1)}, bf16[4,4,64,256]{3,2,1,0:T(8,128)(2,1)S(1)}, s32[3]{0:T(128)S(1)}) custom-call(s32[3]{0:T(128)S(1)} %get-tuple-element.146.pos, f32[6,72,256]{2,1,0:T(8,128)S(1)} %pad_maximum_fusion.2.rate, bf16[8,2,64,256]{3,2,1,0:T(8,128)(2,1)S(1)} %collective-permute-done.26.refs_1_.refs_0_, ...), custom_call_target="tpu_custom_call" | custom-call | flops 1 | bytes 1 | tf_op jit(solution)/shard_map/sweep/pallas_call | solution.py:238
  301.9 6.0 %points.10 = (bf16[4,4,64,256]{3,2,1,0:T(8,128)(2,1)S(1)}, bf16[4,4,64,256]{3,2,1,0:T(8,128)(2,1)S(1)}, s32[3]{0:T(128)S(1)}) custom-call(s32[3]{0:T(128)S(1)} %get-tuple-element.148.pos, bf16[352,128]{1,0:T(8,128)(2,1)S(1)} %pad.13.clone.refs_1_.basis, bf16[128,352]{1,0:T(8,128)(2,1)S(1)} %pad_bitcast_fusion.refs_2_.basis_t, ...), custom_call_target="tpu_custom_call" | custom-call | flops 1 | bytes 1 | tf_op jit(solution)/shard_map/points/pallas_call | solution.py:287
  309.1 2.3 collective-permute-start.39
  311.5 3.3 settle.5
  317.0 12.7 %collective-permute-done.37.refs_1_ = bf16[4,4,64,256]{3,2,1,0:T(8,128)(2,1)S(1)} collective-permute-done((bf16[4,4,64,256]{3,2,1,0:T(8,128)(2,1)S(1)}, bf16[4,4,64,256]{3,2,1,0:T(8,128)(2,1)S(1)}, u32[]{:S(2)}, u32[]{:S(2)}) %collective-permute-start.37) | collective-permute-done | bytes 524320 | tf_op jit(solution)/shard_map/ppermute | solution.py:493
  329.7 6.0 %points.11 = (bf16[4,4,64,256]{3,2,1,0:T(8,128)(2,1)S(1)}, bf16[4,4,64,256]{3,2,1,0:T(8,128)(2,1)S(1)}, s32[3]{0:T(128)S(1)}) custom-call(s32[3]{0:T(128)S(1)} %get-tuple-element.158.pos, bf16[352,128]{1,0:T(8,128)(2,1)S(1)} %pad.13.clone.refs_1_.basis, bf16[128,352]{1,0:T(8,128)(2,1)S(1)} %pad_bitcast_fusion.refs_2_.basis_t, ...), custom_call_target="tpu_custom_call" | custom-call | flops 1 | bytes 1 | tf_op jit(solution)/shard_map/points/pallas_call | solution.py:287
  336.2 4.6 %collective-permute-done.38.refs_1_.refs_2_ = bf16[4,4,64,256]{3,2,1,0:T(8,128)(2,1)S(1)} collective-permute-done((bf16[4,4,64,256]{3,2,1,0:T(8,128)(2,1)S(1)}, bf16[4,4,64,256]{3,2,1,0:T(8,128)(2,1)S(1)}, u32[]{:S(2)}, u32[]{:S(2)}) %collective-permute-start.38) | collective-permute-done | bytes 524320 | tf_op jit(solution)/shard_map/ppermute | solution.py:493
  342.1 3.3 settle.6
  345.6 6.1 %collective-permute-done.41.refs_1_.refs_5_ = bf16[4,4,64,256]{3,2,1,0:T(8,128)(2,1)S(1)} collective-permute-done((bf16[4,4,64,256]{3,2,1,0:T(8,128)(2,1)S(1)}, bf16[4,4,64,256]{3,2,1,0:T(8,128)(2,1)S(1)}, u32[]{:S(2)}, u32[]{:S(2)}) %collective-permute-start.41) | collective-permute-done | bytes 524320 | tf_op jit(solution)/shard_map/ppermute | solution.py:493
  353.0 7.3 %collective-permute-done.42.refs_3_ = bf16[8,2,64,256]{3,2,1,0:T(8,128)(2,1)S(1)} collective-permute-done((bf16[8,2,64,256]{3,2,1,0:T(8,128)(2,1)S(1)}, bf16[8,2,64,256]{3,2,1,0:T(8,128)(2,1)S(1)}, u32[]{:S(2)}, u32[]{:S(2)}) %collective-permute-start.42) | collective-permute-done | bytes 524320 | tf_op jit(solution)/shard_map/ppermute | solution.py:479
  360.3 10.8 %collective-permute-done.43.refs_6_ = bf16[8,2,64,256]{3,2,1,0:T(8,128)(2,1)S(1)} collective-permute-done((bf16[8,2,64,256]{3,2,1,0:T(8,128)(2,1)S(1)}, bf16[8,2,64,256]{3,2,1,0:T(8,128)(2,1)S(1)}, u32[]{:S(2)}, u32[]{:S(2)}) %collective-permute-start.43) | collective-permute-done | bytes 524320 | tf_op jit(solution)/shard_map/ppermute | solution.py:479
  371.1 3.3 settle.7
  374.5 2.6 collective-permute-done.45.arrived
  (123 shorter events, 57.3 us)
Async XLA Ops:
  5.7 46.6 %collective-permute-start.1 = (bf16[2,2,32,80,256]{4,3,2,1,0:T(8,128)(2,1)}, bf16[2,2,32,80,256]{4,3,2,1,0:T(8,128)(2,1)}, u32[]{:S(2)}, u32[]{:S(2)}) collective-permute-start(bf16[2,2,32,80,256]{4,3,2,1,0:T(8,128)(2,1)} %pad_maximum_fusion), channel_id=1, source_target_pairs={{0,1},{1,0},{2,3},{3,2},{4,5},{5,4},{6,7},{7,6},{8,9},{9,8},{10,11... | collective-permute-start | bytes 15728648 | tf_op jit(solution)/shard_map/ppermute | solution.py:488
  9.5 11.7 %collective-permute-start = (bf16[2,2,32,32,256]{4,3,2,1,0:T(8,128)(2,1)}, bf16[2,2,32,32,256]{4,3,2,1,0:T(8,128)(2,1)S(1)}, u32[]{:S(2)}, u32[]{:S(2)}) collective-permute-start(bf16[2,2,32,32,256]{4,3,2,1,0:T(8,128)(2,1)} %pad_maximum_fusion.1), channel_id=1, source_target_pairs={{0,1},{1,0},{2,3},{3,2},{4,5},{5,4},{6,7},{7,6},{8,9},{9,8},{10,11... | collective-permute-start | bytes 6291464 | tf_op jit(solution)/shard_map/ppermute | solution.py:488
  28.2 66.7 %collective-permute-start.3 = (bf16[12,2,64,256]{3,2,1,0:T(8,128)(2,1)}, bf16[12,2,64,256]{3,2,1,0:T(8,128)(2,1)S(1)}, u32[]{:S(2)}, u32[]{:S(2)}) collective-permute-start(bf16[12,2,64,256]{3,2,1,0:T(8,128)(2,1)} %get-tuple-element.94), channel_id=1, source_target_pairs={{0,4},{4,0},{8,12},{12,8},{16,20},{20,16},{24,28},{28,24},{1,5},{5... | collective-permute-start | bytes 2359304 | tf_op jit(solution)/shard_map/ppermute | solution.py:479
  31.1 63.8 %collective-permute-start.4 = (bf16[12,2,64,256]{3,2,1,0:T(8,128)(2,1)S(1)}, bf16[12,2,64,256]{3,2,1,0:T(8,128)(2,1)S(1)}, u32[]{:S(2)}, u32[]{:S(2)}) collective-permute-start(bf16[12,2,64,256]{3,2,1,0:T(8,128)(2,1)S(1)} %get-tuple-element.95.refs_2_.refs_6_), channel_id=1, source_target_pairs={{4,12},{8,0},{12,20},{16,8},{20,28},{24,16},{5,13},{9,1},{13,21},{... | collective-permute-start | bytes 2359304 | tf_op jit(solution)/shard_map/ppermute | solution.py:482
  32.4 19.9 %collective-permute-start.2 = (f32[2,72,256]{2,1,0:T(8,128)S(1)}, f32[2,72,256]{2,1,0:T(8,128)S(1)}, u32[]{:S(2)}, u32[]{:S(2)}) collective-permute-start(f32[2,72,256]{2,1,0:T(8,128)S(1)} %get-tuple-element.186.refs_0_), channel_id=1, source_target_pairs={{0,4},{4,0},{8,12},{12,8},{16,20},{20,16},{24,28},{28,24},{1,5},{5... | collective-permute-start | bytes 442376 | tf_op jit(solution)/shard_map/ppermute | solution.py:479
  59.8 65.4 %collective-permute-start.11 = (bf16[16,2,64,256]{3,2,1,0:T(8,128)(2,1)S(1)}, bf16[16,2,64,256]{3,2,1,0:T(8,128)(2,1)S(1)}, u32[]{:S(2)}, u32[]{:S(2)}) collective-permute-start(bf16[16,2,64,256]{3,2,1,0:T(8,128)(2,1)S(1)} %get-tuple-element.102), channel_id=1, source_target_pairs={{0,4},{4,0},{8,12},{12,8},{16,20},{20,16},{24,28},{28,24},{1,5},{5... | collective-permute-start | bytes 3145736 | tf_op jit(solution)/shard_map/ppermute | solution.py:479
  61.6 63.6 %collective-permute-start.12 = (bf16[16,2,64,256]{3,2,1,0:T(8,128)(2,1)S(1)}, bf16[16,2,64,256]{3,2,1,0:T(8,128)(2,1)S(1)}, u32[]{:S(2)}, u32[]{:S(2)}) collective-permute-start(bf16[16,2,64,256]{3,2,1,0:T(8,128)(2,1)S(1)} %get-tuple-element.103.refs_2_.refs_6_), channel_id=1, source_target_pairs={{4,12},{8,0},{12,20},{16,8},{20,28},{24,16},{5,13},{9,1},{13,21},{... | collective-permute-start | bytes 3145736 | tf_op jit(solution)/shard_map/ppermute | solution.py:482
  62.9 0.7 collective-permute-start.6
  63.7 31.2 %collective-permute-start.5 = (f32[1,72,256]{2,1,0:T(8,128)S(1)}, f32[1,72,256]{2,1,0:T(8,128)S(1)}, u32[]{:S(2)}, u32[]{:S(2)}) collective-permute-start(f32[1,72,256]{2,1,0:T(8,128)S(1)} %slice.8), channel_id=1, source_target_pairs={{4,12},{8,0},{12,20},{16,8},{20,28},{24,16},{5,13},{9,1},{13,21},{... | collective-permute-start | bytes 221192 | tf_op jit(solution)/shard_map/ppermute | solution.py:482
  96.0 24.3 %collective-permute-start.10 = (bf16[12,2,64,256]{3,2,1,0:T(8,128)(2,1)S(1)}, bf16[12,2,64,256]{3,2,1,0:T(8,128)(2,1)S(1)}, u32[]{:S(2)}, u32[]{:S(2)}) collective-permute-start(bf16[12,2,64,256]{3,2,1,0:T(8,128)(2,1)S(1)} %get-tuple-element.100.refs_1_.refs_5_), channel_id=1, source_target_pairs={{12,4},{0,8},{20,12},{8,16},{28,20},{16,24},{13,5},{1,9},{21,13},{... | collective-permute-start | bytes 2359304 | tf_op jit(solution)/shard_map/ppermute | solution.py:485
  100.0 5.1 %collective-permute-start.8 = (bf16[2,64,256]{2,1,0:T(8,128)(2,1)S(1)}, bf16[2,64,256]{2,1,0:T(8,128)(2,1)S(1)}, u32[]{:S(2)}, u32[]{:S(2)}) collective-permute-start(bf16[2,64,256]{2,1,0:T(8,128)(2,1)S(1)} %select_convert_fusion.refs_1_), channel_id=1, source_target_pairs={{0,4},{4,0},{8,12},{12,8},{16,20},{20,16},{24,28},{28,24},{1,5},{5... | collective-permute-start | bytes 196616 | tf_op jit(solution)/shard_map/ppermute | solution.py:479
  100.1 13.3 %collective-permute-start.7 = (bf16[8,2,64,256]{3,2,1,0:T(8,128)(2,1)S(1)}, bf16[8,2,64,256]{3,2,1,0:T(8,128)(2,1)S(1)}, u32[]{:S(2)}, u32[]{:S(2)}) collective-permute-start(bf16[8,2,64,256]{3,2,1,0:T(8,128)(2,1)S(1)} %get-tuple-element.97), channel_id=1, source_target_pairs={{0,4},{4,0},{8,12},{12,8},{16,20},{20,16},{24,28},{28,24},{1,5},{5... | collective-permute-start | bytes 1572872 | tf_op jit(solution)/shard_map/ppermute | solution.py:479
  105.1 12.8 %collective-permute-start.9 = (bf16[8,2,64,256]{3,2,1,0:T(8,128)(2,1)S(1)}, bf16[8,2,64,256]{3,2,1,0:T(8,128)(2,1)S(1)}, u32[]{:S(2)}, u32[]{:S(2)}) collective-permute-start(bf16[8,2,64,256]{3,2,1,0:T(8,128)(2,1)S(1)} %get-tuple-element.98.refs_2_.refs_6_), channel_id=1, source_target_pairs={{4,12},{8,0},{12,20},{16,8},{20,28},{24,16},{5,13},{9,1},{13,21},{... | collective-permute-start | bytes 1572872 | tf_op jit(solution)/shard_map/ppermute | solution.py:482
  113.4 55.4 %collective-permute-start.15 = (bf16[16,2,64,256]{3,2,1,0:T(8,128)(2,1)}, bf16[16,2,64,256]{3,2,1,0:T(8,128)(2,1)S(1)}, u32[]{:S(2)}, u32[]{:S(2)}) collective-permute-start(bf16[16,2,64,256]{3,2,1,0:T(8,128)(2,1)} %get-tuple-element.111), channel_id=1, source_target_pairs={{0,4},{4,0},{8,12},{12,8},{16,20},{20,16},{24,28},{28,24},{1,5},{5... | collective-permute-start | bytes 3145736 | tf_op jit(solution)/shard_map/ppermute | solution.py:479
  117.9 50.9 %collective-permute-start.16 = (bf16[16,2,64,256]{3,2,1,0:T(8,128)(2,1)}, bf16[16,2,64,256]{3,2,1,0:T(8,128)(2,1)S(1)}, u32[]{:S(2)}, u32[]{:S(2)}) collective-permute-start(bf16[16,2,64,256]{3,2,1,0:T(8,128)(2,1)} %get-tuple-element.112.refs_2_.refs_6_), channel_id=1, source_target_pairs={{4,12},{8,0},{12,20},{16,8},{20,28},{24,16},{5,13},{9,1},{13,21},{... | collective-permute-start | bytes 3145736 | tf_op jit(solution)/shard_map/ppermute | solution.py:482
  126.4 48.0 %collective-permute-start.17 = (bf16[16,2,64,256]{3,2,1,0:T(8,128)(2,1)S(1)}, bf16[16,2,64,256]{3,2,1,0:T(8,128)(2,1)S(1)}, u32[]{:S(2)}, u32[]{:S(2)}) collective-permute-start(bf16[16,2,64,256]{3,2,1,0:T(8,128)(2,1)S(1)} %get-tuple-element.114.refs_1_.refs_5_), channel_id=1, source_target_pairs={{12,4},{0,8},{20,12},{8,16},{28,20},{16,24},{13,5},{1,9},{21,13},{... | collective-permute-start | bytes 3145736 | tf_op jit(solution)/shard_map/ppermute | solution.py:485
  131.0 25.3 %collective-permute-start.13 = (bf16[8,2,64,256]{3,2,1,0:T(8,128)(2,1)S(1)}, bf16[8,2,64,256]{3,2,1,0:T(8,128)(2,1)S(1)}, u32[]{:S(2)}, u32[]{:S(2)}) collective-permute-start(bf16[8,2,64,256]{3,2,1,0:T(8,128)(2,1)S(1)} %get-tuple-element.105.refs_1_.refs_5_), channel_id=1, source_target_pairs={{12,4},{0,8},{20,12},{8,16},{28,20},{16,24},{13,5},{1,9},{21,13},{... | collective-permute-start | bytes 1572872 | tf_op jit(solution)/shard_map/ppermute | solution.py:485
  134.6 28.2 %collective-permute-start.14 = (bf16[4,4,64,256]{3,2,1,0:T(8,128)(2,1)S(1)}, bf16[4,4,64,256]{3,2,1,0:T(8,128)(2,1)S(1)}, u32[]{:S(2)}, u32[]{:S(2)}) collective-permute-start(bf16[4,4,64,256]{3,2,1,0:T(8,128)(2,1)S(1)} %get-tuple-element.109), channel_id=1, source_target_pairs={{0,2},{1,3},{2,0},{3,1},{4,6},{5,7},{6,4},{7,5},{8,10},{9,11},{10,... | collective-permute-start | bytes 1572872 | tf_op jit(solution)/shard_map/ppermute | solution.py:493
  161.2 23.4 %collective-permute-start.18 = (bf16[4,4,64,256]{3,2,1,0:T(8,128)(2,1)S(1)}, bf16[4,4,64,256]{3,2,1,0:T(8,128)(2,1)S(1)}, u32[]{:S(2)}, u32[]{:S(2)}) collective-permute-start(bf16[4,4,64,256]{3,2,1,0:T(8,128)(2,1)S(1)} %get-tuple-element.117), channel_id=1, source_target_pairs={{0,2},{1,3},{2,0},{3,1},{4,6},{5,7},{6,4},{7,5},{8,10},{9,11},{10,... | collective-permute-start | bytes 1572872 | tf_op jit(solution)/shard_map/ppermute | solution.py:493
  169.9 49.6 %collective-permute-start.22 = (bf16[16,2,64,256]{3,2,1,0:T(8,128)(2,1)S(1)}, bf16[16,2,64,256]{3,2,1,0:T(8,128)(2,1)S(1)}, u32[]{:S(2)}, u32[]{:S(2)}) collective-permute-start(bf16[16,2,64,256]{3,2,1,0:T(8,128)(2,1)S(1)} %get-tuple-element.125.refs_1_.refs_5_), channel_id=1, source_target_pairs={{12,4},{0,8},{20,12},{8,16},{28,20},{16,24},{13,5},{1,9},{21,13},{... | collective-permute-start | bytes 3145736 | tf_op jit(solution)/shard_map/ppermute | solution.py:485
  174.4 45.1 %copy-start.1 = (bf16[16,2,64,256]{3,2,1,0:T(8,128)(2,1)S(1)}, bf16[16,2,64,256]{3,2,1,0:T(8,128)(2,1)}, u32[]{:S(2)}) copy-start(bf16[16,2,64,256]{3,2,1,0:T(8,128)(2,1)} %get-tuple-element.112.refs_2_.refs_6_) | copy-start | bytes 3145732
  182.5 47.2 %collective-permute-start.23 = (bf16[8,4,64,256]{3,2,1,0:T(8,128)(2,1)S(1)}, bf16[8,4,64,256]{3,2,1,0:T(8,128)(2,1)S(1)}, u32[]{:S(2)}, u32[]{:S(2)}) collective-permute-start(bf16[8,4,64,256]{3,2,1,0:T(8,128)(2,1)S(1)} %get-tuple-element.128), channel_id=1, source_target_pairs={{0,2},{1,3},{2,0},{3,1},{4,6},{5,7},{6,4},{7,5},{8,10},{9,11},{10,... | collective-permute-start | bytes 3145736 | tf_op jit(solution)/shard_map/ppermute | solution.py:493
  183.1 34.0 %collective-permute-start.19 = (bf16[4,4,64,256]{3,2,1,0:T(8,128)(2,1)S(1)}, bf16[4,4,64,256]{3,2,1,0:T(8,128)(2,1)S(1)}, u32[]{:S(2)}, u32[]{:S(2)}) collective-permute-start(bf16[4,4,64,256]{3,2,1,0:T(8,128)(2,1)S(1)} %get-tuple-element.120), channel_id=1, source_target_pairs={{0,2},{1,3},{2,0},{3,1},{4,6},{5,7},{6,4},{7,5},{8,10},{9,11},{10,... | collective-permute-start | bytes 1572872 | tf_op jit(solution)/shard_map/ppermute | solution.py:493
  184.6 33.7 %collective-permute-start.20 = (bf16[8,2,64,256]{3,2,1,0:T(8,128)(2,1)S(1)}, bf16[8,2,64,256]{3,2,1,0:T(8,128)(2,1)S(1)}, u32[]{:S(2)}, u32[]{:S(2)}) collective-permute-start(bf16[8,2,64,256]{3,2,1,0:T(8,128)(2,1)S(1)} %get-tuple-element.122), channel_id=1, source_target_pairs={{0,4},{4,0},{8,12},{12,8},{16,20},{20,16},{24,28},{28,24},{1,5},{5... | collective-permute-start | bytes 1572872 | tf_op jit(solution)/shard_map/ppermute | solution.py:479
  184.6 33.7 %collective-permute-start.21 = (bf16[8,2,64,256]{3,2,1,0:T(8,128)(2,1)S(1)}, bf16[8,2,64,256]{3,2,1,0:T(8,128)(2,1)S(1)}, u32[]{:S(2)}, u32[]{:S(2)}) collective-permute-start(bf16[8,2,64,256]{3,2,1,0:T(8,128)(2,1)S(1)} %get-tuple-element.123.refs_2_.refs_6_), channel_id=1, source_target_pairs={{4,12},{8,0},{12,20},{16,8},{20,28},{24,16},{5,13},{9,1},{13,21},{... | collective-permute-start | bytes 1572872 | tf_op jit(solution)/shard_map/ppermute | solution.py:482
  217.1 24.8 %collective-permute-start.24 = (bf16[4,4,64,256]{3,2,1,0:T(8,128)(2,1)S(1)}, bf16[4,4,64,256]{3,2,1,0:T(8,128)(2,1)S(1)}, u32[]{:S(2)}, u32[]{:S(2)}) collective-permute-start(bf16[4,4,64,256]{3,2,1,0:T(8,128)(2,1)S(1)} %get-tuple-element.131), channel_id=1, source_target_pairs={{0,2},{1,3},{2,0},{3,1},{4,6},{5,7},{6,4},{7,5},{8,10},{9,11},{10,... | collective-permute-start | bytes 1572872 | tf_op jit(solution)/shard_map/ppermute | solution.py:493
  227.6 31.2 %collective-permute-start.28 = (bf16[8,4,64,256]{3,2,1,0:T(8,128)(2,1)S(1)}, bf16[8,4,64,256]{3,2,1,0:T(8,128)(2,1)S(1)}, u32[]{:S(2)}, u32[]{:S(2)}) collective-permute-start(bf16[8,4,64,256]{3,2,1,0:T(8,128)(2,1)S(1)} %get-tuple-element.139), channel_id=1, source_target_pairs={{0,2},{1,3},{2,0},{3,1},{4,6},{5,7},{6,4},{7,5},{8,10},{9,11},{10,... | collective-permute-start | bytes 3145736 | tf_op jit(solution)/shard_map/ppermute | solution.py:493
  240.5 35.9 %collective-permute-start.29 = (bf16[8,4,64,256]{3,2,1,0:T(8,128)(2,1)S(1)}, bf16[8,4,64,256]{3,2,1,0:T(8,128)(2,1)S(1)}, u32[]{:S(2)}, u32[]{:S(2)}) collective-permute-start(bf16[8,4,64,256]{3,2,1,0:T(8,128)(2,1)S(1)} %get-tuple-element.142), channel_id=1, source_target_pairs={{0,2},{1,3},{2,0},{3,1},{4,6},{5,7},{6,4},{7,5},{8,10},{9,11},{10,... | collective-permute-start | bytes 3145736 | tf_op jit(solution)/shard_map/ppermute | solution.py:493
  240.6 9.2 %collective-permute-start.25 = (bf16[8,2,64,256]{3,2,1,0:T(8,128)(2,1)S(1)}, bf16[8,2,64,256]{3,2,1,0:T(8,128)(2,1)S(1)}, u32[]{:S(2)}, u32[]{:S(2)}) collective-permute-start(bf16[8,2,64,256]{3,2,1,0:T(8,128)(2,1)S(1)} %get-tuple-element.133), channel_id=1, source_target_pairs={{0,4},{4,0},{8,12},{12,8},{16,20},{20,16},{24,28},{28,24},{1,5},{5... | collective-permute-start | bytes 1572872 | tf_op jit(solution)/shard_map/ppermute | solution.py:479
  240.6 11.1 %collective-permute-start.26 = (bf16[8,2,64,256]{3,2,1,0:T(8,128)(2,1)S(1)}, bf16[8,2,64,256]{3,2,1,0:T(8,128)(2,1)S(1)}, u32[]{:S(2)}, u32[]{:S(2)}) collective-permute-start(bf16[8,2,64,256]{3,2,1,0:T(8,128)(2,1)S(1)} %get-tuple-element.134.refs_2_), channel_id=1, source_target_pairs={{4,12},{8,0},{12,20},{16,8},{20,28},{24,16},{5,13},{9,1},{13,21},{... | collective-permute-start | bytes 1572872 | tf_op jit(solution)/shard_map/ppermute | solution.py:482
  241.9 11.9 %collective-permute-start.27 = (bf16[8,2,64,256]{3,2,1,0:T(8,128)(2,1)S(1)}, bf16[8,2,64,256]{3,2,1,0:T(8,128)(2,1)S(1)}, u32[]{:S(2)}, u32[]{:S(2)}) collective-permute-start(bf16[8,2,64,256]{3,2,1,0:T(8,128)(2,1)S(1)} %get-tuple-element.136.refs_1_.refs_5_), channel_id=1, source_target_pairs={{12,4},{0,8},{20,12},{8,16},{28,20},{16,24},{13,5},{1,9},{21,13},{... | collective-permute-start | bytes 1572872 | tf_op jit(solution)/shard_map/ppermute | solution.py:485
  249.8 27.8 %collective-permute-start.30 = (bf16[8,2,64,256]{3,2,1,0:T(8,128)(2,1)S(1)}, bf16[8,2,64,256]{3,2,1,0:T(8,128)(2,1)S(1)}, u32[]{:S(2)}, u32[]{:S(2)}) collective-permute-start(bf16[8,2,64,256]{3,2,1,0:T(8,128)(2,1)S(1)} %get-tuple-element.144), channel_id=1, source_target_pairs={{0,4},{4,0},{8,12},{12,8},{16,20},{20,16},{24,28},{28,24},{1,5},{5... | collective-permute-start | bytes 1572872 | tf_op jit(solution)/shard_map/ppermute | solution.py:479
  251.7 25.9 %collective-permute-start.31 = (bf16[8,2,64,256]{3,2,1,0:T(8,128)(2,1)S(1)}, bf16[8,2,64,256]{3,2,1,0:T(8,128)(2,1)S(1)}, u32[]{:S(2)}, u32[]{:S(2)}) collective-permute-start(bf16[8,2,64,256]{3,2,1,0:T(8,128)(2,1)S(1)} %get-tuple-element.145), channel_id=1, source_target_pairs={{0,4},{4,0},{8,12},{12,8},{16,20},{20,16},{24,28},{28,24},{1,5},{5... | collective-permute-start | bytes 1572872 | tf_op jit(solution)/shard_map/ppermute | solution.py:479
  253.8 23.8 %copy-start = (bf16[2,256,256]{2,1,0:T(8,128)(2,1)S(1)}, bf16[2,256,256]{2,1,0:T(8,128)(2,1)}, u32[]{:S(2)}) copy-start(bf16[2,256,256]{2,1,0:T(8,128)(2,1)} %constant.61.clone.turn) | copy-start | bytes 786436
  269.6 38.3 %collective-permute-start.34 = (bf16[8,4,64,256]{3,2,1,0:T(8,128)(2,1)S(1)}, bf16[8,4,64,256]{3,2,1,0:T(8,128)(2,1)S(1)}, u32[]{:S(2)}, u32[]{:S(2)}) collective-permute-start(bf16[8,4,64,256]{3,2,1,0:T(8,128)(2,1)S(1)} %get-tuple-element.153), channel_id=1, source_target_pairs={{0,2},{1,3},{2,0},{3,1},{4,6},{5,7},{6,4},{7,5},{8,10},{9,11},{10,... | collective-permute-start | bytes 3145736 | tf_op jit(solution)/shard_map/ppermute | solution.py:493
  277.6 33.9 %collective-permute-start.35 = (bf16[16,2,64,256]{3,2,1,0:T(8,128)(2,1)S(1)}, bf16[16,2,64,256]{3,2,1,0:T(8,128)(2,1)S(1)}, u32[]{:S(2)}, u32[]{:S(2)}) collective-permute-start(bf16[16,2,64,256]{3,2,1,0:T(8,128)(2,1)S(1)} %get-tuple-element.156), channel_id=1, source_target_pairs={{0,4},{4,0},{8,12},{12,8},{16,20},{20,16},{24,28},{28,24},{1,5},{5... | collective-permute-start | bytes 3145736 | tf_op jit(solution)/shard_map/ppermute | solution.py:479
  281.0 30.5 %collective-permute-start.36 = (bf16[2,2,32,16,256]{4,3,2,1,0:T(8,128)(2,1)S(1)}, bf16[2,2,32,16,256]{4,3,2,1,0:T(8,128)(2,1)S(1)}, u32[]{:S(2)}, u32[]{:S(2)}) collective-permute-start(bf16[2,2,32,16,256]{4,3,2,1,0:T(8,128)(2,1)S(1)} %get-tuple-element.157), channel_id=1, source_target_pairs={{0,1},{1,0},{2,3},{3,2},{4,5},{5,4},{6,7},{7,6},{8,9},{9,8},{10,11... | collective-permute-start | bytes 3145736 | tf_op jit(solution)/shard_map/ppermute | solution.py:488
  281.1 15.9 %collective-permute-start.32 = (bf16[8,2,64,256]{3,2,1,0:T(8,128)(2,1)S(1)}, bf16[8,2,64,256]{3,2,1,0:T(8,128)(2,1)S(1)}, u32[]{:S(2)}, u32[]{:S(2)}) collective-permute-start(bf16[8,2,64,256]{3,2,1,0:T(8,128)(2,1)S(1)} %get-tuple-element.147.refs_1_), channel_id=1, source_target_pairs={{12,4},{0,8},{20,12},{8,16},{28,20},{16,24},{13,5},{1,9},{21,13},{... | collective-permute-start | bytes 1572872 | tf_op jit(solution)/shard_map/ppermute | solution.py:485
  285.2 16.7 %collective-permute-start.33 = (bf16[4,4,64,256]{3,2,1,0:T(8,128)(2,1)S(1)}, bf16[4,4,64,256]{3,2,1,0:T(8,128)(2,1)S(1)}, u32[]{:S(2)}, u32[]{:S(2)}) collective-permute-start(bf16[4,4,64,256]{3,2,1,0:T(8,128)(2,1)S(1)} %get-tuple-element.150), channel_id=1, source_target_pairs={{0,2},{1,3},{2,0},{3,1},{4,6},{5,7},{6,4},{7,5},{8,10},{9,11},{10,... | collective-permute-start | bytes 1572872 | tf_op jit(solution)/shard_map/ppermute | solution.py:493
  309.1 33.0 %collective-permute-start.39 = (bf16[16,2,64,256]{3,2,1,0:T(8,128)(2,1)S(1)}, bf16[16,2,64,256]{3,2,1,0:T(8,128)(2,1)S(1)}, u32[]{:S(2)}, u32[]{:S(2)}) collective-permute-start(bf16[16,2,64,256]{3,2,1,0:T(8,128)(2,1)S(1)} %get-tuple-element.166), channel_id=1, source_target_pairs={{0,4},{4,0},{8,12},{12,8},{16,20},{20,16},{24,28},{28,24},{1,5},{5... | collective-permute-start | bytes 3145736 | tf_op jit(solution)/shard_map/ppermute | solution.py:479
  314.8 27.3 %collective-permute-start.40 = (bf16[2,2,32,16,256]{4,3,2,1,0:T(8,128)(2,1)S(1)}, bf16[2,2,32,16,256]{4,3,2,1,0:T(8,128)(2,1)S(1)}, u32[]{:S(2)}, u32[]{:S(2)}) collective-permute-start(bf16[2,2,32,16,256]{4,3,2,1,0:T(8,128)(2,1)S(1)} %get-tuple-element.167), channel_id=1, source_target_pairs={{0,1},{1,0},{2,3},{3,2},{4,5},{5,4},{6,7},{7,6},{8,9},{9,8},{10,11... | collective-permute-start | bytes 3145736 | tf_op jit(solution)/shard_map/ppermute | solution.py:488
  314.9 14.8 %collective-permute-start.37 = (bf16[4,4,64,256]{3,2,1,0:T(8,128)(2,1)S(1)}, bf16[4,4,64,256]{3,2,1,0:T(8,128)(2,1)S(1)}, u32[]{:S(2)}, u32[]{:S(2)}) collective-permute-start(bf16[4,4,64,256]{3,2,1,0:T(8,128)(2,1)S(1)} %get-tuple-element.160), channel_id=1, source_target_pairs={{0,2},{1,3},{2,0},{3,1},{4,6},{5,7},{6,4},{7,5},{8,10},{9,11},{10,... | collective-permute-start | bytes 1572872 | tf_op jit(solution)/shard_map/ppermute | solution.py:493
  315.5 25.4 %collective-permute-start.38 = (bf16[4,4,64,256]{3,2,1,0:T(8,128)(2,1)S(1)}, bf16[4,4,64,256]{3,2,1,0:T(8,128)(2,1)S(1)}, u32[]{:S(2)}, u32[]{:S(2)}) collective-permute-start(bf16[4,4,64,256]{3,2,1,0:T(8,128)(2,1)S(1)} %get-tuple-element.163), channel_id=1, source_target_pairs={{0,2},{1,3},{2,0},{3,1},{4,6},{5,7},{6,4},{7,5},{8,10},{9,11},{10,... | collective-permute-start | bytes 1572872 | tf_op jit(solution)/shard_map/ppermute | solution.py:493
  335.6 16.1 %collective-permute-start.41 = (bf16[4,4,64,256]{3,2,1,0:T(8,128)(2,1)S(1)}, bf16[4,4,64,256]{3,2,1,0:T(8,128)(2,1)S(1)}, u32[]{:S(2)}, u32[]{:S(2)}) collective-permute-start(bf16[4,4,64,256]{3,2,1,0:T(8,128)(2,1)S(1)} %get-tuple-element.170), channel_id=1, source_target_pairs={{0,2},{1,3},{2,0},{3,1},{4,6},{5,7},{6,4},{7,5},{8,10},{9,11},{10,... | collective-permute-start | bytes 1572872 | tf_op jit(solution)/shard_map/ppermute | solution.py:493
  345.4 25.7 %collective-permute-start.44 = (bf16[2,2,32,16,256]{4,3,2,1,0:T(8,128)(2,1)S(1)}, bf16[2,2,32,16,256]{4,3,2,1,0:T(8,128)(2,1)S(1)}, u32[]{:S(2)}, u32[]{:S(2)}) collective-permute-start(bf16[2,2,32,16,256]{4,3,2,1,0:T(8,128)(2,1)S(1)} %get-tuple-element.175), channel_id=1, source_target_pairs={{0,1},{1,0},{2,3},{3,2},{4,5},{5,4},{6,7},{7,6},{8,9},{9,8},{10,11... | collective-permute-start | bytes 3145736 | tf_op jit(solution)/shard_map/ppermute | solution.py:488
  345.5 14.8 %collective-permute-start.42 = (bf16[8,2,64,256]{3,2,1,0:T(8,128)(2,1)S(1)}, bf16[8,2,64,256]{3,2,1,0:T(8,128)(2,1)S(1)}, u32[]{:S(2)}, u32[]{:S(2)}) collective-permute-start(bf16[8,2,64,256]{3,2,1,0:T(8,128)(2,1)S(1)} %get-tuple-element.173), channel_id=1, source_target_pairs={{0,4},{4,0},{8,12},{12,8},{16,20},{20,16},{24,28},{28,24},{1,5},{5... | collective-permute-start | bytes 1572872 | tf_op jit(solution)/shard_map/ppermute | solution.py:479
  352.9 18.2 %collective-permute-start.43 = (bf16[8,2,64,256]{3,2,1,0:T(8,128)(2,1)S(1)}, bf16[8,2,64,256]{3,2,1,0:T(8,128)(2,1)S(1)}, u32[]{:S(2)}, u32[]{:S(2)}) collective-permute-start(bf16[8,2,64,256]{3,2,1,0:T(8,128)(2,1)S(1)} %get-tuple-element.174), channel_id=1, source_target_pairs={{0,4},{4,0},{8,12},{12,8},{16,20},{20,16},{24,28},{28,24},{1,5},{5... | collective-permute-start | bytes 1572872 | tf_op jit(solution)/shard_map/ppermute | solution.py:479
  374.4 2.7 collective-permute-start.45
  (9 other events, 77.1 us)
